TPU v7x, 32 devices: a whole 2x2x4 slice. The times are simulated.
32 devices in a mesh: groups: 2 (over y), ex: 4 (over z), ckpt: 2 (over x), dim: 2 (over core).
Axes of the slice: x: 2, y: 2, z: 4, core: 2. Of those that a mesh axis runs over, the one named last changes fastest.
Arguments:
- train_features: bfloat16 [8, 8192, 2048], P('ckpt', ('groups', 'ex'), 'dim'), parts along dimension 1, may hold values from -6 to 6
- query_features: bfloat16 [8, 2048, 2048], P('ckpt', ('groups', 'ex'), 'dim'), parts along dimension 1, may hold values from -0.5 to 0.5
- residual_weights: float32 [8, 8192], P('ckpt', ('groups', 'ex')), parts along dimension 1, may hold values from 0.05 to 1
Outputs:
- scores: float32 [1024, 8192], P(('ckpt', 'dim'), ('groups', 'ex')), parts along dimension 1
There are 2 independent parts, one for each index of `groups`. A program takes and returns all parts, laid end to end along the dimension named above; each array names one. Nothing has to cross between parts.
All inputs are finite; a program needn't handle non-finite values.
Results may differ from a plain program's by a relative error of at most 0.0003.
Values may be sent and summed in bfloat16 or wider, within the bound.
No kernel may reach another device: no remote copies, remote signals or barrier semaphores. Data moves between devices by JAX's collectives and lax.ppermute only.
A program may use at most 64 MiB of HBM per device.

v0:
```python
import jax
import jax.numpy as jnp
from jax import lax
from jax.sharding import PartitionSpec as P


def passed_along(value, axis, steps):
    count = lax.axis_size(axis)
    pairs = [(source, (source + steps) % count) for source in range(count)]
    return lax.ppermute(value, axis, pairs)


def block_scores(piece, train_features, residual_weights, scale):
    total = None
    for check in range(piece.shape[0]):
        dots = lax.dot_general(
            piece[check],
            train_features[check],
            (((1,), (1,)), ((), ())),
            preferred_element_type=jnp.float32,
        )
        term = dots * residual_weights[check][None, :]
        total = term if total is None else total + term
    return total * scale


def local(train_features, query_features, residual_weights):
    scale = 1.0 / (train_features.shape[0] * lax.axis_size("ckpt"))
    query_rows = query_features.shape[1]
    cycle_size = lax.axis_size("ex")
    position = lax.axis_index("ex")
    whole = jnp.zeros((query_rows * cycle_size, train_features.shape[1]), jnp.float32)
    first = block_scores(query_features, train_features, residual_weights, scale)
    whole = lax.dynamic_update_slice_in_dim(whole, first, position * query_rows, 0)

    def cycle_step(step, carry):
        piece, filled = carry
        piece = passed_along(piece, "ex", 1)
        owner = (position - step) % cycle_size
        block = block_scores(piece, train_features, residual_weights, scale)
        filled = lax.dynamic_update_slice_in_dim(filled, block, owner * query_rows, 0)
        return (piece, filled)

    unused, terms = lax.fori_loop(1, cycle_size, cycle_step, (query_features, whole))
    summed = lax.psum(terms, "dim")
    mine = lax.psum_scatter(summed, "ckpt", scatter_dimension=0, tiled=True)
    half_rows = mine.shape[0] // lax.axis_size("dim")
    return lax.dynamic_slice_in_dim(mine, lax.axis_index("dim") * half_rows, half_rows, 0)


def solution(mesh):
    in_specs = (
        P("ckpt", ("groups", "ex"), "dim"),
        P("ckpt", ("groups", "ex"), "dim"),
        P("ckpt", ("groups", "ex")),
    )
    out_specs = P(("ckpt", "dim"), ("groups", "ex"))
    return jax.shard_map(local, mesh=mesh, in_specs=in_specs, out_specs=out_specs, check_vma=False)
```

profile of v0, /device:TPU:0, one launch (start us, length us, event | category | flops | bytes accessed | tf_op | source)
XLA Modules:
  0.0 279.3 jit_solution(1579076721946345534)
XLA Ops:
  6.5 0.0 copy-start.2
  6.5 0.0 reduce-scatter.2.cloned.1.call-start
  6.5 3.1 %copy.17 = bf16[4,256,1024]{2,1,0:T(8,128)(2,1)} copy(bf16[4,256,1024]{2,1,0:T(8,128)(2,1)} %param.6) | data formatting | bytes 4194304
  9.6 0.0 copy-done.2
  9.7 2.5 fusion.72
  12.2 2.5 fusion.69
  14.7 2.5 fusion.75
  17.2 0.5 broadcast_in_dim.3
  17.7 2.6 fusion.66
  20.3 0.0 copy-start.1
  20.4 1.9 copy-done.1
  22.3 172.0 %while.17 = (s32[]{:T(128)}, bf16[4,256,1024]{2,1,0:T(8,128)(2,1)}, f32[1024,1024]{1,0:T(8,128)}, bf16[4,1024,1024]{2,1,0:T(8,128)(2,1)}, f32[4,1024]{1,0:T(4,12...) while((s32[]{:T(128)}, bf16[4,256,1024]{2,1,0:T(8,128)(2,1)}, ...), condition=%wide.region_1.2_spmd, body=%wide.region_0.1_spmd.sunk | while | flops 2149580800 | bytes 64012644 | solution.py:44
  22.3 3.0 %collective-permute-start = (bf16[4,256,1024]{2,1,0:T(8,128)(2,1)}, bf16[4,256,1024]{2,1,0:T(8,128)(2,1)S(1)}, u32[]{:S(2)}, u32[]{:S(2)}) collective-permute-start(bf16[4,256,1024]{2,1,0:T(8,128)(2,1)} %get-tuple-element.239), channel_id=1, source_target_pairs={{0,4},{4,8},{8,12},{12,0},{1,5},{5,9},{9,13},{13,1},{2,6},{6,10},{... | collective-permute-start | bytes 6291464 | tf_op jit(solution)/shard_map/while/body/eval_jaxpr/ppermute | solution.py:10
  25.3 47.8 %collective-permute-done = bf16[4,256,1024]{2,1,0:T(8,128)(2,1)S(1)} collective-permute-done((bf16[4,256,1024]{2,1,0:T(8,128)(2,1)}, bf16[4,256,1024]{2,1,0:T(8,128)(2,1)S(1)}, u32[]{:S(2)}, u32[]{:S(2)}) %collective-permute-start) | collective-permute-done | bytes 2097184 | tf_op jit(solution)/shard_map/while/body/eval_jaxpr/ppermute | solution.py:10
  73.2 0.0 copy-start
  73.2 1.3 copy.13
  74.5 3.1 %fusion.104 = f32[256,1024]{1,0:T(8,128)S(1)} fusion(bf16[4,1024,1024]{2,1,0:T(8,128)(2,1)} %get-tuple-element.253, bf16[4,256,1024]{2,1,0:T(8,128)(2,1)S(1)} %collective-permute-done, f32[1024]{0:T(1024)S(1)} %bitcast.119), kind=kOutput, calls=%fused_computation.18.clone.1 | convolution fusion | flops 537133056 | bytes 3674112 | tf_op jit(solution)/shard_map/while/body/eval_jaxpr/dot_general | solution.py:16
  77.6 0.4 copy-done
  77.9 0.7 fusion.103
  78.7 0.7 fusion.102
  79.4 1.8 fusion.105
  81.3 0.0 collective-permute-start
  81.3 48.8 %collective-permute-done = bf16[4,256,1024]{2,1,0:T(8,128)(2,1)S(1)} collective-permute-done((bf16[4,256,1024]{2,1,0:T(8,128)(2,1)}, bf16[4,256,1024]{2,1,0:T(8,128)(2,1)S(1)}, u32[]{:S(2)}, u32[]{:S(2)}) %collective-permute-start) | collective-permute-done | bytes 2097184 | tf_op jit(solution)/shard_map/while/body/eval_jaxpr/ppermute | solution.py:10
  130.1 0.0 copy-start
  130.1 1.3 copy.13
  131.4 3.1 %fusion.104 = f32[256,1024]{1,0:T(8,128)S(1)} fusion(bf16[4,1024,1024]{2,1,0:T(8,128)(2,1)} %get-tuple-element.253, bf16[4,256,1024]{2,1,0:T(8,128)(2,1)S(1)} %collective-permute-done, f32[1024]{0:T(1024)S(1)} %bitcast.119), kind=kOutput, calls=%fused_computation.18.clone.1 | convolution fusion | flops 537133056 | bytes 3674112 | tf_op jit(solution)/shard_map/while/body/eval_jaxpr/dot_general | solution.py:16
  134.5 0.4 copy-done
  134.9 0.7 fusion.103
  135.6 0.7 fusion.102
  136.4 1.8 fusion.105
  138.2 0.0 collective-permute-start
  138.3 47.9 %collective-permute-done = bf16[4,256,1024]{2,1,0:T(8,128)(2,1)S(1)} collective-permute-done((bf16[4,256,1024]{2,1,0:T(8,128)(2,1)}, bf16[4,256,1024]{2,1,0:T(8,128)(2,1)S(1)}, u32[]{:S(2)}, u32[]{:S(2)}) %collective-permute-start) | collective-permute-done | bytes 2097184 | tf_op jit(solution)/shard_map/while/body/eval_jaxpr/ppermute | solution.py:10
  186.1 0.0 copy-start
  186.1 1.3 copy.13
  187.5 3.1 %fusion.104 = f32[256,1024]{1,0:T(8,128)S(1)} fusion(bf16[4,1024,1024]{2,1,0:T(8,128)(2,1)} %get-tuple-element.253, bf16[4,256,1024]{2,1,0:T(8,128)(2,1)S(1)} %collective-permute-done, f32[1024]{0:T(1024)S(1)} %bitcast.119), kind=kOutput, calls=%fused_computation.18.clone.1 | convolution fusion | flops 537133056 | bytes 3674112 | tf_op jit(solution)/shard_map/while/body/eval_jaxpr/dot_general | solution.py:16
  190.6 0.4 copy-done
  190.9 0.7 fusion.103
  191.7 0.8 fusion.102
  192.4 1.9 fusion.105
  194.3 0.0 reduce-scatter.2.cloned.1.call-update
  194.3 0.0 all-reduce.2.cloned.1.call-start
  194.4 52.1 %reduce-scatter.2.cloned.1.call-done = f32[512,1024]{1,0:T(8,128)} async-done(((f32[1024,1024]{1,0:T(8,128)}), f32[512,1024]{1,0:T(8,128)}) %reduce-scatter.2.cloned.1.call-update) | async-done | bytes 2097168 | tf_op jit(solution)/shard_map/reduce_scatter | solution.py:46
  246.5 0.0 all-reduce.2.cloned.1.call-update
  246.5 23.7 %all-reduce.2.cloned.1.call-done = f32[512,1024]{1,0:T(8,128)} async-done(((f32[512,1024]{1,0:T(8,128)}), f32[512,1024]{1,0:T(8,128)}) %all-reduce.2.cloned.1.call-update) | async-done | bytes 2097168 | tf_op jit(solution)/shard_map/psum | solution.py:45
  270.2 2.3 constant_dynamic-slice_fusion
  (4 shorter events, 0.1 us)
Async XLA Ops:
  6.5 3.1 %copy-start.2 = (f32[4,1024]{1,0:T(4,128)S(1)}, f32[4,1024]{1,0:T(4,128)}, u32[]{:S(2)}) copy-start(f32[4,1024]{1,0:T(4,128)} %param.7) | copy-start | bytes 49156
  6.5 240.0 %reduce-scatter.2.cloned.1.call-start = ((), (), s32[]{:S(2)}) async-start(), calls=%async_computation.1 | async-start | bytes 6291456 | tf_op jit(solution)/shard_map/reduce_scatter | solution.py:46
  20.3 1.9 copy-start.1
  22.3 50.9 %collective-permute-start = (bf16[4,256,1024]{2,1,0:T(8,128)(2,1)}, bf16[4,256,1024]{2,1,0:T(8,128)(2,1)S(1)}, u32[]{:S(2)}, u32[]{:S(2)}) collective-permute-start(bf16[4,256,1024]{2,1,0:T(8,128)(2,1)} %get-tuple-element.239), channel_id=1, source_target_pairs={{0,4},{4,8},{8,12},{12,0},{1,5},{5,9},{9,13},{13,1},{2,6},{6,10},{... | collective-permute-start | bytes 6291464 | tf_op jit(solution)/shard_map/while/body/eval_jaxpr/ppermute | solution.py:10
  73.2 4.8 %copy-start = (bf16[4,1024,1024]{2,1,0:T(8,128)(2,1)S(1)}, bf16[4,1024,1024]{2,1,0:T(8,128)(2,1)}, u32[]{:S(2)}) copy-start(bf16[4,1024,1024]{2,1,0:T(8,128)(2,1)} %get-tuple-element.253) | copy-start | bytes 25165828 | tf_op jit(solution)/shard_map/while
  81.3 48.8 %collective-permute-start = (bf16[4,256,1024]{2,1,0:T(8,128)(2,1)}, bf16[4,256,1024]{2,1,0:T(8,128)(2,1)S(1)}, u32[]{:S(2)}, u32[]{:S(2)}) collective-permute-start(bf16[4,256,1024]{2,1,0:T(8,128)(2,1)} %get-tuple-element.239), channel_id=1, source_target_pairs={{0,4},{4,8},{8,12},{12,0},{1,5},{5,9},{9,13},{13,1},{2,6},{6,10},{... | collective-permute-start | bytes 6291464 | tf_op jit(solution)/shard_map/while/body/eval_jaxpr/ppermute | solution.py:10
  130.1 4.8 %copy-start = (bf16[4,1024,1024]{2,1,0:T(8,128)(2,1)S(1)}, bf16[4,1024,1024]{2,1,0:T(8,128)(2,1)}, u32[]{:S(2)}) copy-start(bf16[4,1024,1024]{2,1,0:T(8,128)(2,1)} %get-tuple-element.253) | copy-start | bytes 25165828 | tf_op jit(solution)/shard_map/while
  138.2 47.9 %collective-permute-start = (bf16[4,256,1024]{2,1,0:T(8,128)(2,1)}, bf16[4,256,1024]{2,1,0:T(8,128)(2,1)S(1)}, u32[]{:S(2)}, u32[]{:S(2)}) collective-permute-start(bf16[4,256,1024]{2,1,0:T(8,128)(2,1)} %get-tuple-element.239), channel_id=1, source_target_pairs={{0,4},{4,8},{8,12},{12,0},{1,5},{5,9},{9,13},{13,1},{2,6},{6,10},{... | collective-permute-start | bytes 6291464 | tf_op jit(solution)/shard_map/while/body/eval_jaxpr/ppermute | solution.py:10
  186.1 4.8 %copy-start = (bf16[4,1024,1024]{2,1,0:T(8,128)(2,1)S(1)}, bf16[4,1024,1024]{2,1,0:T(8,128)(2,1)}, u32[]{:S(2)}) copy-start(bf16[4,1024,1024]{2,1,0:T(8,128)(2,1)} %get-tuple-element.253) | copy-start | bytes 25165828 | tf_op jit(solution)/shard_map/while
  194.3 75.9 %all-reduce.2.cloned.1.call-start = ((), (), s32[]{:S(2)}) async-start(), calls=%async_computation.2 | async-start | bytes 4194304 | tf_op jit(solution)/shard_map/psum | solution.py:45
Sparse Core Ops, SparseCore 0:
  194.5 51.9 reduce-scatter.1
  248.9 21.2 all-reduce.1
where the time goes:
time: 280 us; the launch traced here: 279 us
  waiting for transfers between devices  220 us (79%)
  matrix products  29.4 us (10%)
  between operations  13.5 us (5%)
  local copies, waits for them, and re-layouts  12.9 us (5%)
  starting transfers between devices  3.08 us (1%)
    ppermute x3, waiting for transfers between devices, passed_along(): return lax.ppermute(value, axis, pairs)  145 us
    reduce_scatter x1, waiting for transfers between devices, local(): mine = lax.psum_scatter(summed, 'ckpt', scatter_dimension=0, tiled=True)  52.1 us
    dot_general x16, matrix products, block_scores(): lax.dot_general(piece[check], train_features[check], (((1,), (1,)), ((),...  29.4 us
    psum x1, waiting for transfers between devices, local(): summed = lax.psum(terms, 'dim')  23.7 us
  transfers between devices with their start and end apart: 5, of which 5 were waited for; matrix products, arithmetic and copies ran while one was open for 0% of the time, Pallas kernels for 0%

commit v1 on v0

v1 whole, which is shorter than its diff:
```python
import jax
import jax.numpy as jnp
from jax import lax
from jax.sharding import PartitionSpec as P

PLACE = ("ex", "ckpt", "dim")


def block_scores(piece, train_features, residual_weights, scale):
    total = None
    for check in range(piece.shape[0]):
        dots = lax.dot_general(
            piece[check],
            train_features[check],
            (((1,), (1,)), ((), ())),
            preferred_element_type=jnp.float32,
        )
        term = dots * residual_weights[check][None, :]
        total = term if total is None else total + term
    return total * scale


def summed_at_owner(partial, owners):
    ckpts, dims = lax.axis_size("ckpt"), lax.axis_size("dim")

    def index(z, x, c):
        return (z * ckpts + x) * dims + c

    total = partial
    for away in range(1, dims):
        pairs = []
        for z, owner in enumerate(owners):
            if owner is not None:
                for x in range(ckpts):
                    pairs.append((index(z, x, (owner[1] + away) % dims), index(z, x, owner[1])))
        total = total + lax.ppermute(partial, PLACE, pairs)
    whole = total
    for away in range(1, ckpts):
        pairs = []
        for z, owner in enumerate(owners):
            if owner is not None:
                pairs.append((index(z, (owner[0] + away) % ckpts, owner[1]), index(z, *owner)))
        whole = whole + lax.ppermute(total, PLACE, pairs)
    return whole


def local(train_features, query_features, residual_weights):
    planes = lax.axis_size("ex")
    ckpts, dims = lax.axis_size("ckpt"), lax.axis_size("dim")
    z = lax.axis_index("ex")
    place = lax.axis_index("ckpt") * dims + lax.axis_index("dim")
    scale = 1.0 / (train_features.shape[0] * ckpts)
    rows = query_features.shape[1]
    kept = rows * planes // (ckpts * dims)
    ratio = kept // rows
    assert ratio * rows == kept
    pieces = 4 if rows % 64 == 0 else 1

    results = [[None] * pieces for unused in range(ratio)]

    def finish(found, blocks, start):
        owners = []
        for block in blocks:
            if block is None:
                owners.append(None)
            else:
                owner = block // ratio
                owners.append((owner // dims, owner % dims))
        whole = summed_at_owner(found, owners)
        numbers = jnp.array([-1 if block is None else block for block in blocks], jnp.int32)
        number = numbers[z]
        step = rows // pieces
        for j in range(ratio):
            mine = number == place * ratio + j
            for k in range(found.shape[0] // step):
                part = whole[k * step:(k + 1) * step]
                at = start // step + k
                old = results[j][at]
                results[j][at] = part if old is None else jnp.where(mine, part, old)

    def scores(piece):
        return block_scores(piece, train_features, residual_weights, scale)

    rights, lefts = [query_features], [query_features]
    for step in range(1, planes):
        right = [(s, s + 1) for s in range(step - 1, planes - 1)]
        left = [(s, s - 1) for s in range(1, planes - step + 1)]
        cut = pieces if step == planes - 1 else 1
        size = rows // cut
        new_rights, new_lefts = [], []
        for k in range(cut):
            from_left = rights[0] if cut == 1 else rights[0][:, k * size:(k + 1) * size]
            from_right = lefts[0] if cut == 1 else lefts[0][:, k * size:(k + 1) * size]
            if 2 * step > planes + 1:
                sent = jnp.where(z >= step - 1, from_left, from_right)
                got = lax.ppermute(sent, "ex", right + left)
                new_rights.append(got)
                new_lefts.append(got)
            else:
                new_rights.append(lax.ppermute(from_left, "ex", right))
                new_lefts.append(lax.ppermute(from_right, "ex", left))
        if step == 1:
            finish(scores(query_features), list(range(planes)), 0)
        for k in range(cut):
            blocks_right = [s - step if s >= step else None for s in range(planes)]
            blocks_left = [s + step if s + step < planes else None for s in range(planes)]
            if 2 * step >= planes:
                got = jnp.where(z >= step, new_rights[k], new_lefts[k])
                both = [a if a is not None else b for a, b in zip(blocks_right, blocks_left)]
                finish(scores(got), both, k * size)
            else:
                finish(scores(new_rights[k]), blocks_right, k * size)
                finish(scores(new_lefts[k]), blocks_left, k * size)
        rights, lefts = new_rights, new_lefts
    return jnp.concatenate([part for block in results for part in block], axis=0)


def solution(mesh):
    in_specs = (
        P("ckpt", ("groups", "ex"), "dim"),
        P("ckpt", ("groups", "ex"), "dim"),
        P("ckpt", ("groups", "ex")),
    )
    out_specs = P(("ckpt", "dim"), ("groups", "ex"))
    return jax.shard_map(local, mesh=mesh, in_specs=in_specs, out_specs=out_specs, check_vma=False)
```

time: 280 us -> 218 us (0.78); the launches traced: 279 us -> 214 us
  waiting for transfers between devices: 220 us -> 102 us
  starting transfers between devices: 3.08 us -> 43.6 us
  other arithmetic: 0 us -> 17.7 us
  matrix products: 29.4 us -> 41.9 us
  between operations: 13.5 us -> 3.12 us
  local copies, waits for them, and re-layouts: 12.9 us -> 5.85 us
    reduce_scatter x1 -> x0, waiting for transfers between devices: 52.1 us -> none  [local(): mine = lax.psum_scatter(summed, 'ckpt', scatter_dimension=0, tiled=True)]
    ppermute x3 -> x24, waiting for transfers between devices: 145 us -> 102 us  [the longest x2 59.1 us: local(): new_lefts.append(lax.ppermute(from_right, 'ex', left))]
    ppermute x3 -> x24, starting transfers between devices: 3.03 us -> 43.6 us  [the longest x8 15.5 us: summed_at_owner(): total = total + lax.ppermute(partial, PLACE, pairs)]
    psum x1 -> x0, waiting for transfers between devices: 23.7 us -> none  [local(): summed = lax.psum(terms, 'dim')]
    add x0 -> x12, other arithmetic: none -> 12.8 us  [the longest x8 9.65 us: summed_at_owner(): total = total + lax.ppermute(partial, PLACE, pairs)]
    dot_general x16 -> x32, matrix products: 29.4 us -> 41.9 us  [block_scores(): lax.dot_general(piece[check], train_features[check], (((1,), (1,)), ((),...]
    while x9 -> x0, local copies, waits for them, and re-layouts: 5.04 us -> none
    select_n x0 -> x4, other arithmetic: none -> 3.79 us  [the longest x2 1.83 us: finish(): results[j][at] = part if old is None else jnp.where(mine, part, old)]
  transfers between devices with their start and end apart: 5 -> 24, of which waited for: 5 -> 5; matrix products, arithmetic and copies ran while one was open for 0% -> 29% of each run, Pallas kernels for 0% -> 0%
where the time goes in v1:
time: 218 us; the launch traced here: 214 us
  waiting for transfers between devices  102 us (47%)
  starting transfers between devices  43.6 us (20%)
  matrix products  41.9 us (19%)
  other arithmetic  17.7 us (8%)
  local copies, waits for them, and re-layouts  5.85 us (3%)
  between operations  3.12 us (1%)
    ppermute x2, waiting for transfers between devices, local(): new_lefts.append(lax.ppermute(from_right, 'ex', left))  59.1 us
    ppermute x4, waiting for transfers between devices, local(): got = lax.ppermute(sent, 'ex', right + left)  42.3 us
    dot_general x32, matrix products, block_scores(): lax.dot_general(piece[check], train_features[check], (((1,), (1,)), ((),...  41.9 us
    ppermute x8, starting transfers between devices, summed_at_owner(): total = total + lax.ppermute(partial, PLACE, pairs)  15.5 us
    ppermute x8, starting transfers between devices, summed_at_owner(): whole = whole + lax.ppermute(total, PLACE, pairs)  11.3 us
    add x8, other arithmetic, summed_at_owner(): total = total + lax.ppermute(partial, PLACE, pairs)  9.65 us
    ppermute x2, starting transfers between devices, local(): new_rights.append(lax.ppermute(from_left, 'ex', right))  8.96 us
    ppermute x4, starting transfers between devices, local(): got = lax.ppermute(sent, 'ex', right + left)  5.33 us
  transfers between devices with their start and end apart: 24, of which 5 were waited for; matrix products, arithmetic and copies ran while one was open for 29% of the time, Pallas kernels for 0%

profile of v1, /device:TPU:0, one launch (start us, length us, event | category | flops | bytes accessed | tf_op | source)
XLA Modules:
  0.0 213.7 jit_solution(4756636441053509404)
XLA Ops:
  0.0 1.3 collective-permute-start.2
  1.3 6.9 %collective-permute-start = (bf16[4,256,1024]{2,1,0:T(8,128)(2,1)}, bf16[4,256,1024]{2,1,0:T(8,128)(2,1)}, u32[]{:S(2)}, u32[]{:S(2)}) collective-permute-start(bf16[4,256,1024]{2,1,0:T(8,128)(2,1)} %param.11), channel_id=1, source_target_pairs={{0,4},{4,8},{8,12},{1,5},{5,9},{9,13},{2,6},{6,10},{10,14},{3,7},{... | collective-permute-start | bytes 6291464 | tf_op jit(solution)/shard_map/ppermute | solution.py:100
  9.1 2.6 %fusion.133 = f32[256,1024]{1,0:T(8,128)S(1)} fusion(bf16[4,256,1024]{2,1,0:T(8,128)(2,1)} %param.11, f32[1024]{0:T(1024)S(1)} %bitcast.310, bf16[4,1024,1024]{2,1,0:T(8,128)(2,1)} %param.10), kind=kOutput, calls=%fused_computation.88 | convolution fusion | flops 537133056 | bytes 3674112 | tf_op jit(solution)/shard_map/dot_general | solution.py:12
  11.8 3.0 %fusion.157 = f32[256,1024]{1,0:T(8,128)S(1)} fusion(bf16[4,256,1024]{2,1,0:T(8,128)(2,1)} %param.11, f32[1024]{0:T(1024)S(1)} %bitcast.326, bf16[4,1024,1024]{2,1,0:T(8,128)(2,1)} %param.10), kind=kOutput, calls=%fused_computation.96 | convolution fusion | flops 537133056 | bytes 3674112 | tf_op jit(solution)/shard_map/dot_general | solution.py:12
  14.8 1.8 fusion.145
  16.6 1.9 fusion.121
  18.5 1.3 collective-permute-start.13
  19.8 31.1 %collective-permute-done.2 = bf16[4,256,1024]{2,1,0:T(8,128)(2,1)} collective-permute-done((bf16[4,256,1024]{2,1,0:T(8,128)(2,1)}, bf16[4,256,1024]{2,1,0:T(8,128)(2,1)}, u32[]{:S(2)}, u32[]{:S(2)}) %collective-permute-start.2) | collective-permute-done | bytes 2097184 | tf_op jit(solution)/shard_map/ppermute | solution.py:101
  50.9 1.8 fusion.151
  52.7 1.8 fusion.139
  54.5 1.8 fusion.127
  56.3 2.9 %fusion.91 = f32[256,1024]{1,0:T(8,128)} fusion(f32[256,1024]{1,0:T(8,128)S(1)} %fusion.151, f32[256,1024]{1,0:T(8,128)S(1)} %fusion.139, f32[256,1024]{1,0:T(8,128)S(1)} %fusion.127, bf16[4,256,1024]{2,1,0:T(8,128)(2,1)} %collective-permute-done.2, f32[1024]{0:T(1024)S(1)} %bitcast.303, bf16[4,1024,1024]{2,1,0:T(8,128)(2,1)S(1)} %copy-done), kind=kOutput, calls=%fused_computation.74 | convolution fusion | flops 538181632 | bytes 6819840 | tf_op jit(solution)/shard_map/dot_general | solution.py:12
  59.1 2.3 %collective-permute-start.9 = (f32[256,1024]{1,0:T(8,128)}, f32[256,1024]{1,0:T(8,128)}, u32[]{:S(2)}, u32[]{:S(2)}) collective-permute-start(f32[256,1024]{1,0:T(8,128)} %fusion.91), channel_id=1, source_target_pairs={{0,1},{2,3},{5,4},{7,6},{8,9},{10,11},{16,17},{18,19},{21,20},{23,... | collective-permute-start | bytes 3145736 | tf_op jit(solution)/shard_map/ppermute | solution.py:36
  61.4 1.3 collective-permute-start.3
  62.7 2.0 collective-permute-start.1
  64.7 1.8 fusion.154
  66.5 1.8 fusion.142
  68.3 1.8 fusion.130
  70.1 2.9 %fusion.106 = f32[256,1024]{1,0:T(8,128)} fusion(f32[256,1024]{1,0:T(8,128)S(1)} %fusion.154, f32[256,1024]{1,0:T(8,128)S(1)} %fusion.142, f32[256,1024]{1,0:T(8,128)S(1)} %fusion.130, bf16[4,256,1024]{2,1,0:T(8,128)(2,1)} %collective-permute-done, f32[1024]{0:T(1024)S(1)} %bitcast.304, bf16[4,1024,1024]{2,1,0:T(8,128)(2,1)S(1)} %copy-done), kind=kOutput, calls=%fused_computation.79 | convolution fusion | flops 538181632 | bytes 6819840 | tf_op jit(solution)/shard_map/dot_general | solution.py:12
  73.1 1.6 collective-permute-start.11
  74.7 1.9 add.157
  76.6 1.4 collective-permute-start.14
  78.0 1.7 add.147
  80.6 2.4 %add.152 = f32[256,1024]{1,0:T(8,128)S(1)} add(f32[256,1024]{1,0:T(8,128)} %fusion.106, f32[256,1024]{1,0:T(8,128)} %collective-permute-done.11) | non-fusion elementwise | flops 262144 | bytes 3145728 | tf_op jit(solution)/shard_map/add | solution.py:36
  83.8 28.1 %collective-permute-done.3 = bf16[4,256,1024]{2,1,0:T(8,128)(2,1)S(1)} collective-permute-done((bf16[4,256,1024]{2,1,0:T(8,128)(2,1)}, bf16[4,256,1024]{2,1,0:T(8,128)(2,1)S(1)}, u32[]{:S(2)}, u32[]{:S(2)}) %collective-permute-start.3) | collective-permute-done | bytes 2097184 | tf_op jit(solution)/shard_map/ppermute | solution.py:101
  113.6 1.7 slice_select_fusion.3
  115.4 1.5 collective-permute-start.4
  117.6 1.3 collective-permute-start.21
  119.7 12.2 %collective-permute-done.4 = bf16[4,64,1024]{2,1,0:T(8,128)(2,1)S(1)} collective-permute-done((bf16[4,64,1024]{2,1,0:T(8,128)(2,1)S(1)}, bf16[4,64,1024]{2,1,0:T(8,128)(2,1)S(1)}, u32[]{:S(2)}, u32[]{:S(2)}) %collective-permute-start.4) | collective-permute-done | bytes 524320 | tf_op jit(solution)/shard_map/ppermute | solution.py:96
  132.0 1.3 collective-permute-start.18
  135.6 18.4 %collective-permute-done.18 = bf16[4,64,1024]{2,1,0:T(8,128)(2,1)S(1)} collective-permute-done((bf16[4,64,1024]{2,1,0:T(8,128)(2,1)S(1)}, bf16[4,64,1024]{2,1,0:T(8,128)(2,1)S(1)}, u32[]{:S(2)}, u32[]{:S(2)}) %collective-permute-start.18) | collective-permute-done | bytes 524320 | tf_op jit(solution)/shard_map/ppermute | solution.py:96
  153.9 1.3 collective-permute-start.15
  157.5 11.7 %collective-permute-done.15 = bf16[4,64,1024]{2,1,0:T(8,128)(2,1)S(1)} collective-permute-done((bf16[4,64,1024]{2,1,0:T(8,128)(2,1)S(1)}, bf16[4,64,1024]{2,1,0:T(8,128)(2,1)S(1)}, u32[]{:S(2)}, u32[]{:S(2)}) %collective-permute-start.15) | collective-permute-done | bytes 524320 | tf_op jit(solution)/shard_map/ppermute | solution.py:96
  169.2 1.3 collective-permute-start.7
  175.2 3.1 %collective-permute-start.19 = (f32[64,1024]{1,0:T(8,128)S(1)}, f32[64,1024]{1,0:T(8,128)S(1)}, u32[]{:S(2)}, u32[]{:S(2)}) collective-permute-start(f32[64,1024]{1,0:T(8,128)S(1)} %fusion.250), channel_id=1, source_target_pairs={{0,1},{2,3},{13,12},{15,14},{16,17},{18,19},{29,28},{31,30}} | collective-permute-start | bytes 786440 | tf_op jit(solution)/shard_map/ppermute | solution.py:36
  179.2 4.1 %collective-permute-start.8 = (f32[256,1024]{1,0:T(8,128)S(1)}, f32[256,1024]{1,0:T(8,128)}, u32[]{:S(2)}, u32[]{:S(2)}) collective-permute-start(f32[256,1024]{1,0:T(8,128)S(1)} %add.142), channel_id=1, source_target_pairs={{0,2},{5,7},{10,8},{15,13},{16,18},{21,23},{26,24},{31,29}} | collective-permute-start | bytes 3145736 | tf_op jit(solution)/shard_map/ppermute | solution.py:43
  185.0 2.0 collective-permute-start.5
  187.0 1.3 collective-permute-start.16
  188.3 1.5 fusion.253
  189.8 2.6 %collective-permute-start.22 = (f32[64,1024]{1,0:T(8,128)}, f32[64,1024]{1,0:T(8,128)}, u32[]{:S(2)}, u32[]{:S(2)}) collective-permute-start(f32[64,1024]{1,0:T(8,128)} %fusion.253), channel_id=1, source_target_pairs={{0,1},{2,3},{13,12},{15,14},{16,17},{18,19},{29,28},{31,30}} | collective-permute-start | bytes 786440 | tf_op jit(solution)/shard_map/ppermute | solution.py:36
  193.9 1.4 collective-permute-start.20
  196.2 1.4 collective-permute-start.17
  202.7 1.5 add.158
  204.4 1.1 copy-done.4
  207.6 1.1 add.172
  209.4 1.4 add.143
  210.8 1.5 fusion.304
  212.6 1.1 pad_maximum_fusion
  (89 shorter events, 25.8 us)
Async XLA Ops:
  0.0 50.9 %collective-permute-start.2 = (bf16[4,256,1024]{2,1,0:T(8,128)(2,1)}, bf16[4,256,1024]{2,1,0:T(8,128)(2,1)}, u32[]{:S(2)}, u32[]{:S(2)}) collective-permute-start(bf16[4,256,1024]{2,1,0:T(8,128)(2,1)} %param.11), channel_id=1, source_target_pairs={{4,0},{8,4},{12,8},{5,1},{9,5},{13,9},{6,2},{10,6},{14,10},{7,3},{... | collective-permute-start | bytes 6291464 | tf_op jit(solution)/shard_map/ppermute | solution.py:101
  1.3 61.4 %collective-permute-start = (bf16[4,256,1024]{2,1,0:T(8,128)(2,1)}, bf16[4,256,1024]{2,1,0:T(8,128)(2,1)}, u32[]{:S(2)}, u32[]{:S(2)}) collective-permute-start(bf16[4,256,1024]{2,1,0:T(8,128)(2,1)} %param.11), channel_id=1, source_target_pairs={{0,4},{4,8},{8,12},{1,5},{5,9},{9,13},{2,6},{6,10},{10,14},{3,7},{... | collective-permute-start | bytes 6291464 | tf_op jit(solution)/shard_map/ppermute | solution.py:100
  9.1 5.7 %copy-start = (bf16[4,1024,1024]{2,1,0:T(8,128)(2,1)S(1)}, bf16[4,1024,1024]{2,1,0:T(8,128)(2,1)}, u32[]{:S(2)}) copy-start(bf16[4,1024,1024]{2,1,0:T(8,128)(2,1)} %param.10) | copy-start | bytes 25165828
  18.5 34.2 %copy-start.5 = (f32[256,1024]{1,0:T(8,128)}, f32[256,1024]{1,0:T(8,128)S(1)}, u32[]{:S(2)}) copy-start(f32[256,1024]{1,0:T(8,128)S(1)} %fusion.121) | copy-start | bytes 3145732
  18.5 56.2 %collective-permute-start.13 = (f32[256,1024]{1,0:T(8,128)S(1)}, f32[256,1024]{1,0:T(8,128)}, u32[]{:S(2)}, u32[]{:S(2)}) collective-permute-start(f32[256,1024]{1,0:T(8,128)S(1)} %fusion.121), channel_id=1, source_target_pairs={{1,0},{3,2},{4,5},{6,7},{9,8},{11,10},{12,13},{14,15},{17,16},{19,... | collective-permute-start | bytes 3145736 | tf_op jit(solution)/shard_map/ppermute | solution.py:36
  59.1 18.9 %collective-permute-start.9 = (f32[256,1024]{1,0:T(8,128)}, f32[256,1024]{1,0:T(8,128)}, u32[]{:S(2)}, u32[]{:S(2)}) collective-permute-start(f32[256,1024]{1,0:T(8,128)} %fusion.91), channel_id=1, source_target_pairs={{0,1},{2,3},{5,4},{7,6},{8,9},{10,11},{16,17},{18,19},{21,20},{23,... | collective-permute-start | bytes 3145736 | tf_op jit(solution)/shard_map/ppermute | solution.py:36
  61.4 50.4 %collective-permute-start.3 = (bf16[4,256,1024]{2,1,0:T(8,128)(2,1)}, bf16[4,256,1024]{2,1,0:T(8,128)(2,1)S(1)}, u32[]{:S(2)}, u32[]{:S(2)}) collective-permute-start(bf16[4,256,1024]{2,1,0:T(8,128)(2,1)} %collective-permute-done.2), channel_id=1, source_target_pairs={{4,0},{8,4},{5,1},{9,5},{6,2},{10,6},{7,3},{11,7},{20,16},{24,20},... | collective-permute-start | bytes 6291464 | tf_op jit(solution)/shard_map/ppermute | solution.py:101
  62.7 49.1 %collective-permute-start.1 = (bf16[4,256,1024]{2,1,0:T(8,128)(2,1)}, bf16[4,256,1024]{2,1,0:T(8,128)(2,1)}, u32[]{:S(2)}, u32[]{:S(2)}) collective-permute-start(bf16[4,256,1024]{2,1,0:T(8,128)(2,1)} %collective-permute-done), channel_id=1, source_target_pairs={{4,8},{8,12},{5,9},{9,13},{6,10},{10,14},{7,11},{11,15},{20,24},{2... | collective-permute-start | bytes 6291464 | tf_op jit(solution)/shard_map/ppermute | solution.py:100
  73.1 7.5 %collective-permute-start.11 = (f32[256,1024]{1,0:T(8,128)}, f32[256,1024]{1,0:T(8,128)}, u32[]{:S(2)}, u32[]{:S(2)}) collective-permute-start(f32[256,1024]{1,0:T(8,128)} %fusion.106), channel_id=1, source_target_pairs={{5,4},{7,6},{8,9},{10,11},{13,12},{15,14},{21,20},{23,22},{24,25},... | collective-permute-start | bytes 3145736 | tf_op jit(solution)/shard_map/ppermute | solution.py:36
  74.7 37.4 %slice-start = ((s8[8388608]{0:T(1024)(128)(4,1)}), s8[4194304]{0:T(1024)(128)(4,1)S(1)}, s32[]{:S(2)}) async-start(s8[8388608]{0:T(1024)(128)(4,1)} %bitcast.300), calls=%async_computation | async-start | bytes 8388608
  76.6 108.4 %collective-permute-start.14 = (f32[256,1024]{1,0:T(8,128)S(1)}, f32[256,1024]{1,0:T(8,128)S(1)}, u32[]{:S(2)}, u32[]{:S(2)}) collective-permute-start(f32[256,1024]{1,0:T(8,128)S(1)} %add.157), channel_id=1, source_target_pairs={{2,0},{7,5},{8,10},{13,15},{18,16},{23,21},{24,26},{29,31}} | collective-permute-start | bytes 3145736 | tf_op jit(solution)/shard_map/ppermute | solution.py:43
  79.7 32.4 %copy-start.1 = (f32[256,1024]{1,0:T(8,128)}, f32[256,1024]{1,0:T(8,128)S(1)}, u32[]{:S(2)}) copy-start(f32[256,1024]{1,0:T(8,128)S(1)} %add.147) | copy-start | bytes 3145732
  79.7 32.4 %slice-start.1 = ((s8[8388608]{0:T(1024)(128)(4,1)}), s8[4194304]{0:T(1024)(128)(4,1)S(1)}, s32[]{:S(2)}) async-start(s8[8388608]{0:T(1024)(128)(4,1)} %bitcast.300), calls=%async_computation.1 | async-start | bytes 8388608
  79.7 114.2 %collective-permute-start.10 = (f32[256,1024]{1,0:T(8,128)S(1)}, f32[256,1024]{1,0:T(8,128)S(1)}, u32[]{:S(2)}, u32[]{:S(2)}) collective-permute-start(f32[256,1024]{1,0:T(8,128)S(1)} %add.147), channel_id=1, source_target_pairs={{3,1},{4,6},{9,11},{19,17},{20,22},{25,27}} | collective-permute-start | bytes 3145736 | tf_op jit(solution)/shard_map/ppermute | solution.py:43
  83.0 29.1 %copy-start.3 = (f32[256,1024]{1,0:T(8,128)}, f32[256,1024]{1,0:T(8,128)S(1)}, u32[]{:S(2)}) copy-start(f32[256,1024]{1,0:T(8,128)S(1)} %add.152) | copy-start | bytes 3145732
  83.0 112.2 %collective-permute-start.12 = (f32[256,1024]{1,0:T(8,128)S(1)}, f32[256,1024]{1,0:T(8,128)S(1)}, u32[]{:S(2)}, u32[]{:S(2)}) collective-permute-start(f32[256,1024]{1,0:T(8,128)S(1)} %add.152), channel_id=1, source_target_pairs={{6,4},{11,9},{12,14},{22,20},{27,25},{28,30}} | collective-permute-start | bytes 3145736 | tf_op jit(solution)/shard_map/ppermute | solution.py:43
  115.4 16.6 %collective-permute-start.4 = (bf16[4,64,1024]{2,1,0:T(8,128)(2,1)S(1)}, bf16[4,64,1024]{2,1,0:T(8,128)(2,1)S(1)}, u32[]{:S(2)}, u32[]{:S(2)}) collective-permute-start(bf16[4,64,1024]{2,1,0:T(8,128)(2,1)S(1)} %get-tuple-element.7), channel_id=1, source_target_pairs={{8,12},{4,0},{9,13},{5,1},{10,14},{6,2},{11,15},{7,3},{24,28},{20,... | collective-permute-start | bytes 1572872 | tf_op jit(solution)/shard_map/ppermute | solution.py:96
  117.6 57.6 %collective-permute-start.21 = (bf16[4,64,1024]{2,1,0:T(8,128)(2,1)S(1)}, bf16[4,64,1024]{2,1,0:T(8,128)(2,1)S(1)}, u32[]{:S(2)}, u32[]{:S(2)}) collective-permute-start(bf16[4,64,1024]{2,1,0:T(8,128)(2,1)S(1)} %get-tuple-element.8), channel_id=1, source_target_pairs={{8,12},{4,0},{9,13},{5,1},{10,14},{6,2},{11,15},{7,3},{24,28},{20,... | collective-permute-start | bytes 1572872 | tf_op jit(solution)/shard_map/ppermute | solution.py:96
  132.0 21.9 %collective-permute-start.18 = (bf16[4,64,1024]{2,1,0:T(8,128)(2,1)S(1)}, bf16[4,64,1024]{2,1,0:T(8,128)(2,1)S(1)}, u32[]{:S(2)}, u32[]{:S(2)}) collective-permute-start(bf16[4,64,1024]{2,1,0:T(8,128)(2,1)S(1)} %get-tuple-element.9), channel_id=1, source_target_pairs={{8,12},{4,0},{9,13},{5,1},{10,14},{6,2},{11,15},{7,3},{24,28},{20,... | collective-permute-start | bytes 1572872 | tf_op jit(solution)/shard_map/ppermute | solution.py:96
  153.9 15.3 %collective-permute-start.15 = (bf16[4,64,1024]{2,1,0:T(8,128)(2,1)S(1)}, bf16[4,64,1024]{2,1,0:T(8,128)(2,1)S(1)}, u32[]{:S(2)}, u32[]{:S(2)}) collective-permute-start(bf16[4,64,1024]{2,1,0:T(8,128)(2,1)S(1)} %get-tuple-element.10), channel_id=1, source_target_pairs={{8,12},{4,0},{9,13},{5,1},{10,14},{6,2},{11,15},{7,3},{24,28},{20,... | collective-permute-start | bytes 1572872 | tf_op jit(solution)/shard_map/ppermute | solution.py:96
  169.2 9.8 %collective-permute-start.7 = (f32[256,1024]{1,0:T(8,128)S(1)}, f32[256,1024]{1,0:T(8,128)S(1)}, u32[]{:S(2)}, u32[]{:S(2)}) collective-permute-start(f32[256,1024]{1,0:T(8,128)S(1)} %fusion.76), channel_id=1, source_target_pairs={{1,0},{3,2},{4,5},{6,7},{9,8},{11,10},{12,13},{14,15},{17,16},{19,... | collective-permute-start | bytes 3145736 | tf_op jit(solution)/shard_map/ppermute | solution.py:36
  175.2 11.8 %collective-permute-start.19 = (f32[64,1024]{1,0:T(8,128)S(1)}, f32[64,1024]{1,0:T(8,128)S(1)}, u32[]{:S(2)}, u32[]{:S(2)}) collective-permute-start(f32[64,1024]{1,0:T(8,128)S(1)} %fusion.250), channel_id=1, source_target_pairs={{0,1},{2,3},{13,12},{15,14},{16,17},{18,19},{29,28},{31,30}} | collective-permute-start | bytes 786440 | tf_op jit(solution)/shard_map/ppermute | solution.py:36
  179.2 30.2 %collective-permute-start.8 = (f32[256,1024]{1,0:T(8,128)S(1)}, f32[256,1024]{1,0:T(8,128)}, u32[]{:S(2)}, u32[]{:S(2)}) collective-permute-start(f32[256,1024]{1,0:T(8,128)S(1)} %add.142), channel_id=1, source_target_pairs={{0,2},{5,7},{10,8},{15,13},{16,18},{21,23},{26,24},{31,29}} | collective-permute-start | bytes 3145736 | tf_op jit(solution)/shard_map/ppermute | solution.py:43
  184.9 12.7 %copy-start.14 = (s32[4]{0:T(128)S(1)}, s32[4]{0:T(128)}, u32[]{:S(2)}) copy-start(s32[4]{0:T(128)} %constant.32.clone) | copy-start | bytes 52
  184.9 13.4 %copy-start.13 = (s32[4]{0:T(128)S(1)}, s32[4]{0:T(128)}, u32[]{:S(2)}) copy-start(s32[4]{0:T(128)} %constant.31.clone) | copy-start | bytes 52
  184.9 15.3 %copy-start.12 = (s32[4]{0:T(128)S(1)}, s32[4]{0:T(128)}, u32[]{:S(2)}) copy-start(s32[4]{0:T(128)} %constant.30.clone) | copy-start | bytes 52
  184.9 16.5 %copy-start.11 = (s32[4]{0:T(128)S(1)}, s32[4]{0:T(128)}, u32[]{:S(2)}) copy-start(s32[4]{0:T(128)} %constant.29.clone) | copy-start | bytes 52
  184.9 8.9 %copy-start.6 = (f32[256,1024]{1,0:T(8,128)}, f32[256,1024]{1,0:T(8,128)S(1)}, u32[]{:S(2)}) copy-start(f32[256,1024]{1,0:T(8,128)S(1)} %collective-permute-done.14) | copy-start | bytes 3145732
  185.0 21.0 %collective-permute-start.5 = (f32[64,1024]{1,0:T(8,128)S(1)}, f32[64,1024]{1,0:T(8,128)}, u32[]{:S(2)}, u32[]{:S(2)}) collective-permute-start(f32[64,1024]{1,0:T(8,128)S(1)} %fusion.244), channel_id=1, source_target_pairs={{0,1},{2,3},{13,12},{15,14},{16,17},{18,19},{29,28},{31,30}} | collective-permute-start | bytes 786440 | tf_op jit(solution)/shard_map/ppermute | solution.py:36
  187.0 2.8 %collective-permute-start.16 = (f32[64,1024]{1,0:T(8,128)S(1)}, f32[64,1024]{1,0:T(8,128)S(1)}, u32[]{:S(2)}, u32[]{:S(2)}) collective-permute-start(f32[64,1024]{1,0:T(8,128)S(1)} %fusion.247), channel_id=1, source_target_pairs={{0,1},{2,3},{13,12},{15,14},{16,17},{18,19},{29,28},{31,30}} | collective-permute-start | bytes 786440 | tf_op jit(solution)/shard_map/ppermute | solution.py:36
  189.8 17.8 %collective-permute-start.22 = (f32[64,1024]{1,0:T(8,128)}, f32[64,1024]{1,0:T(8,128)}, u32[]{:S(2)}, u32[]{:S(2)}) collective-permute-start(f32[64,1024]{1,0:T(8,128)} %fusion.253), channel_id=1, source_target_pairs={{0,1},{2,3},{13,12},{15,14},{16,17},{18,19},{29,28},{31,30}} | collective-permute-start | bytes 786440 | tf_op jit(solution)/shard_map/ppermute | solution.py:36
  193.1 11.1 %copy-start.2 = (f32[256,1024]{1,0:T(8,128)S(1)}, f32[256,1024]{1,0:T(8,128)}, u32[]{:S(2)}) copy-start(f32[256,1024]{1,0:T(8,128)} %copy-done.1) | copy-start | bytes 3145732
  193.9 1.4 copy-start.7
  193.9 16.9 %collective-permute-start.20 = (f32[64,1024]{1,0:T(8,128)}, f32[64,1024]{1,0:T(8,128)}, u32[]{:S(2)}, u32[]{:S(2)}) collective-permute-start(f32[64,1024]{1,0:T(8,128)} %add.167), channel_id=1, source_target_pairs={{1,3},{14,12},{17,19},{30,28}} | collective-permute-start | bytes 786440 | tf_op jit(solution)/shard_map/ppermute | solution.py:43
  195.3 1.0 copy-start.9
  196.2 14.5 %collective-permute-start.17 = (f32[64,1024]{1,0:T(8,128)}, f32[64,1024]{1,0:T(8,128)}, u32[]{:S(2)}, u32[]{:S(2)}) collective-permute-start(f32[64,1024]{1,0:T(8,128)} %add.162), channel_id=1, source_target_pairs={{1,3},{14,12},{17,19},{30,28}} | collective-permute-start | bytes 786440 | tf_op jit(solution)/shard_map/ppermute | solution.py:43
  202.7 1.5 copy-start.8
  204.2 1.2 copy-start.4
  204.2 1.5 copy-start.10
  206.9 5.3 %collective-permute-start.6 = (f32[64,1024]{1,0:T(8,128)S(1)}, f32[64,1024]{1,0:T(8,128)S(1)}, u32[]{:S(2)}, u32[]{:S(2)}) collective-permute-start(f32[64,1024]{1,0:T(8,128)S(1)} %add.137), channel_id=1, source_target_pairs={{1,3},{14,12},{17,19},{30,28}} | collective-permute-start | bytes 786440 | tf_op jit(solution)/shard_map/ppermute | solution.py:43
  208.7 3.6 %collective-permute-start.23 = (f32[64,1024]{1,0:T(8,128)S(1)}, f32[64,1024]{1,0:T(8,128)S(1)}, u32[]{:S(2)}, u32[]{:S(2)}) collective-permute-start(f32[64,1024]{1,0:T(8,128)S(1)} %add.172), channel_id=1, source_target_pairs={{1,3},{14,12},{17,19},{30,28}} | collective-permute-start | bytes 786440 | tf_op jit(solution)/shard_map/ppermute | solution.py:43

commit v2 on v1

--- a/solution.py
+++ b/solution.py
@@ -81,37 +81,22 @@
     def scores(piece):
         return block_scores(piece, train_features, residual_weights, scale)
 
-    rights, lefts = [query_features], [query_features]
-    for step in range(1, planes):
-        right = [(s, s + 1) for s in range(step - 1, planes - 1)]
-        left = [(s, s - 1) for s in range(1, planes - step + 1)]
-        cut = pieces if step == planes - 1 else 1
-        size = rows // cut
-        new_rights, new_lefts = [], []
-        for k in range(cut):
-            from_left = rights[0] if cut == 1 else rights[0][:, k * size:(k + 1) * size]
-            from_right = lefts[0] if cut == 1 else lefts[0][:, k * size:(k + 1) * size]
-            if 2 * step > planes + 1:
-                sent = jnp.where(z >= step - 1, from_left, from_right)
-                got = lax.ppermute(sent, "ex", right + left)
-                new_rights.append(got)
-                new_lefts.append(got)
-            else:
-                new_rights.append(lax.ppermute(from_left, "ex", right))
-                new_lefts.append(lax.ppermute(from_right, "ex", left))
+    right = [(s, (s + 1) % planes) for s in range(planes)]
+    left = [(s, (s - 1) % planes) for s in range(planes)]
+    from_left = from_right = query_features
+    for step in range(1, planes // 2):
+        from_left = lax.ppermute(from_left, "ex", right)
+        from_right = lax.ppermute(from_right, "ex", left)
         if step == 1:
             finish(scores(query_features), list(range(planes)), 0)
-        for k in range(cut):
-            blocks_right = [s - step if s >= step else None for s in range(planes)]
-            blocks_left = [s + step if s + step < planes else None for s in range(planes)]
-            if 2 * step >= planes:
-                got = jnp.where(z >= step, new_rights[k], new_lefts[k])
-                both = [a if a is not None else b for a, b in zip(blocks_right, blocks_left)]
-                finish(scores(got), both, k * size)
-            else:
-                finish(scores(new_rights[k]), blocks_right, k * size)
-                finish(scores(new_lefts[k]), blocks_left, k * size)
-        rights, lefts = new_rights, new_lefts
+        finish(scores(from_left), [(s - step) % planes for s in range(planes)], 0)
+        finish(scores(from_right), [(s + step) % planes for s in range(planes)], 0)
+    half = rows // 2
+    top = lax.ppermute(from_left[:, :half], "ex", right)
+    low = lax.ppermute(from_right[:, half:], "ex", left)
+    across = [(s + planes // 2) % planes for s in range(planes)]
+    finish(scores(top), across, 0)
+    finish(scores(low), across, half)
     return jnp.concatenate([part for block in results for part in block], axis=0)
 
 

time: 218 us -> 183 us (0.84); the launches traced: 214 us -> 182 us
  matrix products: 41.9 us -> 21.5 us
  waiting for transfers between devices: 102 us -> 117 us
  starting transfers between devices: 43.6 us -> 28.7 us
  other arithmetic: 17.7 us -> 10.3 us
  local copies, waits for them, and re-layouts: 5.85 us -> 2.8 us
    dot_general x32 -> x20, matrix products: 41.9 us -> 21.5 us  [block_scores(): lax.dot_general(piece[check], train_features[check], (((1,), (1,)), ((),...]
    ppermute x8 -> x5, waiting for transfers between devices: 0.02 us -> 13 us  [summed_at_owner(): whole = whole + lax.ppermute(total, PLACE, pairs)]
    ppermute x8 -> x5, starting transfers between devices: 15.5 us -> 6.77 us  [summed_at_owner(): total = total + lax.ppermute(partial, PLACE, pairs)]
    add x8 -> x5, other arithmetic: 9.65 us -> 2.17 us  [summed_at_owner(): total = total + lax.ppermute(partial, PLACE, pairs)]
    ppermute x8 -> x4, starting transfers between devices: 16.8 us -> 10.9 us  [the longest x1 5.05 us: local(): from_right = lax.ppermute(from_right, 'ex', left)]
    add x4 -> x5, other arithmetic: 3.16 us -> 6.6 us  [summed_at_owner(): whole = whole + lax.ppermute(total, PLACE, pairs)]
    ppermute x8 -> x5, waiting for transfers between devices: 0.02 us -> 3.2 us  [summed_at_owner(): total = total + lax.ppermute(partial, PLACE, pairs)]
    unnamed x34 -> x10, local copies, waits for them, and re-layouts: 2.47 us -> 0.03 us
  transfers between devices with their start and end apart: 24 -> 14, of which waited for: 5 -> 7; matrix products, arithmetic and copies ran while one was open for 29% -> 17% of each run, Pallas kernels for 0% -> 0%
where the time goes in v2:
time: 183 us; the launch traced here: 182 us
  waiting for transfers between devices  117 us (64%)
  starting transfers between devices  28.7 us (16%)
  matrix products  21.5 us (12%)
  other arithmetic  10.3 us (6%)
  local copies, waits for them, and re-layouts  2.8 us (2%)
  between operations  2.11 us (1%)
    ppermute x1, waiting for transfers between devices, local(): from_left = lax.ppermute(from_left, 'ex', right)  37 us
    ppermute x1, waiting for transfers between devices, local(): from_right = lax.ppermute(from_right, 'ex', left)  31 us
    dot_general x20, matrix products, block_scores(): lax.dot_general(piece[check], train_features[check], (((1,), (1,)), ((),...  21.5 us
    ppermute x1, waiting for transfers between devices, local(): top = lax.ppermute(from_left[:, :half], 'ex', right)  16.5 us
    ppermute x1, waiting for transfers between devices, local(): low = lax.ppermute(from_right[:, half:], 'ex', left)  16.2 us
    ppermute x5, waiting for transfers between devices, summed_at_owner(): whole = whole + lax.ppermute(total, PLACE, pairs)  13 us
    ppermute x5, starting transfers between devices, summed_at_owner(): whole = whole + lax.ppermute(total, PLACE, pairs)  11 us
    ppermute x5, starting transfers between devices, summed_at_owner(): total = total + lax.ppermute(partial, PLACE, pairs)  6.77 us
  transfers between devices with their start and end apart: 14, of which 7 were waited for; matrix products, arithmetic and copies ran while one was open for 17% of the time, Pallas kernels for 0%

profile of v2, /device:TPU:0, one launch (start us, length us, event | category | flops | bytes accessed | tf_op | source)
XLA Modules:
  0.0 182.2 jit_solution(3596348934558506333)
XLA Ops:
  0.0 5.0 %collective-permute-start.4 = (bf16[4,256,1024]{2,1,0:T(8,128)(2,1)}, bf16[4,256,1024]{2,1,0:T(8,128)(2,1)S(1)}, u32[]{:S(2)}, u32[]{:S(2)}) collective-permute-start(bf16[4,256,1024]{2,1,0:T(8,128)(2,1)} %param.8), channel_id=1, source_target_pairs={{0,12},{4,0},{8,4},{12,8},{1,13},{5,1},{9,5},{13,9},{2,14},{6,2},{... | collective-permute-start | bytes 6291464 | tf_op jit(solution)/shard_map/ppermute | solution.py:89
  5.0 0.9 fusion.196
  5.9 2.6 %fusion.91 = f32[256,1024]{1,0:T(8,128)S(1)} fusion(bf16[4,1024,1024]{2,1,0:T(8,128)(2,1)} %param.7, bf16[4,256,1024]{2,1,0:T(8,128)(2,1)} %param.8, f32[1024]{0:T(1024)S(1)} %bitcast.196), kind=kOutput, calls=%fused_computation.57 | convolution fusion | flops 537133056 | bytes 3674112 | tf_op jit(solution)/shard_map/dot_general | solution.py:12
  8.6 3.0 %fusion.109 = f32[256,1024]{1,0:T(8,128)S(1)} fusion(bf16[4,1024,1024]{2,1,0:T(8,128)(2,1)} %param.7, bf16[4,256,1024]{2,1,0:T(8,128)(2,1)} %param.8, f32[1024]{0:T(1024)S(1)} %bitcast.206), kind=kOutput, calls=%fused_computation.63 | convolution fusion | flops 537133056 | bytes 3674112 | tf_op jit(solution)/shard_map/dot_general | solution.py:12
  11.6 1.9 %fusion.100 = f32[256,1024]{1,0:T(8,128)S(1)} fusion(bf16[4,1024,1024]{2,1,0:T(8,128)(2,1)S(1)} %copy-done, bf16[4,256,1024]{2,1,0:T(8,128)(2,1)} %param.8, f32[1024]{0:T(1024)S(1)} %bitcast.201), kind=kOutput, calls=%fused_computation.60 | convolution fusion | flops 537133056 | bytes 3674112 | tf_op jit(solution)/shard_map/dot_general | solution.py:12
  13.6 0.9 fusion.82
  14.4 1.3 collective-permute-start.9
  15.8 3.2 %collective-permute-done.9 = f32[256,1024]{1,0:T(8,128)S(1)} collective-permute-done((f32[256,1024]{1,0:T(8,128)S(1)}, f32[256,1024]{1,0:T(8,128)S(1)}, u32[]{:S(2)}, u32[]{:S(2)}) %collective-permute-start.9) | collective-permute-done | bytes 1048608 | tf_op jit(solution)/shard_map/ppermute | solution.py:36
  19.2 1.3 collective-permute-start.10
  20.5 31.0 %collective-permute-done.4 = bf16[4,256,1024]{2,1,0:T(8,128)(2,1)S(1)} collective-permute-done((bf16[4,256,1024]{2,1,0:T(8,128)(2,1)}, bf16[4,256,1024]{2,1,0:T(8,128)(2,1)S(1)}, u32[]{:S(2)}, u32[]{:S(2)}) %collective-permute-start.4) | collective-permute-done | bytes 2097184 | tf_op jit(solution)/shard_map/ppermute | solution.py:89
  51.4 0.7 fusion.103
  52.2 0.7 fusion.94
  53.0 0.7 fusion.85
  53.7 0.9 fusion.52
  54.6 1.4 collective-permute-start.5
  56.0 4.2 %collective-permute-start.11 = (bf16[4,128,1024]{2,1,0:T(8,128)(2,1)S(1)}, bf16[4,128,1024]{2,1,0:T(8,128)(2,1)S(1)}, u32[]{:S(2)}, u32[]{:S(2)}) collective-permute-start(bf16[4,128,1024]{2,1,0:T(8,128)(2,1)S(1)} %slice.237), channel_id=1, source_target_pairs={{0,12},{4,0},{8,4},{12,8},{1,13},{5,1},{9,5},{13,9},{2,14},{6,2},{... | collective-permute-start | bytes 3145736 | tf_op jit(solution)/shard_map/ppermute | solution.py:96
  60.2 37.0 %collective-permute-done = bf16[4,256,1024]{2,1,0:T(8,128)(2,1)S(1)} collective-permute-done((bf16[4,256,1024]{2,1,0:T(8,128)(2,1)S(1)}, bf16[4,256,1024]{2,1,0:T(8,128)(2,1)S(1)}, u32[]{:S(2)}, u32[]{:S(2)}) %collective-permute-start) | collective-permute-done | bytes 2097184 | tf_op jit(solution)/shard_map/ppermute | solution.py:88
  97.3 1.6 collective-permute-start.1
  99.6 0.7 fusion.97
  100.4 0.7 fusion.88
  101.1 0.9 fusion.67
  102.0 1.4 collective-permute-start.7
  103.4 16.2 %collective-permute-done.11 = bf16[4,128,1024]{2,1,0:T(8,128)(2,1)S(1)} collective-permute-done((bf16[4,128,1024]{2,1,0:T(8,128)(2,1)S(1)}, bf16[4,128,1024]{2,1,0:T(8,128)(2,1)S(1)}, u32[]{:S(2)}, u32[]{:S(2)}) %collective-permute-start.11) | collective-permute-done | bytes 1048608 | tf_op jit(solution)/shard_map/ppermute | solution.py:96
  119.6 0.8 fusion.157
  120.4 0.8 fusion.151
  121.3 0.8 fusion.145
  122.1 0.9 fusion.139
  123.0 1.5 collective-permute-start.12
  124.5 16.5 %collective-permute-done.1 = bf16[4,128,1024]{2,1,0:T(8,128)(2,1)S(1)} collective-permute-done((bf16[4,128,1024]{2,1,0:T(8,128)(2,1)S(1)}, bf16[4,128,1024]{2,1,0:T(8,128)(2,1)S(1)}, u32[]{:S(2)}, u32[]{:S(2)}) %collective-permute-start.1) | collective-permute-done | bytes 1048608 | tf_op jit(solution)/shard_map/ppermute | solution.py:95
  141.0 0.8 fusion.154
  141.8 0.8 fusion.148
  142.7 0.8 fusion.142
  143.6 0.9 fusion.124
  144.5 1.3 collective-permute-start.2
  145.9 1.6 collective-permute-start.6
  147.8 1.8 collective-permute-start.8
  149.6 0.8 add.109
  150.4 4.2 %collective-permute-start.13 = (f32[128,1024]{1,0:T(8,128)}, f32[128,1024]{1,0:T(8,128)}, u32[]{:S(2)}, u32[]{:S(2)}) collective-permute-start(f32[128,1024]{1,0:T(8,128)} %add.109), channel_id=1, source_target_pairs={{0,2},{5,7},{10,8},{15,13},{16,18},{21,23},{26,24},{31,29}} | collective-permute-start | bytes 1572872 | tf_op jit(solution)/shard_map/ppermute | solution.py:43
  154.6 0.9 add.89
  155.5 2.1 %collective-permute-start.3 = (f32[128,1024]{1,0:T(8,128)}, f32[128,1024]{1,0:T(8,128)}, u32[]{:S(2)}, u32[]{:S(2)}) collective-permute-start(f32[128,1024]{1,0:T(8,128)} %add.89), channel_id=1, source_target_pairs={{0,2},{5,7},{10,8},{15,13},{16,18},{21,23},{26,24},{31,29}} | collective-permute-start | bytes 1572872 | tf_op jit(solution)/shard_map/ppermute | solution.py:43
  161.1 1.4 add.105
  162.4 4.0 %collective-permute-done.13 = f32[128,1024]{1,0:T(8,128)} collective-permute-done((f32[128,1024]{1,0:T(8,128)}, f32[128,1024]{1,0:T(8,128)}, u32[]{:S(2)}, u32[]{:S(2)}) %collective-permute-start.13) | collective-permute-done | bytes 524320 | tf_op jit(solution)/shard_map/ppermute | solution.py:43
  166.4 1.3 add.110
  167.7 9.0 %collective-permute-done.3 = f32[128,1024]{1,0:T(8,128)} collective-permute-done((f32[128,1024]{1,0:T(8,128)}, f32[128,1024]{1,0:T(8,128)}, u32[]{:S(2)}, u32[]{:S(2)}) %collective-permute-start.3) | collective-permute-done | bytes 524320 | tf_op jit(solution)/shard_map/ppermute | solution.py:43
  176.6 1.3 add.90
  177.9 1.4 add.95
  179.3 1.4 add.100
  181.2 1.0 pad_maximum_fusion
  (28 shorter events, 3.7 us)
Async XLA Ops:
  0.0 51.4 %collective-permute-start.4 = (bf16[4,256,1024]{2,1,0:T(8,128)(2,1)}, bf16[4,256,1024]{2,1,0:T(8,128)(2,1)S(1)}, u32[]{:S(2)}, u32[]{:S(2)}) collective-permute-start(bf16[4,256,1024]{2,1,0:T(8,128)(2,1)} %param.8), channel_id=1, source_target_pairs={{0,12},{4,0},{8,4},{12,8},{1,13},{5,1},{9,5},{13,9},{2,14},{6,2},{... | collective-permute-start | bytes 6291464 | tf_op jit(solution)/shard_map/ppermute | solution.py:89
  5.9 5.7 %copy-start = (bf16[4,1024,1024]{2,1,0:T(8,128)(2,1)S(1)}, bf16[4,1024,1024]{2,1,0:T(8,128)(2,1)}, u32[]{:S(2)}) copy-start(bf16[4,1024,1024]{2,1,0:T(8,128)(2,1)} %param.7) | copy-start | bytes 25165828
  11.6 2.0 %copy-start.1 = (bf16[4,256,1024]{2,1,0:T(8,128)(2,1)S(1)}, bf16[4,256,1024]{2,1,0:T(8,128)(2,1)}, u32[]{:S(2)}) copy-start(bf16[4,256,1024]{2,1,0:T(8,128)(2,1)} %param.8) | copy-start | bytes 6291460
  14.4 4.6 %collective-permute-start.9 = (f32[256,1024]{1,0:T(8,128)S(1)}, f32[256,1024]{1,0:T(8,128)S(1)}, u32[]{:S(2)}, u32[]{:S(2)}) collective-permute-start(f32[256,1024]{1,0:T(8,128)S(1)} %fusion.82), channel_id=1, source_target_pairs={{1,0},{3,2},{4,5},{6,7},{9,8},{11,10},{12,13},{14,15},{17,16},{19,... | collective-permute-start | bytes 3145736 | tf_op jit(solution)/shard_map/ppermute | solution.py:36
  15.7 81.4 %collective-permute-start = (bf16[4,256,1024]{2,1,0:T(8,128)(2,1)S(1)}, bf16[4,256,1024]{2,1,0:T(8,128)(2,1)S(1)}, u32[]{:S(2)}, u32[]{:S(2)}) collective-permute-start(bf16[4,256,1024]{2,1,0:T(8,128)(2,1)S(1)} %copy-done.1), channel_id=1, source_target_pairs={{0,4},{4,8},{8,12},{12,0},{1,5},{5,9},{9,13},{13,1},{2,6},{6,10},{... | collective-permute-start | bytes 6291464 | tf_op jit(solution)/shard_map/ppermute | solution.py:88
  19.2 141.9 %collective-permute-start.10 = (f32[256,1024]{1,0:T(8,128)S(1)}, f32[256,1024]{1,0:T(8,128)}, u32[]{:S(2)}, u32[]{:S(2)}) collective-permute-start(f32[256,1024]{1,0:T(8,128)S(1)} %add.104), channel_id=1, source_target_pairs={{2,0},{7,5},{8,10},{13,15},{18,16},{23,21},{24,26},{29,31}} | collective-permute-start | bytes 3145736 | tf_op jit(solution)/shard_map/ppermute | solution.py:43
  54.6 91.2 %collective-permute-start.5 = (f32[256,1024]{1,0:T(8,128)S(1)}, f32[256,1024]{1,0:T(8,128)S(1)}, u32[]{:S(2)}, u32[]{:S(2)}) collective-permute-start(f32[256,1024]{1,0:T(8,128)S(1)} %fusion.52), channel_id=1, source_target_pairs={{0,1},{2,3},{5,4},{7,6},{8,9},{10,11},{13,12},{15,14},{16,17},{18,... | collective-permute-start | bytes 3145736 | tf_op jit(solution)/shard_map/ppermute | solution.py:36
  56.0 63.6 %collective-permute-start.11 = (bf16[4,128,1024]{2,1,0:T(8,128)(2,1)S(1)}, bf16[4,128,1024]{2,1,0:T(8,128)(2,1)S(1)}, u32[]{:S(2)}, u32[]{:S(2)}) collective-permute-start(bf16[4,128,1024]{2,1,0:T(8,128)(2,1)S(1)} %slice.237), channel_id=1, source_target_pairs={{0,12},{4,0},{8,4},{12,8},{1,13},{5,1},{9,5},{13,9},{2,14},{6,2},{... | collective-permute-start | bytes 3145736 | tf_op jit(solution)/shard_map/ppermute | solution.py:96
  97.3 43.7 %collective-permute-start.1 = (bf16[4,128,1024]{2,1,0:T(8,128)(2,1)S(1)}, bf16[4,128,1024]{2,1,0:T(8,128)(2,1)S(1)}, u32[]{:S(2)}, u32[]{:S(2)}) collective-permute-start(bf16[4,128,1024]{2,1,0:T(8,128)(2,1)S(1)} %slice.216), channel_id=1, source_target_pairs={{0,4},{4,8},{8,12},{12,0},{1,5},{5,9},{9,13},{13,1},{2,6},{6,10},{... | collective-permute-start | bytes 3145736 | tf_op jit(solution)/shard_map/ppermute | solution.py:95
  102.0 45.6 %collective-permute-start.7 = (f32[256,1024]{1,0:T(8,128)S(1)}, f32[256,1024]{1,0:T(8,128)S(1)}, u32[]{:S(2)}, u32[]{:S(2)}) collective-permute-start(f32[256,1024]{1,0:T(8,128)S(1)} %fusion.67), channel_id=1, source_target_pairs={{0,1},{2,3},{5,4},{7,6},{8,9},{10,11},{13,12},{15,14},{16,17},{18,... | collective-permute-start | bytes 3145736 | tf_op jit(solution)/shard_map/ppermute | solution.py:36
  123.0 26.6 %collective-permute-start.12 = (f32[128,1024]{1,0:T(8,128)S(1)}, f32[128,1024]{1,0:T(8,128)S(1)}, u32[]{:S(2)}, u32[]{:S(2)}) collective-permute-start(f32[128,1024]{1,0:T(8,128)S(1)} %fusion.139), channel_id=1, source_target_pairs={{1,0},{3,2},{4,5},{6,7},{9,8},{11,10},{12,13},{14,15},{17,16},{19,... | collective-permute-start | bytes 1572872 | tf_op jit(solution)/shard_map/ppermute | solution.py:36
  144.5 10.2 %collective-permute-start.2 = (f32[128,1024]{1,0:T(8,128)S(1)}, f32[128,1024]{1,0:T(8,128)S(1)}, u32[]{:S(2)}, u32[]{:S(2)}) collective-permute-start(f32[128,1024]{1,0:T(8,128)S(1)} %fusion.124), channel_id=1, source_target_pairs={{1,0},{3,2},{4,5},{6,7},{9,8},{11,10},{12,13},{14,15},{17,16},{19,... | collective-permute-start | bytes 1572872 | tf_op jit(solution)/shard_map/ppermute | solution.py:36
  145.9 32.0 %collective-permute-start.6 = (f32[256,1024]{1,0:T(8,128)S(1)}, f32[256,1024]{1,0:T(8,128)}, u32[]{:S(2)}, u32[]{:S(2)}) collective-permute-start(f32[256,1024]{1,0:T(8,128)S(1)} %add.94), channel_id=1, source_target_pairs={{3,1},{4,6},{9,11},{14,12},{19,17},{20,22},{25,27},{30,28}} | collective-permute-start | bytes 3145736 | tf_op jit(solution)/shard_map/ppermute | solution.py:43
  147.7 9.8 %copy-start.4 = (s32[4]{0:T(128)S(1)}, s32[4]{0:T(128)}, u32[]{:S(2)}) copy-start(s32[4]{0:T(128)} %constant.28.clone) | copy-start | bytes 52
  147.8 10.4 %copy-start.3 = (s32[4]{0:T(128)S(1)}, s32[4]{0:T(128)}, u32[]{:S(2)}) copy-start(s32[4]{0:T(128)} %constant.27.clone) | copy-start | bytes 52
  147.8 12.2 %copy-start.2 = (s32[4]{0:T(128)S(1)}, s32[4]{0:T(128)}, u32[]{:S(2)}) copy-start(s32[4]{0:T(128)} %constant.26.clone) | copy-start | bytes 52
  147.8 31.5 %collective-permute-start.8 = (f32[256,1024]{1,0:T(8,128)S(1)}, f32[256,1024]{1,0:T(8,128)}, u32[]{:S(2)}, u32[]{:S(2)}) collective-permute-start(f32[256,1024]{1,0:T(8,128)S(1)} %add.99), channel_id=1, source_target_pairs={{1,3},{6,4},{11,9},{12,14},{17,19},{22,20},{27,25},{28,30}} | collective-permute-start | bytes 3145736 | tf_op jit(solution)/shard_map/ppermute | solution.py:43
  150.4 16.0 %collective-permute-start.13 = (f32[128,1024]{1,0:T(8,128)}, f32[128,1024]{1,0:T(8,128)}, u32[]{:S(2)}, u32[]{:S(2)}) collective-permute-start(f32[128,1024]{1,0:T(8,128)} %add.109), channel_id=1, source_target_pairs={{0,2},{5,7},{10,8},{15,13},{16,18},{21,23},{26,24},{31,29}} | collective-permute-start | bytes 1572872 | tf_op jit(solution)/shard_map/ppermute | solution.py:43
  155.5 21.2 %collective-permute-start.3 = (f32[128,1024]{1,0:T(8,128)}, f32[128,1024]{1,0:T(8,128)}, u32[]{:S(2)}, u32[]{:S(2)}) collective-permute-start(f32[128,1024]{1,0:T(8,128)} %add.89), channel_id=1, source_target_pairs={{0,2},{5,7},{10,8},{15,13},{16,18},{21,23},{26,24},{31,29}} | collective-permute-start | bytes 1572872 | tf_op jit(solution)/shard_map/ppermute | solution.py:43

commit v3 on v0

v3 whole, which is shorter than its diff:
```python
import jax
import jax.numpy as jnp
from jax import lax
from jax.sharding import PartitionSpec as P

PLACE = ("ex", "ckpt", "dim")
CHUNKS = 4


def after(value, *others):
    return lax.optimization_barrier((value,) + others)[0]


def weighted(checks, train, weights, scale):
    total = None
    for piece, examples, weight in zip(checks, train, weights):
        dots = lax.dot_general(
            piece,
            examples,
            (((1,), (1,)), ((), ())),
            preferred_element_type=jnp.float32,
        )
        term = dots * weight[None, :]
        total = term if total is None else total + term
    return total * scale


class Keepers:
    def __init__(self, rows):
        self.ckpts, self.dims = lax.axis_size("ckpt"), lax.axis_size("dim")
        self.planes = lax.axis_size("ex")
        self.z, self.x, self.c = [lax.axis_index(name) for name in PLACE]
        kept = rows * self.planes // (self.ckpts * self.dims)
        self.ratio = kept // rows
        assert self.ratio * rows == kept

    def index(self, z, x, c):
        return (z * self.ckpts + x) * self.dims + c

    def of(self, block):
        owner = block // self.ratio
        return owner // self.dims, owner % self.dims

    def mine(self, blocks, j=0):
        found = jnp.bool_(False)
        for z, block in enumerate(blocks):
            if block is not None and block % self.ratio == j:
                x, c = self.of(block)
                found = found | ((self.z == z) & (self.x == x) & (self.c == c))
        return found

    def sums(self, partial, blocks):
        total = partial
        for away in range(1, self.dims):
            pairs = []
            for z, block in enumerate(blocks):
                if block is not None:
                    c = self.of(block)[1]
                    for x in range(self.ckpts):
                        pairs.append((self.index(z, x, (c + away) % self.dims), self.index(z, x, c)))
            total = total + lax.ppermute(partial, PLACE, pairs)
        whole = total
        for away in range(1, self.ckpts):
            pairs = []
            for z, block in enumerate(blocks):
                if block is not None:
                    x, c = self.of(block)
                    pairs.append((self.index(z, (x + away) % self.ckpts, c), self.index(z, x, c)))
            whole = whole + lax.ppermute(total, PLACE, pairs)
        return whole

    def two_sums(self, one, one_blocks, two, two_blocks):
        keeps_one = jnp.bool_(False)
        swaps, crosses = [], []
        for z, blocks in enumerate(zip(one_blocks, two_blocks)):
            if blocks[0] is None:
                continue
            places = [self.of(block) for block in blocks]
            assert {places[0][1], places[1][1]} == {0, 1}
            keeps_one = keeps_one | ((self.z == z) & (self.c == places[0][1]))
            for at, c in places:
                for x in range(2):
                    swaps.append((self.index(z, x, 1 - c), self.index(z, x, c)))
                crosses.append((self.index(z, 1 - at, c), self.index(z, at, c)))
        got = lax.ppermute(jnp.where(keeps_one, two, one), PLACE, swaps)
        total = jnp.where(keeps_one, one, two) + got
        return total + lax.ppermute(total, PLACE, crosses)


def ring(train_features, query_features, residual_weights, keepers, scale):
    planes, ratio = keepers.planes, keepers.ratio
    rows = query_features.shape[1]
    half = rows // 2
    results = [[None, None] for unused in range(ratio)]

    def finish(piece, blocks, start):
        found = weighted(list(piece), train_features, residual_weights, scale)
        whole = keepers.sums(found, blocks)
        for j in range(ratio):
            mine = keepers.mine(blocks, j)
            for k in range(found.shape[0] // half):
                part = whole[k * half:(k + 1) * half]
                at = start // half + k
                old = results[j][at]
                results[j][at] = part if old is None else jnp.where(mine, part, old)

    right = [(s, (s + 1) % planes) for s in range(planes)]
    left = [(s, (s - 1) % planes) for s in range(planes)]
    from_left = from_right = query_features
    finish(query_features, list(range(planes)), 0)
    for step in range(1, planes // 2):
        from_left = lax.ppermute(from_left, "ex", right)
        from_right = lax.ppermute(from_right, "ex", left)
        finish(from_left, [(s - step) % planes for s in range(planes)], 0)
        finish(from_right, [(s + step) % planes for s in range(planes)], 0)
    across = [(s + planes // 2) % planes for s in range(planes)]
    finish(lax.ppermute(from_left[:, :half], "ex", right), across, 0)
    finish(lax.ppermute(from_right[:, half:], "ex", left), across, half)
    return jnp.concatenate([part for block in results for part in block], axis=0)


def line(train_features, query_features, residual_weights, keepers, scale):
    z = keepers.z
    rows = query_features.shape[1]
    most = train_features.shape[0] - 1
    examples = train_features.shape[1]
    half, cut = examples // 2, rows // CHUNKS
    ends = (z == 0) | (z == 3)

    def inward(value):
        return lax.ppermute(value, "ex", [(0, 1), (3, 2)])

    def between(value):
        return lax.ppermute(value, "ex", [(1, 2), (2, 1)])

    def outward(value):
        return lax.ppermute(value, "ex", [(1, 0), (2, 3)])

    own_many, own_one = query_features[:most], query_features[most]
    train_one = train_features[most]

    out_own = outward(own_many)
    in_one = inward(own_one)
    mid_one = between(own_one)
    in_weight = inward(residual_weights[most:])[0]
    in_train = [inward(after(train_one[:half], in_weight))]
    mid_many = [between(own_many[0])]
    out_many = [outward(mid_many[0])]
    mid_many.append(between(after(own_many[1], mid_one)))
    out_many.append(outward(mid_many[1]))
    mid_many.append(between(after(own_many[2], mid_many[0])))
    out_many.append(outward(mid_many[2]))

    own = weighted(list(query_features), train_features, residual_weights, scale)

    in_first = inward(after(own_many[0], in_one))
    in_train.append(inward(after(train_one[half:], in_train[0])))
    mid_first = between(after(in_first, mid_many[1]))
    out_first = outward(mid_first)

    blocks_own = [0, 1, 2, 3]
    blocks_1 = [1, 2, 1, 2]
    blocks_2 = [2, 0, 3, 1]
    blocks_3 = [3, 3, 0, 0]

    checks = [jnp.where(ends, out_own[i], mid_many[i]) for i in range(most)] + [mid_one]
    found_1 = weighted(checks, train_features, residual_weights, scale)
    result_a = keepers.two_sums(own, blocks_own, found_1, blocks_1)

    beside_0 = [None, 1, 2, None]
    beside_1 = [None, 2, 1, None]
    beside_2 = [None, 3, 0, None]

    def beside(part):
        columns = slice(part * half, (part + 1) * half)

        def of(queries):
            return weighted([queries], [in_train[part]], [in_weight[columns]], scale)

        both = keepers.two_sums(of(own_one), beside_0, of(mid_one), beside_1)
        return both, of

    both_0, of_0 = beside(0)
    mid_in_one = between(after(in_one, both_0, mid_first))
    both_1, of_1 = beside(1)
    third = jnp.concatenate([of_0(mid_in_one), of_1(mid_in_one)], axis=1)
    third = keepers.sums(third, beside_2)
    both = jnp.concatenate([both_0, both_1], axis=1)
    mine_both = keepers.mine(beside_0) | keepers.mine(beside_1)
    returned = jnp.where(mine_both, both, jnp.where(keepers.mine(beside_2), third, 0.0))
    largest = jnp.maximum(jnp.max(jnp.abs(returned)), 1e-30)
    small = (returned * (16384.0 / largest)).astype(jnp.float16)

    results_b = []
    ins = [in_train[1], in_train[1]]
    for k in range(CHUNKS):
        part = slice(k * cut, (k + 1) * cut)
        got = inward(after(own_many[1:, part], ins[-2], *([result_a] if k == CHUNKS - 1 else [])))
        ins.append(got)
        mid = between(got)
        out = outward(mid)
        near_2 = [in_first[part]] + list(got)
        far_2 = [out_many[i][part] for i in range(most)]
        near_3 = [mid_first[part]] + list(mid)
        far_3 = [out_first[part]] + list(out)
        checks_2 = [jnp.where(ends, a, b) for a, b in zip(far_2, near_2)] + [in_one[part]]
        checks_3 = [jnp.where(ends, a, b) for a, b in zip(far_3, near_3)] + [mid_in_one[part]]
        found_2 = weighted(checks_2, train_features, residual_weights, scale)
        found_3 = weighted(checks_3, train_features, residual_weights, scale)
        results_b.append(keepers.two_sums(found_2, blocks_2, found_3, blocks_3))

    unit = outward(jnp.full((8, 128), largest * (1.0 / 16384.0)))
    small = outward(after(small, mid, unit))
    mine_a = keepers.mine(blocks_own) | keepers.mine(blocks_1)
    result = jnp.where(mine_a, result_a, jnp.concatenate(results_b, axis=0))
    return result + small.astype(jnp.float32) * unit[0, 0]


def local(train_features, query_features, residual_weights):
    keepers = Keepers(query_features.shape[1])
    scale = 1.0 / (train_features.shape[0] * keepers.ckpts)
    plan = line if (keepers.planes, keepers.ckpts, keepers.dims) == (4, 2, 2) else ring
    return plan(train_features, query_features, residual_weights, keepers, scale)


def solution(mesh):
    in_specs = (
        P("ckpt", ("groups", "ex"), "dim"),
        P("ckpt", ("groups", "ex"), "dim"),
        P("ckpt", ("groups", "ex")),
    )
    out_specs = P(("ckpt", "dim"), ("groups", "ex"))
    return jax.shard_map(local, mesh=mesh, in_specs=in_specs, out_specs=out_specs, check_vma=False)
```

time: 280 us -> 230 us (0.82)
  waiting for transfers between devices: 220 us -> 79.4 us
  starting transfers between devices: 3.08 us -> 79.2 us
  matrix products: 29.4 us -> 50 us
  between operations: 13.5 us -> 1.63 us
  other arithmetic: 0 us -> 10.5 us
  local copies, waits for them, and re-layouts: 12.9 us -> 7.47 us
    ppermute x3 -> x46, starting transfers between devices: 3.03 us -> 79.2 us  [the longest x9 42.7 us: inward(): return lax.ppermute(value, 'ex', [(0, 1), (3, 2)])]
    ppermute x3 -> x46, waiting for transfers between devices: 145 us -> 79.4 us  [the longest x11 42.2 us: outward(): return lax.ppermute(value, 'ex', [(1, 0), (2, 3)])]
    reduce_scatter x1 -> x0, waiting for transfers between devices: 52.1 us -> none  [local(): mine = lax.psum_scatter(summed, 'ckpt', scatter_dimension=0, tiled=True)]
    psum x1 -> x0, waiting for transfers between devices: 23.7 us -> none  [local(): summed = lax.psum(terms, 'dim')]
    dot_general x16 -> x46, matrix products: 29.4 us -> 50 us  [weighted(): lax.dot_general(piece, examples, (((1,), (1,)), ((), ())), preferred_elem...]
    add x0 -> x16, other arithmetic: none -> 8.51 us  [the longest x7 4.06 us: two_sums(): total = jnp.where(keeps_one, one, two) + got]
    while x9 -> x0, local copies, waits for them, and re-layouts: 5.04 us -> none
    unnamed x5 -> x20, local copies, waits for them, and re-layouts: 5.03 us -> 0.21 us
  transfers between devices with their start and end apart: 5 -> 46, of which waited for: 5 -> 16; matrix products, arithmetic and copies ran while one was open for 0% -> 28% of each run, Pallas kernels for 0% -> 0%
where the time goes in v3:
time: 230 us; the launch traced here: 228 us
  waiting for transfers between devices  79.4 us (35%)
  starting transfers between devices  79.2 us (34%)
  matrix products  50 us (22%)
  other arithmetic  10.5 us (5%)
  local copies, waits for them, and re-layouts  7.47 us (3%)
    dot_general x46, matrix products, weighted(): lax.dot_general(piece, examples, (((1,), (1,)), ((), ())), preferred_elem...  50 us
    ppermute x9, starting transfers between devices, inward(): return lax.ppermute(value, 'ex', [(0, 1), (3, 2)])  42.7 us
    ppermute x11, waiting for transfers between devices, outward(): return lax.ppermute(value, 'ex', [(1, 0), (2, 3)])  42.2 us
    ppermute x9, waiting for transfers between devices, inward(): return lax.ppermute(value, 'ex', [(0, 1), (3, 2)])  31.5 us
    ppermute x11, starting transfers between devices, outward(): return lax.ppermute(value, 'ex', [(1, 0), (2, 3)])  14.2 us
    ppermute x7, starting transfers between devices, two_sums(): return total + lax.ppermute(total, PLACE, crosses)  10.2 us
    ppermute x10, starting transfers between devices, between(): return lax.ppermute(value, 'ex', [(1, 2), (2, 1)])  8.49 us
    ppermute x7, waiting for transfers between devices, two_sums(): return total + lax.ppermute(total, PLACE, crosses)  5.64 us
  transfers between devices with their start and end apart: 46, of which 16 were waited for; matrix products, arithmetic and copies ran while one was open for 28% of the time, Pallas kernels for 0%

profile of v3, /device:TPU:0, one launch (start us, length us, event | category | flops | bytes accessed | tf_op | source)
XLA Modules:
  0.0 228.2 jit_solution(16804492904341136315)
XLA Ops:
  0.0 3.0 %slice_bitcast_fusion.7 = (bf16[256,1024]{1,0:T(8,128)(2,1)}, bf16[256,1024]{1,0:T(8,128)(2,1)}, bf16[256,1024]{1,0:T(8,128)(2,1)}, bf16[256,1024]{1,0:T(8,128)(2,1)}) fusion(bf16[4,256,1024]{2,1,0:T(8,128)(2,1)} %param.4), kind=kLoop, calls=%fused_computation.192 | loop fusion | bytes 4194304 | tf_op jit(solution)/shard_map/unstack | solution.py:154
  3.0 1.6 collective-permute-start.2
  4.6 7.9 %collective-permute-start.8 = (bf16[256,1024]{1,0:T(8,128)(2,1)}, bf16[256,1024]{1,0:T(8,128)(2,1)}, u32[]{:S(2)}, u32[]{:S(2)}) collective-permute-start(bf16[256,1024]{1,0:T(8,128)(2,1)} %get-tuple-element.36), channel_id=1, source_target_pairs={{0,4},{12,8},{1,5},{13,9},{2,6},{14,10},{3,7},{15,11},{16,20},{28,... | collective-permute-start | bytes 1572872 | tf_op jit(solution)/shard_map/ppermute | solution.py:131
  12.5 1.4 collective-permute-start.1
  14.0 1.3 slice.163
  16.6 5.7 %collective-permute-start.19 = (f32[1,1024]{1,0:T(1,128)S(1)}, f32[1,1024]{1,0:T(1,128)S(1)}, u32[]{:S(2)}, u32[]{:S(2)}) collective-permute-start(f32[1,1024]{1,0:T(1,128)S(1)} %get-tuple-element.41), channel_id=1, source_target_pairs={{0,4},{12,8},{1,5},{13,9},{2,6},{14,10},{3,7},{15,11},{16,20},{28,... | collective-permute-start | bytes 12296 | tf_op jit(solution)/shard_map/ppermute | solution.py:131
  22.3 2.3 %fusion.122 = f32[256,1024]{1,0:T(8,128)S(1)} fusion(f32[1024]{0:T(1024)S(1)} %bitcast.421, bf16[4,1024,1024]{2,1,0:T(8,128)(2,1)} %param.3, bf16[4,256,1024]{2,1,0:T(8,128)(2,1)S(1)} %copy-done.1), kind=kOutput, calls=%fused_computation.94 | convolution fusion | flops 537133056 | bytes 3674112 | tf_op jit(solution)/shard_map/dot_general | solution.py:17
  27.0 1.5 slice_bitcast_fusion.1
  29.4 1.3 collective-permute-start.11
  32.2 9.0 %collective-permute-start.9 = (bf16[256,1024]{1,0:T(8,128)(2,1)}, bf16[256,1024]{1,0:T(8,128)(2,1)S(1)}, u32[]{:S(2)}, u32[]{:S(2)}) collective-permute-start(bf16[256,1024]{1,0:T(8,128)(2,1)} %get-tuple-element.18), channel_id=1, source_target_pairs={{0,4},{12,8},{1,5},{13,9},{2,6},{14,10},{3,7},{15,11},{16,20},{28,... | collective-permute-start | bytes 1572872 | tf_op jit(solution)/shard_map/ppermute | solution.py:131
  41.2 2.6 %fusion.272 = f32[64,1024]{1,0:T(8,128)S(1)} fusion(bf16[256,1024]{1,0:T(8,128)(2,1)} %collective-permute-done.8, f32[1024]{0:T(1024)S(1)} %bitcast.422, bf16[4,1024,1024]{2,1,0:T(8,128)(2,1)} %param.3), kind=kOutput, calls=%fused_computation.154 | convolution fusion | flops 134283264 | bytes 2494464 | tf_op jit(solution)/shard_map/dot_general | solution.py:17
  43.8 2.5 %fusion.125 = f32[256,1024]{1,0:T(8,128)S(1)} fusion(bf16[256,1024]{1,0:T(8,128)(2,1)} %collective-permute-done.2, f32[1024]{0:T(1024)S(1)} %bitcast.423, bf16[4,1024,1024]{2,1,0:T(8,128)(2,1)} %param.3), kind=kOutput, calls=%fused_computation.95 | convolution fusion | flops 537133056 | bytes 3674112 | tf_op jit(solution)/shard_map/dot_general | solution.py:17
  46.3 2.6 %fusion.266 = f32[64,1024]{1,0:T(8,128)S(1)} fusion(bf16[256,1024]{1,0:T(8,128)(2,1)} %collective-permute-done.8, f32[1024]{0:T(1024)S(1)} %bitcast.424, bf16[4,1024,1024]{2,1,0:T(8,128)(2,1)} %param.3), kind=kOutput, calls=%fused_computation.152 | convolution fusion | flops 134283264 | bytes 2494464 | tf_op jit(solution)/shard_map/dot_general | solution.py:17
  48.9 5.7 %collective-permute-done.11 = bf16[512,1024]{1,0:T(8,128)(2,1)S(1)} collective-permute-done((bf16[512,1024]{1,0:T(8,128)(2,1)}, bf16[512,1024]{1,0:T(8,128)(2,1)S(1)}, u32[]{:S(2)}, u32[]{:S(2)}) %collective-permute-start.11) | collective-permute-done | bytes 1048608 | tf_op jit(solution)/shard_map/ppermute | solution.py:131
  55.1 1.5 broadcast_select_fusion.1
  57.5 2.4 %fusion.260 = f32[64,1024]{1,0:T(8,128)S(1)} fusion(bf16[256,1024]{1,0:T(8,128)(2,1)} %collective-permute-done.8, f32[1024]{0:T(1024)S(1)} %bitcast.425, bf16[4,1024,1024]{2,1,0:T(8,128)(2,1)} %param.3), kind=kOutput, calls=%fused_computation.150 | convolution fusion | flops 134283264 | bytes 2494464 | tf_op jit(solution)/shard_map/dot_general | solution.py:17
  59.9 1.3 collective-permute-start.7
  61.2 2.6 %collective-permute-done.9 = bf16[256,1024]{1,0:T(8,128)(2,1)S(1)} collective-permute-done((bf16[256,1024]{1,0:T(8,128)(2,1)}, bf16[256,1024]{1,0:T(8,128)(2,1)S(1)}, u32[]{:S(2)}, u32[]{:S(2)}) %collective-permute-start.9) | collective-permute-done | bytes 524320 | tf_op jit(solution)/shard_map/ppermute | solution.py:131
  64.6 1.7 fusion.254
  66.2 6.0 %collective-permute-start.12 = (bf16[512,1024]{1,0:T(8,128)(2,1)S(1)}, bf16[512,1024]{1,0:T(8,128)(2,1)S(1)}, u32[]{:S(2)}, u32[]{:S(2)}) collective-permute-start(bf16[512,1024]{1,0:T(8,128)(2,1)S(1)} %copy-done.3), channel_id=1, source_target_pairs={{0,4},{12,8},{1,5},{13,9},{2,6},{14,10},{3,7},{15,11},{16,20},{28,... | collective-permute-start | bytes 3145736 | tf_op jit(solution)/shard_map/ppermute | solution.py:131
  72.3 1.3 collective-permute-start.14
  74.5 1.3 collective-permute-start.16
  75.8 1.8 fusion.119
  77.6 1.8 fusion.113
  79.4 2.0 broadcast_select_fusion
  81.4 12.3 %collective-permute-done.12 = bf16[512,1024]{1,0:T(8,128)(2,1)S(1)} collective-permute-done((bf16[512,1024]{1,0:T(8,128)(2,1)S(1)}, bf16[512,1024]{1,0:T(8,128)(2,1)S(1)}, u32[]{:S(2)}, u32[]{:S(2)}) %collective-permute-start.12) | collective-permute-done | bytes 1048608 | tf_op jit(solution)/shard_map/ppermute | solution.py:131
  95.1 5.1 %collective-permute-done.16 = bf16[256,1024]{1,0:T(8,128)(2,1)S(1)} collective-permute-done((bf16[256,1024]{1,0:T(8,128)(2,1)S(1)}, bf16[256,1024]{1,0:T(8,128)(2,1)S(1)}, u32[]{:S(2)}, u32[]{:S(2)}) %collective-permute-start.16) | collective-permute-done | bytes 524320 | tf_op jit(solution)/shard_map/ppermute | solution.py:137
  100.3 1.6 collective-permute-start.13
  105.0 1.5 fusion.131
  107.5 4.2 %collective-permute-start.25 = (bf16[2,64,1024]{2,1,0:T(8,128)(2,1)S(1)}, bf16[2,64,1024]{2,1,0:T(8,128)(2,1)S(1)}, u32[]{:S(2)}, u32[]{:S(2)}) collective-permute-start(bf16[2,64,1024]{2,1,0:T(8,128)(2,1)S(1)} %copy-done.5), channel_id=1, source_target_pairs={{0,4},{12,8},{1,5},{13,9},{2,6},{14,10},{3,7},{15,11},{16,20},{28,... | collective-permute-start | bytes 786440 | tf_op jit(solution)/shard_map/ppermute | solution.py:131
  113.2 3.2 %collective-permute-done.25 = bf16[2,64,1024]{2,1,0:T(8,128)(2,1)S(1)} collective-permute-done((bf16[2,64,1024]{2,1,0:T(8,128)(2,1)S(1)}, bf16[2,64,1024]{2,1,0:T(8,128)(2,1)S(1)}, u32[]{:S(2)}, u32[]{:S(2)}) %collective-permute-start.25) | collective-permute-done | bytes 262176 | tf_op jit(solution)/shard_map/ppermute | solution.py:131
  117.8 5.6 %collective-permute-start.30 = (bf16[2,64,1024]{2,1,0:T(8,128)(2,1)S(1)}, bf16[2,64,1024]{2,1,0:T(8,128)(2,1)S(1)}, u32[]{:S(2)}, u32[]{:S(2)}) collective-permute-start(bf16[2,64,1024]{2,1,0:T(8,128)(2,1)S(1)} %copy-done.4), channel_id=1, source_target_pairs={{0,4},{12,8},{1,5},{13,9},{2,6},{14,10},{3,7},{15,11},{16,20},{28,... | collective-permute-start | bytes 786440 | tf_op jit(solution)/shard_map/ppermute | solution.py:131
  127.3 2.4 %collective-permute-done.30 = bf16[2,64,1024]{2,1,0:T(8,128)(2,1)S(1)} collective-permute-done((bf16[2,64,1024]{2,1,0:T(8,128)(2,1)S(1)}, bf16[2,64,1024]{2,1,0:T(8,128)(2,1)S(1)}, u32[]{:S(2)}, u32[]{:S(2)}) %collective-permute-start.30) | collective-permute-done | bytes 262176 | tf_op jit(solution)/shard_map/ppermute | solution.py:131
  142.6 8.8 %collective-permute-done.27 = bf16[2,64,1024]{2,1,0:T(8,128)(2,1)S(1)} collective-permute-done((bf16[2,64,1024]{2,1,0:T(8,128)(2,1)S(1)}, bf16[2,64,1024]{2,1,0:T(8,128)(2,1)S(1)}, u32[]{:S(2)}, u32[]{:S(2)}) %collective-permute-start.27) | collective-permute-done | bytes 262176 | tf_op jit(solution)/shard_map/ppermute | solution.py:137
  157.0 9.7 %collective-permute-done.32 = bf16[2,64,1024]{2,1,0:T(8,128)(2,1)S(1)} collective-permute-done((bf16[2,64,1024]{2,1,0:T(8,128)(2,1)S(1)}, bf16[2,64,1024]{2,1,0:T(8,128)(2,1)S(1)}, u32[]{:S(2)}, u32[]{:S(2)}) %collective-permute-start.32) | collective-permute-done | bytes 262176 | tf_op jit(solution)/shard_map/ppermute | solution.py:137
  167.5 1.6 broadcast_select_fusion.3
  170.3 2.0 collective-permute-start.29
  173.1 2.0 collective-permute-start.24
  175.3 1.3 collective-permute-start.35
  177.6 5.1 %collective-permute-done.35 = bf16[2,64,1024]{2,1,0:T(8,128)(2,1)S(1)} collective-permute-done((bf16[2,64,1024]{2,1,0:T(8,128)(2,1)S(1)}, bf16[2,64,1024]{2,1,0:T(8,128)(2,1)S(1)}, u32[]{:S(2)}, u32[]{:S(2)}) %collective-permute-start.35) | collective-permute-done | bytes 262176 | tf_op jit(solution)/shard_map/ppermute | solution.py:131
  186.9 14.8 %collective-permute-done.37 = bf16[2,64,1024]{2,1,0:T(8,128)(2,1)S(1)} collective-permute-done((bf16[2,64,1024]{2,1,0:T(8,128)(2,1)S(1)}, bf16[2,64,1024]{2,1,0:T(8,128)(2,1)S(1)}, u32[]{:S(2)}, u32[]{:S(2)}) %collective-permute-start.37) | collective-permute-done | bytes 262176 | tf_op jit(solution)/shard_map/ppermute | solution.py:137
  202.5 1.5 broadcast_select_fusion.2
  207.8 3.3 %collective-permute-done.44 = f32[8,128]{1,0:T(8,128)S(1)} collective-permute-done((f32[8,128]{1,0:T(8,128)S(1)}, f32[8,128]{1,0:T(8,128)S(1)}, u32[]{:S(2)}, u32[]{:S(2)}) %collective-permute-start.44) | collective-permute-done | bytes 4128 | tf_op jit(solution)/shard_map/ppermute | solution.py:137
  213.4 2.0 collective-permute-start.34
  216.4 1.3 collective-permute-start.39
  219.9 2.2 collective-permute-done.34
  222.7 3.4 %collective-permute-done.39 = f32[64,1024]{1,0:T(8,128)S(1)} collective-permute-done((f32[64,1024]{1,0:T(8,128)S(1)}, f32[64,1024]{1,0:T(8,128)S(1)}, u32[]{:S(2)}, u32[]{:S(2)}) %collective-permute-start.39) | collective-permute-done | bytes 262176 | tf_op jit(solution)/shard_map/ppermute | solution.py:87
  226.4 1.8 fusion.326
  (139 shorter events, 57.6 us)
Async XLA Ops:
  0.0 24.6 %copy-start = (bf16[4,1024,1024]{2,1,0:T(8,128)(2,1)S(1)}, bf16[4,1024,1024]{2,1,0:T(8,128)(2,1)}, u32[]{:S(2)}) copy-start(bf16[4,1024,1024]{2,1,0:T(8,128)(2,1)} %param.3) | copy-start | bytes 25165828
  3.0 28.5 %collective-permute-start.2 = (bf16[256,1024]{1,0:T(8,128)(2,1)}, bf16[256,1024]{1,0:T(8,128)(2,1)}, u32[]{:S(2)}, u32[]{:S(2)}) collective-permute-start(bf16[256,1024]{1,0:T(8,128)(2,1)} %get-tuple-element.36), channel_id=1, source_target_pairs={{4,8},{8,4},{5,9},{9,5},{6,10},{10,6},{7,11},{11,7},{20,24},{24,20... | collective-permute-start | bytes 1572872 | tf_op jit(solution)/shard_map/ppermute | solution.py:134
  4.6 27.6 %collective-permute-start.8 = (bf16[256,1024]{1,0:T(8,128)(2,1)}, bf16[256,1024]{1,0:T(8,128)(2,1)}, u32[]{:S(2)}, u32[]{:S(2)}) collective-permute-start(bf16[256,1024]{1,0:T(8,128)(2,1)} %get-tuple-element.36), channel_id=1, source_target_pairs={{0,4},{12,8},{1,5},{13,9},{2,6},{14,10},{3,7},{15,11},{16,20},{28,... | collective-permute-start | bytes 1572872 | tf_op jit(solution)/shard_map/ppermute | solution.py:131
  12.5 18.3 %collective-permute-start.1 = (bf16[256,1024]{1,0:T(8,128)(2,1)}, bf16[256,1024]{1,0:T(8,128)(2,1)}, u32[]{:S(2)}, u32[]{:S(2)}) collective-permute-start(bf16[256,1024]{1,0:T(8,128)(2,1)} %get-tuple-element.18), channel_id=1, source_target_pairs={{4,8},{8,4},{5,9},{9,5},{6,10},{10,6},{7,11},{11,7},{20,24},{24,20... | collective-permute-start | bytes 1572872 | tf_op jit(solution)/shard_map/ppermute | solution.py:134
  15.3 59.2 %collective-permute-start = (bf16[3,256,1024]{2,1,0:T(8,128)(2,1)}, bf16[3,256,1024]{2,1,0:T(8,128)(2,1)}, u32[]{:S(2)}, u32[]{:S(2)}) collective-permute-start(bf16[3,256,1024]{2,1,0:T(8,128)(2,1)} %slice.163), channel_id=1, source_target_pairs={{4,0},{8,12},{5,1},{9,13},{6,2},{10,14},{7,3},{11,15},{20,16},{24,... | collective-permute-start | bytes 4718600 | tf_op jit(solution)/shard_map/ppermute | solution.py:137
  16.6 12.9 %collective-permute-start.19 = (f32[1,1024]{1,0:T(1,128)S(1)}, f32[1,1024]{1,0:T(1,128)S(1)}, u32[]{:S(2)}, u32[]{:S(2)}) collective-permute-start(f32[1,1024]{1,0:T(1,128)S(1)} %get-tuple-element.41), channel_id=1, source_target_pairs={{0,4},{12,8},{1,5},{13,9},{2,6},{14,10},{3,7},{15,11},{16,20},{28,... | collective-permute-start | bytes 12296 | tf_op jit(solution)/shard_map/ppermute | solution.py:131
  29.4 25.2 %collective-permute-start.11 = (bf16[512,1024]{1,0:T(8,128)(2,1)}, bf16[512,1024]{1,0:T(8,128)(2,1)S(1)}, u32[]{:S(2)}, u32[]{:S(2)}) collective-permute-start(bf16[512,1024]{1,0:T(8,128)(2,1)} %get-tuple-element.30), channel_id=1, source_target_pairs={{0,4},{12,8},{1,5},{13,9},{2,6},{14,10},{3,7},{15,11},{16,20},{28,... | collective-permute-start | bytes 3145736 | tf_op jit(solution)/shard_map/ppermute | solution.py:131
  30.8 35.4 %collective-permute-start.4 = (bf16[256,1024]{1,0:T(8,128)(2,1)}, bf16[256,1024]{1,0:T(8,128)(2,1)S(1)}, u32[]{:S(2)}, u32[]{:S(2)}) collective-permute-start(bf16[256,1024]{1,0:T(8,128)(2,1)} %get-tuple-element.17), channel_id=1, source_target_pairs={{4,8},{8,4},{5,9},{9,5},{6,10},{10,6},{7,11},{11,7},{20,24},{24,20... | collective-permute-start | bytes 1572872 | tf_op jit(solution)/shard_map/ppermute | solution.py:134
  31.5 28.4 %collective-permute-start.3 = (bf16[256,1024]{1,0:T(8,128)(2,1)}, bf16[256,1024]{1,0:T(8,128)(2,1)S(1)}, u32[]{:S(2)}, u32[]{:S(2)}) collective-permute-start(bf16[256,1024]{1,0:T(8,128)(2,1)} %get-tuple-element.16), channel_id=1, source_target_pairs={{4,8},{8,4},{5,9},{9,5},{6,10},{10,6},{7,11},{11,7},{20,24},{24,20... | collective-permute-start | bytes 1572872 | tf_op jit(solution)/shard_map/ppermute | solution.py:134
  32.2 31.6 %collective-permute-start.9 = (bf16[256,1024]{1,0:T(8,128)(2,1)}, bf16[256,1024]{1,0:T(8,128)(2,1)S(1)}, u32[]{:S(2)}, u32[]{:S(2)}) collective-permute-start(bf16[256,1024]{1,0:T(8,128)(2,1)} %get-tuple-element.18), channel_id=1, source_target_pairs={{0,4},{12,8},{1,5},{13,9},{2,6},{14,10},{3,7},{15,11},{16,20},{28,... | collective-permute-start | bytes 1572872 | tf_op jit(solution)/shard_map/ppermute | solution.py:131
  41.2 23.3 %slice-start = ((s8[8388608]{0:T(1024)(128)(4,1)}), s8[4194304]{0:T(1024)(128)(4,1)S(1)}, s32[]{:S(2)}) async-start(s8[8388608]{0:T(1024)(128)(4,1)} %bitcast.383), calls=%async_computation | async-start | bytes 8388608
  56.7 15.6 %collective-permute-start.20 = (f32[256,512]{1,0:T(8,128)S(1)}, f32[256,512]{1,0:T(8,128)S(1)}, u32[]{:S(2)}, u32[]{:S(2)}) collective-permute-start(f32[256,512]{1,0:T(8,128)S(1)} %get-tuple-element.47), channel_id=1, source_target_pairs={{4,5},{6,7},{5,4},{7,6},{9,8},{11,10},{8,9},{10,11},{20,21},{22,23... | collective-permute-start | bytes 1572872 | tf_op jit(solution)/shard_map/ppermute | solution.py:85
  59.9 65.0 %collective-permute-start.7 = (bf16[256,1024]{1,0:T(8,128)(2,1)}, bf16[256,1024]{1,0:T(8,128)(2,1)S(1)}, u32[]{:S(2)}, u32[]{:S(2)}) collective-permute-start(bf16[256,1024]{1,0:T(8,128)(2,1)} %collective-permute-done.1), channel_id=1, source_target_pairs={{4,0},{8,12},{5,1},{9,13},{6,2},{10,14},{7,3},{11,15},{20,16},{24,... | collective-permute-start | bytes 1572872 | tf_op jit(solution)/shard_map/ppermute | solution.py:137
  63.8 9.9 %collective-permute-start.15 = (bf16[256,1024]{1,0:T(8,128)(2,1)S(1)}, bf16[256,1024]{1,0:T(8,128)(2,1)S(1)}, u32[]{:S(2)}, u32[]{:S(2)}) collective-permute-start(bf16[256,1024]{1,0:T(8,128)(2,1)S(1)} %collective-permute-done.9), channel_id=1, source_target_pairs={{4,8},{8,4},{5,9},{9,5},{6,10},{10,6},{7,11},{11,7},{20,24},{24,20... | collective-permute-start | bytes 1572872 | tf_op jit(solution)/shard_map/ppermute | solution.py:134
  66.2 27.4 %collective-permute-start.12 = (bf16[512,1024]{1,0:T(8,128)(2,1)S(1)}, bf16[512,1024]{1,0:T(8,128)(2,1)S(1)}, u32[]{:S(2)}, u32[]{:S(2)}) collective-permute-start(bf16[512,1024]{1,0:T(8,128)(2,1)S(1)} %copy-done.3), channel_id=1, source_target_pairs={{0,4},{12,8},{1,5},{13,9},{2,6},{14,10},{3,7},{15,11},{16,20},{28,... | collective-permute-start | bytes 3145736 | tf_op jit(solution)/shard_map/ppermute | solution.py:131
  72.3 39.4 %collective-permute-start.14 = (bf16[256,1024]{1,0:T(8,128)(2,1)S(1)}, bf16[256,1024]{1,0:T(8,128)(2,1)S(1)}, u32[]{:S(2)}, u32[]{:S(2)}) collective-permute-start(bf16[256,1024]{1,0:T(8,128)(2,1)S(1)} %collective-permute-done.4), channel_id=1, source_target_pairs={{4,0},{8,12},{5,1},{9,13},{6,2},{10,14},{7,3},{11,15},{20,16},{24,... | collective-permute-start | bytes 1572872 | tf_op jit(solution)/shard_map/ppermute | solution.py:137
  73.7 21.2 %collective-permute-start.21 = (f32[256,512]{1,0:T(8,128)S(1)}, f32[256,512]{1,0:T(8,128)S(1)}, u32[]{:S(2)}, u32[]{:S(2)}) collective-permute-start(f32[256,512]{1,0:T(8,128)S(1)} %select_add_fusion.1), channel_id=1, source_target_pairs={{7,5},{4,6},{8,10},{11,9},{23,21},{20,22},{24,26},{27,25}} | collective-permute-start | bytes 1572872 | tf_op jit(solution)/shard_map/ppermute | solution.py:87
  74.5 25.8 %collective-permute-start.16 = (bf16[256,1024]{1,0:T(8,128)(2,1)S(1)}, bf16[256,1024]{1,0:T(8,128)(2,1)S(1)}, u32[]{:S(2)}, u32[]{:S(2)}) collective-permute-start(bf16[256,1024]{1,0:T(8,128)(2,1)S(1)} %collective-permute-done.15), channel_id=1, source_target_pairs={{4,0},{8,12},{5,1},{9,13},{6,2},{10,14},{7,3},{11,15},{20,16},{24,... | collective-permute-start | bytes 1572872 | tf_op jit(solution)/shard_map/ppermute | solution.py:137
  93.7 24.1 %collective-permute-start.10 = (bf16[256,1024]{1,0:T(8,128)(2,1)S(1)}, bf16[256,1024]{1,0:T(8,128)(2,1)S(1)}, u32[]{:S(2)}, u32[]{:S(2)}) collective-permute-start(bf16[256,1024]{1,0:T(8,128)(2,1)S(1)} %collective-permute-done.3), channel_id=1, source_target_pairs={{4,0},{8,12},{5,1},{9,13},{6,2},{10,14},{7,3},{11,15},{20,16},{24,... | collective-permute-start | bytes 1572872 | tf_op jit(solution)/shard_map/ppermute | solution.py:137
  95.0 39.7 %collective-permute-start.5 = (f32[256,1024]{1,0:T(8,128)S(1)}, f32[256,1024]{1,0:T(8,128)S(1)}, u32[]{:S(2)}, u32[]{:S(2)}) collective-permute-start(f32[256,1024]{1,0:T(8,128)S(1)} %get-tuple-element.45), channel_id=1, source_target_pairs={{1,0},{3,2},{0,1},{2,3},{4,5},{6,7},{5,4},{7,6},{9,8},{11,10},{8,9... | collective-permute-start | bytes 3145736 | tf_op jit(solution)/shard_map/ppermute | solution.py:85
  100.3 7.0 %collective-permute-start.13 = (bf16[2,64,1024]{2,1,0:T(8,128)(2,1)S(1)}, bf16[2,64,1024]{2,1,0:T(8,128)(2,1)S(1)}, u32[]{:S(2)}, u32[]{:S(2)}) collective-permute-start(bf16[2,64,1024]{2,1,0:T(8,128)(2,1)S(1)} %copy-done.6), channel_id=1, source_target_pairs={{0,4},{12,8},{1,5},{13,9},{2,6},{14,10},{3,7},{15,11},{16,20},{28,... | collective-permute-start | bytes 786440 | tf_op jit(solution)/shard_map/ppermute | solution.py:131
  107.5 8.9 %collective-permute-start.25 = (bf16[2,64,1024]{2,1,0:T(8,128)(2,1)S(1)}, bf16[2,64,1024]{2,1,0:T(8,128)(2,1)S(1)}, u32[]{:S(2)}, u32[]{:S(2)}) collective-permute-start(bf16[2,64,1024]{2,1,0:T(8,128)(2,1)S(1)} %copy-done.5), channel_id=1, source_target_pairs={{0,4},{12,8},{1,5},{13,9},{2,6},{14,10},{3,7},{15,11},{16,20},{28,... | collective-permute-start | bytes 786440 | tf_op jit(solution)/shard_map/ppermute | solution.py:131
  111.7 24.5 %collective-permute-start.22 = (bf16[256,1024]{1,0:T(8,128)(2,1)}, bf16[256,1024]{1,0:T(8,128)(2,1)S(1)}, u32[]{:S(2)}, u32[]{:S(2)}) collective-permute-start(bf16[256,1024]{1,0:T(8,128)(2,1)} %collective-permute-done.8), channel_id=1, source_target_pairs={{4,8},{8,4},{5,9},{9,5},{6,10},{10,6},{7,11},{11,7},{20,24},{24,20... | collective-permute-start | bytes 1572872 | tf_op jit(solution)/shard_map/ppermute | solution.py:134
  116.4 25.3 %collective-permute-start.40 = (f32[256,512]{1,0:T(8,128)S(1)}, f32[256,512]{1,0:T(8,128)S(1)}, u32[]{:S(2)}, u32[]{:S(2)}) collective-permute-start(f32[256,512]{1,0:T(8,128)S(1)} %select_bitcast_fusion), channel_id=1, source_target_pairs={{4,5},{6,7},{5,4},{7,6},{9,8},{11,10},{8,9},{10,11},{20,21},{22,23... | collective-permute-start | bytes 1572872 | tf_op jit(solution)/shard_map/ppermute | solution.py:85
  117.8 11.8 %collective-permute-start.30 = (bf16[2,64,1024]{2,1,0:T(8,128)(2,1)S(1)}, bf16[2,64,1024]{2,1,0:T(8,128)(2,1)S(1)}, u32[]{:S(2)}, u32[]{:S(2)}) collective-permute-start(bf16[2,64,1024]{2,1,0:T(8,128)(2,1)S(1)} %copy-done.4), channel_id=1, source_target_pairs={{0,4},{12,8},{1,5},{13,9},{2,6},{14,10},{3,7},{15,11},{16,20},{28,... | collective-permute-start | bytes 786440 | tf_op jit(solution)/shard_map/ppermute | solution.py:131
  125.0 7.7 %collective-permute-start.26 = (bf16[2,64,1024]{2,1,0:T(8,128)(2,1)S(1)}, bf16[2,64,1024]{2,1,0:T(8,128)(2,1)S(1)}, u32[]{:S(2)}, u32[]{:S(2)}) collective-permute-start(bf16[2,64,1024]{2,1,0:T(8,128)(2,1)S(1)} %collective-permute-done.25), channel_id=1, source_target_pairs={{4,8},{8,4},{5,9},{9,5},{6,10},{10,6},{7,11},{11,7},{20,24},{24,20... | collective-permute-start | bytes 786440 | tf_op jit(solution)/shard_map/ppermute | solution.py:134
  129.7 3.7 %collective-permute-start.17 = (bf16[2,64,1024]{2,1,0:T(8,128)(2,1)S(1)}, bf16[2,64,1024]{2,1,0:T(8,128)(2,1)S(1)}, u32[]{:S(2)}, u32[]{:S(2)}) collective-permute-start(bf16[2,64,1024]{2,1,0:T(8,128)(2,1)S(1)} %collective-permute-done.13), channel_id=1, source_target_pairs={{4,8},{8,4},{5,9},{9,5},{6,10},{10,6},{7,11},{11,7},{20,24},{24,20... | collective-permute-start | bytes 786440 | tf_op jit(solution)/shard_map/ppermute | solution.py:134
  132.7 21.1 %collective-permute-start.31 = (bf16[2,64,1024]{2,1,0:T(8,128)(2,1)S(1)}, bf16[2,64,1024]{2,1,0:T(8,128)(2,1)S(1)}, u32[]{:S(2)}, u32[]{:S(2)}) collective-permute-start(bf16[2,64,1024]{2,1,0:T(8,128)(2,1)S(1)} %collective-permute-done.30), channel_id=1, source_target_pairs={{4,8},{8,4},{5,9},{9,5},{6,10},{10,6},{7,11},{11,7},{20,24},{24,20... | collective-permute-start | bytes 786440 | tf_op jit(solution)/shard_map/ppermute | solution.py:134
  133.4 18.0 %collective-permute-start.27 = (bf16[2,64,1024]{2,1,0:T(8,128)(2,1)S(1)}, bf16[2,64,1024]{2,1,0:T(8,128)(2,1)S(1)}, u32[]{:S(2)}, u32[]{:S(2)}) collective-permute-start(bf16[2,64,1024]{2,1,0:T(8,128)(2,1)S(1)} %collective-permute-done.26), channel_id=1, source_target_pairs={{4,0},{8,12},{5,1},{9,13},{6,2},{10,14},{7,3},{11,15},{20,16},{24,... | collective-permute-start | bytes 786440 | tf_op jit(solution)/shard_map/ppermute | solution.py:137
  134.7 19.5 %collective-permute-start.18 = (bf16[2,64,1024]{2,1,0:T(8,128)(2,1)S(1)}, bf16[2,64,1024]{2,1,0:T(8,128)(2,1)S(1)}, u32[]{:S(2)}, u32[]{:S(2)}) collective-permute-start(bf16[2,64,1024]{2,1,0:T(8,128)(2,1)S(1)} %collective-permute-done.17), channel_id=1, source_target_pairs={{4,0},{8,12},{5,1},{9,13},{6,2},{10,14},{7,3},{11,15},{20,16},{24,... | collective-permute-start | bytes 786440 | tf_op jit(solution)/shard_map/ppermute | solution.py:137
  136.3 38.9 %collective-permute-start.6 = (f32[256,1024]{1,0:T(8,128)S(1)}, f32[256,1024]{1,0:T(8,128)S(1)}, u32[]{:S(2)}, u32[]{:S(2)}) collective-permute-start(f32[256,1024]{1,0:T(8,128)S(1)} %select_add_fusion), channel_id=1, source_target_pairs={{2,0},{3,1},{7,5},{4,6},{8,10},{11,9},{13,15},{12,14},{18,16},{19,... | collective-permute-start | bytes 3145736 | tf_op jit(solution)/shard_map/ppermute | solution.py:87
  141.7 35.0 %collective-permute-start.42 = (f32[256,1024]{1,0:T(8,128)S(1)}, f32[256,1024]{1,0:T(8,128)S(1)}, u32[]{:S(2)}, u32[]{:S(2)}) collective-permute-start(f32[256,1024]{1,0:T(8,128)S(1)} %pad_maximum_fusion), channel_id=1, source_target_pairs={{4,5},{6,7},{9,8},{11,10},{20,21},{22,23},{25,24},{27,26}} | collective-permute-start | bytes 3145736 | tf_op jit(solution)/shard_map/ppermute | solution.py:61
  151.3 21.8 %collective-permute-start.41 = (f32[256,512]{1,0:T(8,128)S(1)}, f32[256,512]{1,0:T(8,128)S(1)}, u32[]{:S(2)}, u32[]{:S(2)}) collective-permute-start(f32[256,512]{1,0:T(8,128)S(1)} %bitcast_add_fusion), channel_id=1, source_target_pairs={{7,5},{4,6},{8,10},{11,9},{23,21},{20,22},{24,26},{27,25}} | collective-permute-start | bytes 1572872 | tf_op jit(solution)/shard_map/ppermute | solution.py:87
  153.8 15.2 %collective-permute-start.28 = (f32[64,1024]{1,0:T(8,128)S(1)}, f32[64,1024]{1,0:T(8,128)S(1)}, u32[]{:S(2)}, u32[]{:S(2)}) collective-permute-start(f32[64,1024]{1,0:T(8,128)S(1)} %get-tuple-element.53), channel_id=1, source_target_pairs={{1,0},{3,2},{0,1},{2,3},{5,4},{7,6},{4,5},{6,7},{8,9},{10,11},{9,8... | collective-permute-start | bytes 786440 | tf_op jit(solution)/shard_map/ppermute | solution.py:85
  154.1 12.6 %collective-permute-start.32 = (bf16[2,64,1024]{2,1,0:T(8,128)(2,1)S(1)}, bf16[2,64,1024]{2,1,0:T(8,128)(2,1)S(1)}, u32[]{:S(2)}, u32[]{:S(2)}) collective-permute-start(bf16[2,64,1024]{2,1,0:T(8,128)(2,1)S(1)} %collective-permute-done.31), channel_id=1, source_target_pairs={{4,0},{8,12},{5,1},{9,13},{6,2},{10,14},{7,3},{11,15},{20,16},{24,... | collective-permute-start | bytes 786440 | tf_op jit(solution)/shard_map/ppermute | solution.py:137
  166.7 3.6 %collective-permute-start.23 = (f32[64,1024]{1,0:T(8,128)S(1)}, f32[64,1024]{1,0:T(8,128)S(1)}, u32[]{:S(2)}, u32[]{:S(2)}) collective-permute-start(f32[64,1024]{1,0:T(8,128)S(1)} %get-tuple-element.55), channel_id=1, source_target_pairs={{1,0},{3,2},{0,1},{2,3},{5,4},{7,6},{4,5},{6,7},{8,9},{10,11},{9,8... | collective-permute-start | bytes 786440 | tf_op jit(solution)/shard_map/ppermute | solution.py:85
  169.1 43.4 %collective-permute-start.33 = (f32[64,1024]{1,0:T(8,128)}, f32[64,1024]{1,0:T(8,128)}, u32[]{:S(2)}, u32[]{:S(2)}) collective-permute-start(f32[64,1024]{1,0:T(8,128)} %get-tuple-element.51), channel_id=1, source_target_pairs={{1,0},{3,2},{0,1},{2,3},{5,4},{7,6},{4,5},{6,7},{8,9},{10,11},{9,8... | collective-permute-start | bytes 786440 | tf_op jit(solution)/shard_map/ppermute | solution.py:85
  170.3 47.5 %collective-permute-start.29 = (f32[64,1024]{1,0:T(8,128)}, f32[64,1024]{1,0:T(8,128)}, u32[]{:S(2)}, u32[]{:S(2)}) collective-permute-start(f32[64,1024]{1,0:T(8,128)} %select_add_fusion.4), channel_id=1, source_target_pairs={{0,2},{1,3},{6,4},{5,7},{9,11},{10,8},{15,13},{14,12},{16,18},{17,... | collective-permute-start | bytes 786440 | tf_op jit(solution)/shard_map/ppermute | solution.py:87
  173.1 45.8 %collective-permute-start.24 = (f32[64,1024]{1,0:T(8,128)}, f32[64,1024]{1,0:T(8,128)}, u32[]{:S(2)}, u32[]{:S(2)}) collective-permute-start(f32[64,1024]{1,0:T(8,128)} %select_add_fusion.5), channel_id=1, source_target_pairs={{0,2},{1,3},{6,4},{5,7},{9,11},{10,8},{15,13},{14,12},{16,18},{17,... | collective-permute-start | bytes 786440 | tf_op jit(solution)/shard_map/ppermute | solution.py:87
  175.3 7.3 %collective-permute-start.35 = (bf16[2,64,1024]{2,1,0:T(8,128)(2,1)S(1)}, bf16[2,64,1024]{2,1,0:T(8,128)(2,1)S(1)}, u32[]{:S(2)}, u32[]{:S(2)}) collective-permute-start(bf16[2,64,1024]{2,1,0:T(8,128)(2,1)S(1)} %get-tuple-element.25), channel_id=1, source_target_pairs={{0,4},{12,8},{1,5},{13,9},{2,6},{14,10},{3,7},{15,11},{16,20},{28,... | collective-permute-start | bytes 786440 | tf_op jit(solution)/shard_map/ppermute | solution.py:131
  176.8 27.2 %collective-permute-start.43 = (f32[256,1024]{1,0:T(8,128)S(1)}, f32[256,1024]{1,0:T(8,128)S(1)}, u32[]{:S(2)}, u32[]{:S(2)}) collective-permute-start(f32[256,1024]{1,0:T(8,128)S(1)} %fusion.464), channel_id=1, source_target_pairs={{5,7},{10,8},{21,23},{26,24}} | collective-permute-start | bytes 3145736 | tf_op jit(solution)/shard_map/ppermute | solution.py:69
  183.4 1.4 collective-permute-start.36
  184.8 16.9 %collective-permute-start.37 = (bf16[2,64,1024]{2,1,0:T(8,128)(2,1)S(1)}, bf16[2,64,1024]{2,1,0:T(8,128)(2,1)S(1)}, u32[]{:S(2)}, u32[]{:S(2)}) collective-permute-start(bf16[2,64,1024]{2,1,0:T(8,128)(2,1)S(1)} %collective-permute-done.36), channel_id=1, source_target_pairs={{4,0},{8,12},{5,1},{9,13},{6,2},{10,14},{7,3},{11,15},{20,16},{24,... | collective-permute-start | bytes 786440 | tf_op jit(solution)/shard_map/ppermute | solution.py:137
  204.0 11.4 %collective-permute-start.38 = (f32[64,1024]{1,0:T(8,128)}, f32[64,1024]{1,0:T(8,128)}, u32[]{:S(2)}, u32[]{:S(2)}) collective-permute-start(f32[64,1024]{1,0:T(8,128)} %get-tuple-element.49), channel_id=1, source_target_pairs={{1,0},{3,2},{0,1},{2,3},{5,4},{7,6},{4,5},{6,7},{8,9},{10,11},{9,8... | collective-permute-start | bytes 786440 | tf_op jit(solution)/shard_map/ppermute | solution.py:85
  205.6 5.5 %collective-permute-start.44 = (f32[8,128]{1,0:T(8,128)S(1)}, f32[8,128]{1,0:T(8,128)S(1)}, u32[]{:S(2)}, u32[]{:S(2)}) collective-permute-start(f32[8,128]{1,0:T(8,128)S(1)} %broadcast_in_dim.6), channel_id=1, source_target_pairs={{4,0},{8,12},{5,1},{9,13},{6,2},{10,14},{7,3},{11,15},{20,16},{24,... | collective-permute-start | bytes 12296 | tf_op jit(solution)/shard_map/ppermute | solution.py:137
  211.1 15.3 %collective-permute-start.45 = (f16[256,1024]{1,0:T(8,128)(2,1)}, f16[256,1024]{1,0:T(8,128)(2,1)S(1)}, u32[]{:S(2)}, u32[]{:S(2)}) collective-permute-start(f16[256,1024]{1,0:T(8,128)(2,1)} %multiply_convert_fusion), channel_id=1, source_target_pairs={{4,0},{8,12},{5,1},{9,13},{6,2},{10,14},{7,3},{11,15},{20,16},{24,... | collective-permute-start | bytes 1572872 | tf_op jit(solution)/shard_map/ppermute | solution.py:137
  213.4 8.7 %collective-permute-start.34 = (f32[64,1024]{1,0:T(8,128)S(1)}, f32[64,1024]{1,0:T(8,128)S(1)}, u32[]{:S(2)}, u32[]{:S(2)}) collective-permute-start(f32[64,1024]{1,0:T(8,128)S(1)} %select_add_fusion.3), channel_id=1, source_target_pairs={{0,2},{1,3},{6,4},{5,7},{9,11},{10,8},{15,13},{14,12},{16,18},{17,... | collective-permute-start | bytes 786440 | tf_op jit(solution)/shard_map/ppermute | solution.py:87
  216.4 9.7 %collective-permute-start.39 = (f32[64,1024]{1,0:T(8,128)S(1)}, f32[64,1024]{1,0:T(8,128)S(1)}, u32[]{:S(2)}, u32[]{:S(2)}) collective-permute-start(f32[64,1024]{1,0:T(8,128)S(1)} %select_add_fusion.2), channel_id=1, source_target_pairs={{0,2},{1,3},{6,4},{5,7},{9,11},{10,8},{15,13},{14,12},{16,18},{17,... | collective-permute-start | bytes 786440 | tf_op jit(solution)/shard_map/ppermute | solution.py:87
  (8 other events, 93.3 us)

commit v4 on v3

--- a/solution.py
+++ b/solution.py
@@ -4,7 +4,6 @@
 from jax.sharding import PartitionSpec as P
 
 PLACE = ("ex", "ckpt", "dim")
-CHUNKS = 4
 
 
 def after(value, *others):
@@ -73,15 +72,15 @@
         keeps_one = jnp.bool_(False)
         swaps, crosses = [], []
         for z, blocks in enumerate(zip(one_blocks, two_blocks)):
-            if blocks[0] is None:
-                continue
-            places = [self.of(block) for block in blocks]
-            assert {places[0][1], places[1][1]} == {0, 1}
-            keeps_one = keeps_one | ((self.z == z) & (self.c == places[0][1]))
-            for at, c in places:
-                for x in range(2):
-                    swaps.append((self.index(z, x, 1 - c), self.index(z, x, c)))
-                crosses.append((self.index(z, 1 - at, c), self.index(z, at, c)))
+            places = [None if block is None else self.of(block) for block in blocks]
+            second = places[1][1]
+            assert places[0] is None or places[0][1] == 1 - second
+            keeps_one = keeps_one | ((self.z == z) & (self.c == 1 - second))
+            for place in places:
+                if place is not None:
+                    at, c = place
+                    swaps += [(self.index(z, x, 1 - c), self.index(z, x, c)) for x in range(2)]
+                    crosses.append((self.index(z, 1 - at, c), self.index(z, at, c)))
         got = lax.ppermute(jnp.where(keeps_one, two, one), PLACE, swaps)
         total = jnp.where(keeps_one, one, two) + got
         return total + lax.ppermute(total, PLACE, crosses)
@@ -120,11 +119,11 @@
 
 
 def line(train_features, query_features, residual_weights, keepers, scale):
-    z = keepers.z
-    rows = query_features.shape[1]
-    most = train_features.shape[0] - 1
+    z, x, c = keepers.z, keepers.x, keepers.c
+    rows, depth = query_features.shape[1:]
     examples = train_features.shape[1]
-    half, cut = examples // 2, rows // CHUNKS
+    half, low = examples // 2, rows // 2
+    assert train_features.shape[0] == 4 and half <= depth
     ends = (z == 0) | (z == 3)
 
     def inward(value):
@@ -136,84 +135,103 @@
     def outward(value):
         return lax.ppermute(value, "ex", [(1, 0), (2, 3)])
 
-    own_many, own_one = query_features[:most], query_features[most]
-    train_one = train_features[most]
-
-    out_own = outward(own_many)
-    in_one = inward(own_one)
-    mid_one = between(own_one)
-    in_weight = inward(residual_weights[most:])[0]
-    in_train = [inward(after(train_one[:half], in_weight))]
-    mid_many = [between(own_many[0])]
-    out_many = [outward(mid_many[0])]
-    mid_many.append(between(after(own_many[1], mid_one)))
-    out_many.append(outward(mid_many[1]))
-    mid_many.append(between(after(own_many[2], mid_many[0])))
-    out_many.append(outward(mid_many[2]))
-
-    own = weighted(list(query_features), train_features, residual_weights, scale)
-
-    in_first = inward(after(own_many[0], in_one))
-    in_train.append(inward(after(train_one[half:], in_train[0])))
-    mid_first = between(after(in_first, mid_many[1]))
-    out_first = outward(mid_first)
+    def scores(checks):
+        return weighted(checks, train_features, residual_weights, scale)
+
+    def chosen(far, near):
+        return after(jnp.where(ends, far, near))
+
+    def training(part):
+        columns = slice(part * half, (part + 1) * half)
+        left, pieces = residual_weights[0, columns], []
+        for unused in range(3):
+            rounded = lax.reduce_precision(left, 8, 7)
+            pieces.append(rounded.astype(jnp.bfloat16))
+            left = left - rounded
+        tail = jnp.pad(jnp.stack(pieces), ((0, 13), (0, depth - half)))
+        return jnp.concatenate([train_features[0, columns], tail], axis=0)
+
+    out_own = outward(query_features[1:])
+    in_many = inward(query_features[:3])
+    mid_a = between(query_features[:2])
+    own = scores(list(query_features))
+    mid_b = between(after(query_features[2:], mid_a))
+    out_a = outward(mid_a[1])
+    in_train = [inward(after(training(0), in_many))]
+    out_b = outward(mid_b)
+    mid_c = between(after(in_many[:2], mid_b))
+    in_train.append(inward(after(training(1), in_train[0])))
 
     blocks_own = [0, 1, 2, 3]
     blocks_1 = [1, 2, 1, 2]
-    blocks_2 = [2, 0, 3, 1]
-    blocks_3 = [3, 3, 0, 0]
-
-    checks = [jnp.where(ends, out_own[i], mid_many[i]) for i in range(most)] + [mid_one]
-    found_1 = weighted(checks, train_features, residual_weights, scale)
-    result_a = keepers.two_sums(own, blocks_own, found_1, blocks_1)
-
-    beside_0 = [None, 1, 2, None]
-    beside_1 = [None, 2, 1, None]
-    beside_2 = [None, 3, 0, None]
-
-    def beside(part):
-        columns = slice(part * half, (part + 1) * half)
+    blocks_2 = [2, None, None, 1]
+    blocks_3 = [None, 0, 3, None]
+    blocks_4 = [3, 3, 0, 0]
+
+    one = mid_a[0]
+    checks = [one, chosen(out_own[0], mid_a[1])]
+    later = chosen(out_own[1:], mid_b)
+    found_1 = scores(checks + [later[0], later[1]])
+    result_1 = keepers.two_sums(own, blocks_own, found_1, blocks_1)
+
+    mid_d = between(after(in_many[2], mid_c))
+    out_c = outward(mid_c[1])
+    out_d = outward(mid_d)
+
+    def three(part):
+        block = in_train[part]
+        weights = jnp.sum(block[half:half + 3, :half].astype(jnp.float32), axis=0)
 
         def of(queries):
-            return weighted([queries], [in_train[part]], [in_weight[columns]], scale)
-
-        both = keepers.two_sums(of(own_one), beside_0, of(mid_one), beside_1)
-        return both, of
-
-    both_0, of_0 = beside(0)
-    mid_in_one = between(after(in_one, both_0, mid_first))
-    both_1, of_1 = beside(1)
-    third = jnp.concatenate([of_0(mid_in_one), of_1(mid_in_one)], axis=1)
-    third = keepers.sums(third, beside_2)
-    both = jnp.concatenate([both_0, both_1], axis=1)
-    mine_both = keepers.mine(beside_0) | keepers.mine(beside_1)
-    returned = jnp.where(mine_both, both, jnp.where(keepers.mine(beside_2), third, 0.0))
-    largest = jnp.maximum(jnp.max(jnp.abs(returned)), 1e-30)
-    small = (returned * (16384.0 / largest)).astype(jnp.float16)
-
-    results_b = []
-    ins = [in_train[1], in_train[1]]
-    for k in range(CHUNKS):
-        part = slice(k * cut, (k + 1) * cut)
-        got = inward(after(own_many[1:, part], ins[-2], *([result_a] if k == CHUNKS - 1 else [])))
-        ins.append(got)
-        mid = between(got)
+            return weighted([queries], [block[:half]], [weights], scale)
+
+        first, second, third = of(query_features[0]), of(one), of(mid_c[0])
+        alone = ((z == 1) & (c == 0)) | ((z == 2) & (c == 1))
+        pair = jnp.concatenate([first, third], axis=0)
+        lone = jnp.concatenate([second, second], axis=0)
+        swaps = [(keepers.index(p, q, r), keepers.index(p, q, 1 - r)) for p in (1, 2) for q in range(2) for r in range(2)]
+        got = lax.ppermute(jnp.where(alone, pair, lone), PLACE, swaps)
+        total = jnp.where(alone, lone, pair) + got
+        upper, lower = total[:rows], total[rows:]
+        keeps_first = keepers.mine([None, 1, 2, None])
+        crosses = []
+        for p, blocks in ((1, (1, 2, 3)), (2, (2, 1, 0))):
+            for block in blocks:
+                at, r = keepers.of(block)
+                crosses.append((keepers.index(p, 1 - at, r), keepers.index(p, at, r)))
+        got = lax.ppermute(jnp.where(keeps_first, lower, upper), PLACE, crosses)
+        return jnp.where(keeps_first, upper, lower) + got
+
+    ones = train_features[1:], residual_weights[1:]
+    block_2 = weighted([out_a, out_b[0], out_b[1]], *ones, scale)
+    result_2 = keepers.sums(block_2, blocks_2)
+
+    last = train_features[3:], residual_weights[3:]
+    base_3 = weighted(list(in_many), train_features, residual_weights, scale)
+    checks = [mid_c[0], chosen(out_c, mid_c[1]), chosen(out_d, mid_d)]
+    base_4 = weighted(checks, train_features, residual_weights, scale)
+    results, before = [], in_train[1]
+    for k in range(2):
+        part = slice(k * low, (k + 1) * low)
+        before = inward(after(query_features[3, part], before))
+        mid = between(before)
         out = outward(mid)
-        near_2 = [in_first[part]] + list(got)
-        far_2 = [out_many[i][part] for i in range(most)]
-        near_3 = [mid_first[part]] + list(mid)
-        far_3 = [out_first[part]] + list(out)
-        checks_2 = [jnp.where(ends, a, b) for a, b in zip(far_2, near_2)] + [in_one[part]]
-        checks_3 = [jnp.where(ends, a, b) for a, b in zip(far_3, near_3)] + [mid_in_one[part]]
-        found_2 = weighted(checks_2, train_features, residual_weights, scale)
-        found_3 = weighted(checks_3, train_features, residual_weights, scale)
-        results_b.append(keepers.two_sums(found_2, blocks_2, found_3, blocks_3))
-
-    unit = outward(jnp.full((8, 128), largest * (1.0 / 16384.0)))
-    small = outward(after(small, mid, unit))
-    mine_a = keepers.mine(blocks_own) | keepers.mine(blocks_1)
-    result = jnp.where(mine_a, result_a, jnp.concatenate(results_b, axis=0))
-    return result + small.astype(jnp.float32) * unit[0, 0]
+        block_3 = base_3[part] + weighted([before], *last, scale)
+        block_4 = base_4[part] + weighted([chosen(out, mid)], *last, scale)
+        results.append(keepers.two_sums(block_3, blocks_3, block_4, blocks_4))
+
+    returned = jnp.concatenate([three(0), three(1)], axis=1)
+    returned = jnp.where(keepers.mine([None, 0, 3, None]), 0.0, returned)
+    largest = jnp.clip(jnp.max(jnp.abs(returned)), 1e-30, 1e30)
+    power = jnp.floor(jnp.log2(largest))
+    small = (returned * jnp.exp2(13.0 - power)).astype(jnp.float16)
+    small = jnp.concatenate([small, jnp.full((16, examples), power, jnp.float16)], axis=0)
+    small = outward(after(small, mid))
+    power = small[rows, 0].astype(jnp.float32)
+
+    result = jnp.where(keepers.mine(blocks_2), result_2, jnp.concatenate(results, axis=0))
+    result = jnp.where(keepers.mine(blocks_own) | keepers.mine(blocks_1), result_1, result)
+    return result + small[:rows].astype(jnp.float32) * jnp.exp2(power - 13.0)
 
 
 def local(train_features, query_features, residual_weights):

time: 230 us -> 212 us (0.922)
  starting transfers between devices: 79.2 us -> 53.6 us
  matrix products: 50 us -> 32 us
  waiting for transfers between devices: 79.4 us -> 94.3 us
  local copies, waits for them, and re-layouts: 7.47 us -> 13.6 us
  other arithmetic: 10.5 us -> 14.7 us
    ppermute x11 -> x8, waiting for transfers between devices: 42.2 us -> 81.8 us  [outward(): return lax.ppermute(value, 'ex', [(1, 0), (2, 3)])]
    ppermute x9 -> x5, starting transfers between devices: 42.7 us -> 22 us  [inward(): return lax.ppermute(value, 'ex', [(0, 1), (3, 2)])]
    ppermute x9 -> x5, waiting for transfers between devices: 31.5 us -> 12.4 us  [inward(): return lax.ppermute(value, 'ex', [(0, 1), (3, 2)])]
    dot_general x46 -> x27, matrix products: 50 us -> 32 us  [weighted(): lax.dot_general(piece, examples, (((1,), (1,)), ((), ())), preferred_elem...]
    ppermute x7 -> x3, starting transfers between devices: 10.2 us -> 4.22 us  [two_sums(): return total + lax.ppermute(total, PLACE, crosses)]
    ppermute x7 -> x3, waiting for transfers between devices: 5.64 us -> 0.01 us  [two_sums(): return total + lax.ppermute(total, PLACE, crosses)]
    slice x5 -> x4, local copies, waits for them, and re-layouts: 4.23 us -> 8.28 us  [the longest x1 4.26 us: line(): out_own = outward(query_features[1:])]
    ppermute x11 -> x8, starting transfers between devices: 14.2 us -> 10.3 us  [outward(): return lax.ppermute(value, 'ex', [(1, 0), (2, 3)])]
  transfers between devices with their start and end apart: 46 -> 31, of which waited for: 16 -> 10; matrix products, arithmetic and copies ran while one was open for 28% -> 25% of each run, Pallas kernels for 0% -> 0%
where the time goes in v4:
time: 212 us; the launch traced here: 211 us
  waiting for transfers between devices  94.3 us (44%)
  starting transfers between devices  53.6 us (25%)
  matrix products  32 us (15%)
  other arithmetic  14.7 us (7%)
  local copies, waits for them, and re-layouts  13.6 us (6%)
  between operations  2.32 us (1%)
    ppermute x8, waiting for transfers between devices, outward(): return lax.ppermute(value, 'ex', [(1, 0), (2, 3)])  81.8 us
    dot_general x27, matrix products, weighted(): lax.dot_general(piece, examples, (((1,), (1,)), ((), ())), preferred_elem...  32 us
    ppermute x5, starting transfers between devices, inward(): return lax.ppermute(value, 'ex', [(0, 1), (3, 2)])  22 us
    ppermute x5, waiting for transfers between devices, inward(): return lax.ppermute(value, 'ex', [(0, 1), (3, 2)])  12.4 us
    ppermute x8, starting transfers between devices, outward(): return lax.ppermute(value, 'ex', [(1, 0), (2, 3)])  10.3 us
    ppermute x6, starting transfers between devices, between(): return lax.ppermute(value, 'ex', [(1, 2), (2, 1)])  5.12 us
    slice x1, local copies, waits for them, and re-layouts, line(): out_own = outward(query_features[1:])  4.26 us
  transfers between devices with their start and end apart: 31, of which 10 were waited for; matrix products, arithmetic and copies ran while one was open for 25% of the time, Pallas kernels for 0%

profile of v4, /device:TPU:0, one launch (start us, length us, event | category | flops | bytes accessed | tf_op | source)
XLA Modules:
  0.0 210.6 jit_solution(2380838645132989790)
XLA Ops:
  0.0 4.3 %fusion.257 = (bf16[3,256,1024]{2,1,0:T(8,128)(2,1)}, bf16[3,256,1024]{2,1,0:T(8,128)(2,1)}) fusion(bf16[4,256,1024]{2,1,0:T(8,128)(2,1)} %param.4), kind=kLoop, calls=%fused_computation.226 | loop fusion | bytes 6291456 | tf_op jit(solution)/shard_map/slice | solution.py:154
  4.3 6.3 %collective-permute-start.9 = (bf16[3,256,1024]{2,1,0:T(8,128)(2,1)}, bf16[3,256,1024]{2,1,0:T(8,128)(2,1)}, u32[]{:S(2)}, u32[]{:S(2)}) collective-permute-start(bf16[3,256,1024]{2,1,0:T(8,128)(2,1)} %get-tuple-element.24), channel_id=1, source_target_pairs={{0,4},{12,8},{1,5},{13,9},{2,6},{14,10},{3,7},{15,11},{16,20},{28,... | collective-permute-start | bytes 4718600 | tf_op jit(solution)/shard_map/ppermute | solution.py:130
  10.6 1.6 fusion.258
  12.2 1.6 collective-permute-start
  13.8 1.3 collective-permute-start.1
  17.0 1.7 fusion.135
  18.8 1.7 fusion.105
  20.6 1.4 pad_maximum_fusion.1
  22.1 2.4 %fusion.90 = f32[256,1024]{1,0:T(8,128)S(1)} fusion(bf16[4,1024,1024]{2,1,0:T(8,128)(2,1)} %param.3, f32[1024]{0:T(1024)S(1)} %bitcast.252, bf16[4,256,1024]{2,1,0:T(8,128)(2,1)S(1)} %copy-done.1), kind=kOutput, calls=%fused_computation.58 | convolution fusion | flops 537133056 | bytes 3674112 | tf_op jit(solution)/shard_map/dot_general | solution.py:16
  25.8 1.3 collective-permute-start.5
  27.2 2.6 %fusion.54 = f32[256,1024]{1,0:T(8,128)S(1)} fusion(f32[256,1024]{1,0:T(8,128)S(1)} %copy-done.6, f32[256,1024]{1,0:T(8,128)S(1)} %copy-done.7, f32[256,1024]{1,0:T(8,128)S(1)} %fusion.90, bf16[4,1024,1024]{2,1,0:T(8,128)(2,1)} %param.3, f32[1024]{0:T(1024)S(1)} %bitcast.236, bf16[4,256,1024]{2,1,0:T(8,128)(2,1)S(1)} %copy-done.1), kind=kOutput, calls=%fused_computation.46 | convolution fusion | flops 538181632 | bytes 6819840 | tf_op jit(solution)/shard_map/dot_general | solution.py:16
  30.6 32.4 %collective-permute-done.5 = bf16[256,1024]{1,0:T(8,128)(2,1)S(1)} collective-permute-done((bf16[256,1024]{1,0:T(8,128)(2,1)S(1)}, bf16[256,1024]{1,0:T(8,128)(2,1)S(1)}, u32[]{:S(2)}, u32[]{:S(2)}) %collective-permute-start.5) | collective-permute-done | bytes 524320 | tf_op jit(solution)/shard_map/ppermute | solution.py:136
  63.8 1.5 collective-permute-start.10
  65.3 1.3 fusion.219
  68.4 1.3 slice.170
  69.7 1.8 fusion.123
  71.5 1.8 fusion.99
  73.3 1.8 fusion.81
  75.9 1.4 slice_select_fusion
  78.8 2.0 broadcast_select_fusion.2
  80.8 1.3 collective-permute-start.6
  82.1 5.2 %collective-permute-done.10 = bf16[528,1024]{1,0:T(8,128)(2,1)S(1)} collective-permute-done((bf16[528,1024]{1,0:T(8,128)(2,1)S(1)}, bf16[528,1024]{1,0:T(8,128)(2,1)S(1)}, u32[]{:S(2)}, u32[]{:S(2)}) %collective-permute-start.10) | collective-permute-done | bytes 1081376 | tf_op jit(solution)/shard_map/ppermute | solution.py:130
  87.3 4.6 %collective-permute-start.11 = (bf16[528,1024]{1,0:T(8,128)(2,1)S(1)}, bf16[528,1024]{1,0:T(8,128)(2,1)S(1)}, u32[]{:S(2)}, u32[]{:S(2)}) collective-permute-start(bf16[528,1024]{1,0:T(8,128)(2,1)S(1)} %pad_maximum_fusion), channel_id=1, source_target_pairs={{0,4},{12,8},{1,5},{13,9},{2,6},{14,10},{3,7},{15,11},{16,20},{28,... | collective-permute-start | bytes 3244040 | tf_op jit(solution)/shard_map/ppermute | solution.py:130
  91.9 1.5 fusion.149
  95.6 1.3 collective-permute-start.4
  97.0 1.3 collective-permute-start.14
  98.3 10.4 %collective-permute-done.6 = bf16[2,256,1024]{2,1,0:T(8,128)(2,1)S(1)} collective-permute-done((bf16[2,256,1024]{2,1,0:T(8,128)(2,1)S(1)}, bf16[2,256,1024]{2,1,0:T(8,128)(2,1)S(1)}, u32[]{:S(2)}, u32[]{:S(2)}) %collective-permute-start.6) | collective-permute-done | bytes 1048608 | tf_op jit(solution)/shard_map/ppermute | solution.py:136
  110.9 8.6 %collective-permute-done.14 = bf16[256,1024]{1,0:T(8,128)(2,1)S(1)} collective-permute-done((bf16[256,1024]{1,0:T(8,128)(2,1)S(1)}, bf16[256,1024]{1,0:T(8,128)(2,1)S(1)}, u32[]{:S(2)}, u32[]{:S(2)}) %collective-permute-start.14) | collective-permute-done | bytes 524320 | tf_op jit(solution)/shard_map/ppermute | solution.py:136
  119.5 1.3 collective-permute-start.7
  120.9 1.3 collective-permute-start.16
  123.9 4.6 %collective-permute-start.12 = (bf16[128,1024]{1,0:T(8,128)(2,1)S(1)}, bf16[128,1024]{1,0:T(8,128)(2,1)S(1)}, u32[]{:S(2)}, u32[]{:S(2)}) collective-permute-start(bf16[128,1024]{1,0:T(8,128)(2,1)S(1)} %copy-done.8), channel_id=1, source_target_pairs={{0,4},{12,8},{1,5},{13,9},{2,6},{14,10},{3,7},{15,11},{16,20},{28,... | collective-permute-start | bytes 786440 | tf_op jit(solution)/shard_map/ppermute | solution.py:130
  129.0 1.5 fusion.154
  131.1 3.9 %collective-permute-done.12 = bf16[128,1024]{1,0:T(8,128)(2,1)S(1)} collective-permute-done((bf16[128,1024]{1,0:T(8,128)(2,1)S(1)}, bf16[128,1024]{1,0:T(8,128)(2,1)S(1)}, u32[]{:S(2)}, u32[]{:S(2)}) %collective-permute-start.12) | collective-permute-done | bytes 262176 | tf_op jit(solution)/shard_map/ppermute | solution.py:130
  137.3 4.9 %collective-permute-start.21 = (bf16[128,1024]{1,0:T(8,128)(2,1)S(1)}, bf16[128,1024]{1,0:T(8,128)(2,1)S(1)}, u32[]{:S(2)}, u32[]{:S(2)}) collective-permute-start(bf16[128,1024]{1,0:T(8,128)(2,1)S(1)} %get-tuple-element.19), channel_id=1, source_target_pairs={{0,4},{12,8},{1,5},{13,9},{2,6},{14,10},{3,7},{15,11},{16,20},{28,... | collective-permute-start | bytes 786440 | tf_op jit(solution)/shard_map/ppermute | solution.py:130
  145.1 3.4 %collective-permute-done.21 = bf16[128,1024]{1,0:T(8,128)(2,1)S(1)} collective-permute-done((bf16[128,1024]{1,0:T(8,128)(2,1)S(1)}, bf16[128,1024]{1,0:T(8,128)(2,1)S(1)}, u32[]{:S(2)}, u32[]{:S(2)}) %collective-permute-start.21) | collective-permute-done | bytes 262176 | tf_op jit(solution)/shard_map/ppermute | solution.py:130
  148.4 3.8 %collective-permute-start.8 = (f32[256,1024]{1,0:T(8,128)S(1)}, f32[256,1024]{1,0:T(8,128)}, u32[]{:S(2)}, u32[]{:S(2)}) collective-permute-start(f32[256,1024]{1,0:T(8,128)S(1)} %add.105), channel_id=1, source_target_pairs={{0,2},{15,13},{16,18},{31,29}} | collective-permute-start | bytes 3145736 | tf_op jit(solution)/shard_map/ppermute | solution.py:68
  152.2 1.3 collective-permute-start.18
  154.4 6.1 %collective-permute-done.18 = bf16[128,1024]{1,0:T(8,128)(2,1)S(1)} collective-permute-done((bf16[128,1024]{1,0:T(8,128)(2,1)S(1)}, bf16[128,1024]{1,0:T(8,128)(2,1)S(1)}, u32[]{:S(2)}, u32[]{:S(2)}) %collective-permute-start.18) | collective-permute-done | bytes 262176 | tf_op jit(solution)/shard_map/ppermute | solution.py:136
  162.1 1.3 collective-permute-start.19
  163.4 1.3 collective-permute-start.23
  166.0 12.5 %collective-permute-done.23 = bf16[128,1024]{1,0:T(8,128)(2,1)S(1)} collective-permute-done((bf16[128,1024]{1,0:T(8,128)(2,1)S(1)}, bf16[128,1024]{1,0:T(8,128)(2,1)S(1)}, u32[]{:S(2)}, u32[]{:S(2)}) %collective-permute-start.23) | collective-permute-done | bytes 262176 | tf_op jit(solution)/shard_map/ppermute | solution.py:136
  178.5 1.9 broadcast_select_fusion.5
  180.4 2.6 %collective-permute-start.24 = (f32[128,1024]{1,0:T(8,128)}, f32[128,1024]{1,0:T(8,128)}, u32[]{:S(2)}, u32[]{:S(2)}) collective-permute-start(f32[128,1024]{1,0:T(8,128)} %get-tuple-element.39), channel_id=1, source_target_pairs={{0,1},{2,3},{5,4},{7,6},{4,5},{6,7},{8,9},{10,11},{9,8},{11,10},{1... | collective-permute-start | bytes 1572872 | tf_op jit(solution)/shard_map/ppermute | solution.py:84
  183.9 1.5 collective-permute-start.20
  188.0 1.3 collective-permute-start.30
  190.5 1.5 collective-permute-start.25
  194.3 11.1 %collective-permute-done.30 = f16[272,1024]{1,0:T(8,128)(2,1)} collective-permute-done((f16[272,1024]{1,0:T(8,128)(2,1)}, f16[272,1024]{1,0:T(8,128)(2,1)}, u32[]{:S(2)}, u32[]{:S(2)}) %collective-permute-start.30) | collective-permute-done | bytes 557088 | tf_op jit(solution)/shard_map/ppermute | solution.py:136
  207.3 3.3 %fusion.199 = f32[256,1024]{1,0:T(8,128)} fusion(f32[128,1024]{1,0:T(8,128)S(1)} %add.118, f32[128,1024]{1,0:T(8,128)S(1)} %add.114, f32[256,1024]{1,0:T(8,128)S(1)} %add.105, f32[256,1024]{1,0:T(8,128)} %collective-permute-done.8, f32[256,1024]{1,0:T(8,128)S(1)} %select_add_fusion, f32[256,1024]{1,0:T(8,128)} %collective-permute-done.4, ...), kind=kLoop, calls=%fused_computation.121 | loop fusion | flops 2097152 | bytes 6815750 | tf_op jit(solution)/shard_map/add | solution.py:234
  (107 shorter events, 32.3 us)
Async XLA Ops:
  0.0 10.6 %copy-start.1 = (bf16[4,256,1024]{2,1,0:T(8,128)(2,1)S(1)}, bf16[4,256,1024]{2,1,0:T(8,128)(2,1)}, u32[]{:S(2)}) copy-start(bf16[4,256,1024]{2,1,0:T(8,128)(2,1)} %param.4) | copy-start | bytes 6291460
  0.0 15.8 %copy-start = (bf16[4,1024,1024]{2,1,0:T(8,128)(2,1)S(1)}, bf16[4,1024,1024]{2,1,0:T(8,128)(2,1)}, u32[]{:S(2)}) copy-start(bf16[4,1024,1024]{2,1,0:T(8,128)(2,1)} %param.3) | copy-start | bytes 25165828
  4.3 59.5 %collective-permute-start.9 = (bf16[3,256,1024]{2,1,0:T(8,128)(2,1)}, bf16[3,256,1024]{2,1,0:T(8,128)(2,1)}, u32[]{:S(2)}, u32[]{:S(2)}) collective-permute-start(bf16[3,256,1024]{2,1,0:T(8,128)(2,1)} %get-tuple-element.24), channel_id=1, source_target_pairs={{0,4},{12,8},{1,5},{13,9},{2,6},{14,10},{3,7},{15,11},{16,20},{28,... | collective-permute-start | bytes 4718600 | tf_op jit(solution)/shard_map/ppermute | solution.py:130
  12.2 12.4 %collective-permute-start = (bf16[2,256,1024]{2,1,0:T(8,128)(2,1)}, bf16[2,256,1024]{2,1,0:T(8,128)(2,1)}, u32[]{:S(2)}, u32[]{:S(2)}) collective-permute-start(bf16[2,256,1024]{2,1,0:T(8,128)(2,1)} %get-tuple-element.25), channel_id=1, source_target_pairs={{4,8},{8,4},{5,9},{9,5},{6,10},{10,6},{7,11},{11,7},{20,24},{24,20... | collective-permute-start | bytes 3145736 | tf_op jit(solution)/shard_map/ppermute | solution.py:133
  13.8 51.5 %collective-permute-start.1 = (bf16[3,256,1024]{2,1,0:T(8,128)(2,1)}, bf16[3,256,1024]{2,1,0:T(8,128)(2,1)}, u32[]{:S(2)}, u32[]{:S(2)}) collective-permute-start(bf16[3,256,1024]{2,1,0:T(8,128)(2,1)} %get-tuple-element.23), channel_id=1, source_target_pairs={{4,0},{8,12},{5,1},{9,13},{6,2},{10,14},{7,3},{11,15},{20,16},{24,... | collective-permute-start | bytes 4718600 | tf_op jit(solution)/shard_map/ppermute | solution.py:136
  15.9 1.1 copy-start.9
  20.6 42.4 %slice-start = ((s8[8388608]{0:T(1024)(128)(4,1)}), s8[4194304]{0:T(1024)(128)(4,1)S(1)}, s32[]{:S(2)}) async-start(s8[8388608]{0:T(1024)(128)(4,1)} %bitcast.234), calls=%async_computation | async-start | bytes 8388608
  24.5 2.7 %copy-start.6 = (f32[256,1024]{1,0:T(8,128)S(1)}, f32[256,1024]{1,0:T(8,128)}, u32[]{:S(2)}) copy-start(f32[256,1024]{1,0:T(8,128)} %fusion.135) | copy-start | bytes 3145732
  24.5 2.7 %copy-start.7 = (f32[256,1024]{1,0:T(8,128)S(1)}, f32[256,1024]{1,0:T(8,128)}, u32[]{:S(2)}) copy-start(f32[256,1024]{1,0:T(8,128)} %fusion.105) | copy-start | bytes 3145732
  25.8 37.2 %collective-permute-start.5 = (bf16[256,1024]{1,0:T(8,128)(2,1)S(1)}, bf16[256,1024]{1,0:T(8,128)(2,1)S(1)}, u32[]{:S(2)}, u32[]{:S(2)}) collective-permute-start(bf16[256,1024]{1,0:T(8,128)(2,1)S(1)} %slice_bitcast_fusion.17), channel_id=1, source_target_pairs={{4,0},{8,12},{5,1},{9,13},{6,2},{10,14},{7,3},{11,15},{20,16},{24,... | collective-permute-start | bytes 1572872 | tf_op jit(solution)/shard_map/ppermute | solution.py:136
  27.1 35.9 %slice-start.1 = ((s8[8388608]{0:T(1024)(128)(4,1)}), s8[4194304]{0:T(1024)(128)(4,1)S(1)}, s32[]{:S(2)}) async-start(s8[8388608]{0:T(1024)(128)(4,1)} %bitcast.234), calls=%async_computation.1 | async-start | bytes 8388608
  27.2 2.7 %copy-start.5 = (bf16[2,256,1024]{2,1,0:T(8,128)(2,1)S(1)}, bf16[2,256,1024]{2,1,0:T(8,128)(2,1)}, u32[]{:S(2)}) copy-start(bf16[2,256,1024]{2,1,0:T(8,128)(2,1)} %get-tuple-element.13) | copy-start | bytes 3145732
  29.8 45.3 %collective-permute-start.2 = (bf16[2,256,1024]{2,1,0:T(8,128)(2,1)S(1)}, bf16[2,256,1024]{2,1,0:T(8,128)(2,1)S(1)}, u32[]{:S(2)}, u32[]{:S(2)}) collective-permute-start(bf16[2,256,1024]{2,1,0:T(8,128)(2,1)S(1)} %copy-done.5), channel_id=1, source_target_pairs={{4,8},{8,4},{5,9},{9,5},{6,10},{10,6},{7,11},{11,7},{20,24},{24,20... | collective-permute-start | bytes 3145736 | tf_op jit(solution)/shard_map/ppermute | solution.py:133
  63.8 23.5 %collective-permute-start.10 = (bf16[528,1024]{1,0:T(8,128)(2,1)S(1)}, bf16[528,1024]{1,0:T(8,128)(2,1)S(1)}, u32[]{:S(2)}, u32[]{:S(2)}) collective-permute-start(bf16[528,1024]{1,0:T(8,128)(2,1)S(1)} %pad_maximum_fusion.1), channel_id=1, source_target_pairs={{0,4},{12,8},{1,5},{13,9},{2,6},{14,10},{3,7},{15,11},{16,20},{28,... | collective-permute-start | bytes 3244040 | tf_op jit(solution)/shard_map/ppermute | solution.py:130
  75.1 18.8 %collective-permute-start.13 = (bf16[2,256,1024]{2,1,0:T(8,128)(2,1)S(1)}, bf16[2,256,1024]{2,1,0:T(8,128)(2,1)S(1)}, u32[]{:S(2)}, u32[]{:S(2)}) collective-permute-start(bf16[2,256,1024]{2,1,0:T(8,128)(2,1)S(1)} %slice.170), channel_id=1, source_target_pairs={{4,8},{8,4},{5,9},{9,5},{6,10},{10,6},{7,11},{11,7},{20,24},{24,20... | collective-permute-start | bytes 3145736 | tf_op jit(solution)/shard_map/ppermute | solution.py:133
  80.7 14.6 %collective-permute-start.3 = (f32[256,1024]{1,0:T(8,128)S(1)}, f32[256,1024]{1,0:T(8,128)S(1)}, u32[]{:S(2)}, u32[]{:S(2)}) collective-permute-start(f32[256,1024]{1,0:T(8,128)S(1)} %get-tuple-element.43), channel_id=1, source_target_pairs={{1,0},{3,2},{0,1},{2,3},{4,5},{6,7},{5,4},{7,6},{9,8},{11,10},{8,9... | collective-permute-start | bytes 3145736 | tf_op jit(solution)/shard_map/ppermute | solution.py:84
  80.8 27.8 %collective-permute-start.6 = (bf16[2,256,1024]{2,1,0:T(8,128)(2,1)S(1)}, bf16[2,256,1024]{2,1,0:T(8,128)(2,1)S(1)}, u32[]{:S(2)}, u32[]{:S(2)}) collective-permute-start(bf16[2,256,1024]{2,1,0:T(8,128)(2,1)S(1)} %collective-permute-done.2), channel_id=1, source_target_pairs={{4,0},{8,12},{5,1},{9,13},{6,2},{10,14},{7,3},{11,15},{20,16},{24,... | collective-permute-start | bytes 3145736 | tf_op jit(solution)/shard_map/ppermute | solution.py:136
  87.3 36.4 %collective-permute-start.11 = (bf16[528,1024]{1,0:T(8,128)(2,1)S(1)}, bf16[528,1024]{1,0:T(8,128)(2,1)S(1)}, u32[]{:S(2)}, u32[]{:S(2)}) collective-permute-start(bf16[528,1024]{1,0:T(8,128)(2,1)S(1)} %pad_maximum_fusion), channel_id=1, source_target_pairs={{0,4},{12,8},{1,5},{13,9},{2,6},{14,10},{3,7},{15,11},{16,20},{28,... | collective-permute-start | bytes 3244040 | tf_op jit(solution)/shard_map/ppermute | solution.py:130
  94.6 48.5 %collective-permute-start.26 = (f32[512,512]{1,0:T(8,128)S(1)}, f32[512,512]{1,0:T(8,128)S(1)}, u32[]{:S(2)}, u32[]{:S(2)}) collective-permute-start(f32[512,512]{1,0:T(8,128)S(1)} %fusion.200), channel_id=1, source_target_pairs={{4,5},{5,4},{6,7},{7,6},{8,9},{9,8},{10,11},{11,10},{20,21},{21,20... | collective-permute-start | bytes 3145736 | tf_op jit(solution)/shard_map/ppermute | solution.py:193
  95.6 111.7 %collective-permute-start.4 = (f32[256,1024]{1,0:T(8,128)S(1)}, f32[256,1024]{1,0:T(8,128)}, u32[]{:S(2)}, u32[]{:S(2)}) collective-permute-start(f32[256,1024]{1,0:T(8,128)S(1)} %select_add_fusion), channel_id=1, source_target_pairs={{2,0},{3,1},{7,5},{4,6},{8,10},{11,9},{13,15},{12,14},{18,16},{19,... | collective-permute-start | bytes 3145736 | tf_op jit(solution)/shard_map/ppermute | solution.py:86
  97.0 22.5 %collective-permute-start.14 = (bf16[256,1024]{1,0:T(8,128)(2,1)S(1)}, bf16[256,1024]{1,0:T(8,128)(2,1)S(1)}, u32[]{:S(2)}, u32[]{:S(2)}) collective-permute-start(bf16[256,1024]{1,0:T(8,128)(2,1)S(1)} %slice_bitcast_fusion.2), channel_id=1, source_target_pairs={{4,0},{8,12},{5,1},{9,13},{6,2},{10,14},{7,3},{11,15},{20,16},{24,... | collective-permute-start | bytes 1572872 | tf_op jit(solution)/shard_map/ppermute | solution.py:136
  108.7 12.2 %collective-permute-start.15 = (bf16[256,1024]{1,0:T(8,128)(2,1)S(1)}, bf16[256,1024]{1,0:T(8,128)(2,1)S(1)}, u32[]{:S(2)}, u32[]{:S(2)}) collective-permute-start(bf16[256,1024]{1,0:T(8,128)(2,1)S(1)} %slice_bitcast_fusion.4), channel_id=1, source_target_pairs={{4,8},{8,4},{5,9},{9,5},{6,10},{10,6},{7,11},{11,7},{20,24},{24,20... | collective-permute-start | bytes 1572872 | tf_op jit(solution)/shard_map/ppermute | solution.py:133
  119.5 24.7 %collective-permute-start.7 = (f32[256,1024]{1,0:T(8,128)S(1)}, f32[256,1024]{1,0:T(8,128)S(1)}, u32[]{:S(2)}, u32[]{:S(2)}) collective-permute-start(f32[256,1024]{1,0:T(8,128)S(1)} %fusion.120), channel_id=1, source_target_pairs={{1,0},{3,2},{12,13},{14,15},{17,16},{19,18},{28,29},{30,31}} | collective-permute-start | bytes 3145736 | tf_op jit(solution)/shard_map/ppermute | solution.py:60
  120.9 16.5 %collective-permute-start.16 = (bf16[256,1024]{1,0:T(8,128)(2,1)S(1)}, bf16[256,1024]{1,0:T(8,128)(2,1)S(1)}, u32[]{:S(2)}, u32[]{:S(2)}) collective-permute-start(bf16[256,1024]{1,0:T(8,128)(2,1)S(1)} %collective-permute-done.15), channel_id=1, source_target_pairs={{4,0},{8,12},{5,1},{9,13},{6,2},{10,14},{7,3},{11,15},{20,16},{24,... | collective-permute-start | bytes 1572872 | tf_op jit(solution)/shard_map/ppermute | solution.py:136
  122.9 1.0 copy-start.8
  123.9 11.2 %collective-permute-start.12 = (bf16[128,1024]{1,0:T(8,128)(2,1)S(1)}, bf16[128,1024]{1,0:T(8,128)(2,1)S(1)}, u32[]{:S(2)}, u32[]{:S(2)}) collective-permute-start(bf16[128,1024]{1,0:T(8,128)(2,1)S(1)} %copy-done.8), channel_id=1, source_target_pairs={{0,4},{12,8},{1,5},{13,9},{2,6},{14,10},{3,7},{15,11},{16,20},{28,... | collective-permute-start | bytes 786440 | tf_op jit(solution)/shard_map/ppermute | solution.py:130
  135.1 29.8 %collective-permute-start.28 = (f32[512,512]{1,0:T(8,128)S(1)}, f32[512,512]{1,0:T(8,128)S(1)}, u32[]{:S(2)}, u32[]{:S(2)}) collective-permute-start(f32[512,512]{1,0:T(8,128)S(1)} %fusion.203), channel_id=1, source_target_pairs={{4,5},{5,4},{6,7},{7,6},{8,9},{9,8},{10,11},{11,10},{20,21},{21,20... | collective-permute-start | bytes 3145736 | tf_op jit(solution)/shard_map/ppermute | solution.py:193
  137.3 11.1 %collective-permute-start.21 = (bf16[128,1024]{1,0:T(8,128)(2,1)S(1)}, bf16[128,1024]{1,0:T(8,128)(2,1)S(1)}, u32[]{:S(2)}, u32[]{:S(2)}) collective-permute-start(bf16[128,1024]{1,0:T(8,128)(2,1)S(1)} %get-tuple-element.19), channel_id=1, source_target_pairs={{0,4},{12,8},{1,5},{13,9},{2,6},{14,10},{3,7},{15,11},{16,20},{28,... | collective-permute-start | bytes 786440 | tf_op jit(solution)/shard_map/ppermute | solution.py:130
  143.1 9.1 %collective-permute-start.17 = (bf16[128,1024]{1,0:T(8,128)(2,1)S(1)}, bf16[128,1024]{1,0:T(8,128)(2,1)S(1)}, u32[]{:S(2)}, u32[]{:S(2)}) collective-permute-start(bf16[128,1024]{1,0:T(8,128)(2,1)S(1)} %collective-permute-done.12), channel_id=1, source_target_pairs={{4,8},{8,4},{5,9},{9,5},{6,10},{10,6},{7,11},{11,7},{20,24},{24,20... | collective-permute-start | bytes 786440 | tf_op jit(solution)/shard_map/ppermute | solution.py:133
  144.2 19.2 %collective-permute-start.27 = (f32[256,512]{1,0:T(8,128)S(1)}, f32[256,512]{1,0:T(8,128)S(1)}, u32[]{:S(2)}, u32[]{:S(2)}) collective-permute-start(f32[256,512]{1,0:T(8,128)S(1)} %slice_select_fusion.2), channel_id=1, source_target_pairs={{7,5},{4,6},{5,7},{8,10},{11,9},{10,8},{23,21},{20,22},{21,23},{24... | collective-permute-start | bytes 1572872 | tf_op jit(solution)/shard_map/ppermute | solution.py:202
  148.4 58.9 %collective-permute-start.8 = (f32[256,1024]{1,0:T(8,128)S(1)}, f32[256,1024]{1,0:T(8,128)}, u32[]{:S(2)}, u32[]{:S(2)}) collective-permute-start(f32[256,1024]{1,0:T(8,128)S(1)} %add.105), channel_id=1, source_target_pairs={{0,2},{15,13},{16,18},{31,29}} | collective-permute-start | bytes 3145736 | tf_op jit(solution)/shard_map/ppermute | solution.py:68
  152.2 8.3 %collective-permute-start.18 = (bf16[128,1024]{1,0:T(8,128)(2,1)S(1)}, bf16[128,1024]{1,0:T(8,128)(2,1)S(1)}, u32[]{:S(2)}, u32[]{:S(2)}) collective-permute-start(bf16[128,1024]{1,0:T(8,128)(2,1)S(1)} %collective-permute-done.17), channel_id=1, source_target_pairs={{4,0},{8,12},{5,1},{9,13},{6,2},{10,14},{7,3},{11,15},{20,16},{24,... | collective-permute-start | bytes 786440 | tf_op jit(solution)/shard_map/ppermute | solution.py:136
  154.4 24.1 %copy-start.2 = (f32[128,1024]{1,0:T(8,128)}, f32[128,1024]{1,0:T(8,128)S(1)}, u32[]{:S(2)}) copy-start(f32[128,1024]{1,0:T(8,128)S(1)} %slice_add_fusion) | copy-start | bytes 1572868
  160.5 1.6 collective-permute-start.22
  162.1 20.9 %collective-permute-start.19 = (f32[128,1024]{1,0:T(8,128)S(1)}, f32[128,1024]{1,0:T(8,128)S(1)}, u32[]{:S(2)}, u32[]{:S(2)}) collective-permute-start(f32[128,1024]{1,0:T(8,128)S(1)} %get-tuple-element.41), channel_id=1, source_target_pairs={{0,1},{2,3},{5,4},{7,6},{4,5},{6,7},{8,9},{10,11},{9,8},{11,10},{1... | collective-permute-start | bytes 1572872 | tf_op jit(solution)/shard_map/ppermute | solution.py:84
  163.4 15.0 %collective-permute-start.23 = (bf16[128,1024]{1,0:T(8,128)(2,1)S(1)}, bf16[128,1024]{1,0:T(8,128)(2,1)S(1)}, u32[]{:S(2)}, u32[]{:S(2)}) collective-permute-start(bf16[128,1024]{1,0:T(8,128)(2,1)S(1)} %collective-permute-done.22), channel_id=1, source_target_pairs={{4,0},{8,12},{5,1},{9,13},{6,2},{10,14},{7,3},{11,15},{20,16},{24,... | collective-permute-start | bytes 786440 | tf_op jit(solution)/shard_map/ppermute | solution.py:136
  165.3 20.1 %collective-permute-start.29 = (f32[256,512]{1,0:T(8,128)S(1)}, f32[256,512]{1,0:T(8,128)S(1)}, u32[]{:S(2)}, u32[]{:S(2)}) collective-permute-start(f32[256,512]{1,0:T(8,128)S(1)} %slice_select_fusion.1), channel_id=1, source_target_pairs={{7,5},{4,6},{5,7},{8,10},{11,9},{10,8},{23,21},{20,22},{21,23},{24... | collective-permute-start | bytes 1572872 | tf_op jit(solution)/shard_map/ppermute | solution.py:202
  180.4 8.9 %collective-permute-start.24 = (f32[128,1024]{1,0:T(8,128)}, f32[128,1024]{1,0:T(8,128)}, u32[]{:S(2)}, u32[]{:S(2)}) collective-permute-start(f32[128,1024]{1,0:T(8,128)} %get-tuple-element.39), channel_id=1, source_target_pairs={{0,1},{2,3},{5,4},{7,6},{4,5},{6,7},{8,9},{10,11},{9,8},{11,10},{1... | collective-permute-start | bytes 1572872 | tf_op jit(solution)/shard_map/ppermute | solution.py:84
  183.9 8.0 %collective-permute-start.20 = (f32[128,1024]{1,0:T(8,128)}, f32[128,1024]{1,0:T(8,128)}, u32[]{:S(2)}, u32[]{:S(2)}) collective-permute-start(f32[128,1024]{1,0:T(8,128)} %select_add_fusion.4), channel_id=1, source_target_pairs={{1,3},{6,4},{5,7},{9,11},{10,8},{14,12},{17,19},{22,20},{21,23},{2... | collective-permute-start | bytes 1572872 | tf_op jit(solution)/shard_map/ppermute | solution.py:86
  186.9 2.4 %copy-start.3 = (f32[128,1024]{1,0:T(8,128)S(1)}, f32[128,1024]{1,0:T(8,128)}, u32[]{:S(2)}) copy-start(f32[128,1024]{1,0:T(8,128)} %copy-done.2) | copy-start | bytes 1572868
  187.0 2.4 %copy-start.4 = (f32[128,1024]{1,0:T(8,128)S(1)}, f32[128,1024]{1,0:T(8,128)}, u32[]{:S(2)}) copy-start(f32[128,1024]{1,0:T(8,128)} %get-tuple-element.40) | copy-start | bytes 1572868
  188.0 17.4 %collective-permute-start.30 = (f16[272,1024]{1,0:T(8,128)(2,1)}, f16[272,1024]{1,0:T(8,128)(2,1)}, u32[]{:S(2)}, u32[]{:S(2)}) collective-permute-start(f16[272,1024]{1,0:T(8,128)(2,1)} %concatenate.35), channel_id=1, source_target_pairs={{4,0},{8,12},{5,1},{9,13},{6,2},{10,14},{7,3},{11,15},{20,16},{24,... | collective-permute-start | bytes 1671176 | tf_op jit(solution)/shard_map/ppermute | solution.py:136
  190.5 2.7 %collective-permute-start.25 = (f32[128,1024]{1,0:T(8,128)S(1)}, f32[128,1024]{1,0:T(8,128)}, u32[]{:S(2)}, u32[]{:S(2)}) collective-permute-start(f32[128,1024]{1,0:T(8,128)S(1)} %select_add_fusion.3), channel_id=1, source_target_pairs={{1,3},{6,4},{5,7},{9,11},{10,8},{14,12},{17,19},{22,20},{21,23},{2... | collective-permute-start | bytes 1572872 | tf_op jit(solution)/shard_map/ppermute | solution.py:86

commit v5 on v4

v5 whole, which is shorter than its diff:
```python
import jax
import jax.numpy as jnp
from jax import lax
from jax.sharding import PartitionSpec as P

PLACE = ("ex", "ckpt", "dim")


def after(value, *others):
    return lax.optimization_barrier((value,) + others)[0]


def weighted(checks, train, weights, scale):
    total = None
    for piece, examples, weight in zip(checks, train, weights):
        dots = lax.dot_general(
            piece,
            examples,
            (((1,), (1,)), ((), ())),
            preferred_element_type=jnp.float32,
        )
        term = dots * weight[None, :]
        total = term if total is None else total + term
    return total * scale


class Keepers:
    def __init__(self, rows):
        self.ckpts, self.dims = lax.axis_size("ckpt"), lax.axis_size("dim")
        self.planes = lax.axis_size("ex")
        self.z, self.x, self.c = [lax.axis_index(name) for name in PLACE]
        kept = rows * self.planes // (self.ckpts * self.dims)
        self.ratio = kept // rows
        assert self.ratio * rows == kept

    def index(self, z, x, c):
        return (z * self.ckpts + x) * self.dims + c

    def of(self, block):
        owner = block // self.ratio
        return owner // self.dims, owner % self.dims

    def mine(self, blocks, j=0):
        found = jnp.bool_(False)
        for z, block in enumerate(blocks):
            if block is not None and block % self.ratio == j:
                x, c = self.of(block)
                found = found | ((self.z == z) & (self.x == x) & (self.c == c))
        return found

    def sums(self, partial, blocks):
        return self.far_sums(self.near_sums(partial, blocks), blocks)

    def near_sums(self, partial, blocks):
        total = partial
        for away in range(1, self.dims):
            pairs = []
            for z, block in enumerate(blocks):
                if block is not None:
                    c = self.of(block)[1]
                    for x in range(self.ckpts):
                        pairs.append((self.index(z, x, (c + away) % self.dims), self.index(z, x, c)))
            total = total + lax.ppermute(partial, PLACE, pairs)
        return total

    def far_sums(self, total, *held):
        whole = total
        for away in range(1, self.ckpts):
            pairs = []
            for z in range(self.planes):
                for blocks in held:
                    if blocks[z] is not None:
                        x, c = self.of(blocks[z])
                        pairs.append((self.index(z, (x + away) % self.ckpts, c), self.index(z, x, c)))
            whole = whole + lax.ppermute(total, PLACE, pairs)
        return whole

    def two_near_sums(self, one, one_blocks, two, two_blocks):
        keeps_one = jnp.bool_(False)
        swaps = []
        for z, blocks in enumerate(zip(one_blocks, two_blocks)):
            second = self.of(blocks[1])[1]
            assert blocks[0] is None or self.of(blocks[0])[1] == 1 - second
            keeps_one = keeps_one | ((self.z == z) & (self.c == 1 - second))
            for block in blocks:
                if block is not None:
                    c = self.of(block)[1]
                    swaps += [(self.index(z, x, 1 - c), self.index(z, x, c)) for x in range(2)]
        got = lax.ppermute(jnp.where(keeps_one, two, one), PLACE, swaps)
        return jnp.where(keeps_one, one, two) + got


def ring(train_features, query_features, residual_weights, keepers, scale):
    planes, ratio = keepers.planes, keepers.ratio
    rows = query_features.shape[1]
    half = rows // 2
    results = [[None, None] for unused in range(ratio)]

    def finish(piece, blocks, start):
        found = weighted(list(piece), train_features, residual_weights, scale)
        whole = keepers.sums(found, blocks)
        for j in range(ratio):
            mine = keepers.mine(blocks, j)
            for k in range(found.shape[0] // half):
                part = whole[k * half:(k + 1) * half]
                at = start // half + k
                old = results[j][at]
                results[j][at] = part if old is None else jnp.where(mine, part, old)

    right = [(s, (s + 1) % planes) for s in range(planes)]
    left = [(s, (s - 1) % planes) for s in range(planes)]
    from_left = from_right = query_features
    finish(query_features, list(range(planes)), 0)
    for step in range(1, planes // 2):
        from_left = lax.ppermute(from_left, "ex", right)
        from_right = lax.ppermute(from_right, "ex", left)
        finish(from_left, [(s - step) % planes for s in range(planes)], 0)
        finish(from_right, [(s + step) % planes for s in range(planes)], 0)
    across = [(s + planes // 2) % planes for s in range(planes)]
    finish(lax.ppermute(from_left[:, :half], "ex", right), across, 0)
    finish(lax.ppermute(from_right[:, half:], "ex", left), across, half)
    return jnp.concatenate([part for block in results for part in block], axis=0)


def packed(value):
    largest = jnp.clip(jnp.max(jnp.abs(value)), 1e-30, 1e30)
    power = jnp.floor(jnp.log2(largest))
    small = (value * jnp.exp2(13.0 - power)).astype(jnp.float16)
    return jnp.concatenate([small, jnp.full((16, value.shape[1]), power, jnp.float16)], axis=0)


def unpacked(small):
    power = small[-16, 0].astype(jnp.float32)
    return small[:-16].astype(jnp.float32) * jnp.exp2(power - 13.0)


def line(train_features, query_features, residual_weights, keepers, scale):
    z, c = keepers.z, keepers.c
    rows, depth = query_features.shape[1:]
    examples = train_features.shape[1]
    low = rows // 2
    assert train_features.shape[0] == 4 and examples <= depth
    ends = (z == 0) | (z == 3)

    def inward(value):
        return lax.ppermute(value, "ex", [(0, 1), (3, 2)])

    def between(value):
        return lax.ppermute(value, "ex", [(1, 2), (2, 1)])

    def outward(value):
        return lax.ppermute(value, "ex", [(1, 0), (2, 3)])

    def scores(checks, first=0):
        return weighted(checks, train_features[first:], residual_weights[first:], scale)

    def chosen(far, near):
        return after(jnp.where(ends, far, near))

    left, pieces = residual_weights[0], []
    for unused in range(3):
        rounded = lax.reduce_precision(left, 8, 7)
        pieces.append(rounded.astype(jnp.bfloat16))
        left = left - rounded
    tail = jnp.pad(jnp.stack(pieces), ((0, 13), (0, depth - examples)))
    training = jnp.concatenate([train_features[0], tail], axis=0)

    in_many = inward(query_features[:3])
    mid_own = between(query_features[1:])
    out_own = outward(query_features[1:])
    own = scores(list(query_features))
    out_next = outward(mid_own)
    mid_edge = between(after(in_many[1:], mid_own))
    in_train = inward(after(training, in_many))
    out_edge = outward(mid_edge)
    mid_first = between(after(jnp.stack([query_features[0], in_many[0]]), mid_edge))
    one, far_one = mid_first[0], mid_first[1]

    blocks_own = [0, 1, 2, 3]
    blocks_1 = [1, 2, 1, 2]
    blocks_2 = [2, None, None, 1]
    blocks_3 = [None, 0, 3, None]
    blocks_4 = [3, 3, 0, 0]

    checks = chosen(after(out_own, in_many), mid_own)
    found_1 = scores(list(checks), 1)
    found_2 = scores(list(after(out_next, mid_edge)), 1)
    total_2 = keepers.near_sums(found_2, blocks_2)
    result_2 = keepers.far_sums(total_2, blocks_2)

    weights = jnp.sum(in_train[examples:examples + 3, :examples].astype(jnp.float32), axis=0)

    def beside(queries):
        return weighted([queries], [in_train[:examples]], [weights], scale)

    first, second, third = beside(query_features[0]), beside(one), beside(far_one)
    alone = ((z == 1) & (c == 0)) | ((z == 2) & (c == 1))
    pair = jnp.concatenate([first, third], axis=0)
    lone = jnp.concatenate([second, second], axis=0)
    swaps = [(keepers.index(p, q, r), keepers.index(p, q, 1 - r)) for p in (1, 2) for q in range(2) for r in range(2)]
    got = lax.ppermute(jnp.where(alone, pair, lone), PLACE, swaps)
    total = jnp.where(alone, lone, pair) + got
    keeps_first = keepers.mine([None, 1, 2, None])
    crosses = []
    for p, blocks in ((1, (1, 2, 3)), (2, (2, 1, 0))):
        for block in blocks:
            at, r = keepers.of(block)
            crosses.append((keepers.index(p, 1 - at, r), keepers.index(p, at, r)))
    crossing = packed(jnp.where(keeps_first, total[rows:], total[:rows]))
    got = lax.ppermute(crossing, PLACE, crosses)
    returned = jnp.where(keeps_first, total[:rows], total[rows:]) + unpacked(got)
    returned = packed(jnp.where(keepers.mine([None, 0, 3, None]), 0.0, returned))

    found_1 = found_1 + scores([one])
    total_1 = keepers.two_near_sums(own, blocks_own, found_1, blocks_1)
    result_1 = keepers.far_sums(total_1, blocks_own, blocks_1)

    base_3 = scores(list(in_many))
    checks = chosen(after(out_edge, in_train), mid_edge)
    base_4 = scores([far_one, checks[0], checks[1]])
    results, before = [], in_train
    for k in range(2):
        part = slice(k * low, (k + 1) * low)
        before = inward(after(query_features[3, part], before, total_2))
        mid = between(after(before, total_1 if k == 0 else crossing))
        out = outward(mid)
        block_3 = base_3[part] + scores([before], 3)
        block_4 = base_4[part] + scores([chosen(out, mid)], 3)
        total = keepers.two_near_sums(block_3, blocks_3, block_4, blocks_4)
        results.append(keepers.far_sums(total, blocks_3, blocks_4))
    returned = unpacked(outward(after(returned, mid)))

    result = jnp.where(keepers.mine(blocks_2), result_2, jnp.concatenate(results, axis=0))
    result = jnp.where(keepers.mine(blocks_own) | keepers.mine(blocks_1), result_1, result)
    return result + returned


def local(train_features, query_features, residual_weights):
    keepers = Keepers(query_features.shape[1])
    scale = 1.0 / (train_features.shape[0] * keepers.ckpts)
    plan = line if (keepers.planes, keepers.ckpts, keepers.dims) == (4, 2, 2) else ring
    return plan(train_features, query_features, residual_weights, keepers, scale)


def solution(mesh):
    in_specs = (
        P("ckpt", ("groups", "ex"), "dim"),
        P("ckpt", ("groups", "ex"), "dim"),
        P("ckpt", ("groups", "ex")),
    )
    out_specs = P(("ckpt", "dim"), ("groups", "ex"))
    return jax.shard_map(local, mesh=mesh, in_specs=in_specs, out_specs=out_specs, check_vma=False)
```

time: 212 us -> 200 us (0.943)
  waiting for transfers between devices: 94.3 us -> 83.6 us
  starting transfers between devices: 53.6 us -> 47.1 us
  matrix products: 32 us -> 37 us
  local copies, waits for them, and re-layouts: 13.6 us -> 10.6 us
  other arithmetic: 14.7 us -> 17 us
    ppermute x8 -> x6, waiting for transfers between devices: 81.8 us -> 63.9 us  [outward(): return lax.ppermute(value, 'ex', [(1, 0), (2, 3)])]
    ppermute x5 -> x4, waiting for transfers between devices: 12.4 us -> 19.7 us  [inward(): return lax.ppermute(value, 'ex', [(0, 1), (3, 2)])]
    dot_general x27 -> x24, matrix products: 32 us -> 37 us  [weighted(): lax.dot_general(piece, examples, (((1,), (1,)), ((), ())), preferred_elem...]
    ppermute x5 -> x4, starting transfers between devices: 22 us -> 17.7 us  [inward(): return lax.ppermute(value, 'ex', [(0, 1), (3, 2)])]
    squeeze x4 -> x1, local copies, waits for them, and re-layouts: 3.14 us -> 0.04 us  [line(): before = inward(after(query_features[3, part], before, total_2))]
    ppermute x8 -> x6, starting transfers between devices: 10.3 us -> 7.74 us  [outward(): return lax.ppermute(value, 'ex', [(1, 0), (2, 3)])]
    add x11 -> x8, other arithmetic: 9.03 us -> 10.2 us  [the longest x1 3.59 us: line(): return result + returned]
    ppermute x6 -> x5, starting transfers between devices: 5.12 us -> 5.46 us  [between(): return lax.ppermute(value, 'ex', [(1, 2), (2, 1)])]
  transfers between devices with their start and end apart: 31 -> 25, of which waited for: 10 -> 6; matrix products, arithmetic and copies ran while one was open for 25% -> 28% of each run, Pallas kernels for 0% -> 0%
where the time goes in v5:
time: 200 us; the launch traced here: 199 us
  waiting for transfers between devices  83.6 us (42%)
  starting transfers between devices  47.1 us (24%)
  matrix products  37 us (18%)
  other arithmetic  17 us (8%)
  local copies, waits for them, and re-layouts  10.6 us (5%)
  between operations  3.59 us (2%)
    ppermute x6, waiting for transfers between devices, outward(): return lax.ppermute(value, 'ex', [(1, 0), (2, 3)])  63.9 us
    dot_general x24, matrix products, weighted(): lax.dot_general(piece, examples, (((1,), (1,)), ((), ())), preferred_elem...  37 us
    ppermute x4, waiting for transfers between devices, inward(): return lax.ppermute(value, 'ex', [(0, 1), (3, 2)])  19.7 us
    ppermute x4, starting transfers between devices, inward(): return lax.ppermute(value, 'ex', [(0, 1), (3, 2)])  17.7 us
    ppermute x4, starting transfers between devices, far_sums(): whole = whole + lax.ppermute(total, PLACE, pairs)  8.58 us
    ppermute x6, starting transfers between devices, outward(): return lax.ppermute(value, 'ex', [(1, 0), (2, 3)])  7.74 us
    ppermute x5, starting transfers between devices, between(): return lax.ppermute(value, 'ex', [(1, 2), (2, 1)])  5.46 us
    ppermute x3, starting transfers between devices, two_near_sums(): got = lax.ppermute(jnp.where(keeps_one, two, one), PLACE, swaps)  4.65 us
  transfers between devices with their start and end apart: 25, of which 6 were waited for; matrix products, arithmetic and copies ran while one was open for 28% of the time, Pallas kernels for 0%

profile of v5, /device:TPU:0, one launch (start us, length us, event | category | flops | bytes accessed | tf_op | source)
XLA Modules:
  0.0 198.9 jit_solution(4068363302484113470)
XLA Ops:
  0.0 4.3 %fusion.224 = (bf16[3,256,1024]{2,1,0:T(8,128)(2,1)}, bf16[3,256,1024]{2,1,0:T(8,128)(2,1)}) fusion(bf16[4,256,1024]{2,1,0:T(8,128)(2,1)} %param.4), kind=kLoop, calls=%fused_computation.179 | loop fusion | bytes 6291456 | tf_op jit(solution)/shard_map/slice | solution.py:170
  4.3 1.9 collective-permute-start.2
  6.1 1.3 collective-permute-start
  7.4 9.0 %collective-permute-start.1 = (bf16[3,256,1024]{2,1,0:T(8,128)(2,1)}, bf16[3,256,1024]{2,1,0:T(8,128)(2,1)}, u32[]{:S(2)}, u32[]{:S(2)}) collective-permute-start(bf16[3,256,1024]{2,1,0:T(8,128)(2,1)} %get-tuple-element.28), channel_id=1, source_target_pairs={{0,4},{12,8},{1,5},{13,9},{2,6},{14,10},{3,7},{15,11},{16,20},{28,... | collective-permute-start | bytes 4718600 | tf_op jit(solution)/shard_map/ppermute | solution.py:146
  16.4 2.3 %fusion.133 = f32[256,1024]{1,0:T(8,128)S(1)} fusion(bf16[4,1024,1024]{2,1,0:T(8,128)(2,1)} %param.3, f32[1024]{0:T(1024)S(1)} %bitcast.205, bf16[4,256,1024]{2,1,0:T(8,128)(2,1)S(1)} %copy-done), kind=kOutput, calls=%fused_computation.78 | convolution fusion | flops 537133056 | bytes 3674112 | tf_op jit(solution)/shard_map/dot_general | solution.py:16
  18.8 3.3 %fusion.112 = f32[256,1024]{1,0:T(8,128)} fusion(bf16[4,1024,1024]{2,1,0:T(8,128)(2,1)} %param.3, f32[1024]{0:T(1024)S(1)} %bitcast.216, bf16[4,256,1024]{2,1,0:T(8,128)(2,1)S(1)} %copy-done), kind=kOutput, calls=%fused_computation.71 | convolution fusion | flops 537133056 | bytes 3674112 | tf_op jit(solution)/shard_map/dot_general | solution.py:16
  22.2 2.3 %convolution_multiply_fusion.3 = f32[256,1024]{1,0:T(8,128)S(1)} fusion(f32[1024]{0:T(1024)S(1)} %bitcast.212, bf16[4,256,1024]{2,1,0:T(8,128)(2,1)S(1)} %copy-done, bf16[4,1024,1024]{2,1,0:T(8,128)(2,1)} %param.3), kind=kOutput, calls=%fused_computation.88 | convolution fusion | flops 537133056 | bytes 3674112 | tf_op jit(solution)/shard_map/dot_general | solution.py:16
  24.5 1.9 slice_bitcast_fusion
  26.6 2.6 %fusion.76 = f32[256,1024]{1,0:T(8,128)S(1)} fusion(f32[256,1024]{1,0:T(8,128)S(1)} %fusion.133, f32[256,1024]{1,0:T(8,128)S(1)} %copy-done.8, f32[256,1024]{1,0:T(8,128)S(1)} %convolution_multiply_fusion.3, bf16[4,1024,1024]{2,1,0:T(8,128)(2,1)} %param.3, f32[1024]{0:T(1024)S(1)} %bitcast.200, bf16[4,256,1024]{2,1,0:T(8,128)(2,1)S(1)} %copy-done), kind=kOutput, calls=%fused_computation.59 | convolution fusion | flops 538181632 | bytes 6819840 | tf_op jit(solution)/shard_map/dot_general | solution.py:16
  29.2 19.7 %collective-permute-done.1 = bf16[3,256,1024]{2,1,0:T(8,128)(2,1)} collective-permute-done((bf16[3,256,1024]{2,1,0:T(8,128)(2,1)}, bf16[3,256,1024]{2,1,0:T(8,128)(2,1)}, u32[]{:S(2)}, u32[]{:S(2)}) %collective-permute-start.1) | collective-permute-done | bytes 1572896 | tf_op jit(solution)/shard_map/ppermute | solution.py:146
  48.8 4.5 %collective-permute-start.10 = (bf16[1040,1024]{1,0:T(8,128)(2,1)S(1)}, bf16[1040,1024]{1,0:T(8,128)(2,1)S(1)}, u32[]{:S(2)}, u32[]{:S(2)}) collective-permute-start(bf16[1040,1024]{1,0:T(8,128)(2,1)S(1)} %pad_maximum_fusion), channel_id=1, source_target_pairs={{0,4},{12,8},{1,5},{13,9},{2,6},{14,10},{3,7},{15,11},{16,20},{28,... | collective-permute-start | bytes 6389768 | tf_op jit(solution)/shard_map/ppermute | solution.py:146
  53.4 1.3 slice.116
  55.4 1.6 broadcast_select_fusion
  57.0 1.3 collective-permute-start.7
  60.2 1.8 fusion.106
  62.0 1.8 fusion.121
  63.9 1.8 fusion.145
  67.2 1.3 collective-permute-start.12
  68.5 27.9 %collective-permute-done.7 = bf16[3,256,1024]{2,1,0:T(8,128)(2,1)S(1)} collective-permute-done((bf16[3,256,1024]{2,1,0:T(8,128)(2,1)}, bf16[3,256,1024]{2,1,0:T(8,128)(2,1)S(1)}, u32[]{:S(2)}, u32[]{:S(2)}) %collective-permute-start.7) | collective-permute-done | bytes 1572896 | tf_op jit(solution)/shard_map/ppermute | solution.py:152
  98.7 1.5 collective-permute-start.8
  105.4 1.2 collective-permute-start.5
  106.7 9.8 %collective-permute-done.12 = bf16[2,256,1024]{2,1,0:T(8,128)(2,1)S(1)} collective-permute-done((bf16[2,256,1024]{2,1,0:T(8,128)(2,1)S(1)}, bf16[2,256,1024]{2,1,0:T(8,128)(2,1)S(1)}, u32[]{:S(2)}, u32[]{:S(2)}) %collective-permute-start.12) | collective-permute-done | bytes 1048608 | tf_op jit(solution)/shard_map/ppermute | solution.py:152
  118.3 1.5 collective-permute-start.11
  119.8 1.8 fusion.130
  121.6 4.4 %collective-permute-start.9 = (f32[256,1024]{1,0:T(8,128)S(1)}, f32[256,1024]{1,0:T(8,128)}, u32[]{:S(2)}, u32[]{:S(2)}) collective-permute-start(f32[256,1024]{1,0:T(8,128)S(1)} %add.102), channel_id=1, source_target_pairs={{0,2},{15,13},{16,18},{31,29}} | collective-permute-start | bytes 3145736 | tf_op jit(solution)/shard_map/ppermute | solution.py:75
  126.0 2.7 %collective-permute-start.17 = (bf16[128,1024]{1,0:T(8,128)(2,1)S(1)}, bf16[128,1024]{1,0:T(8,128)(2,1)}, u32[]{:S(2)}, u32[]{:S(2)}) collective-permute-start(bf16[128,1024]{1,0:T(8,128)(2,1)S(1)} %get-tuple-element.24), channel_id=1, source_target_pairs={{0,4},{12,8},{1,5},{13,9},{2,6},{14,10},{3,7},{15,11},{16,20},{28,... | collective-permute-start | bytes 786440 | tf_op jit(solution)/shard_map/ppermute | solution.py:146
  128.7 1.2 select_add_fusion
  130.0 1.3 collective-permute-start.13
  131.3 1.6 slice_add_fusion.1
  133.0 1.3 collective-permute-start.6
  134.3 1.3 collective-permute-start.14
  139.1 2.5 %slice_add_fusion = f32[128,1024]{1,0:T(8,128)S(1)} fusion(f32[256,1024]{1,0:T(8,128)S(1)} %copy-done.7, bf16[128,1024]{1,0:T(8,128)(2,1)} %collective-permute-done.17, bf16[4,1024,1024]{2,1,0:T(8,128)(2,1)} %param.3, f32[1024]{0:T(1024)S(1)} %bitcast.209), kind=kOutput, calls=%fused_computation.128 | convolution fusion | flops 268828672 | bytes 3411968 | tf_op jit(solution)/shard_map/dot_general | solution.py:16
  141.7 2.8 %collective-permute-done.14 = bf16[128,1024]{1,0:T(8,128)(2,1)} collective-permute-done((bf16[128,1024]{1,0:T(8,128)(2,1)}, bf16[128,1024]{1,0:T(8,128)(2,1)}, u32[]{:S(2)}, u32[]{:S(2)}) %collective-permute-start.14) | collective-permute-done | bytes 262176 | tf_op jit(solution)/shard_map/ppermute | solution.py:152
  145.5 1.3 collective-permute-start.20
  146.8 2.4 %broadcast_select_fusion.6 = (f32[128,1024]{1,0:T(8,128)S(1)}, f32[128,1024]{1,0:T(8,128)S(1)}) fusion(f32[128,1024]{1,0:T(8,128)S(1)} %copy-done.3, pred[]{:T(512)S(6)} %or.71, f32[1024]{0:T(1024)S(1)} %bitcast.210, bf16[128,1024]{1,0:T(8,128)(2,1)S(1)} %broadcast_select_fusion.4, bf16[4,1024,1024]{2,1,0:T(8,128)(2,1)} %param.3, f32[256,1024]{1,0:T(8,128)S(1)} %copy-done.9), kind=kOutput, calls=%fused_computation.162 | convolution fusion | flops 268959744 | bytes 4460545 | tf_op jit(solution)/shard_map/dot_general | solution.py:16
  149.2 1.3 collective-permute-start.15
  151.3 7.5 %collective-permute-done.20 = bf16[128,1024]{1,0:T(8,128)(2,1)S(1)} collective-permute-done((bf16[128,1024]{1,0:T(8,128)(2,1)S(1)}, bf16[128,1024]{1,0:T(8,128)(2,1)S(1)}, u32[]{:S(2)}, u32[]{:S(2)}) %collective-permute-start.20) | collective-permute-done | bytes 262176 | tf_op jit(solution)/shard_map/ppermute | solution.py:152
  158.8 3.4 %broadcast_select_fusion.5 = (f32[128,1024]{1,0:T(8,128)}, f32[128,1024]{1,0:T(8,128)}) fusion(f32[128,1024]{1,0:T(8,128)S(1)} %slice_add_fusion, pred[]{:T(512)S(6)} %or.71, f32[1024]{0:T(1024)S(1)} %bitcast.211, bf16[128,1024]{1,0:T(8,128)(2,1)S(1)} %broadcast_select_fusion.3, bf16[4,1024,1024]{2,1,0:T(8,128)(2,1)} %param.3, f32[256,1024]{1,0:T(8,128)S(1)} %copy-done.9), kind=kOutput, calls=%fused_computation.161 | convolution fusion | flops 268959744 | bytes 4460545 | tf_op jit(solution)/shard_map/dot_general | solution.py:16
  162.3 2.1 %collective-permute-start.21 = (f32[128,1024]{1,0:T(8,128)}, f32[128,1024]{1,0:T(8,128)}, u32[]{:S(2)}, u32[]{:S(2)}) collective-permute-start(f32[128,1024]{1,0:T(8,128)} %get-tuple-element.38), channel_id=1, source_target_pairs={{0,1},{2,3},{5,4},{7,6},{4,5},{6,7},{8,9},{10,11},{9,8},{11,10},{1... | collective-permute-start | bytes 1572872 | tf_op jit(solution)/shard_map/ppermute | solution.py:89
  165.2 1.4 collective-permute-start.16
  169.6 1.4 multiply_convert_fusion
  171.1 1.3 collective-permute-start.24
  172.5 1.2 select_add_fusion.1
  173.6 1.5 collective-permute-start.22
  175.1 1.3 add.111
  176.4 15.9 %collective-permute-done.24 = f16[272,1024]{1,0:T(8,128)(2,1)} collective-permute-done((f16[272,1024]{1,0:T(8,128)(2,1)S(1)}, f16[272,1024]{1,0:T(8,128)(2,1)}, u32[]{:S(2)}, u32[]{:S(2)}) %collective-permute-start.24) | collective-permute-done | bytes 557088 | tf_op jit(solution)/shard_map/ppermute | solution.py:152
  192.3 1.2 slice.132
  195.3 3.6 %fusion.187 = f32[256,1024]{1,0:T(8,128)} fusion(f32[128,1024]{1,0:T(8,128)S(1)} %add.116, f32[128,1024]{1,0:T(8,128)S(1)} %add.111, f32[256,1024]{1,0:T(8,128)S(1)} %add.102, f32[256,1024]{1,0:T(8,128)} %collective-permute-done.9, f32[256,1024]{1,0:T(8,128)} %select_add_fusion, f32[256,1024]{1,0:T(8,128)} %collective-permute-done.6, ...), kind=kLoop, calls=%fused_computation.112 | loop fusion | flops 2097152 | bytes 6815750 | tf_op jit(solution)/shard_map/add | solution.py:235
  (86 shorter events, 21.7 us)
Async XLA Ops:
  0.0 16.4 %copy-start = (bf16[4,256,1024]{2,1,0:T(8,128)(2,1)S(1)}, bf16[4,256,1024]{2,1,0:T(8,128)(2,1)}, u32[]{:S(2)}) copy-start(bf16[4,256,1024]{2,1,0:T(8,128)(2,1)} %param.4) | copy-start | bytes 6291460
  0.0 16.4 %copy-start.10 = (f32[4,1024]{1,0:T(4,128)S(1)}, f32[4,1024]{1,0:T(4,128)}, u32[]{:S(2)}) copy-start(f32[4,1024]{1,0:T(4,128)} %param.5) | copy-start | bytes 49156
  4.3 50.4 %collective-permute-start.2 = (bf16[3,256,1024]{2,1,0:T(8,128)(2,1)}, bf16[3,256,1024]{2,1,0:T(8,128)(2,1)}, u32[]{:S(2)}, u32[]{:S(2)}) collective-permute-start(bf16[3,256,1024]{2,1,0:T(8,128)(2,1)} %get-tuple-element.27), channel_id=1, source_target_pairs={{4,8},{8,4},{5,9},{9,5},{6,10},{10,6},{7,11},{11,7},{20,24},{24,20... | collective-permute-start | bytes 4718600 | tf_op jit(solution)/shard_map/ppermute | solution.py:149
  6.1 49.3 %collective-permute-start = (bf16[3,256,1024]{2,1,0:T(8,128)(2,1)}, bf16[3,256,1024]{2,1,0:T(8,128)(2,1)}, u32[]{:S(2)}, u32[]{:S(2)}) collective-permute-start(bf16[3,256,1024]{2,1,0:T(8,128)(2,1)} %get-tuple-element.27), channel_id=1, source_target_pairs={{4,0},{8,12},{5,1},{9,13},{6,2},{10,14},{7,3},{11,15},{20,16},{24,... | collective-permute-start | bytes 4718600 | tf_op jit(solution)/shard_map/ppermute | solution.py:152
  7.4 41.4 %collective-permute-start.1 = (bf16[3,256,1024]{2,1,0:T(8,128)(2,1)}, bf16[3,256,1024]{2,1,0:T(8,128)(2,1)}, u32[]{:S(2)}, u32[]{:S(2)}) collective-permute-start(bf16[3,256,1024]{2,1,0:T(8,128)(2,1)} %get-tuple-element.28), channel_id=1, source_target_pairs={{0,4},{12,8},{1,5},{13,9},{2,6},{14,10},{3,7},{15,11},{16,20},{28,... | collective-permute-start | bytes 4718600 | tf_op jit(solution)/shard_map/ppermute | solution.py:146
  24.5 2.1 %copy-start.8 = (f32[256,1024]{1,0:T(8,128)S(1)}, f32[256,1024]{1,0:T(8,128)}, u32[]{:S(2)}) copy-start(f32[256,1024]{1,0:T(8,128)} %fusion.112) | copy-start | bytes 3145732
  26.4 31.9 %slice-start = ((s8[8388608]{0:T(1024)(128)(4,1)}), s8[4194304]{0:T(1024)(128)(4,1)S(1)}, s32[]{:S(2)}) async-start(s8[8388608]{0:T(1024)(128)(4,1)} %bitcast.198), calls=%async_computation | async-start | bytes 8388608
  26.6 31.7 %slice-start.1 = ((s8[8388608]{0:T(1024)(128)(4,1)}), s8[4194304]{0:T(1024)(128)(4,1)S(1)}, s32[]{:S(2)}) async-start(s8[8388608]{0:T(1024)(128)(4,1)} %bitcast.198), calls=%async_computation.1 | async-start | bytes 8388608
  48.8 52.1 %collective-permute-start.10 = (bf16[1040,1024]{1,0:T(8,128)(2,1)S(1)}, bf16[1040,1024]{1,0:T(8,128)(2,1)S(1)}, u32[]{:S(2)}, u32[]{:S(2)}) collective-permute-start(bf16[1040,1024]{1,0:T(8,128)(2,1)S(1)} %pad_maximum_fusion), channel_id=1, source_target_pairs={{0,4},{12,8},{1,5},{13,9},{2,6},{14,10},{3,7},{15,11},{16,20},{28,... | collective-permute-start | bytes 6389768 | tf_op jit(solution)/shard_map/ppermute | solution.py:146
  54.7 11.1 %collective-permute-start.3 = (bf16[2,256,1024]{2,1,0:T(8,128)(2,1)S(1)}, bf16[2,256,1024]{2,1,0:T(8,128)(2,1)S(1)}, u32[]{:S(2)}, u32[]{:S(2)}) collective-permute-start(bf16[2,256,1024]{2,1,0:T(8,128)(2,1)S(1)} %slice.116), channel_id=1, source_target_pairs={{4,8},{8,4},{5,9},{9,5},{6,10},{10,6},{7,11},{11,7},{20,24},{24,20... | collective-permute-start | bytes 3145736 | tf_op jit(solution)/shard_map/ppermute | solution.py:149
  57.0 39.4 %collective-permute-start.7 = (bf16[3,256,1024]{2,1,0:T(8,128)(2,1)}, bf16[3,256,1024]{2,1,0:T(8,128)(2,1)S(1)}, u32[]{:S(2)}, u32[]{:S(2)}) collective-permute-start(bf16[3,256,1024]{2,1,0:T(8,128)(2,1)} %collective-permute-done.2), channel_id=1, source_target_pairs={{4,0},{8,12},{5,1},{9,13},{6,2},{10,14},{7,3},{11,15},{20,16},{24,... | collective-permute-start | bytes 4718600 | tf_op jit(solution)/shard_map/ppermute | solution.py:152
  61.9 1.9 slice-start.2
  65.7 65.6 %copy-start.6 = (f32[256,1024]{1,0:T(8,128)}, f32[256,1024]{1,0:T(8,128)S(1)}, u32[]{:S(2)}) copy-start(f32[256,1024]{1,0:T(8,128)S(1)} %fusion.145) | copy-start | bytes 3145732
  65.8 34.4 %collective-permute-start.4 = (bf16[2,256,1024]{2,1,0:T(8,128)(2,1)S(1)}, bf16[2,256,1024]{2,1,0:T(8,128)(2,1)S(1)}, u32[]{:S(2)}, u32[]{:S(2)}) collective-permute-start(bf16[2,256,1024]{2,1,0:T(8,128)(2,1)S(1)} %pad_maximum_fusion.3), channel_id=1, source_target_pairs={{4,8},{8,4},{5,9},{9,5},{6,10},{10,6},{7,11},{11,7},{20,24},{24,20... | collective-permute-start | bytes 3145736 | tf_op jit(solution)/shard_map/ppermute | solution.py:149
  67.2 49.2 %collective-permute-start.12 = (bf16[2,256,1024]{2,1,0:T(8,128)(2,1)S(1)}, bf16[2,256,1024]{2,1,0:T(8,128)(2,1)S(1)}, u32[]{:S(2)}, u32[]{:S(2)}) collective-permute-start(bf16[2,256,1024]{2,1,0:T(8,128)(2,1)S(1)} %collective-permute-done.3), channel_id=1, source_target_pairs={{4,0},{8,12},{5,1},{9,13},{6,2},{10,14},{7,3},{11,15},{20,16},{24,... | collective-permute-start | bytes 3145736 | tf_op jit(solution)/shard_map/ppermute | solution.py:152
  98.7 19.4 %collective-permute-start.8 = (f32[256,1024]{1,0:T(8,128)S(1)}, f32[256,1024]{1,0:T(8,128)S(1)}, u32[]{:S(2)}, u32[]{:S(2)}) collective-permute-start(f32[256,1024]{1,0:T(8,128)S(1)} %fusion.103), channel_id=1, source_target_pairs={{1,0},{3,2},{12,13},{14,15},{17,16},{19,18},{28,29},{30,31}} | collective-permute-start | bytes 3145736 | tf_op jit(solution)/shard_map/ppermute | solution.py:63
  103.7 31.9 %collective-permute-start.18 = (f32[512,1024]{1,0:T(8,128)S(1)}, f32[512,1024]{1,0:T(8,128)S(1)}, u32[]{:S(2)}, u32[]{:S(2)}) collective-permute-start(f32[512,1024]{1,0:T(8,128)S(1)} %fusion), channel_id=1, source_target_pairs={{4,5},{5,4},{6,7},{7,6},{8,9},{9,8},{10,11},{11,10},{20,21},{21,20... | collective-permute-start | bytes 6291464 | tf_op jit(solution)/shard_map/ppermute | solution.py:201
  105.4 23.3 %collective-permute-start.5 = (f32[256,1024]{1,0:T(8,128)S(1)}, f32[256,1024]{1,0:T(8,128)S(1)}, u32[]{:S(2)}, u32[]{:S(2)}) collective-permute-start(f32[256,1024]{1,0:T(8,128)S(1)} %get-tuple-element.40), channel_id=1, source_target_pairs={{1,0},{3,2},{0,1},{2,3},{4,5},{6,7},{5,4},{7,6},{9,8},{11,10},{8,9... | collective-permute-start | bytes 3145736 | tf_op jit(solution)/shard_map/ppermute | solution.py:89
  118.3 7.7 %collective-permute-start.11 = (bf16[128,1024]{1,0:T(8,128)(2,1)S(1)}, bf16[128,1024]{1,0:T(8,128)(2,1)S(1)}, u32[]{:S(2)}, u32[]{:S(2)}) collective-permute-start(bf16[128,1024]{1,0:T(8,128)(2,1)S(1)} %get-tuple-element.21), channel_id=1, source_target_pairs={{0,4},{12,8},{1,5},{13,9},{2,6},{14,10},{3,7},{15,11},{16,20},{28,... | collective-permute-start | bytes 786440 | tf_op jit(solution)/shard_map/ppermute | solution.py:146
  121.6 73.7 %collective-permute-start.9 = (f32[256,1024]{1,0:T(8,128)S(1)}, f32[256,1024]{1,0:T(8,128)}, u32[]{:S(2)}, u32[]{:S(2)}) collective-permute-start(f32[256,1024]{1,0:T(8,128)S(1)} %add.102), channel_id=1, source_target_pairs={{0,2},{15,13},{16,18},{31,29}} | collective-permute-start | bytes 3145736 | tf_op jit(solution)/shard_map/ppermute | solution.py:75
  126.0 12.3 %collective-permute-start.17 = (bf16[128,1024]{1,0:T(8,128)(2,1)S(1)}, bf16[128,1024]{1,0:T(8,128)(2,1)}, u32[]{:S(2)}, u32[]{:S(2)}) collective-permute-start(bf16[128,1024]{1,0:T(8,128)(2,1)S(1)} %get-tuple-element.24), channel_id=1, source_target_pairs={{0,4},{12,8},{1,5},{13,9},{2,6},{14,10},{3,7},{15,11},{16,20},{28,... | collective-permute-start | bytes 786440 | tf_op jit(solution)/shard_map/ppermute | solution.py:146
  130.0 4.3 %collective-permute-start.13 = (bf16[128,1024]{1,0:T(8,128)(2,1)S(1)}, bf16[128,1024]{1,0:T(8,128)(2,1)}, u32[]{:S(2)}, u32[]{:S(2)}) collective-permute-start(bf16[128,1024]{1,0:T(8,128)(2,1)S(1)} %collective-permute-done.11), channel_id=1, source_target_pairs={{4,8},{8,4},{5,9},{9,5},{6,10},{10,6},{7,11},{11,7},{20,24},{24,20... | collective-permute-start | bytes 786440 | tf_op jit(solution)/shard_map/ppermute | solution.py:149
  133.0 62.3 %collective-permute-start.6 = (f32[256,1024]{1,0:T(8,128)}, f32[256,1024]{1,0:T(8,128)}, u32[]{:S(2)}, u32[]{:S(2)}) collective-permute-start(f32[256,1024]{1,0:T(8,128)} %select_add_fusion), channel_id=1, source_target_pairs={{2,0},{3,1},{7,5},{4,6},{8,10},{11,9},{13,15},{12,14},{18,16},{19,... | collective-permute-start | bytes 3145736 | tf_op jit(solution)/shard_map/ppermute | solution.py:75
  134.3 10.2 %collective-permute-start.14 = (bf16[128,1024]{1,0:T(8,128)(2,1)}, bf16[128,1024]{1,0:T(8,128)(2,1)}, u32[]{:S(2)}, u32[]{:S(2)}) collective-permute-start(bf16[128,1024]{1,0:T(8,128)(2,1)} %collective-permute-done.13), channel_id=1, source_target_pairs={{4,0},{8,12},{5,1},{9,13},{6,2},{10,14},{7,3},{11,15},{20,16},{24,... | collective-permute-start | bytes 786440 | tf_op jit(solution)/shard_map/ppermute | solution.py:152
  137.9 1.2 copy-start.7
  138.3 8.5 %copy-start.3 = (f32[128,1024]{1,0:T(8,128)S(1)}, f32[128,1024]{1,0:T(8,128)}, u32[]{:S(2)}) copy-start(f32[128,1024]{1,0:T(8,128)} %slice_add_fusion.1) | copy-start | bytes 1572868
  138.3 8.5 %copy-start.9 = (f32[256,1024]{1,0:T(8,128)S(1)}, f32[256,1024]{1,0:T(8,128)}, u32[]{:S(2)}) copy-start(f32[256,1024]{1,0:T(8,128)} %fusion.130) | copy-start | bytes 3145732
  138.3 7.2 %collective-permute-start.19 = (bf16[128,1024]{1,0:T(8,128)(2,1)}, bf16[128,1024]{1,0:T(8,128)(2,1)S(1)}, u32[]{:S(2)}, u32[]{:S(2)}) collective-permute-start(bf16[128,1024]{1,0:T(8,128)(2,1)} %collective-permute-done.17), channel_id=1, source_target_pairs={{4,8},{8,4},{5,9},{9,5},{6,10},{10,6},{7,11},{11,7},{20,24},{24,20... | collective-permute-start | bytes 786440 | tf_op jit(solution)/shard_map/ppermute | solution.py:149
  141.7 17.2 %copy-start.1 = (f32[128,1024]{1,0:T(8,128)}, f32[128,1024]{1,0:T(8,128)S(1)}, u32[]{:S(2)}) copy-start(f32[128,1024]{1,0:T(8,128)S(1)} %slice_add_fusion) | copy-start | bytes 1572868
  145.5 13.3 %collective-permute-start.20 = (bf16[128,1024]{1,0:T(8,128)(2,1)S(1)}, bf16[128,1024]{1,0:T(8,128)(2,1)S(1)}, u32[]{:S(2)}, u32[]{:S(2)}) collective-permute-start(bf16[128,1024]{1,0:T(8,128)(2,1)S(1)} %collective-permute-done.19), channel_id=1, source_target_pairs={{4,0},{8,12},{5,1},{9,13},{6,2},{10,14},{7,3},{11,15},{20,16},{24,... | collective-permute-start | bytes 786440 | tf_op jit(solution)/shard_map/ppermute | solution.py:152
  149.2 15.1 %collective-permute-start.15 = (f32[128,1024]{1,0:T(8,128)S(1)}, f32[128,1024]{1,0:T(8,128)S(1)}, u32[]{:S(2)}, u32[]{:S(2)}) collective-permute-start(f32[128,1024]{1,0:T(8,128)S(1)} %get-tuple-element.42), channel_id=1, source_target_pairs={{0,1},{2,3},{5,4},{7,6},{4,5},{6,7},{8,9},{10,11},{9,8},{11,10},{1... | collective-permute-start | bytes 1572872 | tf_op jit(solution)/shard_map/ppermute | solution.py:89
  150.6 16.1 %collective-permute-start.23 = (f16[272,1024]{1,0:T(8,128)(2,1)S(1)}, f16[272,1024]{1,0:T(8,128)(2,1)S(1)}, u32[]{:S(2)}, u32[]{:S(2)}) collective-permute-start(f16[272,1024]{1,0:T(8,128)(2,1)S(1)} %concatenate.21), channel_id=1, source_target_pairs={{7,5},{4,6},{5,7},{8,10},{11,9},{10,8},{23,21},{20,22},{21,23},{24... | collective-permute-start | bytes 1671176 | tf_op jit(solution)/shard_map/ppermute | solution.py:210
  162.3 10.2 %collective-permute-start.21 = (f32[128,1024]{1,0:T(8,128)}, f32[128,1024]{1,0:T(8,128)}, u32[]{:S(2)}, u32[]{:S(2)}) collective-permute-start(f32[128,1024]{1,0:T(8,128)} %get-tuple-element.38), channel_id=1, source_target_pairs={{0,1},{2,3},{5,4},{7,6},{4,5},{6,7},{8,9},{10,11},{9,8},{11,10},{1... | collective-permute-start | bytes 1572872 | tf_op jit(solution)/shard_map/ppermute | solution.py:89
  165.2 9.9 %collective-permute-start.16 = (f32[128,1024]{1,0:T(8,128)}, f32[128,1024]{1,0:T(8,128)}, u32[]{:S(2)}, u32[]{:S(2)}) collective-permute-start(f32[128,1024]{1,0:T(8,128)} %select_add_fusion.2), channel_id=1, source_target_pairs={{1,3},{6,4},{5,7},{9,11},{10,8},{14,12},{17,19},{22,20},{21,23},{2... | collective-permute-start | bytes 1572872 | tf_op jit(solution)/shard_map/ppermute | solution.py:75
  166.7 1.3 copy-start.5
  169.6 2.9 %copy-start.2 = (f32[128,1024]{1,0:T(8,128)S(1)}, f32[128,1024]{1,0:T(8,128)}, u32[]{:S(2)}) copy-start(f32[128,1024]{1,0:T(8,128)} %copy-done.1) | copy-start | bytes 1572868
  169.6 2.9 %copy-start.4 = (f32[128,1024]{1,0:T(8,128)S(1)}, f32[128,1024]{1,0:T(8,128)}, u32[]{:S(2)}) copy-start(f32[128,1024]{1,0:T(8,128)} %get-tuple-element.39) | copy-start | bytes 1572868
  171.1 21.1 %collective-permute-start.24 = (f16[272,1024]{1,0:T(8,128)(2,1)S(1)}, f16[272,1024]{1,0:T(8,128)(2,1)}, u32[]{:S(2)}, u32[]{:S(2)}) collective-permute-start(f16[272,1024]{1,0:T(8,128)(2,1)S(1)} %concatenate.23), channel_id=1, source_target_pairs={{4,0},{8,12},{5,1},{9,13},{6,2},{10,14},{7,3},{11,15},{20,16},{24,... | collective-permute-start | bytes 1671176 | tf_op jit(solution)/shard_map/ppermute | solution.py:152
  173.6 20.5 %collective-permute-start.22 = (f32[128,1024]{1,0:T(8,128)S(1)}, f32[128,1024]{1,0:T(8,128)}, u32[]{:S(2)}, u32[]{:S(2)}) collective-permute-start(f32[128,1024]{1,0:T(8,128)S(1)} %select_add_fusion.1), channel_id=1, source_target_pairs={{1,3},{6,4},{5,7},{9,11},{10,8},{14,12},{17,19},{22,20},{21,23},{2... | collective-permute-start | bytes 1572872 | tf_op jit(solution)/shard_map/ppermute | solution.py:75

commit v6 on v5

--- a/solution.py
+++ b/solution.py
@@ -66,26 +66,28 @@
     def far_sums(self, total, *held):
         whole = total
         for away in range(1, self.ckpts):
-            pairs = []
-            for z in range(self.planes):
-                for blocks in held:
-                    if blocks[z] is not None:
-                        x, c = self.of(blocks[z])
-                        pairs.append((self.index(z, (x + away) % self.ckpts, c), self.index(z, x, c)))
-            whole = whole + lax.ppermute(total, PLACE, pairs)
+            whole = whole + self.far_moves(total, *held, away=away)
         return whole
+
+    def far_moves(self, total, *held, away=1):
+        pairs = []
+        for z in range(self.planes):
+            for blocks in held:
+                if blocks[z] is not None:
+                    x, c = self.of(blocks[z])
+                    pairs.append((self.index(z, (x + away) % self.ckpts, c), self.index(z, x, c)))
+        return lax.ppermute(total, PLACE, pairs)
 
     def two_near_sums(self, one, one_blocks, two, two_blocks):
         keeps_one = jnp.bool_(False)
         swaps = []
         for z, blocks in enumerate(zip(one_blocks, two_blocks)):
+            if blocks[0] is None:
+                continue
             second = self.of(blocks[1])[1]
-            assert blocks[0] is None or self.of(blocks[0])[1] == 1 - second
+            assert self.of(blocks[0])[1] == 1 - second
             keeps_one = keeps_one | ((self.z == z) & (self.c == 1 - second))
-            for block in blocks:
-                if block is not None:
-                    c = self.of(block)[1]
-                    swaps += [(self.index(z, x, 1 - c), self.index(z, x, c)) for x in range(2)]
+            swaps += [(self.index(z, x, c), self.index(z, x, 1 - c)) for x in range(2) for c in range(2)]
         got = lax.ppermute(jnp.where(keeps_one, two, one), PLACE, swaps)
         return jnp.where(keeps_one, one, two) + got
 
@@ -135,12 +137,15 @@
 
 
 def line(train_features, query_features, residual_weights, keepers, scale):
-    z, c = keepers.z, keepers.c
+    z = keepers.z
     rows, depth = query_features.shape[1:]
     examples = train_features.shape[1]
     low = rows // 2
     assert train_features.shape[0] == 4 and examples <= depth
     ends = (z == 0) | (z == 3)
+
+    def aside(value):
+        return lax.ppermute(value, "ex", [(0, 1), (1, 0), (2, 3), (3, 2)])
 
     def inward(value):
         return lax.ppermute(value, "ex", [(0, 1), (3, 2)])
@@ -165,27 +170,27 @@
     tail = jnp.pad(jnp.stack(pieces), ((0, 13), (0, depth - examples)))
     training = jnp.concatenate([train_features[0], tail], axis=0)
 
-    in_many = inward(query_features[:3])
-    mid_own = between(query_features[1:])
-    out_own = outward(query_features[1:])
+    side = aside(query_features)
+    middle = between(query_features)
     own = scores(list(query_features))
-    out_next = outward(mid_own)
-    mid_edge = between(after(in_many[1:], mid_own))
-    in_train = inward(after(training, in_many))
-    out_edge = outward(mid_edge)
-    mid_first = between(after(jnp.stack([query_features[0], in_many[0]]), mid_edge))
-    one, far_one = mid_first[0], mid_first[1]
-
+    in_train = inward(after(training, side))
+    out_next = outward(middle[1:])
+    parts = [slice(0, low), slice(low, rows)]
     blocks_own = [0, 1, 2, 3]
-    blocks_1 = [1, 2, 1, 2]
-    blocks_2 = [2, None, None, 1]
-    blocks_3 = [None, 0, 3, None]
-    blocks_4 = [3, 3, 0, 0]
-
-    checks = chosen(after(out_own, in_many), mid_own)
-    found_1 = scores(list(checks), 1)
-    found_2 = scores(list(after(out_next, mid_edge)), 1)
-    total_2 = keepers.near_sums(found_2, blocks_2)
+    blocks_1 = [1, 0, 3, 2]
+    blocks_2 = [2, 2, 1, 1]
+    blocks_3 = [3, 3, 0, 0]
+
+    total_1 = keepers.two_near_sums(own, blocks_own, scores(list(side)), blocks_1)
+    result_1 = keepers.far_sums(total_1, blocks_own, blocks_1)
+
+    mid_edge = [between(side[1:, parts[0]])]
+    mid_edge.append(between(after(side[1:, parts[1]], mid_edge[0], total_1)))
+    out_edge = [outward(part) for part in mid_edge]
+    far_one = between(after(side[0], mid_edge[1]))
+
+    checks = chosen(out_next, middle[1:])
+    total_2 = keepers.near_sums(scores([middle[0]] + list(checks)), blocks_2)
     result_2 = keepers.far_sums(total_2, blocks_2)
 
     weights = jnp.sum(in_train[examples:examples + 3, :examples].astype(jnp.float32), axis=0)
@@ -193,42 +198,26 @@
     def beside(queries):
         return weighted([queries], [in_train[:examples]], [weights], scale)
 
-    first, second, third = beside(query_features[0]), beside(one), beside(far_one)
-    alone = ((z == 1) & (c == 0)) | ((z == 2) & (c == 1))
-    pair = jnp.concatenate([first, third], axis=0)
-    lone = jnp.concatenate([second, second], axis=0)
-    swaps = [(keepers.index(p, q, r), keepers.index(p, q, 1 - r)) for p in (1, 2) for q in range(2) for r in range(2)]
-    got = lax.ppermute(jnp.where(alone, pair, lone), PLACE, swaps)
-    total = jnp.where(alone, lone, pair) + got
-    keeps_first = keepers.mine([None, 1, 2, None])
-    crosses = []
-    for p, blocks in ((1, (1, 2, 3)), (2, (2, 1, 0))):
-        for block in blocks:
-            at, r = keepers.of(block)
-            crosses.append((keepers.index(p, 1 - at, r), keepers.index(p, at, r)))
-    crossing = packed(jnp.where(keeps_first, total[rows:], total[:rows]))
-    got = lax.ppermute(crossing, PLACE, crosses)
-    returned = jnp.where(keeps_first, total[:rows], total[rows:]) + unpacked(got)
-    returned = packed(jnp.where(keepers.mine([None, 0, 3, None]), 0.0, returned))
-
-    found_1 = found_1 + scores([one])
-    total_1 = keepers.two_near_sums(own, blocks_own, found_1, blocks_1)
-    result_1 = keepers.far_sums(total_1, blocks_own, blocks_1)
-
-    base_3 = scores(list(in_many))
-    checks = chosen(after(out_edge, in_train), mid_edge)
-    base_4 = scores([far_one, checks[0], checks[1]])
-    results, before = [], in_train
-    for k in range(2):
-        part = slice(k * low, (k + 1) * low)
-        before = inward(after(query_features[3, part], before, total_2))
-        mid = between(after(before, total_1 if k == 0 else crossing))
-        out = outward(mid)
-        block_3 = base_3[part] + scores([before], 3)
-        block_4 = base_4[part] + scores([chosen(out, mid)], 3)
-        total = keepers.two_near_sums(block_3, blocks_3, block_4, blocks_4)
-        results.append(keepers.far_sums(total, blocks_3, blocks_4))
-    returned = unpacked(outward(after(returned, mid)))
+    beside_2 = [None, 2, 1, None]
+    beside_3 = [None, 3, 0, None]
+    total = keepers.two_near_sums(beside(middle[0]), beside_2, beside(far_one), beside_3)
+    crossing = packed(after(total, result_1, total_2))
+    returned = total + unpacked(keepers.far_moves(crossing, beside_2, beside_3))
+    returned = jnp.where(keepers.mine(beside_2) | keepers.mine(beside_3), returned, 0.0)
+
+    def last(k, *before):
+        checks = chosen(after(out_edge[k], *before), mid_edge[k])
+        found = scores([far_one[parts[k]]] + list(checks))
+        return keepers.near_sums(found, blocks_3)
+
+    total_3 = [last(0, crossing)]
+    results = [keepers.far_sums(total_3[0], blocks_3)]
+    returned = packed(after(returned, result_2, total_3[0]))
+    halves = [after(jnp.concatenate([returned[part], returned[rows:]], axis=0)) for part in parts]
+    total_3.append(last(1, *halves))
+    halves = [outward(half) for half in halves]
+    results.append(keepers.far_sums(after(total_3[1], halves[0]), blocks_3))
+    returned = jnp.concatenate([unpacked(part) for part in halves], axis=0)
 
     result = jnp.where(keepers.mine(blocks_2), result_2, jnp.concatenate(results, axis=0))
     result = jnp.where(keepers.mine(blocks_own) | keepers.mine(blocks_1), result_1, result)

time: 200 us -> 218 us (1.090)
  waiting for transfers between devices: 83.6 us -> 102 us
  starting transfers between devices: 47.1 us -> 37 us
  matrix products: 37 us -> 43 us
    ppermute x6, waiting for transfers between devices: 0.02 us -> 34.8 us  [the longest x1 34.8 us: aside(): return lax.ppermute(value, 'ex', [(0, 1), (1, 0), (2, 3), (3, 2)])]
    ppermute x6 -> x5, waiting for transfers between devices: 63.9 us -> 53.6 us  [outward(): return lax.ppermute(value, 'ex', [(1, 0), (2, 3)])]
    ppermute x4 -> x1, starting transfers between devices: 17.7 us -> 9.06 us  [inward(): return lax.ppermute(value, 'ex', [(0, 1), (3, 2)])]
    dot_general x24 -> x22, matrix products: 37 us -> 43 us  [weighted(): lax.dot_general(piece, examples, (((1,), (1,)), ((), ())), preferred_elem...]
    ppermute x4 -> x1, waiting for transfers between devices: 19.7 us -> 13.7 us  [inward(): return lax.ppermute(value, 'ex', [(0, 1), (3, 2)])]
    ppermute x1 -> x3, starting transfers between devices: 1.47 us -> 5.41 us  [near_sums(): total = total + lax.ppermute(partial, PLACE, pairs)]
    ppermute x3 -> x2, starting transfers between devices: 4.65 us -> 0.72 us  [two_near_sums(): got = lax.ppermute(jnp.where(keeps_one, two, one), PLACE, swaps)]
    slice x3, local copies, waits for them, and re-layouts: 6.66 us -> 3.05 us  [the longest x1 1.65 us: line(): mid_edge = [between(side[1:, parts[0]])]]
  transfers between devices with their start and end apart: 25 -> 21, of which waited for: 6 -> 6; matrix products, arithmetic and copies ran while one was open for 28% -> 27% of each run, Pallas kernels for 0% -> 0%
where the time goes in v6:
time: 218 us; the launch traced here: 215 us
  waiting for transfers between devices  102 us (47%)
  matrix products  43 us (20%)
  starting transfers between devices  37 us (17%)
  other arithmetic  18.4 us (8%)
  local copies, waits for them, and re-layouts  10.4 us (5%)
  between operations  4.34 us (2%)
    ppermute x5, waiting for transfers between devices, outward(): return lax.ppermute(value, 'ex', [(1, 0), (2, 3)])  53.6 us
    dot_general x22, matrix products, weighted(): lax.dot_general(piece, examples, (((1,), (1,)), ((), ())), preferred_elem...  43 us
    ppermute x1, waiting for transfers between devices, aside(): return lax.ppermute(value, 'ex', [(0, 1), (1, 0), (2, 3), (3, 2)])  34.8 us
    ppermute x1, waiting for transfers between devices, inward(): return lax.ppermute(value, 'ex', [(0, 1), (3, 2)])  13.7 us
    ppermute x1, starting transfers between devices, inward(): return lax.ppermute(value, 'ex', [(0, 1), (3, 2)])  9.06 us
    ppermute x5, starting transfers between devices, far_moves(): return lax.ppermute(total, PLACE, pairs)  8.5 us
    ppermute x5, starting transfers between devices, outward(): return lax.ppermute(value, 'ex', [(1, 0), (2, 3)])  6.44 us
    ppermute x3, starting transfers between devices, near_sums(): total = total + lax.ppermute(partial, PLACE, pairs)  5.41 us
  transfers between devices with their start and end apart: 21, of which 6 were waited for; matrix products, arithmetic and copies ran while one was open for 27% of the time, Pallas kernels for 0%

profile of v6, /device:TPU:0, one launch (start us, length us, event | category | flops | bytes accessed | tf_op | source)
XLA Modules:
  0.0 215.3 jit_solution(15891468206615092999)
XLA Ops:
  0.0 3.0 %collective-permute-start = (bf16[4,256,1024]{2,1,0:T(8,128)(2,1)}, bf16[4,256,1024]{2,1,0:T(8,128)(2,1)}, u32[]{:S(2)}, u32[]{:S(2)}) collective-permute-start(bf16[4,256,1024]{2,1,0:T(8,128)(2,1)} %param.4), channel_id=1, source_target_pairs={{0,4},{4,0},{8,12},{12,8},{1,5},{5,1},{9,13},{13,9},{2,6},{6,2},{1... | collective-permute-start | bytes 6291464 | tf_op jit(solution)/shard_map/ppermute | solution.py:148
  4.8 2.6 %convolution_multiply_fusion.2 = f32[256,1024]{1,0:T(8,128)S(1)} fusion(f32[1024]{0:T(1024)S(1)} %bitcast.172, bf16[4,256,1024]{2,1,0:T(8,128)(2,1)} %param.4, bf16[4,1024,1024]{2,1,0:T(8,128)(2,1)} %param.3), kind=kOutput, calls=%fused_computation.65 | convolution fusion | flops 537133056 | bytes 3674112 | tf_op jit(solution)/shard_map/dot_general | solution.py:16
  7.4 3.0 %fusion.70 = f32[256,1024]{1,0:T(8,128)S(1)} fusion(bf16[4,1024,1024]{2,1,0:T(8,128)(2,1)} %param.3, f32[1024]{0:T(1024)S(1)} %bitcast.167, bf16[4,256,1024]{2,1,0:T(8,128)(2,1)} %param.4), kind=kOutput, calls=%fused_computation.49 | convolution fusion | flops 537133056 | bytes 3674112 | tf_op jit(solution)/shard_map/dot_general | solution.py:16
  10.4 1.8 fusion.88
  12.2 1.9 fusion.61
  14.2 34.8 %collective-permute-done = bf16[4,256,1024]{2,1,0:T(8,128)(2,1)} collective-permute-done((bf16[4,256,1024]{2,1,0:T(8,128)(2,1)}, bf16[4,256,1024]{2,1,0:T(8,128)(2,1)}, u32[]{:S(2)}, u32[]{:S(2)}) %collective-permute-start) | collective-permute-done | bytes 2097184 | tf_op jit(solution)/shard_map/ppermute | solution.py:148
  49.0 1.8 fusion.64
  50.8 1.8 fusion.73
  52.6 1.8 fusion.91
  54.4 3.3 %broadcast_select_fusion.4 = (f32[256,1024]{1,0:T(8,128)}, f32[256,1024]{1,0:T(8,128)}) fusion(f32[256,1024]{1,0:T(8,128)S(1)} %fusion.61, pred[]{:T(512)S(6)} %or.63, f32[256,1024]{1,0:T(8,128)S(1)} %fusion.91, f32[256,1024]{1,0:T(8,128)S(1)} %fusion.73, f32[256,1024]{1,0:T(8,128)S(1)} %fusion.64, f32[1024]{0:T(1024)S(1)} %bitcast.173, ...), kind=kOutput, calls=%fused_computation.128 | convolution fusion | flops 538443776 | bytes 8916993 | tf_op jit(solution)/shard_map/dot_general | solution.py:16
  57.7 1.4 slice.72
  59.5 1.3 collective-permute-start.4
  61.0 1.6 fusion.174
  62.7 1.7 collective-permute-start.7
  64.6 9.1 %collective-permute-start.11 = (bf16[1040,1024]{1,0:T(8,128)(2,1)S(1)}, bf16[1040,1024]{1,0:T(8,128)(2,1)S(1)}, u32[]{:S(2)}, u32[]{:S(2)}) collective-permute-start(bf16[1040,1024]{1,0:T(8,128)(2,1)S(1)} %pad_maximum_fusion), channel_id=1, source_target_pairs={{0,4},{12,8},{1,5},{13,9},{2,6},{14,10},{3,7},{15,11},{16,20},{28,... | collective-permute-start | bytes 6389768 | tf_op jit(solution)/shard_map/ppermute | solution.py:151
  73.6 1.2 slice_bitcast_fusion.14
  74.9 1.6 select_add_fusion.1
  76.6 1.3 collective-permute-start.2
  78.6 19.9 %collective-permute-done.4 = bf16[3,256,1024]{2,1,0:T(8,128)(2,1)} collective-permute-done((bf16[3,256,1024]{2,1,0:T(8,128)(2,1)}, bf16[3,256,1024]{2,1,0:T(8,128)(2,1)}, u32[]{:S(2)}, u32[]{:S(2)}) %collective-permute-start.4) | collective-permute-done | bytes 1572896 | tf_op jit(solution)/shard_map/ppermute | solution.py:157
  98.5 1.6 broadcast_select_fusion
  104.0 1.5 collective-permute-start.5
  105.4 13.7 %collective-permute-done.11 = bf16[1040,1024]{1,0:T(8,128)(2,1)S(1)} collective-permute-done((bf16[1040,1024]{1,0:T(8,128)(2,1)S(1)}, bf16[1040,1024]{1,0:T(8,128)(2,1)S(1)}, u32[]{:S(2)}, u32[]{:S(2)}) %collective-permute-start.11) | collective-permute-done | bytes 2129952 | tf_op jit(solution)/shard_map/ppermute | solution.py:151
  121.5 1.3 collective-permute-start.10
  123.1 4.4 %collective-permute-start.6 = (f32[256,1024]{1,0:T(8,128)S(1)}, f32[256,1024]{1,0:T(8,128)}, u32[]{:S(2)}, u32[]{:S(2)}) collective-permute-start(f32[256,1024]{1,0:T(8,128)S(1)} %add.101), channel_id=1, source_target_pairs={{0,2},{4,6},{11,9},{15,13},{16,18},{20,22},{27,25},{31,29}} | collective-permute-start | bytes 3145736 | tf_op jit(solution)/shard_map/ppermute | solution.py:79
  130.3 1.5 collective-permute-start.16
  131.7 15.8 %collective-permute-done.10 = bf16[3,128,1024]{2,1,0:T(8,128)(2,1)} collective-permute-done((bf16[3,128,1024]{2,1,0:T(8,128)(2,1)}, bf16[3,128,1024]{2,1,0:T(8,128)(2,1)}, u32[]{:S(2)}, u32[]{:S(2)}) %collective-permute-start.10) | collective-permute-done | bytes 786464 | tf_op jit(solution)/shard_map/ppermute | solution.py:157
  147.6 1.2 broadcast_select_fusion.2
  148.8 2.5 %fusion.102 = f32[128,1024]{1,0:T(8,128)S(1)} fusion(bf16[4,1024,1024]{2,1,0:T(8,128)(2,1)} %param.3, bf16[3,128,1024]{2,1,0:T(8,128)(2,1)S(1)} %broadcast_select_fusion.2, f32[1024]{0:T(1024)S(1)} %bitcast.180), kind=kOutput, calls=%fused_computation.66 | convolution fusion | flops 268566528 | bytes 2887680 | tf_op jit(solution)/shard_map/dot_general | solution.py:16
  151.3 2.4 %fusion.139 = f32[128,1024]{1,0:T(8,128)S(1)} fusion(f32[128,1024]{1,0:T(8,128)S(1)} %fusion.102, bf16[256,1024]{1,0:T(8,128)(2,1)S(1)} %copy-done.9, f32[1024]{0:T(1024)S(1)} %bitcast.175, bf16[4,1024,1024]{2,1,0:T(8,128)(2,1)} %param.3), kind=kOutput, calls=%fused_computation.81 | convolution fusion | flops 268697600 | bytes 3411968 | tf_op jit(solution)/shard_map/dot_general | solution.py:16
  153.7 2.4 %fusion.132 = f32[128,1024]{1,0:T(8,128)S(1)} fusion(bf16[4,1024,1024]{2,1,0:T(8,128)(2,1)} %param.3, bf16[3,128,1024]{2,1,0:T(8,128)(2,1)S(1)} %broadcast_select_fusion.2, f32[1024]{0:T(1024)S(1)} %bitcast.185), kind=kOutput, calls=%fused_computation.76 | convolution fusion | flops 268566528 | bytes 2887680 | tf_op jit(solution)/shard_map/dot_general | solution.py:16
  156.2 3.3 %fusion.117 = f32[128,1024]{1,0:T(8,128)} fusion(f32[128,1024]{1,0:T(8,128)S(1)} %fusion.132, f32[128,1024]{1,0:T(8,128)S(1)} %fusion.139, bf16[4,1024,1024]{2,1,0:T(8,128)(2,1)} %param.3, bf16[3,128,1024]{2,1,0:T(8,128)(2,1)S(1)} %broadcast_select_fusion.2, f32[1024]{0:T(1024)S(1)} %bitcast.170), kind=kOutput, calls=%fused_computation.71 | convolution fusion | flops 268959744 | bytes 3936256 | tf_op jit(solution)/shard_map/dot_general | solution.py:16
  159.4 2.6 %collective-permute-start.13 = (f32[128,1024]{1,0:T(8,128)}, f32[128,1024]{1,0:T(8,128)}, u32[]{:S(2)}, u32[]{:S(2)}) collective-permute-start(f32[128,1024]{1,0:T(8,128)} %fusion.117), channel_id=1, source_target_pairs={{0,1},{2,3},{4,5},{6,7},{9,8},{11,10},{13,12},{15,14},{16,17},{18,... | collective-permute-start | bytes 1572872 | tf_op jit(solution)/shard_map/ppermute | solution.py:63
  162.0 1.3 collective-permute-start.15
  163.3 2.3 %add.102 = f32[256,1024]{1,0:T(8,128)} add(f32[256,1024]{1,0:T(8,128)S(1)} %add.101, f32[256,1024]{1,0:T(8,128)} %collective-permute-done.6) | non-fusion elementwise | flops 262144 | bytes 3145728 | tf_op jit(solution)/shard_map/add | solution.py:69
  165.7 2.1 add.107
  169.6 1.3 add_select_fusion
  172.7 9.6 %collective-permute-done.15 = bf16[3,128,1024]{2,1,0:T(8,128)(2,1)} collective-permute-done((bf16[3,128,1024]{2,1,0:T(8,128)(2,1)}, bf16[3,128,1024]{2,1,0:T(8,128)(2,1)}, u32[]{:S(2)}, u32[]{:S(2)}) %collective-permute-start.15) | collective-permute-done | bytes 786464 | tf_op jit(solution)/shard_map/ppermute | solution.py:157
  182.3 1.2 broadcast_select_fusion.1
  183.5 2.4 %fusion.105 = f32[128,1024]{1,0:T(8,128)S(1)} fusion(bf16[4,1024,1024]{2,1,0:T(8,128)(2,1)} %param.3, bf16[3,128,1024]{2,1,0:T(8,128)(2,1)S(1)} %broadcast_select_fusion.1, f32[1024]{0:T(1024)S(1)} %bitcast.181), kind=kOutput, calls=%fused_computation.67 | convolution fusion | flops 268566528 | bytes 2887680 | tf_op jit(solution)/shard_map/dot_general | solution.py:16
  186.0 2.5 %fusion.135 = f32[128,1024]{1,0:T(8,128)S(1)} fusion(bf16[4,1024,1024]{2,1,0:T(8,128)(2,1)} %param.3, bf16[3,128,1024]{2,1,0:T(8,128)(2,1)S(1)} %broadcast_select_fusion.1, f32[1024]{0:T(1024)S(1)} %bitcast.186), kind=kOutput, calls=%fused_computation.77 | convolution fusion | flops 268566528 | bytes 2887680 | tf_op jit(solution)/shard_map/dot_general | solution.py:16
  188.5 2.4 %fusion.138 = f32[128,1024]{1,0:T(8,128)S(1)} fusion(f32[128,1024]{1,0:T(8,128)S(1)} %fusion.105, bf16[256,1024]{1,0:T(8,128)(2,1)S(1)} %copy-done.10, f32[1024]{0:T(1024)S(1)} %bitcast.176, bf16[4,1024,1024]{2,1,0:T(8,128)(2,1)} %param.3), kind=kOutput, calls=%fused_computation.79 | convolution fusion | flops 268697600 | bytes 3411968 | tf_op jit(solution)/shard_map/dot_general | solution.py:16
  190.9 2.5 %fusion.129 = f32[128,1024]{1,0:T(8,128)S(1)} fusion(f32[128,1024]{1,0:T(8,128)S(1)} %fusion.135, f32[128,1024]{1,0:T(8,128)S(1)} %fusion.138, bf16[4,1024,1024]{2,1,0:T(8,128)(2,1)} %param.3, bf16[3,128,1024]{2,1,0:T(8,128)(2,1)S(1)} %broadcast_select_fusion.1, f32[1024]{0:T(1024)S(1)} %bitcast.171), kind=kOutput, calls=%fused_computation.75 | convolution fusion | flops 268959744 | bytes 3936256 | tf_op jit(solution)/shard_map/dot_general | solution.py:16
  193.4 1.3 collective-permute-start.17
  194.7 1.3 collective-permute-start.18
  196.0 1.3 collective-permute-start.20
  198.1 8.2 %collective-permute-done.18 = f16[144,1024]{1,0:T(8,128)(2,1)S(1)} collective-permute-done((f16[144,1024]{1,0:T(8,128)(2,1)S(1)}, f16[144,1024]{1,0:T(8,128)(2,1)S(1)}, u32[]{:S(2)}, u32[]{:S(2)}) %collective-permute-start.18) | collective-permute-done | bytes 294944 | tf_op jit(solution)/shard_map/ppermute | solution.py:157
  207.8 1.2 slice.84
  214.0 1.4 fusion.156
  (82 shorter events, 19.5 us)
Async XLA Ops:
  0.0 49.0 %collective-permute-start = (bf16[4,256,1024]{2,1,0:T(8,128)(2,1)}, bf16[4,256,1024]{2,1,0:T(8,128)(2,1)}, u32[]{:S(2)}, u32[]{:S(2)}) collective-permute-start(bf16[4,256,1024]{2,1,0:T(8,128)(2,1)} %param.4), channel_id=1, source_target_pairs={{0,4},{4,0},{8,12},{12,8},{1,5},{5,1},{9,13},{13,9},{2,6},{6,2},{1... | collective-permute-start | bytes 6291464 | tf_op jit(solution)/shard_map/ppermute | solution.py:148
  3.0 54.6 %collective-permute-start.3 = (bf16[4,256,1024]{2,1,0:T(8,128)(2,1)}, bf16[4,256,1024]{2,1,0:T(8,128)(2,1)S(1)}, u32[]{:S(2)}, u32[]{:S(2)}) collective-permute-start(bf16[4,256,1024]{2,1,0:T(8,128)(2,1)} %param.4), channel_id=1, source_target_pairs={{4,8},{8,4},{5,9},{9,5},{6,10},{10,6},{7,11},{11,7},{20,24},{24,20... | collective-permute-start | bytes 6291464 | tf_op jit(solution)/shard_map/ppermute | solution.py:154
  4.7 5.7 %copy-start = (bf16[4,1024,1024]{2,1,0:T(8,128)(2,1)S(1)}, bf16[4,1024,1024]{2,1,0:T(8,128)(2,1)}, u32[]{:S(2)}) copy-start(bf16[4,1024,1024]{2,1,0:T(8,128)(2,1)} %param.3) | copy-start | bytes 25165828
  57.6 17.2 %collective-permute-start.1 = (f32[256,1024]{1,0:T(8,128)}, f32[256,1024]{1,0:T(8,128)}, u32[]{:S(2)}, u32[]{:S(2)}) collective-permute-start(f32[256,1024]{1,0:T(8,128)} %get-tuple-element.30), channel_id=1, source_target_pairs={{0,1},{1,0},{2,3},{3,2},{4,5},{5,4},{6,7},{7,6},{8,9},{9,8},{10,11... | collective-permute-start | bytes 3145736 | tf_op jit(solution)/shard_map/ppermute | solution.py:91
  57.7 1.8 copy-start.1
  59.5 39.0 %collective-permute-start.4 = (bf16[3,256,1024]{2,1,0:T(8,128)(2,1)}, bf16[3,256,1024]{2,1,0:T(8,128)(2,1)}, u32[]{:S(2)}, u32[]{:S(2)}) collective-permute-start(bf16[3,256,1024]{2,1,0:T(8,128)(2,1)} %slice.72), channel_id=1, source_target_pairs={{4,0},{8,12},{5,1},{9,13},{6,2},{10,14},{7,3},{11,15},{20,16},{24,... | collective-permute-start | bytes 4718600 | tf_op jit(solution)/shard_map/ppermute | solution.py:157
  61.0 39.1 %slice-start = ((s8[8388608]{0:T(1024)(128)(4,1)}), s8[4194304]{0:T(1024)(128)(4,1)S(1)}, s32[]{:S(2)}) async-start(s8[8388608]{0:T(1024)(128)(4,1)} %bitcast.165), calls=%async_computation | async-start | bytes 8388608
  62.7 12.2 %copy-start.4 = (f32[256,1024]{1,0:T(8,128)S(1)}, f32[256,1024]{1,0:T(8,128)}, u32[]{:S(2)}) copy-start(f32[256,1024]{1,0:T(8,128)} %get-tuple-element.31) | copy-start | bytes 3145732
  62.7 15.2 %collective-permute-start.7 = (bf16[3,128,1024]{2,1,0:T(8,128)(2,1)S(1)}, bf16[3,128,1024]{2,1,0:T(8,128)(2,1)}, u32[]{:S(2)}, u32[]{:S(2)}) collective-permute-start(bf16[3,128,1024]{2,1,0:T(8,128)(2,1)S(1)} %get-tuple-element.21), channel_id=1, source_target_pairs={{4,8},{8,4},{5,9},{9,5},{6,10},{10,6},{7,11},{11,7},{20,24},{24,20... | collective-permute-start | bytes 2359304 | tf_op jit(solution)/shard_map/ppermute | solution.py:154
  64.6 54.6 %collective-permute-start.11 = (bf16[1040,1024]{1,0:T(8,128)(2,1)S(1)}, bf16[1040,1024]{1,0:T(8,128)(2,1)S(1)}, u32[]{:S(2)}, u32[]{:S(2)}) collective-permute-start(bf16[1040,1024]{1,0:T(8,128)(2,1)S(1)} %pad_maximum_fusion), channel_id=1, source_target_pairs={{0,4},{12,8},{1,5},{13,9},{2,6},{14,10},{3,7},{15,11},{16,20},{28,... | collective-permute-start | bytes 6389768 | tf_op jit(solution)/shard_map/ppermute | solution.py:151
  73.6 24.9 %copy-start.2 = (bf16[4,256,1024]{2,1,0:T(8,128)(2,1)S(1)}, bf16[4,256,1024]{2,1,0:T(8,128)(2,1)}, u32[]{:S(2)}) copy-start(bf16[4,256,1024]{2,1,0:T(8,128)(2,1)} %copy-done.1) | copy-start | bytes 6291460
  74.9 25.2 %slice-start.1 = ((s8[8388608]{0:T(1024)(128)(4,1)}), s8[4194304]{0:T(1024)(128)(4,1)S(1)}, s32[]{:S(2)}) async-start(s8[8388608]{0:T(1024)(128)(4,1)} %bitcast.165), calls=%async_computation.1 | async-start | bytes 8388608
  76.6 46.2 %collective-permute-start.2 = (f32[256,1024]{1,0:T(8,128)S(1)}, f32[256,1024]{1,0:T(8,128)S(1)}, u32[]{:S(2)}, u32[]{:S(2)}) collective-permute-start(f32[256,1024]{1,0:T(8,128)S(1)} %select_add_fusion.1), channel_id=1, source_target_pairs={{2,0},{3,1},{7,5},{6,4},{8,10},{9,11},{13,15},{12,14},{18,16},{19,... | collective-permute-start | bytes 3145736 | tf_op jit(solution)/shard_map/ppermute | solution.py:79
  77.9 24.6 %collective-permute-start.8 = (bf16[3,128,1024]{2,1,0:T(8,128)(2,1)S(1)}, bf16[3,128,1024]{2,1,0:T(8,128)(2,1)S(1)}, u32[]{:S(2)}, u32[]{:S(2)}) collective-permute-start(bf16[3,128,1024]{2,1,0:T(8,128)(2,1)S(1)} %get-tuple-element.13), channel_id=1, source_target_pairs={{4,8},{8,4},{5,9},{9,5},{6,10},{10,6},{7,11},{11,7},{20,24},{24,20... | collective-permute-start | bytes 2359304 | tf_op jit(solution)/shard_map/ppermute | solution.py:154
  102.4 1.5 copy-start.6
  102.5 17.5 %collective-permute-start.9 = (bf16[256,1024]{1,0:T(8,128)(2,1)S(1)}, bf16[256,1024]{1,0:T(8,128)(2,1)S(1)}, u32[]{:S(2)}, u32[]{:S(2)}) collective-permute-start(bf16[256,1024]{1,0:T(8,128)(2,1)S(1)} %slice_bitcast_fusion.14), channel_id=1, source_target_pairs={{4,8},{8,4},{5,9},{9,5},{6,10},{10,6},{7,11},{11,7},{20,24},{24,20... | collective-permute-start | bytes 1572872 | tf_op jit(solution)/shard_map/ppermute | solution.py:154
  104.0 19.0 %collective-permute-start.5 = (f32[256,1024]{1,0:T(8,128)S(1)}, f32[256,1024]{1,0:T(8,128)S(1)}, u32[]{:S(2)}, u32[]{:S(2)}) collective-permute-start(f32[256,1024]{1,0:T(8,128)S(1)} %fusion.85), channel_id=1, source_target_pairs={{1,0},{3,2},{5,4},{7,6},{8,9},{10,11},{12,13},{14,15},{17,16},{19,... | collective-permute-start | bytes 3145736 | tf_op jit(solution)/shard_map/ppermute | solution.py:63
  120.0 0.8 copy-start.8
  120.8 6.7 %collective-permute-start.12 = (f32[256,1024]{1,0:T(8,128)S(1)}, f32[256,1024]{1,0:T(8,128)S(1)}, u32[]{:S(2)}, u32[]{:S(2)}) collective-permute-start(f32[256,1024]{1,0:T(8,128)S(1)} %get-tuple-element.32), channel_id=1, source_target_pairs={{4,5},{5,4},{6,7},{7,6},{8,9},{9,8},{10,11},{11,10},{20,21},{21,20... | collective-permute-start | bytes 3145736 | tf_op jit(solution)/shard_map/ppermute | solution.py:91
  121.5 26.1 %collective-permute-start.10 = (bf16[3,128,1024]{2,1,0:T(8,128)(2,1)}, bf16[3,128,1024]{2,1,0:T(8,128)(2,1)}, u32[]{:S(2)}, u32[]{:S(2)}) collective-permute-start(bf16[3,128,1024]{2,1,0:T(8,128)(2,1)} %collective-permute-done.7), channel_id=1, source_target_pairs={{4,0},{8,12},{5,1},{9,13},{6,2},{10,14},{7,3},{11,15},{20,16},{24,... | collective-permute-start | bytes 2359304 | tf_op jit(solution)/shard_map/ppermute | solution.py:157
  123.1 40.2 %collective-permute-start.6 = (f32[256,1024]{1,0:T(8,128)S(1)}, f32[256,1024]{1,0:T(8,128)}, u32[]{:S(2)}, u32[]{:S(2)}) collective-permute-start(f32[256,1024]{1,0:T(8,128)S(1)} %add.101), channel_id=1, source_target_pairs={{0,2},{4,6},{11,9},{15,13},{16,18},{20,22},{27,25},{31,29}} | collective-permute-start | bytes 3145736 | tf_op jit(solution)/shard_map/ppermute | solution.py:79
  130.3 37.5 %collective-permute-start.16 = (f16[272,1024]{1,0:T(8,128)(2,1)}, f16[272,1024]{1,0:T(8,128)(2,1)}, u32[]{:S(2)}, u32[]{:S(2)}) collective-permute-start(f16[272,1024]{1,0:T(8,128)(2,1)} %concatenate.19), channel_id=1, source_target_pairs={{4,6},{5,7},{11,9},{10,8},{20,22},{21,23},{27,25},{26,24}} | collective-permute-start | bytes 1671176 | tf_op jit(solution)/shard_map/ppermute | solution.py:79
  148.8 2.5 %copy-start.9 = (bf16[256,1024]{1,0:T(8,128)(2,1)S(1)}, bf16[256,1024]{1,0:T(8,128)(2,1)}, u32[]{:S(2)}) copy-start(bf16[256,1024]{1,0:T(8,128)(2,1)} %copy-done.8) | copy-start | bytes 1572868
  159.4 6.3 %collective-permute-start.13 = (f32[128,1024]{1,0:T(8,128)}, f32[128,1024]{1,0:T(8,128)}, u32[]{:S(2)}, u32[]{:S(2)}) collective-permute-start(f32[128,1024]{1,0:T(8,128)} %fusion.117), channel_id=1, source_target_pairs={{0,1},{2,3},{4,5},{6,7},{9,8},{11,10},{13,12},{15,14},{16,17},{18,... | collective-permute-start | bytes 1572872 | tf_op jit(solution)/shard_map/ppermute | solution.py:63
  162.0 20.3 %collective-permute-start.15 = (bf16[3,128,1024]{2,1,0:T(8,128)(2,1)}, bf16[3,128,1024]{2,1,0:T(8,128)(2,1)}, u32[]{:S(2)}, u32[]{:S(2)}) collective-permute-start(bf16[3,128,1024]{2,1,0:T(8,128)(2,1)} %copy-done.6), channel_id=1, source_target_pairs={{4,0},{8,12},{5,1},{9,13},{6,2},{10,14},{7,3},{11,15},{20,16},{24,... | collective-permute-start | bytes 2359304 | tf_op jit(solution)/shard_map/ppermute | solution.py:157
  170.9 1.6 copy-start.12
  170.9 11.4 %copy-start.7 = (bf16[3,128,1024]{2,1,0:T(8,128)(2,1)S(1)}, bf16[3,128,1024]{2,1,0:T(8,128)(2,1)}, u32[]{:S(2)}) copy-start(bf16[3,128,1024]{2,1,0:T(8,128)(2,1)} %copy-done.6) | copy-start | bytes 2359300
  186.0 2.5 %copy-start.10 = (bf16[256,1024]{1,0:T(8,128)(2,1)S(1)}, bf16[256,1024]{1,0:T(8,128)(2,1)}, u32[]{:S(2)}) copy-start(bf16[256,1024]{1,0:T(8,128)(2,1)} %copy-done.8) | copy-start | bytes 1572868
  190.9 6.4 %copy-start.5 = (f32[128,1024]{1,0:T(8,128)S(1)}, f32[128,1024]{1,0:T(8,128)}, u32[]{:S(2)}) copy-start(f32[128,1024]{1,0:T(8,128)} %add.107) | copy-start | bytes 1572868
  193.4 4.6 %collective-permute-start.17 = (f32[128,1024]{1,0:T(8,128)S(1)}, f32[128,1024]{1,0:T(8,128)S(1)}, u32[]{:S(2)}, u32[]{:S(2)}) collective-permute-start(f32[128,1024]{1,0:T(8,128)S(1)} %fusion.129), channel_id=1, source_target_pairs={{0,1},{2,3},{4,5},{6,7},{9,8},{11,10},{13,12},{15,14},{16,17},{18,... | collective-permute-start | bytes 1572872 | tf_op jit(solution)/shard_map/ppermute | solution.py:63
  194.7 11.6 %collective-permute-start.18 = (f16[144,1024]{1,0:T(8,128)(2,1)S(1)}, f16[144,1024]{1,0:T(8,128)(2,1)S(1)}, u32[]{:S(2)}, u32[]{:S(2)}) collective-permute-start(f16[144,1024]{1,0:T(8,128)(2,1)S(1)} %slice_select_fusion), channel_id=1, source_target_pairs={{4,0},{8,12},{5,1},{9,13},{6,2},{10,14},{7,3},{11,15},{20,16},{24,... | collective-permute-start | bytes 884744 | tf_op jit(solution)/shard_map/ppermute | solution.py:157
  196.0 13.7 %collective-permute-start.20 = (f16[144,1024]{1,0:T(8,128)(2,1)S(1)}, f16[144,1024]{1,0:T(8,128)(2,1)}, u32[]{:S(2)}, u32[]{:S(2)}) collective-permute-start(f16[144,1024]{1,0:T(8,128)(2,1)S(1)} %concatenate.21), channel_id=1, source_target_pairs={{4,0},{8,12},{5,1},{9,13},{6,2},{10,14},{7,3},{11,15},{20,16},{24,... | collective-permute-start | bytes 884744 | tf_op jit(solution)/shard_map/ppermute | solution.py:157
  197.3 16.4 %collective-permute-start.14 = (f32[128,1024]{1,0:T(8,128)S(1)}, f32[128,1024]{1,0:T(8,128)S(1)}, u32[]{:S(2)}, u32[]{:S(2)}) collective-permute-start(f32[128,1024]{1,0:T(8,128)S(1)} %copy-done.5), channel_id=1, source_target_pairs={{1,3},{5,7},{10,8},{14,12},{17,19},{21,23},{26,24},{30,28}} | collective-permute-start | bytes 1572872 | tf_op jit(solution)/shard_map/ppermute | solution.py:79
  206.4 0.7 copy-start.11
  207.1 6.7 %collective-permute-start.19 = (f32[128,1024]{1,0:T(8,128)S(1)}, f32[128,1024]{1,0:T(8,128)S(1)}, u32[]{:S(2)}, u32[]{:S(2)}) collective-permute-start(f32[128,1024]{1,0:T(8,128)S(1)} %add.113), channel_id=1, source_target_pairs={{1,3},{5,7},{10,8},{14,12},{17,19},{21,23},{26,24},{30,28}} | collective-permute-start | bytes 1572872 | tf_op jit(solution)/shard_map/ppermute | solution.py:79
  212.7 1.3 copy-start.3

commit v7 on v6

--- a/solution.py
+++ b/solution.py
@@ -1,9 +1,14 @@
+import functools
+
 import jax
 import jax.numpy as jnp
 from jax import lax
+from jax.experimental import pallas as pl
+from jax.experimental.pallas import tpu as pltpu
 from jax.sharding import PartitionSpec as P
 
 PLACE = ("ex", "ckpt", "dim")
+VMEM = 48 * 1024 * 1024
 
 
 def after(value, *others):
@@ -78,18 +83,19 @@
                     pairs.append((self.index(z, (x + away) % self.ckpts, c), self.index(z, x, c)))
         return lax.ppermute(total, PLACE, pairs)
 
-    def two_near_sums(self, one, one_blocks, two, two_blocks):
-        keeps_one = jnp.bool_(False)
-        swaps = []
-        for z, blocks in enumerate(zip(one_blocks, two_blocks)):
-            if blocks[0] is None:
-                continue
-            second = self.of(blocks[1])[1]
-            assert self.of(blocks[0])[1] == 1 - second
-            keeps_one = keeps_one | ((self.z == z) & (self.c == 1 - second))
-            swaps += [(self.index(z, x, c), self.index(z, x, 1 - c)) for x in range(2) for c in range(2)]
-        got = lax.ppermute(jnp.where(keeps_one, two, one), PLACE, swaps)
-        return jnp.where(keeps_one, one, two) + got
+    def keeps_first(self, blocks):
+        found = jnp.bool_(False)
+        for z, block in enumerate(blocks):
+            if block is not None:
+                found = found | ((self.z == z) & (self.c == self.of(block)[1]))
+        return found
+
+    def swapped(self, value, planes):
+        pairs = []
+        for z in planes:
+            for x in range(self.ckpts):
+                pairs += [(self.index(z, x, c), self.index(z, x, 1 - c)) for c in range(2)]
+        return lax.ppermute(value, PLACE, pairs)
 
 
 def ring(train_features, query_features, residual_weights, keepers, scale):
@@ -136,12 +142,91 @@
     return small[:-16].astype(jnp.float32) * jnp.exp2(power - 13.0)
 
 
+def product(queries, examples):
+    return lax.dot_general(
+        queries,
+        examples,
+        (((1,), (1,)), ((), ())),
+        preferred_element_type=jnp.float32,
+    )
+
+
+def pair_kernel(scale, flag_ref, one_ref, two_ref, train_ref, weight_ref, sent_ref, kept_ref):
+    keeps_one = flag_ref[0] == 1
+    sent = kept = None
+    for check in range(train_ref.shape[0]):
+        one, two = one_ref[check], two_ref[check]
+        weight = jnp.sum(weight_ref[check].astype(jnp.float32), axis=0, keepdims=True)
+        both = []
+        for first, second in ((two, one), (one, two)):
+            term = product(jnp.where(keeps_one, first, second), train_ref[check]) * weight
+            both.append(term)
+        sent = both[0] if sent is None else sent + both[0]
+        kept = both[1] if kept is None else kept + both[1]
+    sent_ref[...] = sent * scale
+    kept_ref[...] = kept * scale
+
+
+def pair_scores(keeps_one, one, two, train, weights, scale, examples):
+    checks, rows, depth = one.shape
+    tile = 256
+    return pl.pallas_call(
+        functools.partial(pair_kernel, scale),
+        grid_spec=pltpu.PrefetchScalarGridSpec(
+            num_scalar_prefetch=1,
+            grid=(examples // tile,),
+            in_specs=[
+                pl.BlockSpec((checks, rows, depth), lambda i, flag: (0, 0, 0)),
+                pl.BlockSpec((checks, rows, depth), lambda i, flag: (0, 0, 0)),
+                pl.BlockSpec((checks, tile, depth), lambda i, flag: (0, i, 0)),
+                pl.BlockSpec((checks, weights.shape[1], tile), lambda i, flag: (0, 0, i)),
+            ],
+            out_specs=[pl.BlockSpec((rows, tile), lambda i, flag: (0, i))] * 2,
+        ),
+        out_shape=[jax.ShapeDtypeStruct((rows, examples), jnp.float32)] * 2,
+        compiler_params=pltpu.CompilerParams(vmem_limit_bytes=VMEM),
+        cost_estimate=pl.CostEstimate(flops=0, bytes_accessed=0, transcendentals=0),
+    )(keeps_one.astype(jnp.int32).reshape(1), one, two, train, weights)
+
+
+def block_kernel(scale, flag_ref, far_ref, near_ref, first_ref, train_ref, weight_ref, out_ref):
+    is_end = flag_ref[0] == 1
+    total = product(first_ref[...], train_ref[0]) * weight_ref[0]
+    for check in range(1, train_ref.shape[0]):
+        queries = jnp.where(is_end, far_ref[check - 1], near_ref[check - 1])
+        total = total + product(queries, train_ref[check]) * weight_ref[check]
+    out_ref[...] = total * scale
+
+
+def block_scores(is_end, far, near, first, train, weights, scale):
+    checks, rows, depth = far.shape
+    examples, tile = train.shape[1], 256
+    whole = pl.BlockSpec((checks, rows, depth), lambda i, flag: (0, 0, 0))
+    return pl.pallas_call(
+        functools.partial(block_kernel, scale),
+        grid_spec=pltpu.PrefetchScalarGridSpec(
+            num_scalar_prefetch=1,
+            grid=(examples // tile,),
+            in_specs=[
+                whole,
+                whole,
+                pl.BlockSpec((rows, depth), lambda i, flag: (0, 0)),
+                pl.BlockSpec((checks + 1, tile, depth), lambda i, flag: (0, i, 0)),
+                pl.BlockSpec((checks + 1, 1, tile), lambda i, flag: (0, 0, i)),
+            ],
+            out_specs=pl.BlockSpec((rows, tile), lambda i, flag: (0, i)),
+        ),
+        out_shape=jax.ShapeDtypeStruct((rows, examples), jnp.float32),
+        compiler_params=pltpu.CompilerParams(vmem_limit_bytes=VMEM),
+        cost_estimate=pl.CostEstimate(flops=0, bytes_accessed=0, transcendentals=0),
+    )(is_end.astype(jnp.int32).reshape(1), far, near, first, train, weights)
+
+
 def line(train_features, query_features, residual_weights, keepers, scale):
     z = keepers.z
     rows, depth = query_features.shape[1:]
     examples = train_features.shape[1]
-    low = rows // 2
-    assert train_features.shape[0] == 4 and examples <= depth
+    assert train_features.shape[0] == 4 and examples <= depth and examples % 256 == 0
     ends = (z == 0) | (z == 3)
 
     def aside(value):
@@ -155,12 +240,6 @@
 
     def outward(value):
         return lax.ppermute(value, "ex", [(1, 0), (2, 3)])
-
-    def scores(checks, first=0):
-        return weighted(checks, train_features[first:], residual_weights[first:], scale)
-
-    def chosen(far, near):
-        return after(jnp.where(ends, far, near))
 
     left, pieces = residual_weights[0], []
     for unused in range(3):
@@ -169,57 +248,48 @@
         left = left - rounded
     tail = jnp.pad(jnp.stack(pieces), ((0, 13), (0, depth - examples)))
     training = jnp.concatenate([train_features[0], tail], axis=0)
+    weights = residual_weights[:, None]
 
     side = aside(query_features)
     middle = between(query_features)
-    own = scores(list(query_features))
     in_train = inward(after(training, side))
     out_next = outward(middle[1:])
-    parts = [slice(0, low), slice(low, rows)]
+    mid_edge = between(side[1:])
+    out_edge = [outward(mid_edge[:1])]
+    out_edge.append(outward(after(mid_edge[1:], out_edge[0])))
     blocks_own = [0, 1, 2, 3]
     blocks_1 = [1, 0, 3, 2]
     blocks_2 = [2, 2, 1, 1]
     blocks_3 = [3, 3, 0, 0]
 
-    total_1 = keepers.two_near_sums(own, blocks_own, scores(list(side)), blocks_1)
+    sent, kept = pair_scores(
+        keepers.keeps_first(blocks_own), query_features, side, train_features, weights, scale, examples)
+    total_1 = kept + keepers.swapped(sent, range(4))
     result_1 = keepers.far_sums(total_1, blocks_own, blocks_1)
-
-    mid_edge = [between(side[1:, parts[0]])]
-    mid_edge.append(between(after(side[1:, parts[1]], mid_edge[0], total_1)))
-    out_edge = [outward(part) for part in mid_edge]
-    far_one = between(after(side[0], mid_edge[1]))
-
-    checks = chosen(out_next, middle[1:])
-    total_2 = keepers.near_sums(scores([middle[0]] + list(checks)), blocks_2)
+    far_one = between(after(side[0], mid_edge, total_1))
+
+    found = block_scores(ends, out_next, middle[1:], middle[0], train_features, weights, scale)
+    total_2 = keepers.near_sums(found, blocks_2)
     result_2 = keepers.far_sums(total_2, blocks_2)
-
-    weights = jnp.sum(in_train[examples:examples + 3, :examples].astype(jnp.float32), axis=0)
-
-    def beside(queries):
-        return weighted([queries], [in_train[:examples]], [weights], scale)
 
     beside_2 = [None, 2, 1, None]
     beside_3 = [None, 3, 0, None]
-    total = keepers.two_near_sums(beside(middle[0]), beside_2, beside(far_one), beside_3)
-    crossing = packed(after(total, result_1, total_2))
+    in_train = after(in_train, total_2)
+    sent, kept = pair_scores(
+        keepers.keeps_first(beside_2), middle[:1], far_one[None], in_train[None],
+        in_train[None, examples:examples + 3, :examples], scale, examples)
+    total = kept + keepers.swapped(sent, (1, 2))
+    crossing = after(packed(after(total, result_1, out_edge[0])))
     returned = total + unpacked(keepers.far_moves(crossing, beside_2, beside_3))
     returned = jnp.where(keepers.mine(beside_2) | keepers.mine(beside_3), returned, 0.0)
-
-    def last(k, *before):
-        checks = chosen(after(out_edge[k], *before), mid_edge[k])
-        found = scores([far_one[parts[k]]] + list(checks))
-        return keepers.near_sums(found, blocks_3)
-
-    total_3 = [last(0, crossing)]
-    results = [keepers.far_sums(total_3[0], blocks_3)]
-    returned = packed(after(returned, result_2, total_3[0]))
-    halves = [after(jnp.concatenate([returned[part], returned[rows:]], axis=0)) for part in parts]
-    total_3.append(last(1, *halves))
-    halves = [outward(half) for half in halves]
-    results.append(keepers.far_sums(after(total_3[1], halves[0]), blocks_3))
-    returned = jnp.concatenate([unpacked(part) for part in halves], axis=0)
-
-    result = jnp.where(keepers.mine(blocks_2), result_2, jnp.concatenate(results, axis=0))
+    returned = after(packed(after(returned, result_2)))
+    out_edge = after(jnp.concatenate(out_edge, axis=0), crossing)
+    returned = unpacked(outward(returned))
+
+    found = block_scores(ends, out_edge, mid_edge, far_one, train_features, weights, scale)
+    result_3 = keepers.far_sums(keepers.near_sums(found, blocks_3), blocks_3)
+
+    result = jnp.where(keepers.mine(blocks_2), result_2, result_3)
     result = jnp.where(keepers.mine(blocks_own) | keepers.mine(blocks_1), result_1, result)
     return result + returned
 

time: 218 us -> 203 us (0.931)
  matrix products: 43 us -> 0 us
  Pallas kernels: 0 us -> 25.9 us
  local copies, waits for them, and re-layouts: 10.4 us -> 18.6 us
  starting transfers between devices: 37 us -> 33.3 us
  waiting for transfers between devices: 102 us -> 99.5 us
    dot_general x22 -> x0, matrix products: 43 us -> none  [weighted(): lax.dot_general(piece, examples, (((1,), (1,)), ((), ())), preferred_elem...]
    pallas_call x0 -> x4, Pallas kernels: none -> 25.9 us  [the longest x2 13.4 us: block_scores(): pl.pallas_call(functools.partial(block_kernel, scale), grid_spec=pltpu.Pr...]
    ppermute x1, waiting for transfers between devices: 13.7 us -> 0.01 us  [inward(): return lax.ppermute(value, 'ex', [(0, 1), (3, 2)])]
    ppermute x5 -> x4, waiting for transfers between devices: 0.01 us -> 6.83 us  [far_moves(): return lax.ppermute(total, PLACE, pairs)]
    unnamed x30 -> x24, local copies, waits for them, and re-layouts: 1.35 us -> 6.05 us
    ppermute x1, waiting for transfers between devices: 34.8 us -> 39.4 us  [aside(): return lax.ppermute(value, 'ex', [(0, 1), (1, 0), (2, 3), (3, 2)])]
    select_n x3 -> x0, other arithmetic: 4.05 us -> none  [chosen(): return after(jnp.where(ends, far, near))]
    squeeze x0 -> x2, local copies, waits for them, and re-layouts: none -> 3.63 us  [the longest x1 1.87 us: line(): far_one = between(after(side[0], mid_edge, total_1))]
  transfers between devices with their start and end apart: 21 -> 17, of which waited for: 6 -> 6; matrix products, arithmetic and copies ran while one was open for 27% -> 14% of each run, Pallas kernels for 0% -> 13%
where the time goes in v7:
time: 203 us; the launch traced here: 201 us
  waiting for transfers between devices  99.5 us (49%)
  starting transfers between devices  33.3 us (16%)
  Pallas kernels  25.9 us (13%)
  other arithmetic  20 us (10%)
  local copies, waits for them, and re-layouts  18.6 us (9%)
  between operations  3.32 us (2%)
    ppermute x4, waiting for transfers between devices, outward(): return lax.ppermute(value, 'ex', [(1, 0), (2, 3)])  53.3 us
    ppermute x1, waiting for transfers between devices, aside(): return lax.ppermute(value, 'ex', [(0, 1), (1, 0), (2, 3), (3, 2)])  39.4 us
    pallas_call x2, Pallas kernels, block_scores(): pl.pallas_call(functools.partial(block_kernel, scale), grid_spec=pltpu.Pr...  13.4 us
    pallas_call x2, Pallas kernels, pair_scores(): pl.pallas_call(functools.partial(pair_kernel, scale), grid_spec=pltpu.Pre...  12.5 us
    ppermute x1, starting transfers between devices, inward(): return lax.ppermute(value, 'ex', [(0, 1), (3, 2)])  9.16 us
    ppermute x4, waiting for transfers between devices, far_moves(): return lax.ppermute(total, PLACE, pairs)  6.83 us
    ppermute x4, starting transfers between devices, far_moves(): return lax.ppermute(total, PLACE, pairs)  6.77 us
    unnamed x24, local copies, waits for them, and re-layouts  6.05 us
  transfers between devices with their start and end apart: 17, of which 6 were waited for; matrix products, arithmetic and copies ran while one was open for 14% of the time, Pallas kernels for 13%

profile of v7, /device:TPU:0, one launch (start us, length us, event | category | flops | bytes accessed | tf_op | source)
XLA Modules:
  0.0 200.7 jit_solution(11939733171230905637)
XLA Ops:
  0.0 0.8 collective-permute-start.3
  0.8 5.8 %collective-permute-start = (bf16[4,256,1024]{2,1,0:T(8,128)(2,1)}, bf16[4,256,1024]{2,1,0:T(8,128)(2,1)S(1)}, u32[]{:S(2)}, u32[]{:S(2)}) collective-permute-start(bf16[4,256,1024]{2,1,0:T(8,128)(2,1)} %one_ref.1), channel_id=1, source_target_pairs={{0,4},{4,0},{8,12},{12,8},{1,5},{5,1},{9,13},{13,9},{2,6},{6,2},{1... | collective-permute-start | bytes 6291464 | tf_op jit(solution)/shard_map/ppermute | solution.py:233
  6.6 1.8 slice_bitcast_fusion
  8.4 1.4 copy-done.10
  9.9 1.3 collective-permute-start.4
  11.2 1.5 pad_maximum_fusion
  12.7 39.4 %collective-permute-done.two_ref = bf16[4,256,1024]{2,1,0:T(8,128)(2,1)S(1)} collective-permute-done((bf16[4,256,1024]{2,1,0:T(8,128)(2,1)}, bf16[4,256,1024]{2,1,0:T(8,128)(2,1)S(1)}, u32[]{:S(2)}, u32[]{:S(2)}) %collective-permute-start) | collective-permute-done | bytes 2097184 | tf_op jit(solution)/shard_map/ppermute | solution.py:233
  52.1 9.2 %collective-permute-start.11 = (bf16[1040,1024]{1,0:T(8,128)(2,1)}, bf16[1040,1024]{1,0:T(8,128)(2,1)}, u32[]{:S(2)}, u32[]{:S(2)}) collective-permute-start(bf16[1040,1024]{1,0:T(8,128)(2,1)} %pad_maximum_fusion), channel_id=1, source_target_pairs={{0,4},{12,8},{1,5},{13,9},{2,6},{14,10},{3,7},{15,11},{16,20},{28,... | collective-permute-start | bytes 6389768 | tf_op jit(solution)/shard_map/ppermute | solution.py:236
  61.3 1.3 slice.56
  62.6 0.7 collective-permute-start.7
  63.4 1.6 copy-done
  65.0 8.6 %shard_map.37 = (f32[256,1024]{1,0:T(8,128)}, f32[256,1024]{1,0:T(8,128)S(1)}) custom-call(s32[1]{0:T(128)} %bitcast.flag_ref, bf16[4,256,1024]{2,1,0:T(8,128)(2,1)S(1)} %copy-done, bf16[4,256,1024]{2,1,0:T(8,128)(2,1)} %copy-done.8, bf16[4,1024,1024]{2,1,0:T(8,128)(2,1)} %train_ref.5, f32[4,1,1024]{2,1,0:T(1,128)S(1)} %broadcast_in_dim.18.weight_ref), custom_call_target="tpu_custom_call" | custom-call | tf_op jit(solution)/shard_map/pallas_call | solution.py:173
  73.6 1.0 copy-done.4
  74.6 2.0 fusion.7
  76.6 12.3 %collective-permute-done.4.far_ref = bf16[3,256,1024]{2,1,0:T(8,128)(2,1)} collective-permute-done((bf16[3,256,1024]{2,1,0:T(8,128)(2,1)S(1)}, bf16[3,256,1024]{2,1,0:T(8,128)(2,1)}, u32[]{:S(2)}, u32[]{:S(2)}) %collective-permute-start.4) | collective-permute-done | bytes 1572896 | tf_op jit(solution)/shard_map/ppermute | solution.py:242
  88.9 6.9 %shard_map.38 = f32[256,1024]{1,0:T(8,128)} custom-call(s32[1]{0:T(128)} %bitcast.1.flag_ref, bf16[3,256,1024]{2,1,0:T(8,128)(2,1)} %collective-permute-done.4.far_ref, bf16[3,256,1024]{2,1,0:T(8,128)(2,1)S(1)} %slice.54.near_ref, bf16[256,1024]{1,0:T(8,128)(2,1)S(1)} %get-tuple-element.28.first_ref, bf16[4,1024,1024]{2,1,0:T(8,128)(2,1)} %train_ref.5, ...), custom_call_target="tpu_custom_call" | custom-call | tf_op jit(solution)/shard_map/pallas_call | solution.py:205
  95.8 1.4 collective-permute-start.5
  97.3 0.8 slice.57
  98.1 1.3 collective-permute-start.8
  99.4 1.9 slice_bitcast_fusion.1
  101.3 1.4 add.37
  103.3 1.3 collective-permute-start.2
  104.7 9.1 %collective-permute-done.8 = bf16[1,256,1024]{2,1,0:T(8,128)(2,1)} collective-permute-done((bf16[1,256,1024]{2,1,0:T(8,128)(2,1)}, bf16[1,256,1024]{2,1,0:T(8,128)(2,1)}, u32[]{:S(2)}, u32[]{:S(2)}) %collective-permute-start.8) | collective-permute-done | bytes 524320 | tf_op jit(solution)/shard_map/ppermute | solution.py:242
  113.8 1.3 collective-permute-start.9
  115.1 2.7 %add.39 = f32[256,1024]{1,0:T(8,128)} add(f32[256,1024]{1,0:T(8,128)} %shard_map.38, f32[256,1024]{1,0:T(8,128)} %collective-permute-done.5) | non-fusion elementwise | flops 262144 | bytes 3145728 | tf_op jit(solution)/shard_map/add | solution.py:68
  118.6 3.9 %shard_map.39 = (f32[256,1024]{1,0:T(8,128)S(1)}, f32[256,1024]{1,0:T(8,128)S(1)}) custom-call(s32[1]{0:T(128)} %bitcast.3.flag_ref, bf16[1,256,1024]{2,1,0:T(8,128)(2,1)S(1)} %copy-done.3, bf16[1,256,1024]{2,1,0:T(8,128)(2,1)S(1)} %bitcast.15, bf16[1,1040,1024]{2,1,0:T(8,128)(2,1)} %bitcast.7.train_ref, bf16[1,3,1024]{2,1,0:T(4,128)(2,1)S(1)} %slice_bitcast_fusion.2.weight_ref), custom_call_target="tpu_custom_call" | custom-call | tf_op jit(solution)/shard_map/pallas_call | solution.py:173
  122.5 0.7 collective-permute-start.12
  123.2 6.8 %collective-permute-done.2 = f32[256,1024]{1,0:T(8,128)S(1)} collective-permute-done((f32[256,1024]{1,0:T(8,128)S(1)}, f32[256,1024]{1,0:T(8,128)S(1)}, u32[]{:S(2)}, u32[]{:S(2)}) %collective-permute-start.2) | collective-permute-done | bytes 1048608 | tf_op jit(solution)/shard_map/ppermute | solution.py:84
  130.0 1.1 add.38
  131.1 2.4 %collective-permute-start.6 = (f32[256,1024]{1,0:T(8,128)}, f32[256,1024]{1,0:T(8,128)}, u32[]{:S(2)}, u32[]{:S(2)}) collective-permute-start(f32[256,1024]{1,0:T(8,128)} %add.39), channel_id=1, source_target_pairs={{0,2},{4,6},{11,9},{15,13},{16,18},{20,22},{27,25},{31,29}} | collective-permute-start | bytes 3145736 | tf_op jit(solution)/shard_map/ppermute | solution.py:84
  133.5 7.9 %collective-permute-done.9 = bf16[2,256,1024]{2,1,0:T(8,128)(2,1)S(1)} collective-permute-done((bf16[2,256,1024]{2,1,0:T(8,128)(2,1)S(1)}, bf16[2,256,1024]{2,1,0:T(8,128)(2,1)S(1)}, u32[]{:S(2)}, u32[]{:S(2)}) %collective-permute-start.9) | collective-permute-done | bytes 1048608 | tf_op jit(solution)/shard_map/ppermute | solution.py:242
  141.5 1.2 pad_maximum_fusion.1.far_ref
  142.8 1.0 copy-done.6
  145.3 2.1 %multiply_convert_fusion.1 = f16[256,1024]{1,0:T(8,128)(2,1)} fusion(f32[256,1024]{1,0:T(8,128)} %copy-done.6, f32[]{:T(128)S(6)} %exp2.33), kind=kLoop, calls=%fused_computation.7 | loop fusion | flops 524288 | bytes 1572868 | tf_op jit(solution)/shard_map/convert_element_type | solution.py:136
  147.4 1.9 concatenate.14
  149.3 1.0 copy-done.2
  150.4 6.5 %shard_map.40 = f32[256,1024]{1,0:T(8,128)} custom-call(s32[1]{0:T(128)} %bitcast.1.flag_ref, bf16[3,256,1024]{2,1,0:T(8,128)(2,1)S(1)} %pad_maximum_fusion.1.far_ref, bf16[3,256,1024]{2,1,0:T(8,128)(2,1)S(1)} %collective-permute-done.7.near_ref, bf16[256,1024]{1,0:T(8,128)(2,1)S(1)} %copy-done.2, bf16[4,1024,1024]{2,1,0:T(8,128)(2,1)} %train_ref.5, ...), custom_call_target="tpu_custom_call" | custom-call | tf_op jit(solution)/shard_map/pallas_call | solution.py:205
  156.8 2.1 %collective-permute-start.13 = (f32[256,1024]{1,0:T(8,128)}, f32[256,1024]{1,0:T(8,128)S(1)}, u32[]{:S(2)}, u32[]{:S(2)}) collective-permute-start(f32[256,1024]{1,0:T(8,128)} %shard_map.40), channel_id=1, source_target_pairs={{0,1},{2,3},{4,5},{6,7},{9,8},{11,10},{13,12},{15,14},{16,17},{18,... | collective-permute-start | bytes 3145736 | tf_op jit(solution)/shard_map/ppermute | solution.py:68
  159.0 1.5 collective-permute-start.15
  160.4 1.7 add.40
  162.1 1.3 slice.61
  164.2 2.4 %add.42 = f32[256,1024]{1,0:T(8,128)} add(f32[256,1024]{1,0:T(8,128)} %shard_map.40, f32[256,1024]{1,0:T(8,128)S(1)} %collective-permute-done.13) | non-fusion elementwise | flops 262144 | bytes 3145728 | tf_op jit(solution)/shard_map/add | solution.py:68
  166.5 1.6 collective-permute-start.14
  168.1 1.2 add_select_fusion
  169.4 0.7 abs_reduce_fusion
  171.1 1.3 collective-permute-start.16
  172.5 23.9 %collective-permute-done.16 = f16[272,1024]{1,0:T(8,128)(2,1)S(1)} collective-permute-done((f16[272,1024]{1,0:T(8,128)(2,1)S(1)}, f16[272,1024]{1,0:T(8,128)(2,1)S(1)}, u32[]{:S(2)}, u32[]{:S(2)}) %collective-permute-start.16) | collective-permute-done | bytes 557088 | tf_op jit(solution)/shard_map/ppermute | solution.py:242
  197.7 3.0 %multiply_add_fusion = f32[256,1024]{1,0:T(8,128)} fusion(f32[256,1024]{1,0:T(8,128)S(1)} %copy-done.9, f32[256,1024]{1,0:T(8,128)S(1)} %add.40, f32[256,1024]{1,0:T(8,128)} %add.42, f32[256,1024]{1,0:T(8,128)} %collective-permute-done.14, f16[272,1024]{1,0:T(8,128)(2,1)S(1)} %collective-permute-done.16, f32[]{:T(128)} %bitcast.10, pred[]{:T(512)S(6)} %or.66, ...), kind=kLoop, calls=%fused_computation.3 | loop fusion | flops 1572864 | bytes 5767174 | tf_op jit(solution)/shard_map/add | solution.py:294
  (43 shorter events, 3.4 us)
Async XLA Ops:
  0.0 8.4 %collective-permute-start.3 = (bf16[4,256,1024]{2,1,0:T(8,128)(2,1)}, bf16[4,256,1024]{2,1,0:T(8,128)(2,1)S(1)}, u32[]{:S(2)}, u32[]{:S(2)}) collective-permute-start(bf16[4,256,1024]{2,1,0:T(8,128)(2,1)} %one_ref.1), channel_id=1, source_target_pairs={{4,8},{8,4},{5,9},{9,5},{6,10},{10,6},{7,11},{11,7},{20,24},{24,20... | collective-permute-start | bytes 6291464 | tf_op jit(solution)/shard_map/ppermute | solution.py:239
  0.8 51.3 %collective-permute-start = (bf16[4,256,1024]{2,1,0:T(8,128)(2,1)}, bf16[4,256,1024]{2,1,0:T(8,128)(2,1)S(1)}, u32[]{:S(2)}, u32[]{:S(2)}) collective-permute-start(bf16[4,256,1024]{2,1,0:T(8,128)(2,1)} %one_ref.1), channel_id=1, source_target_pairs={{0,4},{4,0},{8,12},{12,8},{1,5},{5,1},{9,13},{13,9},{2,6},{6,2},{1... | collective-permute-start | bytes 6291464 | tf_op jit(solution)/shard_map/ppermute | solution.py:233
  8.3 2.8 %copy-start.11 = (f32[4,1024]{1,0:T(4,128)S(1)}, f32[4,1024]{1,0:T(4,128)}, u32[]{:S(2)}) copy-start(f32[4,1024]{1,0:T(4,128)} %param.5) | copy-start | bytes 49156
  8.4 1.4 copy-start.10
  9.9 79.0 %collective-permute-start.4 = (bf16[3,256,1024]{2,1,0:T(8,128)(2,1)S(1)}, bf16[3,256,1024]{2,1,0:T(8,128)(2,1)}, u32[]{:S(2)}, u32[]{:S(2)}) collective-permute-start(bf16[3,256,1024]{2,1,0:T(8,128)(2,1)S(1)} %slice.54.near_ref), channel_id=1, source_target_pairs={{4,0},{8,12},{5,1},{9,13},{6,2},{10,14},{7,3},{11,15},{20,16},{24,... | collective-permute-start | bytes 4718600 | tf_op jit(solution)/shard_map/ppermute | solution.py:242
  52.1 9.2 %copy-start.8 = (bf16[4,256,1024]{2,1,0:T(8,128)(2,1)}, bf16[4,256,1024]{2,1,0:T(8,128)(2,1)S(1)}, u32[]{:S(2)}) copy-start(bf16[4,256,1024]{2,1,0:T(8,128)(2,1)S(1)} %collective-permute-done.two_ref) | copy-start | bytes 6291460
  52.1 65.7 %collective-permute-start.11 = (bf16[1040,1024]{1,0:T(8,128)(2,1)}, bf16[1040,1024]{1,0:T(8,128)(2,1)}, u32[]{:S(2)}, u32[]{:S(2)}) collective-permute-start(bf16[1040,1024]{1,0:T(8,128)(2,1)} %pad_maximum_fusion), channel_id=1, source_target_pairs={{0,4},{12,8},{1,5},{13,9},{2,6},{14,10},{3,7},{15,11},{16,20},{28,... | collective-permute-start | bytes 6389768 | tf_op jit(solution)/shard_map/ppermute | solution.py:236
  62.6 34.7 %collective-permute-start.7 = (bf16[3,256,1024]{2,1,0:T(8,128)(2,1)}, bf16[3,256,1024]{2,1,0:T(8,128)(2,1)S(1)}, u32[]{:S(2)}, u32[]{:S(2)}) collective-permute-start(bf16[3,256,1024]{2,1,0:T(8,128)(2,1)} %slice.56), channel_id=1, source_target_pairs={{4,8},{8,4},{5,9},{9,5},{6,10},{10,6},{7,11},{11,7},{20,24},{24,20... | collective-permute-start | bytes 4718600 | tf_op jit(solution)/shard_map/ppermute | solution.py:239
  63.4 1.6 copy-start
  73.6 1.0 copy-start.4
  74.6 26.6 %collective-permute-start.1 = (f32[256,1024]{1,0:T(8,128)}, f32[256,1024]{1,0:T(8,128)}, u32[]{:S(2)}, u32[]{:S(2)}) collective-permute-start(f32[256,1024]{1,0:T(8,128)} %get-tuple-element.17), channel_id=1, source_target_pairs={{0,1},{1,0},{2,3},{3,2},{4,5},{5,4},{6,7},{7,6},{8,9},{9,8},{10,11... | collective-permute-start | bytes 3145736 | tf_op jit(solution)/shard_map/ppermute | solution.py:98
  95.8 5.4 %copy-start.5 = (f32[256,1024]{1,0:T(8,128)S(1)}, f32[256,1024]{1,0:T(8,128)}, u32[]{:S(2)}) copy-start(f32[256,1024]{1,0:T(8,128)} %copy-done.4) | copy-start | bytes 3145732
  95.8 19.3 %collective-permute-start.5 = (f32[256,1024]{1,0:T(8,128)}, f32[256,1024]{1,0:T(8,128)}, u32[]{:S(2)}, u32[]{:S(2)}) collective-permute-start(f32[256,1024]{1,0:T(8,128)} %shard_map.38), channel_id=1, source_target_pairs={{1,0},{3,2},{5,4},{7,6},{8,9},{10,11},{12,13},{14,15},{17,16},{19,... | collective-permute-start | bytes 3145736 | tf_op jit(solution)/shard_map/ppermute | solution.py:68
  98.1 15.7 %collective-permute-start.8 = (bf16[1,256,1024]{2,1,0:T(8,128)(2,1)}, bf16[1,256,1024]{2,1,0:T(8,128)(2,1)}, u32[]{:S(2)}, u32[]{:S(2)}) collective-permute-start(bf16[1,256,1024]{2,1,0:T(8,128)(2,1)} %slice.57), channel_id=1, source_target_pairs={{4,0},{8,12},{5,1},{9,13},{6,2},{10,14},{7,3},{11,15},{20,16},{24,... | collective-permute-start | bytes 1572872 | tf_op jit(solution)/shard_map/ppermute | solution.py:242
  102.6 15.9 %collective-permute-start.10 = (bf16[256,1024]{1,0:T(8,128)(2,1)}, bf16[256,1024]{1,0:T(8,128)(2,1)S(1)}, u32[]{:S(2)}, u32[]{:S(2)}) collective-permute-start(bf16[256,1024]{1,0:T(8,128)(2,1)} %slice_bitcast_fusion.1), channel_id=1, source_target_pairs={{4,8},{8,4},{5,9},{9,5},{6,10},{10,6},{7,11},{11,7},{20,24},{24,20... | collective-permute-start | bytes 1572872 | tf_op jit(solution)/shard_map/ppermute | solution.py:239
  103.3 26.7 %collective-permute-start.2 = (f32[256,1024]{1,0:T(8,128)S(1)}, f32[256,1024]{1,0:T(8,128)S(1)}, u32[]{:S(2)}, u32[]{:S(2)}) collective-permute-start(f32[256,1024]{1,0:T(8,128)S(1)} %add.37), channel_id=1, source_target_pairs={{2,0},{3,1},{7,5},{6,4},{8,10},{9,11},{13,15},{12,14},{18,16},{19,... | collective-permute-start | bytes 3145736 | tf_op jit(solution)/shard_map/ppermute | solution.py:84
  104.7 13.9 %copy-start.3 = (bf16[1,256,1024]{2,1,0:T(8,128)(2,1)S(1)}, bf16[1,256,1024]{2,1,0:T(8,128)(2,1)}, u32[]{:S(2)}) copy-start(bf16[1,256,1024]{2,1,0:T(8,128)(2,1)} %get-tuple-element.27.one_ref) | copy-start | bytes 1572868
  113.8 27.6 %collective-permute-start.9 = (bf16[2,256,1024]{2,1,0:T(8,128)(2,1)S(1)}, bf16[2,256,1024]{2,1,0:T(8,128)(2,1)S(1)}, u32[]{:S(2)}, u32[]{:S(2)}) collective-permute-start(bf16[2,256,1024]{2,1,0:T(8,128)(2,1)S(1)} %slice.58), channel_id=1, source_target_pairs={{4,0},{8,12},{5,1},{9,13},{6,2},{10,14},{7,3},{11,15},{20,16},{24,... | collective-permute-start | bytes 3145736 | tf_op jit(solution)/shard_map/ppermute | solution.py:242
  118.6 12.6 %copy-start.1 = (bf16[256,1024]{1,0:T(8,128)(2,1)}, bf16[256,1024]{1,0:T(8,128)(2,1)S(1)}, u32[]{:S(2)}) copy-start(bf16[256,1024]{1,0:T(8,128)(2,1)S(1)} %collective-permute-done.10.first_ref) | copy-start | bytes 1572868
  122.5 20.2 %collective-permute-start.12 = (f32[256,1024]{1,0:T(8,128)S(1)}, f32[256,1024]{1,0:T(8,128)S(1)}, u32[]{:S(2)}, u32[]{:S(2)}) collective-permute-start(f32[256,1024]{1,0:T(8,128)S(1)} %get-tuple-element.23), channel_id=1, source_target_pairs={{4,5},{5,4},{6,7},{7,6},{8,9},{9,8},{10,11},{11,10},{20,21},{21,20... | collective-permute-start | bytes 3145736 | tf_op jit(solution)/shard_map/ppermute | solution.py:98
  131.1 29.3 %collective-permute-start.6 = (f32[256,1024]{1,0:T(8,128)}, f32[256,1024]{1,0:T(8,128)}, u32[]{:S(2)}, u32[]{:S(2)}) collective-permute-start(f32[256,1024]{1,0:T(8,128)} %add.39), channel_id=1, source_target_pairs={{0,2},{4,6},{11,9},{15,13},{16,18},{20,22},{27,25},{31,29}} | collective-permute-start | bytes 3145736 | tf_op jit(solution)/shard_map/ppermute | solution.py:84
  142.8 1.0 copy-start.6
  149.3 1.0 copy-start.2
  156.8 7.3 %collective-permute-start.13 = (f32[256,1024]{1,0:T(8,128)}, f32[256,1024]{1,0:T(8,128)S(1)}, u32[]{:S(2)}, u32[]{:S(2)}) collective-permute-start(f32[256,1024]{1,0:T(8,128)} %shard_map.40), channel_id=1, source_target_pairs={{0,1},{2,3},{4,5},{6,7},{9,8},{11,10},{13,12},{15,14},{16,17},{18,... | collective-permute-start | bytes 3145736 | tf_op jit(solution)/shard_map/ppermute | solution.py:68
  159.0 3.2 %collective-permute-start.15 = (f16[272,1024]{1,0:T(8,128)(2,1)}, f16[272,1024]{1,0:T(8,128)(2,1)}, u32[]{:S(2)}, u32[]{:S(2)}) collective-permute-start(f16[272,1024]{1,0:T(8,128)(2,1)} %concatenate.14), channel_id=1, source_target_pairs={{4,6},{5,7},{11,9},{10,8},{20,22},{21,23},{27,25},{26,24}} | collective-permute-start | bytes 1671176 | tf_op jit(solution)/shard_map/ppermute | solution.py:84
  162.1 6.0 %copy-start.7 = (f32[256,1024]{1,0:T(8,128)S(1)}, f32[256,1024]{1,0:T(8,128)}, u32[]{:S(2)}) copy-start(f32[256,1024]{1,0:T(8,128)} %copy-done.6) | copy-start | bytes 3145732
  166.5 31.2 %collective-permute-start.14 = (f32[256,1024]{1,0:T(8,128)}, f32[256,1024]{1,0:T(8,128)}, u32[]{:S(2)}, u32[]{:S(2)}) collective-permute-start(f32[256,1024]{1,0:T(8,128)} %add.42), channel_id=1, source_target_pairs={{1,3},{5,7},{10,8},{14,12},{17,19},{21,23},{26,24},{30,28}} | collective-permute-start | bytes 3145736 | tf_op jit(solution)/shard_map/ppermute | solution.py:84
  169.4 28.4 %copy-start.9 = (f32[256,1024]{1,0:T(8,128)S(1)}, f32[256,1024]{1,0:T(8,128)}, u32[]{:S(2)}) copy-start(f32[256,1024]{1,0:T(8,128)} %add.38) | copy-start | bytes 3145732
  171.1 25.3 %collective-permute-start.16 = (f16[272,1024]{1,0:T(8,128)(2,1)S(1)}, f16[272,1024]{1,0:T(8,128)(2,1)S(1)}, u32[]{:S(2)}, u32[]{:S(2)}) collective-permute-start(f16[272,1024]{1,0:T(8,128)(2,1)S(1)} %concatenate.15), channel_id=1, source_target_pairs={{4,0},{8,12},{5,1},{9,13},{6,2},{10,14},{7,3},{11,15},{20,16},{24,... | collective-permute-start | bytes 1671176 | tf_op jit(solution)/shard_map/ppermute | solution.py:242

commit v8 on v7

v8 whole, which is shorter than its diff:
```python
import functools

import jax
import jax.numpy as jnp
from jax import lax
from jax.experimental import pallas as pl
from jax.experimental.pallas import tpu as pltpu
from jax.sharding import PartitionSpec as P

PLACE = ("ex", "ckpt", "dim")
VMEM = 48 * 1024 * 1024


def after(value, *others):
    return lax.optimization_barrier((value,) + others)[0]


class Keepers:
    def __init__(self, rows):
        self.ckpts, self.dims = lax.axis_size("ckpt"), lax.axis_size("dim")
        self.planes = lax.axis_size("ex")
        self.z, self.x, self.c = [lax.axis_index(name) for name in PLACE]
        kept = rows * self.planes // (self.ckpts * self.dims)
        self.ratio = kept // rows
        assert self.ratio * rows == kept

    def index(self, z, x, c):
        return (z * self.ckpts + x) * self.dims + c

    def of(self, block):
        owner = block // self.ratio
        return owner // self.dims, owner % self.dims

    def mine(self, blocks, j=0):
        found = jnp.bool_(False)
        for z, block in enumerate(blocks):
            if block is not None and block % self.ratio == j:
                x, c = self.of(block)
                found = found | ((self.z == z) & (self.x == x) & (self.c == c))
        return found

    def sums(self, partial, blocks):
        return self.far_sums(self.near_sums(partial, blocks), blocks)

    def near_sums(self, partial, blocks):
        total = partial
        for away in range(1, self.dims):
            pairs = []
            for z, block in enumerate(blocks):
                if block is not None:
                    c = self.of(block)[1]
                    for x in range(self.ckpts):
                        pairs.append((self.index(z, x, (c + away) % self.dims), self.index(z, x, c)))
            total = total + lax.ppermute(partial, PLACE, pairs)
        return total

    def far_sums(self, total, *held):
        whole = total
        for away in range(1, self.ckpts):
            whole = whole + self.far_moves(total, *held, away=away)
        return whole

    def far_moves(self, total, *held, away=1):
        pairs = []
        for z in range(self.planes):
            for blocks in held:
                if blocks[z] is not None:
                    x, c = self.of(blocks[z])
                    pairs.append((self.index(z, (x + away) % self.ckpts, c), self.index(z, x, c)))
        return lax.ppermute(total, PLACE, pairs)

    def keeps_first(self, blocks):
        found = jnp.bool_(False)
        for z, block in enumerate(blocks):
            if block is not None:
                found = found | ((self.z == z) & (self.c == self.of(block)[1]))
        return found

    def swapped(self, value, planes):
        pairs = []
        for z in planes:
            for x in range(self.ckpts):
                pairs += [(self.index(z, x, c), self.index(z, x, 1 - c)) for c in range(2)]
        return lax.ppermute(value, PLACE, pairs)


def product(queries, examples):
    return lax.dot_general(
        queries,
        examples,
        (((1,), (1,)), ((), ())),
        preferred_element_type=jnp.float32,
    )


def pair_kernel(scale, flag_ref, one_ref, two_ref, train_ref, weight_ref, sent_ref, kept_ref):
    keeps_one = flag_ref[0] == 1
    sent = kept = None
    for check in range(train_ref.shape[0]):
        one, two = one_ref[check], two_ref[check]
        weight = jnp.sum(weight_ref[check].astype(jnp.float32), axis=0, keepdims=True)
        both = []
        for first, second in ((two, one), (one, two)):
            term = product(jnp.where(keeps_one, first, second), train_ref[check]) * weight
            both.append(term)
        sent = both[0] if sent is None else sent + both[0]
        kept = both[1] if kept is None else kept + both[1]
    sent_ref[...] = sent * scale
    kept_ref[...] = kept * scale


def pair_scores(keeps_one, one, two, train, weights, scale, examples):
    checks, rows, depth = one.shape
    tile = 256
    return pl.pallas_call(
        functools.partial(pair_kernel, scale),
        grid_spec=pltpu.PrefetchScalarGridSpec(
            num_scalar_prefetch=1,
            grid=(examples // tile,),
            in_specs=[
                pl.BlockSpec((checks, rows, depth), lambda i, flag: (0, 0, 0)),
                pl.BlockSpec((checks, rows, depth), lambda i, flag: (0, 0, 0)),
                pl.BlockSpec((checks, tile, depth), lambda i, flag: (0, i, 0)),
                pl.BlockSpec((checks, weights.shape[1], tile), lambda i, flag: (0, 0, i)),
            ],
            out_specs=[pl.BlockSpec((rows, tile), lambda i, flag: (0, i))] * 2,
        ),
        out_shape=[jax.ShapeDtypeStruct((rows, examples), jnp.float32)] * 2,
        compiler_params=pltpu.CompilerParams(vmem_limit_bytes=VMEM),
        cost_estimate=pl.CostEstimate(flops=0, bytes_accessed=0, transcendentals=0),
    )(keeps_one.astype(jnp.int32).reshape(1), one, two, train, weights)


def block_kernel(scale, queries_ref, train_ref, weight_ref, out_ref):
    total = None
    for check in range(train_ref.shape[0]):
        term = product(queries_ref[check], train_ref[check]) * weight_ref[check]
        total = term if total is None else total + term
    out_ref[...] = total * scale


def block_scores(queries, train, weights, scale):
    checks, rows, depth = queries.shape
    examples, tile = train.shape[1], 256
    return pl.pallas_call(
        functools.partial(block_kernel, scale),
        grid=(examples // tile,),
        in_specs=[
            pl.BlockSpec((checks, rows, depth), lambda i: (0, 0, 0)),
            pl.BlockSpec((checks, tile, depth), lambda i: (0, i, 0)),
            pl.BlockSpec((checks, 1, tile), lambda i: (0, 0, i)),
        ],
        out_specs=pl.BlockSpec((rows, tile), lambda i: (0, i)),
        out_shape=jax.ShapeDtypeStruct((rows, examples), jnp.float32),
        compiler_params=pltpu.CompilerParams(vmem_limit_bytes=VMEM),
        cost_estimate=pl.CostEstimate(flops=0, bytes_accessed=0, transcendentals=0),
    )(queries, train, weights)


def ring(train_features, query_features, residual_weights, keepers, scale):
    planes, ratio = keepers.planes, keepers.ratio
    rows = query_features.shape[1]
    cut = rows // 4
    weights = residual_weights[:, None]
    right = [(s, (s + 1) % planes) for s in range(planes)]
    left = [(s, (s - 1) % planes) for s in range(planes)]

    def blocks_at(step):
        return [(s + step) % planes for s in range(planes)]

    def one_block(queries, step):
        found = block_scores(queries, train_features, weights, scale)
        return keepers.sums(found, blocks_at(step))

    def chosen(parts):
        found = []
        for j in range(ratio):
            kept = None
            for step, whole in parts:
                mine = keepers.mine(blocks_at(step), j)
                kept = whole if kept is None else jnp.where(mine, whole, kept)
            found.append(kept)
        return found

    from_left = from_right = query_features
    whole, parts = None, []
    for step in range(1, planes // 2):
        from_right = lax.ppermute(from_right, "ex", left)
        from_left = lax.ppermute(from_left, "ex", right)
        if step < planes // 2 - 1:
            parts += [(step, one_block(from_right, step)), (-step, one_block(from_left, -step))]
    low = lax.ppermute(from_right[:, cut:], "ex", left)
    step = planes // 2 - 1
    own = after(query_features, from_right)
    if keepers.dims == 2 and ratio == 1 and step == 1:
        sent, kept = pair_scores(
            keepers.keeps_first(blocks_at(0)), own, from_right, train_features, weights, scale,
            train_features.shape[1])
        total = kept + keepers.swapped(sent, range(planes))
        ahead = keepers.far_sums(total, blocks_at(0), blocks_at(1))
        parts += [(0, ahead), (1, ahead)]
    else:
        ahead = one_block(from_right, step)
        parts += [(0, one_block(own, 0)), (step, ahead)]
    top = lax.ppermute(after(from_left[:, :cut], low), "ex", right)
    behind = one_block(after(from_left, low, ahead), -step)
    parts.append((-step, behind))
    below = one_block(low, planes // 2)
    above = one_block(after(top, behind, below), planes // 2)
    tops = chosen([(step, part[:cut]) for step, part in parts] + [(planes // 2, above)])
    lows = chosen([(step, part[cut:]) for step, part in parts] + [(planes // 2, below)])
    return jnp.concatenate([part for both in zip(tops, lows) for part in both], axis=0)


def local(train_features, query_features, residual_weights):
    keepers = Keepers(query_features.shape[1])
    scale = 1.0 / (train_features.shape[0] * keepers.ckpts)
    return ring(train_features, query_features, residual_weights, keepers, scale)


def solution(mesh):
    in_specs = (
        P("ckpt", ("groups", "ex"), "dim"),
        P("ckpt", ("groups", "ex"), "dim"),
        P("ckpt", ("groups", "ex")),
    )
    out_specs = P(("ckpt", "dim"), ("groups", "ex"))
    return jax.shard_map(local, mesh=mesh, in_specs=in_specs, out_specs=out_specs, check_vma=False)
```

time: 203 us -> 204 us (level)
  waiting for transfers between devices: 99.5 us -> 143 us
  other arithmetic: 20 us -> 4.48 us
  local copies, waits for them, and re-layouts: 18.6 us -> 6.01 us
  starting transfers between devices: 33.3 us -> 25 us
  between operations: 3.32 us -> 0.15 us
    ppermute x4, waiting for transfers between devices: 6.83 us -> 44.5 us  [far_moves(): return lax.ppermute(total, PLACE, pairs)]
    ppermute x9 -> x4, starting transfers between devices: 22.3 us -> 9.35 us  [the longest x1 5.05 us: ring(): from_right = lax.ppermute(from_right, 'ex', left)]
    ppermute x4, starting transfers between devices: 6.77 us -> 11.6 us  [far_moves(): return lax.ppermute(total, PLACE, pairs)]
    add x2 -> x3, other arithmetic: 5.05 us -> 0.26 us  [near_sums(): total = total + lax.ppermute(partial, PLACE, pairs)]
    pallas_call x2 -> x1, Pallas kernels: 12.5 us -> 7.96 us  [pair_scores(): pl.pallas_call(functools.partial(pair_kernel, scale), grid_spec=pltpu.Pre...]
    add x3 -> x1, other arithmetic: 4.53 us -> 0.14 us  [ring(): total = kept + keepers.swapped(sent, range(planes))]
    pallas_call x2 -> x3, Pallas kernels: 13.4 us -> 17.3 us  [block_scores(): pl.pallas_call(functools.partial(block_kernel, scale), grid=(examples //...]
    slice x7 -> x2, local copies, waits for them, and re-layouts: 6.17 us -> 2.35 us  [the longest x1 1.53 us: ring(): low = lax.ppermute(from_right[:, cut:], 'ex', left)]
  transfers between devices with their start and end apart: 17 -> 12, of which waited for: 6 -> 8; matrix products, arithmetic and copies ran while one was open for 14% -> 3% of each run, Pallas kernels for 13% -> 3%
where the time goes in v8:
time: 204 us
  waiting for transfers between devices  143 us (70%)
  Pallas kernels  25.2 us (12%)
  starting transfers between devices  25 us (12%)
  local copies, waits for them, and re-layouts  6.01 us (3%)
  other arithmetic  4.48 us (2%)
    ppermute x4, waiting for transfers between devices, far_moves(): return lax.ppermute(total, PLACE, pairs)  44.5 us
    ppermute x1, waiting for transfers between devices, ring(): from_right = lax.ppermute(from_right, 'ex', left)  44.5 us
    ppermute x1, waiting for transfers between devices, ring(): low = lax.ppermute(from_right[:, cut:], 'ex', left)  32.6 us
    ppermute x1, waiting for transfers between devices, ring(): from_left = lax.ppermute(from_left, 'ex', right)  17.5 us
    pallas_call x3, Pallas kernels, block_scores(): pl.pallas_call(functools.partial(block_kernel, scale), grid=(examples //...  17.3 us
    ppermute x4, starting transfers between devices, far_moves(): return lax.ppermute(total, PLACE, pairs)  11.6 us
    pallas_call x1, Pallas kernels, pair_scores(): pl.pallas_call(functools.partial(pair_kernel, scale), grid_spec=pltpu.Pre...  7.96 us
    ppermute x1, starting transfers between devices, ring(): from_right = lax.ppermute(from_right, 'ex', left)  5.05 us
  transfers between devices with their start and end apart: 12, of which 8 were waited for; matrix products, arithmetic and copies ran while one was open for 3% of the time, Pallas kernels for 3%

profile of v8, /device:TPU:0, one launch (start us, length us, event | category | flops | bytes accessed | tf_op | source)
XLA Modules:
  0.0 203.7 jit_solution(6784473218328081571)
XLA Ops:
  0.0 5.0 %collective-permute-start.1 = (bf16[4,256,1024]{2,1,0:T(8,128)(2,1)}, bf16[4,256,1024]{2,1,0:T(8,128)(2,1)S(1)}, u32[]{:S(2)}, u32[]{:S(2)}) collective-permute-start(bf16[4,256,1024]{2,1,0:T(8,128)(2,1)} %one_ref), channel_id=1, source_target_pairs={{0,12},{4,0},{8,4},{12,8},{1,13},{5,1},{9,5},{13,9},{2,14},{6,2},{... | collective-permute-start | bytes 6291464 | tf_op jit(solution)/shard_map/ppermute | solution.py:188
  5.0 0.7 broadcast_in_dim.3.weight_ref
  5.8 44.5 %collective-permute-done.1.two_ref = bf16[4,256,1024]{2,1,0:T(8,128)(2,1)S(1)} collective-permute-done((bf16[4,256,1024]{2,1,0:T(8,128)(2,1)}, bf16[4,256,1024]{2,1,0:T(8,128)(2,1)S(1)}, u32[]{:S(2)}, u32[]{:S(2)}) %collective-permute-start.1) | collective-permute-done | bytes 2097184 | tf_op jit(solution)/shard_map/ppermute | solution.py:188
  50.3 0.0 copy-start.1
  50.3 1.3 copy-done.1
  51.6 0.0 copy-start
  51.6 1.6 copy-done
  53.2 8.0 %shard_map.37 = (f32[256,1024]{1,0:T(8,128)S(1)}, f32[256,1024]{1,0:T(8,128)S(1)}) custom-call(s32[1]{0:T(128)} %bitcast.flag_ref, bf16[4,256,1024]{2,1,0:T(8,128)(2,1)S(1)} %copy-done, bf16[4,256,1024]{2,1,0:T(8,128)(2,1)} %copy-done.1, bf16[4,1024,1024]{2,1,0:T(8,128)(2,1)} %train_ref.7, f32[4,1,1024]{2,1,0:T(1,128)S(1)} %broadcast_in_dim.3.weight_ref), custom_call_target="tpu_custom_call" | custom-call | tf_op jit(solution)/shard_map/pallas_call | solution.py:115
  61.2 0.1 collective-permute-start.4
  61.2 0.4 collective-permute-start
  61.6 1.5 slice.27
  63.2 3.9 %collective-permute-start.2 = (bf16[4,192,1024]{2,1,0:T(8,128)(2,1)S(1)}, bf16[4,192,1024]{2,1,0:T(8,128)(2,1)S(1)}, u32[]{:S(2)}, u32[]{:S(2)}) collective-permute-start(bf16[4,192,1024]{2,1,0:T(8,128)(2,1)S(1)} %slice.27), channel_id=1, source_target_pairs={{0,12},{4,0},{8,4},{12,8},{1,13},{5,1},{9,5},{13,9},{2,14},{6,2},{... | collective-permute-start | bytes 4718600 | tf_op jit(solution)/shard_map/ppermute | solution.py:192
  67.1 0.0 collective-permute-done.4
  67.1 0.1 add.24
  67.2 1.3 collective-permute-start.5
  68.5 25.8 %collective-permute-done.5 = f32[256,1024]{1,0:T(8,128)S(1)} collective-permute-done((f32[256,1024]{1,0:T(8,128)S(1)}, f32[256,1024]{1,0:T(8,128)S(1)}, u32[]{:S(2)}, u32[]{:S(2)}) %collective-permute-start.5) | collective-permute-done | bytes 1048608 | tf_op jit(solution)/shard_map/ppermute | solution.py:70
  94.3 0.2 add.25
  94.5 17.5 %collective-permute-done.queries_ref = bf16[4,256,1024]{2,1,0:T(8,128)(2,1)S(1)} collective-permute-done((bf16[4,256,1024]{2,1,0:T(8,128)(2,1)S(1)}, bf16[4,256,1024]{2,1,0:T(8,128)(2,1)S(1)}, u32[]{:S(2)}, u32[]{:S(2)}) %collective-permute-start) | collective-permute-done | bytes 2097184 | tf_op jit(solution)/shard_map/ppermute | solution.py:189
  112.0 32.6 %collective-permute-done.2.queries_ref = bf16[4,192,1024]{2,1,0:T(8,128)(2,1)S(1)} collective-permute-done((bf16[4,192,1024]{2,1,0:T(8,128)(2,1)S(1)}, bf16[4,192,1024]{2,1,0:T(8,128)(2,1)S(1)}, u32[]{:S(2)}, u32[]{:S(2)}) %collective-permute-start.2) | collective-permute-done | bytes 1572896 | tf_op jit(solution)/shard_map/ppermute | solution.py:192
  144.6 5.7 %shard_map.38 = f32[256,1024]{1,0:T(8,128)S(1)} custom-call(bf16[4,256,1024]{2,1,0:T(8,128)(2,1)S(1)} %collective-permute-done.queries_ref, bf16[4,1024,1024]{2,1,0:T(8,128)(2,1)} %train_ref.7, f32[4,1,1024]{2,1,0:T(1,128)S(1)} %broadcast_in_dim.3.weight_ref), custom_call_target="tpu_custom_call" | custom-call | tf_op jit(solution)/shard_map/pallas_call | solution.py:145
  150.3 1.4 collective-permute-start.6
  151.6 6.0 %shard_map.39 = f32[192,1024]{1,0:T(8,128)S(1)} custom-call(bf16[4,192,1024]{2,1,0:T(8,128)(2,1)S(1)} %collective-permute-done.2.queries_ref, bf16[4,1024,1024]{2,1,0:T(8,128)(2,1)} %train_ref.7, f32[4,1,1024]{2,1,0:T(1,128)S(1)} %broadcast_in_dim.3.weight_ref), custom_call_target="tpu_custom_call" | custom-call | tf_op jit(solution)/shard_map/pallas_call | solution.py:145
  157.6 1.3 collective-permute-start.8
  158.9 0.0 collective-permute-done.6
  158.9 0.1 add.26
  159.1 1.7 collective-permute-start.7
  160.7 1.1 collective-permute-done.8
  161.8 0.1 add.28
  161.9 4.4 %collective-permute-start.9 = (f32[192,1024]{1,0:T(8,128)S(1)}, f32[192,1024]{1,0:T(8,128)}, u32[]{:S(2)}, u32[]{:S(2)}) collective-permute-start(f32[192,1024]{1,0:T(8,128)S(1)} %add.28), channel_id=1, source_target_pairs={{0,2},{5,7},{10,8},{15,13},{16,18},{21,23},{26,24},{31,29}} | collective-permute-start | bytes 2359304 | tf_op jit(solution)/shard_map/ppermute | solution.py:70
  166.2 0.8 slice.26
  167.1 0.0 collective-permute-start.3
  167.1 0.0 collective-permute-done.7
  167.1 1.4 add.27
  168.4 14.8 %collective-permute-done.9 = f32[192,1024]{1,0:T(8,128)} collective-permute-done((f32[192,1024]{1,0:T(8,128)S(1)}, f32[192,1024]{1,0:T(8,128)}, u32[]{:S(2)}, u32[]{:S(2)}) %collective-permute-start.9) | collective-permute-done | bytes 786464 | tf_op jit(solution)/shard_map/ppermute | solution.py:70
  183.3 1.4 fusion
  184.7 0.0 collective-permute-done.3.queries_ref
  184.7 5.7 %shard_map.40 = f32[64,1024]{1,0:T(8,128)S(1)} custom-call(bf16[4,64,1024]{2,1,0:T(8,128)(2,1)S(1)} %collective-permute-done.3.queries_ref, bf16[4,1024,1024]{2,1,0:T(8,128)(2,1)} %train_ref.7, f32[4,1,1024]{2,1,0:T(1,128)S(1)} %broadcast_in_dim.3.weight_ref), custom_call_target="tpu_custom_call" | custom-call | tf_op jit(solution)/shard_map/pallas_call | solution.py:145
  190.4 1.3 collective-permute-start.10
  191.7 2.7 %collective-permute-done.10 = f32[64,1024]{1,0:T(8,128)S(1)} collective-permute-done((f32[64,1024]{1,0:T(8,128)S(1)}, f32[64,1024]{1,0:T(8,128)S(1)}, u32[]{:S(2)}, u32[]{:S(2)}) %collective-permute-start.10) | collective-permute-done | bytes 262176 | tf_op jit(solution)/shard_map/ppermute | solution.py:54
  194.4 4.3 %collective-permute-start.11 = (f32[64,1024]{1,0:T(8,128)S(1)}, f32[64,1024]{1,0:T(8,128)S(1)}, u32[]{:S(2)}, u32[]{:S(2)}) collective-permute-start(f32[64,1024]{1,0:T(8,128)S(1)} %add.30), channel_id=1, source_target_pairs={{0,2},{5,7},{10,8},{15,13},{16,18},{21,23},{26,24},{31,29}} | collective-permute-start | bytes 786440 | tf_op jit(solution)/shard_map/ppermute | solution.py:70
  198.7 3.9 %collective-permute-done.11 = f32[64,1024]{1,0:T(8,128)S(1)} collective-permute-done((f32[64,1024]{1,0:T(8,128)S(1)}, f32[64,1024]{1,0:T(8,128)S(1)}, u32[]{:S(2)}, u32[]{:S(2)}) %collective-permute-start.11) | collective-permute-done | bytes 262176 | tf_op jit(solution)/shard_map/ppermute | solution.py:70
  202.6 0.1 fusion.1
  202.7 1.1 pad_maximum_fusion
  (1 shorter events, 0.0 us)
Async XLA Ops:
  0.0 50.3 %collective-permute-start.1 = (bf16[4,256,1024]{2,1,0:T(8,128)(2,1)}, bf16[4,256,1024]{2,1,0:T(8,128)(2,1)S(1)}, u32[]{:S(2)}, u32[]{:S(2)}) collective-permute-start(bf16[4,256,1024]{2,1,0:T(8,128)(2,1)} %one_ref), channel_id=1, source_target_pairs={{0,12},{4,0},{8,4},{12,8},{1,13},{5,1},{9,5},{13,9},{2,14},{6,2},{... | collective-permute-start | bytes 6291464 | tf_op jit(solution)/shard_map/ppermute | solution.py:188
  50.3 1.3 copy-start.1
  51.6 1.6 copy-start
  61.2 5.9 %collective-permute-start.4 = (f32[256,1024]{1,0:T(8,128)S(1)}, f32[256,1024]{1,0:T(8,128)S(1)}, u32[]{:S(2)}, u32[]{:S(2)}) collective-permute-start(f32[256,1024]{1,0:T(8,128)S(1)} %get-tuple-element.14), channel_id=1, source_target_pairs={{0,1},{1,0},{2,3},{3,2},{4,5},{5,4},{6,7},{7,6},{8,9},{9,8},{10,11... | collective-permute-start | bytes 3145736 | tf_op jit(solution)/shard_map/ppermute | solution.py:84
  61.2 50.8 %collective-permute-start = (bf16[4,256,1024]{2,1,0:T(8,128)(2,1)S(1)}, bf16[4,256,1024]{2,1,0:T(8,128)(2,1)S(1)}, u32[]{:S(2)}, u32[]{:S(2)}) collective-permute-start(bf16[4,256,1024]{2,1,0:T(8,128)(2,1)S(1)} %copy-done), channel_id=1, source_target_pairs={{0,4},{4,8},{8,12},{12,0},{1,5},{5,9},{9,13},{13,1},{2,6},{6,10},{... | collective-permute-start | bytes 6291464 | tf_op jit(solution)/shard_map/ppermute | solution.py:189
  63.2 81.5 %collective-permute-start.2 = (bf16[4,192,1024]{2,1,0:T(8,128)(2,1)S(1)}, bf16[4,192,1024]{2,1,0:T(8,128)(2,1)S(1)}, u32[]{:S(2)}, u32[]{:S(2)}) collective-permute-start(bf16[4,192,1024]{2,1,0:T(8,128)(2,1)S(1)} %slice.27), channel_id=1, source_target_pairs={{0,12},{4,0},{8,4},{12,8},{1,13},{5,1},{9,5},{13,9},{2,14},{6,2},{... | collective-permute-start | bytes 4718600 | tf_op jit(solution)/shard_map/ppermute | solution.py:192
  67.2 27.1 %collective-permute-start.5 = (f32[256,1024]{1,0:T(8,128)S(1)}, f32[256,1024]{1,0:T(8,128)S(1)}, u32[]{:S(2)}, u32[]{:S(2)}) collective-permute-start(f32[256,1024]{1,0:T(8,128)S(1)} %add.24), channel_id=1, source_target_pairs={{2,0},{3,1},{7,5},{4,6},{8,10},{9,11},{13,15},{14,12},{18,16},{19,... | collective-permute-start | bytes 3145736 | tf_op jit(solution)/shard_map/ppermute | solution.py:70
  150.3 8.6 %collective-permute-start.6 = (f32[256,1024]{1,0:T(8,128)S(1)}, f32[256,1024]{1,0:T(8,128)S(1)}, u32[]{:S(2)}, u32[]{:S(2)}) collective-permute-start(f32[256,1024]{1,0:T(8,128)S(1)} %shard_map.38), channel_id=1, source_target_pairs={{0,1},{2,3},{5,4},{7,6},{8,9},{10,11},{13,12},{15,14},{16,17},{18,... | collective-permute-start | bytes 3145736 | tf_op jit(solution)/shard_map/ppermute | solution.py:54
  157.6 4.2 %collective-permute-start.8 = (f32[192,1024]{1,0:T(8,128)S(1)}, f32[192,1024]{1,0:T(8,128)S(1)}, u32[]{:S(2)}, u32[]{:S(2)}) collective-permute-start(f32[192,1024]{1,0:T(8,128)S(1)} %shard_map.39), channel_id=1, source_target_pairs={{1,0},{3,2},{4,5},{6,7},{9,8},{11,10},{12,13},{14,15},{17,16},{19,... | collective-permute-start | bytes 2359304 | tf_op jit(solution)/shard_map/ppermute | solution.py:54
  159.1 8.0 %collective-permute-start.7 = (f32[256,1024]{1,0:T(8,128)S(1)}, f32[256,1024]{1,0:T(8,128)}, u32[]{:S(2)}, u32[]{:S(2)}) collective-permute-start(f32[256,1024]{1,0:T(8,128)S(1)} %add.26), channel_id=1, source_target_pairs={{1,3},{6,4},{11,9},{12,14},{17,19},{22,20},{27,25},{28,30}} | collective-permute-start | bytes 3145736 | tf_op jit(solution)/shard_map/ppermute | solution.py:70
  161.9 21.4 %collective-permute-start.9 = (f32[192,1024]{1,0:T(8,128)S(1)}, f32[192,1024]{1,0:T(8,128)}, u32[]{:S(2)}, u32[]{:S(2)}) collective-permute-start(f32[192,1024]{1,0:T(8,128)S(1)} %add.28), channel_id=1, source_target_pairs={{0,2},{5,7},{10,8},{15,13},{16,18},{21,23},{26,24},{31,29}} | collective-permute-start | bytes 2359304 | tf_op jit(solution)/shard_map/ppermute | solution.py:70
  167.1 17.6 %collective-permute-start.3 = (bf16[4,64,1024]{2,1,0:T(8,128)(2,1)}, bf16[4,64,1024]{2,1,0:T(8,128)(2,1)S(1)}, u32[]{:S(2)}, u32[]{:S(2)}) collective-permute-start(bf16[4,64,1024]{2,1,0:T(8,128)(2,1)} %slice.26), channel_id=1, source_target_pairs={{0,4},{4,8},{8,12},{12,0},{1,5},{5,9},{9,13},{13,1},{2,6},{6,10},{... | collective-permute-start | bytes 1572872 | tf_op jit(solution)/shard_map/ppermute | solution.py:205
  190.4 4.0 %collective-permute-start.10 = (f32[64,1024]{1,0:T(8,128)S(1)}, f32[64,1024]{1,0:T(8,128)S(1)}, u32[]{:S(2)}, u32[]{:S(2)}) collective-permute-start(f32[64,1024]{1,0:T(8,128)S(1)} %shard_map.40), channel_id=1, source_target_pairs={{1,0},{3,2},{4,5},{6,7},{9,8},{11,10},{12,13},{14,15},{17,16},{19,... | collective-permute-start | bytes 786440 | tf_op jit(solution)/shard_map/ppermute | solution.py:54
  194.4 8.2 %collective-permute-start.11 = (f32[64,1024]{1,0:T(8,128)S(1)}, f32[64,1024]{1,0:T(8,128)S(1)}, u32[]{:S(2)}, u32[]{:S(2)}) collective-permute-start(f32[64,1024]{1,0:T(8,128)S(1)} %add.30), channel_id=1, source_target_pairs={{0,2},{5,7},{10,8},{15,13},{16,18},{21,23},{26,24},{31,29}} | collective-permute-start | bytes 786440 | tf_op jit(solution)/shard_map/ppermute | solution.py:70

commit v9 on v0

v9 whole, which is shorter than its diff:
```python
import jax
import jax.numpy as jnp
from jax import lax
from jax.sharding import PartitionSpec as P

PLACE = ("ex", "ckpt", "dim")


def after(value, *others):
    return lax.optimization_barrier((value,) + others)[0]


def weighted(checks, train, weights, scale):
    total = None
    for piece, examples, weight in zip(checks, train, weights):
        dots = lax.dot_general(
            piece,
            examples,
            (((1,), (1,)), ((), ())),
            preferred_element_type=jnp.float32,
        )
        term = dots * weight[None, :]
        total = term if total is None else total + term
    return total * scale


class Keepers:
    def __init__(self, rows):
        self.ckpts, self.dims = lax.axis_size("ckpt"), lax.axis_size("dim")
        self.planes = lax.axis_size("ex")
        self.z, self.x, self.c = [lax.axis_index(name) for name in PLACE]
        kept = rows * self.planes // (self.ckpts * self.dims)
        self.ratio = kept // rows
        assert self.ratio * rows == kept

    def index(self, z, x, c):
        return (z * self.ckpts + x) * self.dims + c

    def of(self, block):
        owner = block // self.ratio
        return owner // self.dims, owner % self.dims

    def mine(self, blocks, j=0):
        found = jnp.bool_(False)
        for z, block in enumerate(blocks):
            if block is not None and block % self.ratio == j:
                x, c = self.of(block)
                found = found | ((self.z == z) & (self.x == x) & (self.c == c))
        return found

    def near_sums(self, partial, blocks):
        total = partial
        for away in range(1, self.dims):
            pairs = []
            for z, block in enumerate(blocks):
                c = self.of(block)[1]
                for x in range(self.ckpts):
                    pairs.append((self.index(z, x, (c + away) % self.dims), self.index(z, x, c)))
            total = total + lax.ppermute(partial, PLACE, pairs)
        return total

    def far_sums(self, total, blocks):
        whole = total
        for away in range(1, self.ckpts):
            pairs = []
            for z, block in enumerate(blocks):
                x, c = self.of(block)
                pairs.append((self.index(z, (x + away) % self.ckpts, c), self.index(z, x, c)))
            whole = whole + lax.ppermute(total, PLACE, pairs)
        return whole


def ring(train_features, query_features, residual_weights, keepers, scale):
    planes, ratio = keepers.planes, keepers.ratio
    rows = query_features.shape[1]
    cut = rows // 2
    right = [(s, (s + 1) % planes) for s in range(planes)]
    left = [(s, (s - 1) % planes) for s in range(planes)]
    parts = []

    def finish(queries, step, *earlier):
        blocks = [(s + step) % planes for s in range(planes)]
        found = weighted(list(queries), train_features, residual_weights, scale)
        whole = keepers.far_sums(after(keepers.near_sums(found, blocks), *earlier), blocks)
        parts.append((blocks, whole))
        return whole

    def chosen(parts):
        found = []
        for j in range(ratio):
            kept = None
            for blocks, whole in parts:
                kept = whole if kept is None else jnp.where(keepers.mine(blocks, j), whole, kept)
            found.append(kept)
        return found

    from_left = from_right = query_features
    for step in range(1, planes // 2):
        from_right = lax.ppermute(from_right, "ex", left)
        from_left = lax.ppermute(from_left, "ex", right)
        if step == 1:
            own = finish(query_features, 0)
        ahead = finish(from_right, step)
        if step < planes // 2 - 1:
            finish(from_left, -step)
    low = lax.ppermute(from_right[:, cut:], "ex", left)
    top = lax.ppermute(after(from_left[:, :cut], low, own), "ex", right)
    behind = finish(after(from_left, low), -(planes // 2 - 1))
    earlier = list(parts)
    below = finish(low, planes // 2)
    above = finish(top, planes // 2, ahead, behind, below)
    across = parts[-1][0]
    tops = chosen([(blocks, whole[:cut]) for blocks, whole in earlier] + [(across, above)])
    lows = chosen([(blocks, whole[cut:]) for blocks, whole in earlier] + [(across, below)])
    return jnp.concatenate([part for both in zip(tops, lows) for part in both], axis=0)


def local(train_features, query_features, residual_weights):
    keepers = Keepers(query_features.shape[1])
    scale = 1.0 / (train_features.shape[0] * keepers.ckpts)
    return ring(train_features, query_features, residual_weights, keepers, scale)


def solution(mesh):
    in_specs = (
        P("ckpt", ("groups", "ex"), "dim"),
        P("ckpt", ("groups", "ex"), "dim"),
        P("ckpt", ("groups", "ex")),
    )
    out_specs = P(("ckpt", "dim"), ("groups", "ex"))
    return jax.shard_map(local, mesh=mesh, in_specs=in_specs, out_specs=out_specs, check_vma=False)
```

time: 280 us -> 186 us (0.66)
  waiting for transfers between devices: 220 us -> 119 us
  starting transfers between devices: 3.08 us -> 34.6 us
  between operations: 13.5 us -> 0.35 us
  local copies, waits for them, and re-layouts: 12.9 us -> 1.03 us
  other arithmetic: 0 us -> 8.19 us
  matrix products: 29.4 us -> 22.3 us
    reduce_scatter x1 -> x0, waiting for transfers between devices: 52.1 us -> none  [local(): mine = lax.psum_scatter(summed, 'ckpt', scatter_dimension=0, tiled=True)]
    ppermute x3 -> x14, starting transfers between devices: 3.03 us -> 34.6 us  [the longest x5 15.4 us: far_sums(): whole = whole + lax.ppermute(total, PLACE, pairs)]
    ppermute x3 -> x14, waiting for transfers between devices: 145 us -> 119 us  [the longest x1 36.8 us: ring(): from_left = lax.ppermute(from_left, 'ex', right)]
    psum x1 -> x0, waiting for transfers between devices: 23.7 us -> none  [local(): summed = lax.psum(terms, 'dim')]
    dot_general x16 -> x20, matrix products: 29.4 us -> 22.3 us  [weighted(): lax.dot_general(piece, examples, (((1,), (1,)), ((), ())), preferred_elem...]
    add x0 -> x8, other arithmetic: none -> 5.44 us  [the longest x3 2.86 us: far_sums(): whole = whole + lax.ppermute(total, PLACE, pairs)]
    while x9 -> x0, local copies, waits for them, and re-layouts: 5.04 us -> none
    unnamed x5 -> x4, local copies, waits for them, and re-layouts: 5.03 us -> 0.01 us
  transfers between devices with their start and end apart: 5 -> 14, of which waited for: 5 -> 7; matrix products, arithmetic and copies ran while one was open for 0% -> 15% of each run, Pallas kernels for 0% -> 0%
where the time goes in v9:
time: 186 us; the launch traced here: 185 us
  waiting for transfers between devices  119 us (64%)
  starting transfers between devices  34.6 us (19%)
  matrix products  22.3 us (12%)
  other arithmetic  8.19 us (4%)
    ppermute x1, waiting for transfers between devices, ring(): from_left = lax.ppermute(from_left, 'ex', right)  36.8 us
    ppermute x1, waiting for transfers between devices, ring(): from_right = lax.ppermute(from_right, 'ex', left)  30.9 us
    dot_general x20, matrix products, weighted(): lax.dot_general(piece, examples, (((1,), (1,)), ((), ())), preferred_elem...  22.3 us
    ppermute x1, waiting for transfers between devices, ring(): low = lax.ppermute(from_right[:, cut:], 'ex', left)  21.1 us
    ppermute x1, waiting for transfers between devices, ring(): top = lax.ppermute(after(from_left[:, :cut], low, own), 'ex', right)  17.9 us
    ppermute x5, starting transfers between devices, far_sums(): whole = whole + lax.ppermute(total, PLACE, pairs)  15.4 us
    ppermute x5, waiting for transfers between devices, far_sums(): whole = whole + lax.ppermute(total, PLACE, pairs)  8.82 us
    ppermute x5, starting transfers between devices, near_sums(): total = total + lax.ppermute(partial, PLACE, pairs)  6.68 us
  transfers between devices with their start and end apart: 14, of which 7 were waited for; matrix products, arithmetic and copies ran while one was open for 15% of the time, Pallas kernels for 0%

profile of v9, /device:TPU:0, one launch (start us, length us, event | category | flops | bytes accessed | tf_op | source)
XLA Modules:
  0.0 185.3 jit_solution(8473102411442405859)
XLA Ops:
  0.0 5.0 %collective-permute-start.1 = (bf16[4,256,1024]{2,1,0:T(8,128)(2,1)}, bf16[4,256,1024]{2,1,0:T(8,128)(2,1)S(1)}, u32[]{:S(2)}, u32[]{:S(2)}) collective-permute-start(bf16[4,256,1024]{2,1,0:T(8,128)(2,1)} %param.4), channel_id=1, source_target_pairs={{0,12},{4,0},{8,4},{12,8},{1,13},{5,1},{9,5},{13,9},{2,14},{6,2},{... | collective-permute-start | bytes 6291464 | tf_op jit(solution)/shard_map/ppermute | solution.py:99
  5.0 0.9 fusion.200
  5.9 2.6 %fusion.103 = f32[256,1024]{1,0:T(8,128)S(1)} fusion(bf16[4,1024,1024]{2,1,0:T(8,128)(2,1)} %param.3, f32[1024]{0:T(1024)S(1)} %bitcast.203, bf16[4,256,1024]{2,1,0:T(8,128)(2,1)} %param.4), kind=kOutput, calls=%fused_computation.61 | convolution fusion | flops 537133056 | bytes 3674112 | tf_op jit(solution)/shard_map/dot_general | solution.py:16
  8.6 3.0 %fusion.94 = f32[256,1024]{1,0:T(8,128)S(1)} fusion(bf16[4,1024,1024]{2,1,0:T(8,128)(2,1)} %param.3, f32[1024]{0:T(1024)S(1)} %bitcast.198, bf16[4,256,1024]{2,1,0:T(8,128)(2,1)} %param.4), kind=kOutput, calls=%fused_computation.58 | convolution fusion | flops 537133056 | bytes 3674112 | tf_op jit(solution)/shard_map/dot_general | solution.py:16
  11.6 1.9 %fusion.85 = f32[256,1024]{1,0:T(8,128)S(1)} fusion(bf16[4,1024,1024]{2,1,0:T(8,128)(2,1)S(1)} %copy-done, f32[1024]{0:T(1024)S(1)} %bitcast.193, bf16[4,256,1024]{2,1,0:T(8,128)(2,1)} %param.4), kind=kOutput, calls=%fused_computation.55 | convolution fusion | flops 537133056 | bytes 3674112 | tf_op jit(solution)/shard_map/dot_general | solution.py:16
  13.6 0.9 fusion.52
  14.5 1.3 collective-permute-start.3
  15.9 3.2 %collective-permute-done.3 = f32[256,1024]{1,0:T(8,128)S(1)} collective-permute-done((f32[256,1024]{1,0:T(8,128)S(1)}, f32[256,1024]{1,0:T(8,128)S(1)}, u32[]{:S(2)}, u32[]{:S(2)}) %collective-permute-start.3) | collective-permute-done | bytes 1048608 | tf_op jit(solution)/shard_map/ppermute | solution.py:59
  19.2 1.3 collective-permute-start.4
  20.5 30.9 %collective-permute-done.1 = bf16[4,256,1024]{2,1,0:T(8,128)(2,1)S(1)} collective-permute-done((bf16[4,256,1024]{2,1,0:T(8,128)(2,1)}, bf16[4,256,1024]{2,1,0:T(8,128)(2,1)S(1)}, u32[]{:S(2)}, u32[]{:S(2)}) %collective-permute-start.1) | collective-permute-done | bytes 2097184 | tf_op jit(solution)/shard_map/ppermute | solution.py:99
  51.5 4.2 %collective-permute-start.2 = (bf16[4,128,1024]{2,1,0:T(8,128)(2,1)S(1)}, bf16[4,128,1024]{2,1,0:T(8,128)(2,1)S(1)}, u32[]{:S(2)}, u32[]{:S(2)}) collective-permute-start(bf16[4,128,1024]{2,1,0:T(8,128)(2,1)S(1)} %slice.33), channel_id=1, source_target_pairs={{0,12},{4,0},{8,4},{12,8},{1,13},{5,1},{9,5},{13,9},{2,14},{6,2},{... | collective-permute-start | bytes 3145736 | tf_op jit(solution)/shard_map/ppermute | solution.py:106
  55.7 0.7 fusion.106
  56.5 0.7 fusion.97
  57.2 0.7 fusion.88
  58.0 0.9 fusion.67
  58.9 1.4 collective-permute-start.7
  60.4 36.8 %collective-permute-done = bf16[4,256,1024]{2,1,0:T(8,128)(2,1)S(1)} collective-permute-done((bf16[4,256,1024]{2,1,0:T(8,128)(2,1)S(1)}, bf16[4,256,1024]{2,1,0:T(8,128)(2,1)S(1)}, u32[]{:S(2)}, u32[]{:S(2)}) %collective-permute-start) | collective-permute-done | bytes 2097184 | tf_op jit(solution)/shard_map/ppermute | solution.py:100
  97.3 21.1 %collective-permute-done.2 = bf16[4,128,1024]{2,1,0:T(8,128)(2,1)S(1)} collective-permute-done((bf16[4,128,1024]{2,1,0:T(8,128)(2,1)S(1)}, bf16[4,128,1024]{2,1,0:T(8,128)(2,1)S(1)}, u32[]{:S(2)}, u32[]{:S(2)}) %collective-permute-start.2) | collective-permute-done | bytes 1048608 | tf_op jit(solution)/shard_map/ppermute | solution.py:106
  118.4 0.7 fusion.109
  119.1 0.8 fusion.100
  119.9 0.7 fusion.91
  120.8 1.7 collective-permute-start.8
  122.4 0.8 fusion.82
  123.3 1.5 collective-permute-start.9
  124.8 3.2 %collective-permute-start.5 = (bf16[4,128,1024]{2,1,0:T(8,128)(2,1)S(1)}, bf16[4,128,1024]{2,1,0:T(8,128)(2,1)S(1)}, u32[]{:S(2)}, u32[]{:S(2)}) collective-permute-start(bf16[4,128,1024]{2,1,0:T(8,128)(2,1)S(1)} %slice.32), channel_id=1, source_target_pairs={{0,4},{4,8},{8,12},{12,0},{1,5},{5,9},{9,13},{13,1},{2,6},{6,10},{... | collective-permute-start | bytes 3145736 | tf_op jit(solution)/shard_map/ppermute | solution.py:107
  128.0 0.8 fusion.157
  128.8 0.8 fusion.151
  129.7 0.8 fusion.145
  130.6 0.9 fusion.139
  131.4 1.3 collective-permute-start.11
  132.9 1.6 collective-permute-start.10
  134.6 17.9 %collective-permute-done.5 = bf16[4,128,1024]{2,1,0:T(8,128)(2,1)S(1)} collective-permute-done((bf16[4,128,1024]{2,1,0:T(8,128)(2,1)S(1)}, bf16[4,128,1024]{2,1,0:T(8,128)(2,1)S(1)}, u32[]{:S(2)}, u32[]{:S(2)}) %collective-permute-start.5) | collective-permute-done | bytes 1048608 | tf_op jit(solution)/shard_map/ppermute | solution.py:107
  152.5 0.8 fusion.154
  153.4 0.8 fusion.148
  154.2 0.8 fusion.142
  155.1 1.7 fusion.124
  156.8 1.3 collective-permute-start.6
  158.1 0.9 add.97
  158.9 6.3 %collective-permute-start.12 = (f32[128,1024]{1,0:T(8,128)}, f32[128,1024]{1,0:T(8,128)}, u32[]{:S(2)}, u32[]{:S(2)}) collective-permute-start(f32[128,1024]{1,0:T(8,128)} %add.97), channel_id=1, source_target_pairs={{0,2},{5,7},{10,8},{15,13},{16,18},{21,23},{26,24},{31,29}} | collective-permute-start | bytes 1572872 | tf_op jit(solution)/shard_map/ppermute | solution.py:69
  165.3 1.4 add.88
  166.6 1.3 add.83
  167.9 1.4 add.93
  169.3 2.2 %collective-permute-done.12 = f32[128,1024]{1,0:T(8,128)} collective-permute-done((f32[128,1024]{1,0:T(8,128)}, f32[128,1024]{1,0:T(8,128)}, u32[]{:S(2)}, u32[]{:S(2)}) %collective-permute-start.12) | collective-permute-done | bytes 524320 | tf_op jit(solution)/shard_map/ppermute | solution.py:69
  171.4 1.4 fusion.181
  172.9 4.4 %collective-permute-start.13 = (f32[128,1024]{1,0:T(8,128)S(1)}, f32[128,1024]{1,0:T(8,128)S(1)}, u32[]{:S(2)}, u32[]{:S(2)}) collective-permute-start(f32[128,1024]{1,0:T(8,128)S(1)} %add.83), channel_id=1, source_target_pairs={{0,2},{5,7},{10,8},{15,13},{16,18},{21,23},{26,24},{31,29}} | collective-permute-start | bytes 1572872 | tf_op jit(solution)/shard_map/ppermute | solution.py:69
  177.3 6.6 %collective-permute-done.13 = f32[128,1024]{1,0:T(8,128)S(1)} collective-permute-done((f32[128,1024]{1,0:T(8,128)S(1)}, f32[128,1024]{1,0:T(8,128)S(1)}, u32[]{:S(2)}, u32[]{:S(2)}) %collective-permute-start.13) | collective-permute-done | bytes 524320 | tf_op jit(solution)/shard_map/ppermute | solution.py:69
  184.0 0.2 fusion.183
  184.2 1.1 pad_maximum_fusion
  (18 shorter events, 0.8 us)
Async XLA Ops:
  0.0 51.4 %collective-permute-start.1 = (bf16[4,256,1024]{2,1,0:T(8,128)(2,1)}, bf16[4,256,1024]{2,1,0:T(8,128)(2,1)S(1)}, u32[]{:S(2)}, u32[]{:S(2)}) collective-permute-start(bf16[4,256,1024]{2,1,0:T(8,128)(2,1)} %param.4), channel_id=1, source_target_pairs={{0,12},{4,0},{8,4},{12,8},{1,13},{5,1},{9,5},{13,9},{2,14},{6,2},{... | collective-permute-start | bytes 6291464 | tf_op jit(solution)/shard_map/ppermute | solution.py:99
  5.9 5.7 %copy-start = (bf16[4,1024,1024]{2,1,0:T(8,128)(2,1)S(1)}, bf16[4,1024,1024]{2,1,0:T(8,128)(2,1)}, u32[]{:S(2)}) copy-start(bf16[4,1024,1024]{2,1,0:T(8,128)(2,1)} %param.3) | copy-start | bytes 25165828
  11.6 2.0 %copy-start.1 = (bf16[4,256,1024]{2,1,0:T(8,128)(2,1)S(1)}, bf16[4,256,1024]{2,1,0:T(8,128)(2,1)}, u32[]{:S(2)}) copy-start(bf16[4,256,1024]{2,1,0:T(8,128)(2,1)} %param.4) | copy-start | bytes 6291460
  14.5 4.6 %collective-permute-start.3 = (f32[256,1024]{1,0:T(8,128)S(1)}, f32[256,1024]{1,0:T(8,128)S(1)}, u32[]{:S(2)}, u32[]{:S(2)}) collective-permute-start(f32[256,1024]{1,0:T(8,128)S(1)} %fusion.52), channel_id=1, source_target_pairs={{1,0},{3,2},{4,5},{6,7},{9,8},{11,10},{12,13},{14,15},{17,16},{19,... | collective-permute-start | bytes 3145736 | tf_op jit(solution)/shard_map/ppermute | solution.py:59
  15.8 81.4 %collective-permute-start = (bf16[4,256,1024]{2,1,0:T(8,128)(2,1)S(1)}, bf16[4,256,1024]{2,1,0:T(8,128)(2,1)S(1)}, u32[]{:S(2)}, u32[]{:S(2)}) collective-permute-start(bf16[4,256,1024]{2,1,0:T(8,128)(2,1)S(1)} %copy-done.1), channel_id=1, source_target_pairs={{0,4},{4,8},{8,12},{12,0},{1,5},{5,9},{9,13},{13,1},{2,6},{6,10},{... | collective-permute-start | bytes 6291464 | tf_op jit(solution)/shard_map/ppermute | solution.py:100
  19.2 41.0 %collective-permute-start.4 = (f32[256,1024]{1,0:T(8,128)S(1)}, f32[256,1024]{1,0:T(8,128)S(1)}, u32[]{:S(2)}, u32[]{:S(2)}) collective-permute-start(f32[256,1024]{1,0:T(8,128)S(1)} %add.78), channel_id=1, source_target_pairs={{2,0},{7,5},{8,10},{13,15},{18,16},{23,21},{24,26},{29,31}} | collective-permute-start | bytes 3145736 | tf_op jit(solution)/shard_map/ppermute | solution.py:69
  51.5 66.8 %collective-permute-start.2 = (bf16[4,128,1024]{2,1,0:T(8,128)(2,1)S(1)}, bf16[4,128,1024]{2,1,0:T(8,128)(2,1)S(1)}, u32[]{:S(2)}, u32[]{:S(2)}) collective-permute-start(bf16[4,128,1024]{2,1,0:T(8,128)(2,1)S(1)} %slice.33), channel_id=1, source_target_pairs={{0,12},{4,0},{8,4},{12,8},{1,13},{5,1},{9,5},{13,9},{2,14},{6,2},{... | collective-permute-start | bytes 3145736 | tf_op jit(solution)/shard_map/ppermute | solution.py:106
  58.9 61.8 %collective-permute-start.7 = (f32[256,1024]{1,0:T(8,128)S(1)}, f32[256,1024]{1,0:T(8,128)S(1)}, u32[]{:S(2)}, u32[]{:S(2)}) collective-permute-start(f32[256,1024]{1,0:T(8,128)S(1)} %fusion.67), channel_id=1, source_target_pairs={{0,1},{2,3},{5,4},{7,6},{8,9},{10,11},{13,12},{15,14},{16,17},{18,... | collective-permute-start | bytes 3145736 | tf_op jit(solution)/shard_map/ppermute | solution.py:59
  120.8 44.5 %collective-permute-start.8 = (f32[256,1024]{1,0:T(8,128)S(1)}, f32[256,1024]{1,0:T(8,128)}, u32[]{:S(2)}, u32[]{:S(2)}) collective-permute-start(f32[256,1024]{1,0:T(8,128)S(1)} %add.87), channel_id=1, source_target_pairs={{3,1},{4,6},{9,11},{14,12},{19,17},{20,22},{25,27},{30,28}} | collective-permute-start | bytes 3145736 | tf_op jit(solution)/shard_map/ppermute | solution.py:69
  123.3 9.5 %collective-permute-start.9 = (f32[256,1024]{1,0:T(8,128)S(1)}, f32[256,1024]{1,0:T(8,128)S(1)}, u32[]{:S(2)}, u32[]{:S(2)}) collective-permute-start(f32[256,1024]{1,0:T(8,128)S(1)} %fusion.82), channel_id=1, source_target_pairs={{0,1},{2,3},{5,4},{7,6},{8,9},{10,11},{13,12},{15,14},{16,17},{18,... | collective-permute-start | bytes 3145736 | tf_op jit(solution)/shard_map/ppermute | solution.py:59
  124.8 27.7 %collective-permute-start.5 = (bf16[4,128,1024]{2,1,0:T(8,128)(2,1)S(1)}, bf16[4,128,1024]{2,1,0:T(8,128)(2,1)S(1)}, u32[]{:S(2)}, u32[]{:S(2)}) collective-permute-start(bf16[4,128,1024]{2,1,0:T(8,128)(2,1)S(1)} %slice.32), channel_id=1, source_target_pairs={{0,4},{4,8},{8,12},{12,0},{1,5},{5,9},{9,13},{13,1},{2,6},{6,10},{... | collective-permute-start | bytes 3145736 | tf_op jit(solution)/shard_map/ppermute | solution.py:107
  131.4 26.6 %collective-permute-start.11 = (f32[128,1024]{1,0:T(8,128)S(1)}, f32[128,1024]{1,0:T(8,128)S(1)}, u32[]{:S(2)}, u32[]{:S(2)}) collective-permute-start(f32[128,1024]{1,0:T(8,128)S(1)} %fusion.139), channel_id=1, source_target_pairs={{1,0},{3,2},{4,5},{6,7},{9,8},{11,10},{12,13},{14,15},{17,16},{19,... | collective-permute-start | bytes 1572872 | tf_op jit(solution)/shard_map/ppermute | solution.py:59
  132.9 35.0 %collective-permute-start.10 = (f32[256,1024]{1,0:T(8,128)S(1)}, f32[256,1024]{1,0:T(8,128)}, u32[]{:S(2)}, u32[]{:S(2)}) collective-permute-start(f32[256,1024]{1,0:T(8,128)S(1)} %add.92), channel_id=1, source_target_pairs={{1,3},{6,4},{11,9},{12,14},{17,19},{22,20},{27,25},{28,30}} | collective-permute-start | bytes 3145736 | tf_op jit(solution)/shard_map/ppermute | solution.py:69
  156.8 9.9 %collective-permute-start.6 = (f32[128,1024]{1,0:T(8,128)}, f32[128,1024]{1,0:T(8,128)}, u32[]{:S(2)}, u32[]{:S(2)}) collective-permute-start(f32[128,1024]{1,0:T(8,128)} %fusion.124), channel_id=1, source_target_pairs={{1,0},{3,2},{4,5},{6,7},{9,8},{11,10},{12,13},{14,15},{17,16},{19,... | collective-permute-start | bytes 1572872 | tf_op jit(solution)/shard_map/ppermute | solution.py:59
  158.9 12.5 %collective-permute-start.12 = (f32[128,1024]{1,0:T(8,128)}, f32[128,1024]{1,0:T(8,128)}, u32[]{:S(2)}, u32[]{:S(2)}) collective-permute-start(f32[128,1024]{1,0:T(8,128)} %add.97), channel_id=1, source_target_pairs={{0,2},{5,7},{10,8},{15,13},{16,18},{21,23},{26,24},{31,29}} | collective-permute-start | bytes 1572872 | tf_op jit(solution)/shard_map/ppermute | solution.py:69
  172.9 11.1 %collective-permute-start.13 = (f32[128,1024]{1,0:T(8,128)S(1)}, f32[128,1024]{1,0:T(8,128)S(1)}, u32[]{:S(2)}, u32[]{:S(2)}) collective-permute-start(f32[128,1024]{1,0:T(8,128)S(1)} %add.83), channel_id=1, source_target_pairs={{0,2},{5,7},{10,8},{15,13},{16,18},{21,23},{26,24},{31,29}} | collective-permute-start | bytes 1572872 | tf_op jit(solution)/shard_map/ppermute | solution.py:69

commit v10 on v9

--- a/solution.py
+++ b/solution.py
@@ -73,7 +73,7 @@
 def ring(train_features, query_features, residual_weights, keepers, scale):
     planes, ratio = keepers.planes, keepers.ratio
     rows = query_features.shape[1]
-    cut = rows // 2
+    cut = 3 * rows // 8
     right = [(s, (s + 1) % planes) for s in range(planes)]
     left = [(s, (s - 1) % planes) for s in range(planes)]
     parts = []
@@ -81,7 +81,7 @@
     def finish(queries, step, *earlier):
         blocks = [(s + step) % planes for s in range(planes)]
         found = weighted(list(queries), train_features, residual_weights, scale)
-        whole = keepers.far_sums(after(keepers.near_sums(found, blocks), *earlier), blocks)
+        whole = keepers.far_sums(keepers.near_sums(after(found, *earlier), blocks), blocks)
         parts.append((blocks, whole))
         return whole
 
@@ -105,10 +105,10 @@
             finish(from_left, -step)
     low = lax.ppermute(from_right[:, cut:], "ex", left)
     top = lax.ppermute(after(from_left[:, :cut], low, own), "ex", right)
-    behind = finish(after(from_left, low), -(planes // 2 - 1))
+    behind = finish(from_left, -(planes // 2 - 1), low, ahead)
     earlier = list(parts)
     below = finish(low, planes // 2)
-    above = finish(top, planes // 2, ahead, behind, below)
+    above = finish(after(top, behind), planes // 2, below)
     across = parts[-1][0]
     tops = chosen([(blocks, whole[:cut]) for blocks, whole in earlier] + [(across, above)])
     lows = chosen([(blocks, whole[cut:]) for blocks, whole in earlier] + [(across, below)])

time: 186 us -> 174 us (0.935)
  starting transfers between devices: 34.6 us -> 24.3 us
  matrix products: 22.3 us -> 29.7 us
  waiting for transfers between devices: 119 us -> 112 us
  other arithmetic: 8.19 us -> 5.08 us
    ppermute x1, waiting for transfers between devices: 17.9 us -> 5.39 us  [ring(): top = lax.ppermute(after(from_left[:, :cut], low, own), 'ex', right)]
    dot_general x20, matrix products: 22.3 us -> 29.7 us  [weighted(): lax.dot_general(piece, examples, (((1,), (1,)), ((), ())), preferred_elem...]
    ppermute x5, starting transfers between devices: 15.4 us -> 8.44 us  [far_sums(): whole = whole + lax.ppermute(total, PLACE, pairs)]
    ppermute x5, waiting for transfers between devices: 3.2 us -> 7.39 us  [near_sums(): total = total + lax.ppermute(partial, PLACE, pairs)]
    ppermute x1, waiting for transfers between devices: 30.9 us -> 34.8 us  [ring(): from_right = lax.ppermute(from_right, 'ex', left)]
    ppermute x5, waiting for transfers between devices: 8.82 us -> 5.26 us  [far_sums(): whole = whole + lax.ppermute(total, PLACE, pairs)]
    ppermute x1, starting transfers between devices: 3.23 us -> 0.06 us  [ring(): top = lax.ppermute(after(from_left[:, :cut], low, own), 'ex', right)]
    ppermute x1, waiting for transfers between devices: 21.1 us -> 23.6 us  [ring(): low = lax.ppermute(from_right[:, cut:], 'ex', left)]
  transfers between devices with their start and end apart: 14 -> 14, of which waited for: 7 -> 7; matrix products, arithmetic and copies ran while one was open for 15% -> 20% of each run, Pallas kernels for 0% -> 0%
where the time goes in v10:
time: 174 us; the launch traced here: 173 us
  waiting for transfers between devices  112 us (64%)
  matrix products  29.7 us (17%)
  starting transfers between devices  24.3 us (14%)
  other arithmetic  5.08 us (3%)
  local copies, waits for them, and re-layouts  1.92 us (1%)
    ppermute x1, waiting for transfers between devices, ring(): from_left = lax.ppermute(from_left, 'ex', right)  35.2 us
    ppermute x1, waiting for transfers between devices, ring(): from_right = lax.ppermute(from_right, 'ex', left)  34.8 us
    dot_general x20, matrix products, weighted(): lax.dot_general(piece, examples, (((1,), (1,)), ((), ())), preferred_elem...  29.7 us
    ppermute x1, waiting for transfers between devices, ring(): low = lax.ppermute(from_right[:, cut:], 'ex', left)  23.6 us
    ppermute x5, starting transfers between devices, far_sums(): whole = whole + lax.ppermute(total, PLACE, pairs)  8.44 us
    ppermute x5, waiting for transfers between devices, near_sums(): total = total + lax.ppermute(partial, PLACE, pairs)  7.39 us
    ppermute x5, starting transfers between devices, near_sums(): total = total + lax.ppermute(partial, PLACE, pairs)  7.14 us
    ppermute x1, waiting for transfers between devices, ring(): top = lax.ppermute(after(from_left[:, :cut], low, own), 'ex', right)  5.39 us
  transfers between devices with their start and end apart: 14, of which 7 were waited for; matrix products, arithmetic and copies ran while one was open for 20% of the time, Pallas kernels for 0%

profile of v10, /device:TPU:0, one launch (start us, length us, event | category | flops | bytes accessed | tf_op | source)
XLA Modules:
  0.0 173.1 jit_solution(13013552653875531059)
XLA Ops:
  0.0 5.0 %collective-permute-start.1 = (bf16[4,256,1024]{2,1,0:T(8,128)(2,1)}, bf16[4,256,1024]{2,1,0:T(8,128)(2,1)S(1)}, u32[]{:S(2)}, u32[]{:S(2)}) collective-permute-start(bf16[4,256,1024]{2,1,0:T(8,128)(2,1)} %param.4), channel_id=1, source_target_pairs={{0,12},{4,0},{8,4},{12,8},{1,13},{5,1},{9,5},{13,9},{2,14},{6,2},{... | collective-permute-start | bytes 6291464 | tf_op jit(solution)/shard_map/ppermute | solution.py:99
  5.1 0.9 fusion.200
  6.0 2.6 %fusion.103 = f32[256,1024]{1,0:T(8,128)S(1)} fusion(bf16[4,1024,1024]{2,1,0:T(8,128)(2,1)} %param.3, f32[1024]{0:T(1024)S(1)} %bitcast.203, bf16[4,256,1024]{2,1,0:T(8,128)(2,1)} %param.4), kind=kOutput, calls=%fused_computation.61 | convolution fusion | flops 537133056 | bytes 3674112 | tf_op jit(solution)/shard_map/dot_general | solution.py:16
  8.6 3.0 %fusion.85 = f32[256,1024]{1,0:T(8,128)S(1)} fusion(bf16[4,1024,1024]{2,1,0:T(8,128)(2,1)} %param.3, f32[1024]{0:T(1024)S(1)} %bitcast.198, bf16[4,256,1024]{2,1,0:T(8,128)(2,1)} %param.4), kind=kOutput, calls=%fused_computation.55 | convolution fusion | flops 537133056 | bytes 3674112 | tf_op jit(solution)/shard_map/dot_general | solution.py:16
  11.6 1.8 %fusion.94 = f32[256,1024]{1,0:T(8,128)S(1)} fusion(bf16[4,1024,1024]{2,1,0:T(8,128)(2,1)S(1)} %copy-done, f32[1024]{0:T(1024)S(1)} %bitcast.193, bf16[4,256,1024]{2,1,0:T(8,128)(2,1)} %param.4), kind=kOutput, calls=%fused_computation.58 | convolution fusion | flops 537133056 | bytes 3674112 | tf_op jit(solution)/shard_map/dot_general | solution.py:16
  13.4 1.9 %fusion.52 = f32[256,1024]{1,0:T(8,128)S(1)} fusion(f32[256,1024]{1,0:T(8,128)S(1)} %fusion.103, f32[256,1024]{1,0:T(8,128)S(1)} %fusion.94, f32[256,1024]{1,0:T(8,128)S(1)} %fusion.85, bf16[4,1024,1024]{2,1,0:T(8,128)(2,1)S(1)} %copy-done, f32[1024]{0:T(1024)S(1)} %bitcast.188, bf16[4,256,1024]{2,1,0:T(8,128)(2,1)} %param.4), kind=kOutput, calls=%fused_computation.44 | convolution fusion | flops 538181632 | bytes 6819840 | tf_op jit(solution)/shard_map/dot_general | solution.py:16
  15.3 1.3 collective-permute-start.3
  16.6 34.8 %collective-permute-done.1 = bf16[4,256,1024]{2,1,0:T(8,128)(2,1)S(1)} collective-permute-done((bf16[4,256,1024]{2,1,0:T(8,128)(2,1)}, bf16[4,256,1024]{2,1,0:T(8,128)(2,1)S(1)}, u32[]{:S(2)}, u32[]{:S(2)}) %collective-permute-start.1) | collective-permute-done | bytes 2097184 | tf_op jit(solution)/shard_map/ppermute | solution.py:99
  51.4 0.7 fusion.100
  52.2 0.7 fusion.109
  52.9 0.7 fusion.91
  53.7 0.8 fusion.82
  54.5 1.4 collective-permute-start.6
  55.9 0.2 add.78
  56.1 1.3 collective-permute-start.4
  57.5 3.6 %collective-permute-start.2 = (bf16[4,160,1024]{2,1,0:T(8,128)(2,1)S(1)}, bf16[4,160,1024]{2,1,0:T(8,128)(2,1)S(1)}, u32[]{:S(2)}, u32[]{:S(2)}) collective-permute-start(bf16[4,160,1024]{2,1,0:T(8,128)(2,1)S(1)} %slice.33), channel_id=1, source_target_pairs={{0,12},{4,0},{8,4},{12,8},{1,13},{5,1},{9,5},{13,9},{2,14},{6,2},{... | collective-permute-start | bytes 3932168 | tf_op jit(solution)/shard_map/ppermute | solution.py:106
  61.1 0.2 add.86
  61.3 0.7 collective-permute-start.7
  62.0 35.2 %collective-permute-done = bf16[4,256,1024]{2,1,0:T(8,128)(2,1)S(1)} collective-permute-done((bf16[4,256,1024]{2,1,0:T(8,128)(2,1)}, bf16[4,256,1024]{2,1,0:T(8,128)(2,1)S(1)}, u32[]{:S(2)}, u32[]{:S(2)}) %collective-permute-start) | collective-permute-done | bytes 2097184 | tf_op jit(solution)/shard_map/ppermute | solution.py:100
  97.2 0.7 fusion.106
  97.9 0.7 fusion.88
  98.7 0.7 fusion.97
  99.4 0.8 fusion.67
  100.5 23.6 %collective-permute-done.2 = bf16[4,160,1024]{2,1,0:T(8,128)(2,1)S(1)} collective-permute-done((bf16[4,160,1024]{2,1,0:T(8,128)(2,1)S(1)}, bf16[4,160,1024]{2,1,0:T(8,128)(2,1)S(1)}, u32[]{:S(2)}, u32[]{:S(2)}) %collective-permute-start.2) | collective-permute-done | bytes 1310752 | tf_op jit(solution)/shard_map/ppermute | solution.py:106
  124.1 1.9 %collective-permute-start.8 = (f32[256,1024]{1,0:T(8,128)S(1)}, f32[256,1024]{1,0:T(8,128)S(1)}, u32[]{:S(2)}, u32[]{:S(2)}) collective-permute-start(f32[256,1024]{1,0:T(8,128)S(1)} %fusion.67), channel_id=1, source_target_pairs={{0,1},{2,3},{5,4},{7,6},{8,9},{10,11},{13,12},{15,14},{16,17},{18,... | collective-permute-start | bytes 3145736 | tf_op jit(solution)/shard_map/ppermute | solution.py:59
  126.0 0.9 slice.32
  127.2 0.8 fusion.127
  128.0 0.8 fusion.130
  129.0 1.6 collective-permute-start.9
  130.7 0.8 fusion.133
  131.5 1.7 %fusion.124 = f32[160,1024]{1,0:T(8,128)} fusion(f32[160,1024]{1,0:T(8,128)S(1)} %fusion.133, f32[160,1024]{1,0:T(8,128)S(1)} %fusion.130, f32[160,1024]{1,0:T(8,128)S(1)} %fusion.127, bf16[4,1024,1024]{2,1,0:T(8,128)(2,1)S(1)} %copy-done, bf16[4,160,1024]{2,1,0:T(8,128)(2,1)S(1)} %collective-permute-done.2, f32[1024]{0:T(1024)S(1)} %bitcast.191), kind=kOutput, calls=%fused_computation.68 | convolution fusion | flops 336363520 | bytes 5050368 | tf_op jit(solution)/shard_map/dot_general | solution.py:16
  133.2 1.3 collective-permute-start.10
  134.6 5.1 %collective-permute-done.10 = f32[160,1024]{1,0:T(8,128)} collective-permute-done((f32[160,1024]{1,0:T(8,128)}, f32[160,1024]{1,0:T(8,128)}, u32[]{:S(2)}, u32[]{:S(2)}) %collective-permute-start.10) | collective-permute-done | bytes 655392 | tf_op jit(solution)/shard_map/ppermute | solution.py:59
  139.7 1.4 add.96
  141.0 1.3 collective-permute-start.11
  142.4 1.4 add.89
  143.8 5.4 %collective-permute-done.5 = bf16[4,96,1024]{2,1,0:T(8,128)(2,1)} collective-permute-done((bf16[4,96,1024]{2,1,0:T(8,128)(2,1)}, bf16[4,96,1024]{2,1,0:T(8,128)(2,1)}, u32[]{:S(2)}, u32[]{:S(2)}) %collective-permute-start.5) | collective-permute-done | bytes 786464 | tf_op jit(solution)/shard_map/ppermute | solution.py:107
  149.1 2.5 %fusion.136 = f32[96,1024]{1,0:T(8,128)S(1)} fusion(bf16[4,1024,1024]{2,1,0:T(8,128)(2,1)} %param.3, f32[1024]{0:T(1024)S(1)} %bitcast.192, bf16[4,96,1024]{2,1,0:T(8,128)(2,1)} %collective-permute-done.5), kind=kOutput, calls=%fused_computation.72 | convolution fusion | flops 201424896 | bytes 2691072 | tf_op jit(solution)/shard_map/dot_general | solution.py:16
  151.6 2.5 %fusion.154 = f32[96,1024]{1,0:T(8,128)S(1)} fusion(f32[96,1024]{1,0:T(8,128)S(1)} %fusion.136, bf16[4,1024,1024]{2,1,0:T(8,128)(2,1)} %param.3, f32[1024]{0:T(1024)S(1)} %bitcast.202, bf16[4,96,1024]{2,1,0:T(8,128)(2,1)} %collective-permute-done.5), kind=kOutput, calls=%fused_computation.78 | convolution fusion | flops 201523200 | bytes 3084288 | tf_op jit(solution)/shard_map/dot_general | solution.py:16
  154.1 2.5 %fusion.151 = f32[96,1024]{1,0:T(8,128)S(1)} fusion(f32[96,1024]{1,0:T(8,128)S(1)} %fusion.154, bf16[4,1024,1024]{2,1,0:T(8,128)(2,1)} %param.3, f32[1024]{0:T(1024)S(1)} %bitcast.197, bf16[4,96,1024]{2,1,0:T(8,128)(2,1)} %collective-permute-done.5), kind=kOutput, calls=%fused_computation.77 | convolution fusion | flops 201523200 | bytes 3084288 | tf_op jit(solution)/shard_map/dot_general | solution.py:16
  156.6 2.5 %fusion.157 = f32[96,1024]{1,0:T(8,128)S(1)} fusion(f32[96,1024]{1,0:T(8,128)S(1)} %fusion.151, bf16[4,1024,1024]{2,1,0:T(8,128)(2,1)} %param.3, f32[1024]{0:T(1024)S(1)} %bitcast.207, bf16[4,96,1024]{2,1,0:T(8,128)(2,1)} %collective-permute-done.5), kind=kOutput, calls=%fused_computation.79 | convolution fusion | flops 201621504 | bytes 3084288 | tf_op jit(solution)/shard_map/dot_general | solution.py:16
  159.1 0.3 fusion.181
  159.5 1.3 collective-permute-start.12
  160.8 2.3 %collective-permute-done.12 = f32[96,1024]{1,0:T(8,128)S(1)} collective-permute-done((f32[96,1024]{1,0:T(8,128)S(1)}, f32[96,1024]{1,0:T(8,128)S(1)}, u32[]{:S(2)}, u32[]{:S(2)}) %collective-permute-start.12) | collective-permute-done | bytes 393248 | tf_op jit(solution)/shard_map/ppermute | solution.py:59
  163.2 3.4 %collective-permute-start.13 = (f32[96,1024]{1,0:T(8,128)S(1)}, f32[96,1024]{1,0:T(8,128)S(1)}, u32[]{:S(2)}, u32[]{:S(2)}) collective-permute-start(f32[96,1024]{1,0:T(8,128)S(1)} %add.98), channel_id=1, source_target_pairs={{0,2},{5,7},{10,8},{15,13},{16,18},{21,23},{26,24},{31,29}} | collective-permute-start | bytes 1179656 | tf_op jit(solution)/shard_map/ppermute | solution.py:69
  166.6 5.3 %collective-permute-done.13 = f32[96,1024]{1,0:T(8,128)S(1)} collective-permute-done((f32[96,1024]{1,0:T(8,128)S(1)}, f32[96,1024]{1,0:T(8,128)S(1)}, u32[]{:S(2)}, u32[]{:S(2)}) %collective-permute-start.13) | collective-permute-done | bytes 393248 | tf_op jit(solution)/shard_map/ppermute | solution.py:69
  171.8 0.2 fusion.191
  172.0 1.0 pad_maximum_fusion
  (16 shorter events, 0.6 us)
Async XLA Ops:
  0.0 51.4 %collective-permute-start.1 = (bf16[4,256,1024]{2,1,0:T(8,128)(2,1)}, bf16[4,256,1024]{2,1,0:T(8,128)(2,1)S(1)}, u32[]{:S(2)}, u32[]{:S(2)}) collective-permute-start(bf16[4,256,1024]{2,1,0:T(8,128)(2,1)} %param.4), channel_id=1, source_target_pairs={{0,12},{4,0},{8,4},{12,8},{1,13},{5,1},{9,5},{13,9},{2,14},{6,2},{... | collective-permute-start | bytes 6291464 | tf_op jit(solution)/shard_map/ppermute | solution.py:99
  5.0 92.1 %collective-permute-start = (bf16[4,256,1024]{2,1,0:T(8,128)(2,1)}, bf16[4,256,1024]{2,1,0:T(8,128)(2,1)S(1)}, u32[]{:S(2)}, u32[]{:S(2)}) collective-permute-start(bf16[4,256,1024]{2,1,0:T(8,128)(2,1)} %param.4), channel_id=1, source_target_pairs={{0,4},{4,8},{8,12},{12,0},{1,5},{5,9},{9,13},{13,1},{2,6},{6,10},{... | collective-permute-start | bytes 6291464 | tf_op jit(solution)/shard_map/ppermute | solution.py:100
  5.9 5.7 %copy-start = (bf16[4,1024,1024]{2,1,0:T(8,128)(2,1)S(1)}, bf16[4,1024,1024]{2,1,0:T(8,128)(2,1)}, u32[]{:S(2)}) copy-start(bf16[4,1024,1024]{2,1,0:T(8,128)(2,1)} %param.3) | copy-start | bytes 25165828
  15.3 40.6 %collective-permute-start.3 = (f32[256,1024]{1,0:T(8,128)S(1)}, f32[256,1024]{1,0:T(8,128)S(1)}, u32[]{:S(2)}, u32[]{:S(2)}) collective-permute-start(f32[256,1024]{1,0:T(8,128)S(1)} %fusion.52), channel_id=1, source_target_pairs={{1,0},{3,2},{4,5},{6,7},{9,8},{11,10},{12,13},{14,15},{17,16},{19,... | collective-permute-start | bytes 3145736 | tf_op jit(solution)/shard_map/ppermute | solution.py:59
  54.5 6.6 %collective-permute-start.6 = (f32[256,1024]{1,0:T(8,128)S(1)}, f32[256,1024]{1,0:T(8,128)S(1)}, u32[]{:S(2)}, u32[]{:S(2)}) collective-permute-start(f32[256,1024]{1,0:T(8,128)S(1)} %fusion.82), channel_id=1, source_target_pairs={{0,1},{2,3},{5,4},{7,6},{8,9},{10,11},{13,12},{15,14},{16,17},{18,... | collective-permute-start | bytes 3145736 | tf_op jit(solution)/shard_map/ppermute | solution.py:59
  56.1 70.9 %collective-permute-start.4 = (f32[256,1024]{1,0:T(8,128)S(1)}, f32[256,1024]{1,0:T(8,128)S(1)}, u32[]{:S(2)}, u32[]{:S(2)}) collective-permute-start(f32[256,1024]{1,0:T(8,128)S(1)} %add.78), channel_id=1, source_target_pairs={{2,0},{7,5},{8,10},{13,15},{18,16},{23,21},{24,26},{29,31}} | collective-permute-start | bytes 3145736 | tf_op jit(solution)/shard_map/ppermute | solution.py:69
  57.5 66.6 %collective-permute-start.2 = (bf16[4,160,1024]{2,1,0:T(8,128)(2,1)S(1)}, bf16[4,160,1024]{2,1,0:T(8,128)(2,1)S(1)}, u32[]{:S(2)}, u32[]{:S(2)}) collective-permute-start(bf16[4,160,1024]{2,1,0:T(8,128)(2,1)S(1)} %slice.33), channel_id=1, source_target_pairs={{0,12},{4,0},{8,4},{12,8},{1,13},{5,1},{9,5},{13,9},{2,14},{6,2},{... | collective-permute-start | bytes 3932168 | tf_op jit(solution)/shard_map/ppermute | solution.py:106
  61.3 39.0 %collective-permute-start.7 = (f32[256,1024]{1,0:T(8,128)S(1)}, f32[256,1024]{1,0:T(8,128)S(1)}, u32[]{:S(2)}, u32[]{:S(2)}) collective-permute-start(f32[256,1024]{1,0:T(8,128)S(1)} %add.86), channel_id=1, source_target_pairs={{3,1},{4,6},{9,11},{14,12},{19,17},{20,22},{25,27},{30,28}} | collective-permute-start | bytes 3145736 | tf_op jit(solution)/shard_map/ppermute | solution.py:69
  124.1 4.8 %collective-permute-start.8 = (f32[256,1024]{1,0:T(8,128)S(1)}, f32[256,1024]{1,0:T(8,128)S(1)}, u32[]{:S(2)}, u32[]{:S(2)}) collective-permute-start(f32[256,1024]{1,0:T(8,128)S(1)} %fusion.67), channel_id=1, source_target_pairs={{0,1},{2,3},{5,4},{7,6},{8,9},{10,11},{13,12},{15,14},{16,17},{18,... | collective-permute-start | bytes 3145736 | tf_op jit(solution)/shard_map/ppermute | solution.py:59
  127.1 22.0 %collective-permute-start.5 = (bf16[4,96,1024]{2,1,0:T(8,128)(2,1)}, bf16[4,96,1024]{2,1,0:T(8,128)(2,1)}, u32[]{:S(2)}, u32[]{:S(2)}) collective-permute-start(bf16[4,96,1024]{2,1,0:T(8,128)(2,1)} %slice.32), channel_id=1, source_target_pairs={{0,4},{4,8},{8,12},{12,0},{1,5},{5,9},{9,13},{13,1},{2,6},{6,10},{... | collective-permute-start | bytes 2359304 | tf_op jit(solution)/shard_map/ppermute | solution.py:107
  129.0 13.4 %collective-permute-start.9 = (f32[256,1024]{1,0:T(8,128)S(1)}, f32[256,1024]{1,0:T(8,128)}, u32[]{:S(2)}, u32[]{:S(2)}) collective-permute-start(f32[256,1024]{1,0:T(8,128)S(1)} %add.88), channel_id=1, source_target_pairs={{1,3},{6,4},{11,9},{12,14},{17,19},{22,20},{27,25},{28,30}} | collective-permute-start | bytes 3145736 | tf_op jit(solution)/shard_map/ppermute | solution.py:69
  133.2 6.4 %collective-permute-start.10 = (f32[160,1024]{1,0:T(8,128)}, f32[160,1024]{1,0:T(8,128)}, u32[]{:S(2)}, u32[]{:S(2)}) collective-permute-start(f32[160,1024]{1,0:T(8,128)} %fusion.124), channel_id=1, source_target_pairs={{1,0},{3,2},{4,5},{6,7},{9,8},{11,10},{12,13},{14,15},{17,16},{19,... | collective-permute-start | bytes 1966088 | tf_op jit(solution)/shard_map/ppermute | solution.py:59
  141.0 18.1 %collective-permute-start.11 = (f32[160,1024]{1,0:T(8,128)S(1)}, f32[160,1024]{1,0:T(8,128)S(1)}, u32[]{:S(2)}, u32[]{:S(2)}) collective-permute-start(f32[160,1024]{1,0:T(8,128)S(1)} %add.96), channel_id=1, source_target_pairs={{0,2},{5,7},{10,8},{15,13},{16,18},{21,23},{26,24},{31,29}} | collective-permute-start | bytes 1966088 | tf_op jit(solution)/shard_map/ppermute | solution.py:69
  159.5 3.6 %collective-permute-start.12 = (f32[96,1024]{1,0:T(8,128)S(1)}, f32[96,1024]{1,0:T(8,128)S(1)}, u32[]{:S(2)}, u32[]{:S(2)}) collective-permute-start(f32[96,1024]{1,0:T(8,128)S(1)} %fusion.157), channel_id=1, source_target_pairs={{1,0},{3,2},{4,5},{6,7},{9,8},{11,10},{12,13},{14,15},{17,16},{19,... | collective-permute-start | bytes 1179656 | tf_op jit(solution)/shard_map/ppermute | solution.py:59
  163.2 8.7 %collective-permute-start.13 = (f32[96,1024]{1,0:T(8,128)S(1)}, f32[96,1024]{1,0:T(8,128)S(1)}, u32[]{:S(2)}, u32[]{:S(2)}) collective-permute-start(f32[96,1024]{1,0:T(8,128)S(1)} %add.98), channel_id=1, source_target_pairs={{0,2},{5,7},{10,8},{15,13},{16,18},{21,23},{26,24},{31,29}} | collective-permute-start | bytes 1179656 | tf_op jit(solution)/shard_map/ppermute | solution.py:69

commit v11 on v10

--- a/solution.py
+++ b/solution.py
@@ -73,7 +73,7 @@
 def ring(train_features, query_features, residual_weights, keepers, scale):
     planes, ratio = keepers.planes, keepers.ratio
     rows = query_features.shape[1]
-    cut = 3 * rows // 8
+    cut = rows // 4
     right = [(s, (s + 1) % planes) for s in range(planes)]
     left = [(s, (s - 1) % planes) for s in range(planes)]
     parts = []

time: 174 us -> 188 us (1.080)
  waiting for transfers between devices: 112 us -> 127 us
  matrix products: 29.7 us -> 27.2 us
    ppermute x1, waiting for transfers between devices: 34.8 us -> 45.5 us  [ring(): from_right = lax.ppermute(from_right, 'ex', left)]
    ppermute x1, waiting for transfers between devices: 35.2 us -> 27.8 us  [ring(): from_left = lax.ppermute(from_left, 'ex', right)]
    ppermute x5, waiting for transfers between devices: 5.26 us -> 11 us  [far_sums(): whole = whole + lax.ppermute(total, PLACE, pairs)]
    ppermute x1, waiting for transfers between devices: 23.6 us -> 29.2 us  [ring(): low = lax.ppermute(from_right[:, cut:], 'ex', left)]
    dot_general x20, matrix products: 29.7 us -> 27.2 us  [weighted(): lax.dot_general(piece, examples, (((1,), (1,)), ((), ())), preferred_elem...]
  transfers between devices with their start and end apart: 14 -> 14, of which waited for: 7 -> 7; matrix products, arithmetic and copies ran while one was open for 20% -> 17% of each run, Pallas kernels for 0% -> 0%
where the time goes in v11:
time: 188 us; the launch traced here: 187 us
  waiting for transfers between devices  127 us (68%)
  matrix products  27.2 us (14%)
  starting transfers between devices  26 us (14%)
  other arithmetic  5.11 us (3%)
    ppermute x1, waiting for transfers between devices, ring(): from_right = lax.ppermute(from_right, 'ex', left)  45.5 us
    ppermute x1, waiting for transfers between devices, ring(): low = lax.ppermute(from_right[:, cut:], 'ex', left)  29.2 us
    ppermute x1, waiting for transfers between devices, ring(): from_left = lax.ppermute(from_left, 'ex', right)  27.8 us
    dot_general x20, matrix products, weighted(): lax.dot_general(piece, examples, (((1,), (1,)), ((), ())), preferred_elem...  27.2 us
    ppermute x5, waiting for transfers between devices, far_sums(): whole = whole + lax.ppermute(total, PLACE, pairs)  11 us
    ppermute x5, starting transfers between devices, far_sums(): whole = whole + lax.ppermute(total, PLACE, pairs)  9.59 us
    ppermute x5, starting transfers between devices, near_sums(): total = total + lax.ppermute(partial, PLACE, pairs)  7.14 us
    ppermute x1, waiting for transfers between devices, ring(): top = lax.ppermute(after(from_left[:, :cut], low, own), 'ex', right)  6.87 us
  transfers between devices with their start and end apart: 14, of which 7 were waited for; matrix products, arithmetic and copies ran while one was open for 17% of the time, Pallas kernels for 0%

profile of v11, /device:TPU:0, one launch (start us, length us, event | category | flops | bytes accessed | tf_op | source)
XLA Modules:
  0.0 187.3 jit_solution(8514095360500091689)
XLA Ops:
  0.0 5.0 %collective-permute-start.1 = (bf16[4,256,1024]{2,1,0:T(8,128)(2,1)}, bf16[4,256,1024]{2,1,0:T(8,128)(2,1)S(1)}, u32[]{:S(2)}, u32[]{:S(2)}) collective-permute-start(bf16[4,256,1024]{2,1,0:T(8,128)(2,1)} %param.4), channel_id=1, source_target_pairs={{0,12},{4,0},{8,4},{12,8},{1,13},{5,1},{9,5},{13,9},{2,14},{6,2},{... | collective-permute-start | bytes 6291464 | tf_op jit(solution)/shard_map/ppermute | solution.py:99
  5.1 0.9 fusion.200
  5.9 45.5 %collective-permute-done.1 = bf16[4,256,1024]{2,1,0:T(8,128)(2,1)S(1)} collective-permute-done((bf16[4,256,1024]{2,1,0:T(8,128)(2,1)}, bf16[4,256,1024]{2,1,0:T(8,128)(2,1)S(1)}, u32[]{:S(2)}, u32[]{:S(2)}) %collective-permute-start.1) | collective-permute-done | bytes 2097184 | tf_op jit(solution)/shard_map/ppermute | solution.py:99
  51.4 2.5 %fusion.100 = f32[256,1024]{1,0:T(8,128)S(1)} fusion(bf16[4,1024,1024]{2,1,0:T(8,128)(2,1)} %param.3, bf16[4,256,1024]{2,1,0:T(8,128)(2,1)S(1)} %collective-permute-done.1, f32[1024]{0:T(1024)S(1)} %bitcast.198), kind=kOutput, calls=%fused_computation.60 | convolution fusion | flops 537133056 | bytes 3674112 | tf_op jit(solution)/shard_map/dot_general | solution.py:16
  53.9 2.9 %fusion.109 = f32[256,1024]{1,0:T(8,128)S(1)} fusion(bf16[4,1024,1024]{2,1,0:T(8,128)(2,1)} %param.3, bf16[4,256,1024]{2,1,0:T(8,128)(2,1)S(1)} %collective-permute-done.1, f32[1024]{0:T(1024)S(1)} %bitcast.193), kind=kOutput, calls=%fused_computation.63 | convolution fusion | flops 537133056 | bytes 3674112 | tf_op jit(solution)/shard_map/dot_general | solution.py:16
  56.8 0.7 fusion.91
  57.5 0.9 fusion.82
  58.4 1.4 collective-permute-start.6
  59.8 0.7 fusion.103
  60.5 0.7 fusion.85
  61.3 0.7 fusion.94
  62.2 4.2 %collective-permute-start.2 = (bf16[4,192,1024]{2,1,0:T(8,128)(2,1)S(1)}, bf16[4,192,1024]{2,1,0:T(8,128)(2,1)S(1)}, u32[]{:S(2)}, u32[]{:S(2)}) collective-permute-start(bf16[4,192,1024]{2,1,0:T(8,128)(2,1)S(1)} %slice.33), channel_id=1, source_target_pairs={{0,12},{4,0},{8,4},{12,8},{1,13},{5,1},{9,5},{13,9},{2,14},{6,2},{... | collective-permute-start | bytes 4718600 | tf_op jit(solution)/shard_map/ppermute | solution.py:106
  66.3 0.9 fusion.52
  67.2 1.3 collective-permute-start.3
  68.5 0.2 add.86
  68.7 0.7 collective-permute-start.7
  69.4 27.8 %collective-permute-done = bf16[4,256,1024]{2,1,0:T(8,128)(2,1)S(1)} collective-permute-done((bf16[4,256,1024]{2,1,0:T(8,128)(2,1)}, bf16[4,256,1024]{2,1,0:T(8,128)(2,1)S(1)}, u32[]{:S(2)}, u32[]{:S(2)}) %collective-permute-start) | collective-permute-done | bytes 2097184 | tf_op jit(solution)/shard_map/ppermute | solution.py:100
  97.2 0.7 fusion.106
  97.9 0.7 fusion.88
  98.7 0.7 fusion.97
  99.4 0.8 fusion.67
  100.3 0.1 add.87
  100.5 29.2 %collective-permute-done.2 = bf16[4,192,1024]{2,1,0:T(8,128)(2,1)S(1)} collective-permute-done((bf16[4,192,1024]{2,1,0:T(8,128)(2,1)S(1)}, bf16[4,192,1024]{2,1,0:T(8,128)(2,1)S(1)}, u32[]{:S(2)}, u32[]{:S(2)}) %collective-permute-start.2) | collective-permute-done | bytes 1572896 | tf_op jit(solution)/shard_map/ppermute | solution.py:106
  129.7 1.9 %collective-permute-start.8 = (f32[256,1024]{1,0:T(8,128)S(1)}, f32[256,1024]{1,0:T(8,128)S(1)}, u32[]{:S(2)}, u32[]{:S(2)}) collective-permute-start(f32[256,1024]{1,0:T(8,128)S(1)} %fusion.67), channel_id=1, source_target_pairs={{0,1},{2,3},{5,4},{7,6},{8,9},{10,11},{13,12},{15,14},{16,17},{18,... | collective-permute-start | bytes 3145736 | tf_op jit(solution)/shard_map/ppermute | solution.py:59
  131.8 1.3 collective-permute-start.4
  133.1 0.9 fusion.127
  133.9 0.9 fusion.130
  134.8 0.9 fusion.133
  135.7 0.1 add.88
  135.8 1.6 collective-permute-start.9
  137.5 1.8 fusion.124
  139.3 1.3 collective-permute-start.10
  140.5 0.8 slice.32
  141.4 7.1 %collective-permute-done.4 = f32[256,1024]{1,0:T(8,128)S(1)} collective-permute-done((f32[256,1024]{1,0:T(8,128)S(1)}, f32[256,1024]{1,0:T(8,128)S(1)}, u32[]{:S(2)}, u32[]{:S(2)}) %collective-permute-start.4) | collective-permute-done | bytes 1048608 | tf_op jit(solution)/shard_map/ppermute | solution.py:69
  148.8 1.5 add.96
  150.2 1.5 collective-permute-start.11
  151.7 1.4 add.89
  153.1 6.9 %collective-permute-done.5 = bf16[4,64,1024]{2,1,0:T(8,128)(2,1)} collective-permute-done((bf16[4,64,1024]{2,1,0:T(8,128)(2,1)}, bf16[4,64,1024]{2,1,0:T(8,128)(2,1)}, u32[]{:S(2)}, u32[]{:S(2)}) %collective-permute-start.5) | collective-permute-done | bytes 524320 | tf_op jit(solution)/shard_map/ppermute | solution.py:107
  160.0 2.4 %fusion.145 = f32[64,1024]{1,0:T(8,128)S(1)} fusion(bf16[4,1024,1024]{2,1,0:T(8,128)(2,1)} %param.3, f32[1024]{0:T(1024)S(1)} %bitcast.207, bf16[4,64,1024]{2,1,0:T(8,128)(2,1)} %collective-permute-done.5), kind=kOutput, calls=%fused_computation.75 | convolution fusion | flops 134283264 | bytes 2494464 | tf_op jit(solution)/shard_map/dot_general | solution.py:16
  162.4 2.4 %fusion.148 = f32[64,1024]{1,0:T(8,128)S(1)} fusion(bf16[4,1024,1024]{2,1,0:T(8,128)(2,1)} %param.3, f32[1024]{0:T(1024)S(1)} %bitcast.202, bf16[4,64,1024]{2,1,0:T(8,128)(2,1)} %collective-permute-done.5), kind=kOutput, calls=%fused_computation.76 | convolution fusion | flops 134283264 | bytes 2494464 | tf_op jit(solution)/shard_map/dot_general | solution.py:16
  164.8 2.4 %fusion.142 = f32[64,1024]{1,0:T(8,128)S(1)} fusion(f32[64,1024]{1,0:T(8,128)S(1)} %fusion.148, f32[64,1024]{1,0:T(8,128)S(1)} %fusion.145, bf16[4,1024,1024]{2,1,0:T(8,128)(2,1)} %param.3, f32[1024]{0:T(1024)S(1)} %bitcast.192, bf16[4,64,1024]{2,1,0:T(8,128)(2,1)} %collective-permute-done.5), kind=kOutput, calls=%fused_computation.74 | convolution fusion | flops 134414336 | bytes 3018752 | tf_op jit(solution)/shard_map/dot_general | solution.py:16
  167.3 2.4 %fusion.157 = f32[64,1024]{1,0:T(8,128)S(1)} fusion(f32[64,1024]{1,0:T(8,128)S(1)} %fusion.142, bf16[4,1024,1024]{2,1,0:T(8,128)(2,1)} %param.3, f32[1024]{0:T(1024)S(1)} %bitcast.197, bf16[4,64,1024]{2,1,0:T(8,128)(2,1)} %collective-permute-done.5), kind=kOutput, calls=%fused_computation.79 | convolution fusion | flops 134414336 | bytes 2756608 | tf_op jit(solution)/shard_map/dot_general | solution.py:16
  169.7 0.4 fusion.181
  170.1 1.3 collective-permute-start.12
  171.4 6.4 %collective-permute-done.12 = f32[64,1024]{1,0:T(8,128)S(1)} collective-permute-done((f32[64,1024]{1,0:T(8,128)S(1)}, f32[64,1024]{1,0:T(8,128)S(1)}, u32[]{:S(2)}, u32[]{:S(2)}) %collective-permute-start.12) | collective-permute-done | bytes 262176 | tf_op jit(solution)/shard_map/ppermute | solution.py:59
  177.9 4.4 %collective-permute-start.13 = (f32[64,1024]{1,0:T(8,128)S(1)}, f32[64,1024]{1,0:T(8,128)S(1)}, u32[]{:S(2)}, u32[]{:S(2)}) collective-permute-start(f32[64,1024]{1,0:T(8,128)S(1)} %add.98), channel_id=1, source_target_pairs={{0,2},{5,7},{10,8},{15,13},{16,18},{21,23},{26,24},{31,29}} | collective-permute-start | bytes 786440 | tf_op jit(solution)/shard_map/ppermute | solution.py:69
  182.3 3.9 %collective-permute-done.13 = f32[64,1024]{1,0:T(8,128)S(1)} collective-permute-done((f32[64,1024]{1,0:T(8,128)S(1)}, f32[64,1024]{1,0:T(8,128)S(1)}, u32[]{:S(2)}, u32[]{:S(2)}) %collective-permute-start.13) | collective-permute-done | bytes 262176 | tf_op jit(solution)/shard_map/ppermute | solution.py:69
  186.3 1.0 pad_maximum_fusion
  (18 shorter events, 0.6 us)
Async XLA Ops:
  0.0 51.4 %collective-permute-start.1 = (bf16[4,256,1024]{2,1,0:T(8,128)(2,1)}, bf16[4,256,1024]{2,1,0:T(8,128)(2,1)S(1)}, u32[]{:S(2)}, u32[]{:S(2)}) collective-permute-start(bf16[4,256,1024]{2,1,0:T(8,128)(2,1)} %param.4), channel_id=1, source_target_pairs={{0,12},{4,0},{8,4},{12,8},{1,13},{5,1},{9,5},{13,9},{2,14},{6,2},{... | collective-permute-start | bytes 6291464 | tf_op jit(solution)/shard_map/ppermute | solution.py:99
  5.0 92.1 %collective-permute-start = (bf16[4,256,1024]{2,1,0:T(8,128)(2,1)}, bf16[4,256,1024]{2,1,0:T(8,128)(2,1)S(1)}, u32[]{:S(2)}, u32[]{:S(2)}) collective-permute-start(bf16[4,256,1024]{2,1,0:T(8,128)(2,1)} %param.4), channel_id=1, source_target_pairs={{0,4},{4,8},{8,12},{12,0},{1,5},{5,9},{9,13},{13,1},{2,6},{6,10},{... | collective-permute-start | bytes 6291464 | tf_op jit(solution)/shard_map/ppermute | solution.py:100
  51.4 5.4 %copy-start = (bf16[4,1024,1024]{2,1,0:T(8,128)(2,1)S(1)}, bf16[4,1024,1024]{2,1,0:T(8,128)(2,1)}, u32[]{:S(2)}) copy-start(bf16[4,1024,1024]{2,1,0:T(8,128)(2,1)} %param.3) | copy-start | bytes 25165828
  57.5 2.2 %copy-start.1 = (bf16[4,256,1024]{2,1,0:T(8,128)(2,1)S(1)}, bf16[4,256,1024]{2,1,0:T(8,128)(2,1)}, u32[]{:S(2)}) copy-start(bf16[4,256,1024]{2,1,0:T(8,128)(2,1)} %param.4) | copy-start | bytes 6291460
  58.4 10.1 %collective-permute-start.6 = (f32[256,1024]{1,0:T(8,128)S(1)}, f32[256,1024]{1,0:T(8,128)S(1)}, u32[]{:S(2)}, u32[]{:S(2)}) collective-permute-start(f32[256,1024]{1,0:T(8,128)S(1)} %fusion.82), channel_id=1, source_target_pairs={{0,1},{2,3},{5,4},{7,6},{8,9},{10,11},{13,12},{15,14},{16,17},{18,... | collective-permute-start | bytes 3145736 | tf_op jit(solution)/shard_map/ppermute | solution.py:59
  62.2 67.5 %collective-permute-start.2 = (bf16[4,192,1024]{2,1,0:T(8,128)(2,1)S(1)}, bf16[4,192,1024]{2,1,0:T(8,128)(2,1)S(1)}, u32[]{:S(2)}, u32[]{:S(2)}) collective-permute-start(bf16[4,192,1024]{2,1,0:T(8,128)(2,1)S(1)} %slice.33), channel_id=1, source_target_pairs={{0,12},{4,0},{8,4},{12,8},{1,13},{5,1},{9,5},{13,9},{2,14},{6,2},{... | collective-permute-start | bytes 4718600 | tf_op jit(solution)/shard_map/ppermute | solution.py:106
  67.2 64.4 %collective-permute-start.3 = (f32[256,1024]{1,0:T(8,128)S(1)}, f32[256,1024]{1,0:T(8,128)S(1)}, u32[]{:S(2)}, u32[]{:S(2)}) collective-permute-start(f32[256,1024]{1,0:T(8,128)S(1)} %fusion.52), channel_id=1, source_target_pairs={{1,0},{3,2},{4,5},{6,7},{9,8},{11,10},{12,13},{14,15},{17,16},{19,... | collective-permute-start | bytes 3145736 | tf_op jit(solution)/shard_map/ppermute | solution.py:59
  68.7 31.6 %collective-permute-start.7 = (f32[256,1024]{1,0:T(8,128)S(1)}, f32[256,1024]{1,0:T(8,128)S(1)}, u32[]{:S(2)}, u32[]{:S(2)}) collective-permute-start(f32[256,1024]{1,0:T(8,128)S(1)} %add.86), channel_id=1, source_target_pairs={{3,1},{4,6},{9,11},{14,12},{19,17},{20,22},{25,27},{30,28}} | collective-permute-start | bytes 3145736 | tf_op jit(solution)/shard_map/ppermute | solution.py:69
  129.7 6.0 %collective-permute-start.8 = (f32[256,1024]{1,0:T(8,128)S(1)}, f32[256,1024]{1,0:T(8,128)S(1)}, u32[]{:S(2)}, u32[]{:S(2)}) collective-permute-start(f32[256,1024]{1,0:T(8,128)S(1)} %fusion.67), channel_id=1, source_target_pairs={{0,1},{2,3},{5,4},{7,6},{8,9},{10,11},{13,12},{15,14},{16,17},{18,... | collective-permute-start | bytes 3145736 | tf_op jit(solution)/shard_map/ppermute | solution.py:59
  131.8 16.7 %collective-permute-start.4 = (f32[256,1024]{1,0:T(8,128)S(1)}, f32[256,1024]{1,0:T(8,128)S(1)}, u32[]{:S(2)}, u32[]{:S(2)}) collective-permute-start(f32[256,1024]{1,0:T(8,128)S(1)} %add.78), channel_id=1, source_target_pairs={{2,0},{7,5},{8,10},{13,15},{18,16},{23,21},{24,26},{29,31}} | collective-permute-start | bytes 3145736 | tf_op jit(solution)/shard_map/ppermute | solution.py:69
  135.8 15.9 %collective-permute-start.9 = (f32[256,1024]{1,0:T(8,128)S(1)}, f32[256,1024]{1,0:T(8,128)}, u32[]{:S(2)}, u32[]{:S(2)}) collective-permute-start(f32[256,1024]{1,0:T(8,128)S(1)} %add.88), channel_id=1, source_target_pairs={{1,3},{6,4},{11,9},{12,14},{17,19},{22,20},{27,25},{28,30}} | collective-permute-start | bytes 3145736 | tf_op jit(solution)/shard_map/ppermute | solution.py:69
  139.3 9.5 %collective-permute-start.10 = (f32[192,1024]{1,0:T(8,128)}, f32[192,1024]{1,0:T(8,128)}, u32[]{:S(2)}, u32[]{:S(2)}) collective-permute-start(f32[192,1024]{1,0:T(8,128)} %fusion.124), channel_id=1, source_target_pairs={{1,0},{3,2},{4,5},{6,7},{9,8},{11,10},{12,13},{14,15},{17,16},{19,... | collective-permute-start | bytes 2359304 | tf_op jit(solution)/shard_map/ppermute | solution.py:59
  148.6 11.4 %collective-permute-start.5 = (bf16[4,64,1024]{2,1,0:T(8,128)(2,1)}, bf16[4,64,1024]{2,1,0:T(8,128)(2,1)}, u32[]{:S(2)}, u32[]{:S(2)}) collective-permute-start(bf16[4,64,1024]{2,1,0:T(8,128)(2,1)} %slice.32), channel_id=1, source_target_pairs={{0,4},{4,8},{8,12},{12,0},{1,5},{5,9},{9,13},{13,1},{2,6},{6,10},{... | collective-permute-start | bytes 1572872 | tf_op jit(solution)/shard_map/ppermute | solution.py:107
  150.2 19.5 %collective-permute-start.11 = (f32[192,1024]{1,0:T(8,128)S(1)}, f32[192,1024]{1,0:T(8,128)S(1)}, u32[]{:S(2)}, u32[]{:S(2)}) collective-permute-start(f32[192,1024]{1,0:T(8,128)S(1)} %add.96), channel_id=1, source_target_pairs={{0,2},{5,7},{10,8},{15,13},{16,18},{21,23},{26,24},{31,29}} | collective-permute-start | bytes 2359304 | tf_op jit(solution)/shard_map/ppermute | solution.py:69
  170.1 7.7 %collective-permute-start.12 = (f32[64,1024]{1,0:T(8,128)S(1)}, f32[64,1024]{1,0:T(8,128)S(1)}, u32[]{:S(2)}, u32[]{:S(2)}) collective-permute-start(f32[64,1024]{1,0:T(8,128)S(1)} %fusion.157), channel_id=1, source_target_pairs={{1,0},{3,2},{4,5},{6,7},{9,8},{11,10},{12,13},{14,15},{17,16},{19,... | collective-permute-start | bytes 786440 | tf_op jit(solution)/shard_map/ppermute | solution.py:59
  177.9 8.3 %collective-permute-start.13 = (f32[64,1024]{1,0:T(8,128)S(1)}, f32[64,1024]{1,0:T(8,128)S(1)}, u32[]{:S(2)}, u32[]{:S(2)}) collective-permute-start(f32[64,1024]{1,0:T(8,128)S(1)} %add.98), channel_id=1, source_target_pairs={{0,2},{5,7},{10,8},{15,13},{16,18},{21,23},{26,24},{31,29}} | collective-permute-start | bytes 786440 | tf_op jit(solution)/shard_map/ppermute | solution.py:69

commit v12 on v10

--- a/solution.py
+++ b/solution.py
@@ -76,43 +76,47 @@
     cut = 3 * rows // 8
     right = [(s, (s + 1) % planes) for s in range(planes)]
     left = [(s, (s - 1) % planes) for s in range(planes)]
-    parts = []
+    tops, lows = [], []
 
-    def finish(queries, step, *earlier):
+    def finish(queries, step, into, near=(), far=()):
         blocks = [(s + step) % planes for s in range(planes)]
         found = weighted(list(queries), train_features, residual_weights, scale)
-        whole = keepers.far_sums(keepers.near_sums(after(found, *earlier), blocks), blocks)
-        parts.append((blocks, whole))
+        total = keepers.near_sums(after(found, *near) if near else found, blocks)
+        whole = keepers.far_sums(after(total, *far) if far else total, blocks)
+        for parts in into:
+            part = whole
+            if len(into) == 2:
+                part = whole[:cut] if parts is tops else whole[cut:]
+            parts.append((blocks, part))
         return whole
 
     def chosen(parts):
         found = []
         for j in range(ratio):
             kept = None
-            for blocks, whole in parts:
-                kept = whole if kept is None else jnp.where(keepers.mine(blocks, j), whole, kept)
+            for blocks, part in parts:
+                kept = part if kept is None else jnp.where(keepers.mine(blocks, j), part, kept)
             found.append(kept)
         return found
 
+    both = (tops, lows)
+    half = planes // 2
     from_left = from_right = query_features
-    for step in range(1, planes // 2):
+    for step in range(1, half - 1):
         from_right = lax.ppermute(from_right, "ex", left)
         from_left = lax.ppermute(from_left, "ex", right)
-        if step == 1:
-            own = finish(query_features, 0)
-        ahead = finish(from_right, step)
-        if step < planes // 2 - 1:
-            finish(from_left, -step)
+        finish(from_right, step, both)
+        finish(from_left, -step, both)
+    own = finish(query_features, 0, both)
+    from_right = lax.ppermute(from_right, "ex", left)
+    from_left = lax.ppermute(from_left, "ex", right)
     low = lax.ppermute(from_right[:, cut:], "ex", left)
-    top = lax.ppermute(after(from_left[:, :cut], low, own), "ex", right)
-    behind = finish(from_left, -(planes // 2 - 1), low, ahead)
-    earlier = list(parts)
-    below = finish(low, planes // 2)
-    above = finish(after(top, behind), planes // 2, below)
-    across = parts[-1][0]
-    tops = chosen([(blocks, whole[:cut]) for blocks, whole in earlier] + [(across, above)])
-    lows = chosen([(blocks, whole[cut:]) for blocks, whole in earlier] + [(across, below)])
-    return jnp.concatenate([part for both in zip(tops, lows) for part in both], axis=0)
+    top = lax.ppermute(after(from_right[:, :cut], low), "ex", left)
+    ahead = finish(from_right, half - 1, both)
+    behind = finish(from_left, 1 - half, both, far=(low, own, ahead))
+    below = finish(low, half, (lows,))
+    finish(top, half, (tops,), near=(behind,), far=(below,))
+    return jnp.concatenate([part for pair in zip(chosen(tops), chosen(lows)) for part in pair], axis=0)
 
 
 def local(train_features, query_features, residual_weights):

time: 174 us -> 174 us (level)
  matrix products: 29.7 us -> 21.2 us
  starting transfers between devices: 24.3 us -> 30.4 us
  waiting for transfers between devices: 112 us -> 115 us
    dot_general x20, matrix products: 29.7 us -> 21.2 us  [weighted(): lax.dot_general(piece, examples, (((1,), (1,)), ((), ())), preferred_elem...]
    ppermute x5, waiting for transfers between devices: 5.26 us -> 11.1 us  [far_sums(): whole = whole + lax.ppermute(total, PLACE, pairs)]
    ppermute x5, waiting for transfers between devices: 7.39 us -> 11.5 us  [near_sums(): total = total + lax.ppermute(partial, PLACE, pairs)]
    ppermute x1, waiting for transfers between devices: 34.8 us -> 31 us  [ring(): from_right = lax.ppermute(from_right, 'ex', left)]
    ppermute x1, starting transfers between devices: 0.06 us -> 3.42 us  [ring(): top = lax.ppermute(after(from_right[:, :cut], low), 'ex', left)]
    ppermute x1, waiting for transfers between devices: 5.39 us -> 2.53 us  [ring(): top = lax.ppermute(after(from_right[:, :cut], low), 'ex', left)]
    ppermute x5, starting transfers between devices: 8.44 us -> 11.1 us  [far_sums(): whole = whole + lax.ppermute(total, PLACE, pairs)]
    ppermute x1, waiting for transfers between devices: 23.6 us -> 21.5 us  [ring(): low = lax.ppermute(from_right[:, cut:], 'ex', left)]
  transfers between devices with their start and end apart: 14 -> 14, of which waited for: 7 -> 9; matrix products, arithmetic and copies ran while one was open for 20% -> 15% of each run, Pallas kernels for 0% -> 0%
where the time goes in v12:
time: 174 us; the launch traced here: 173 us
  waiting for transfers between devices  115 us (66%)
  starting transfers between devices  30.4 us (17%)
  matrix products  21.2 us (12%)
  other arithmetic  5.65 us (3%)
    ppermute x1, waiting for transfers between devices, ring(): from_left = lax.ppermute(from_left, 'ex', right)  37 us
    ppermute x1, waiting for transfers between devices, ring(): from_right = lax.ppermute(from_right, 'ex', left)  31 us
    ppermute x1, waiting for transfers between devices, ring(): low = lax.ppermute(from_right[:, cut:], 'ex', left)  21.5 us
    dot_general x20, matrix products, weighted(): lax.dot_general(piece, examples, (((1,), (1,)), ((), ())), preferred_elem...  21.2 us
    ppermute x5, waiting for transfers between devices, near_sums(): total = total + lax.ppermute(partial, PLACE, pairs)  11.5 us
    ppermute x5, waiting for transfers between devices, far_sums(): whole = whole + lax.ppermute(total, PLACE, pairs)  11.1 us
    ppermute x5, starting transfers between devices, far_sums(): whole = whole + lax.ppermute(total, PLACE, pairs)  11.1 us
    ppermute x5, starting transfers between devices, near_sums(): total = total + lax.ppermute(partial, PLACE, pairs)  6.59 us
  transfers between devices with their start and end apart: 14, of which 9 were waited for; matrix products, arithmetic and copies ran while one was open for 15% of the time, Pallas kernels for 0%

profile of v12, /device:TPU:0, one launch (start us, length us, event | category | flops | bytes accessed | tf_op | source)
XLA Modules:
  0.0 173.3 jit_solution(8862719566728854355)
XLA Ops:
  0.0 5.0 %collective-permute-start = (bf16[4,256,1024]{2,1,0:T(8,128)(2,1)}, bf16[4,256,1024]{2,1,0:T(8,128)(2,1)S(1)}, u32[]{:S(2)}, u32[]{:S(2)}) collective-permute-start(bf16[4,256,1024]{2,1,0:T(8,128)(2,1)} %param.4), channel_id=1, source_target_pairs={{0,12},{4,0},{8,4},{12,8},{1,13},{5,1},{9,5},{13,9},{2,14},{6,2},{... | collective-permute-start | bytes 6291464 | tf_op jit(solution)/shard_map/ppermute | solution.py:111
  5.0 0.9 fusion.192
  5.9 2.6 %fusion.88 = f32[256,1024]{1,0:T(8,128)S(1)} fusion(bf16[4,1024,1024]{2,1,0:T(8,128)(2,1)} %param.3, bf16[4,256,1024]{2,1,0:T(8,128)(2,1)} %param.4, f32[1024]{0:T(1024)S(1)} %bitcast.193), kind=kOutput, calls=%fused_computation.56 | convolution fusion | flops 537133056 | bytes 3674112 | tf_op jit(solution)/shard_map/dot_general | solution.py:16
  8.6 3.0 %fusion.106 = f32[256,1024]{1,0:T(8,128)S(1)} fusion(bf16[4,1024,1024]{2,1,0:T(8,128)(2,1)} %param.3, bf16[4,256,1024]{2,1,0:T(8,128)(2,1)} %param.4, f32[1024]{0:T(1024)S(1)} %bitcast.203), kind=kOutput, calls=%fused_computation.62 | convolution fusion | flops 537133056 | bytes 3674112 | tf_op jit(solution)/shard_map/dot_general | solution.py:16
  11.6 1.9 %fusion.97 = f32[256,1024]{1,0:T(8,128)S(1)} fusion(bf16[4,1024,1024]{2,1,0:T(8,128)(2,1)S(1)} %copy-done, bf16[4,256,1024]{2,1,0:T(8,128)(2,1)} %param.4, f32[1024]{0:T(1024)S(1)} %bitcast.198), kind=kOutput, calls=%fused_computation.59 | convolution fusion | flops 537133056 | bytes 3674112 | tf_op jit(solution)/shard_map/dot_general | solution.py:16
  13.6 0.9 fusion.67
  14.4 1.3 collective-permute-start.5
  15.8 3.2 %collective-permute-done.5 = f32[256,1024]{1,0:T(8,128)S(1)} collective-permute-done((f32[256,1024]{1,0:T(8,128)S(1)}, f32[256,1024]{1,0:T(8,128)S(1)}, u32[]{:S(2)}, u32[]{:S(2)}) %collective-permute-start.5) | collective-permute-done | bytes 1048608 | tf_op jit(solution)/shard_map/ppermute | solution.py:59
  19.0 0.2 add.85
  19.2 1.3 collective-permute-start.6
  20.5 31.0 %collective-permute-done = bf16[4,256,1024]{2,1,0:T(8,128)(2,1)S(1)} collective-permute-done((bf16[4,256,1024]{2,1,0:T(8,128)(2,1)}, bf16[4,256,1024]{2,1,0:T(8,128)(2,1)S(1)}, u32[]{:S(2)}, u32[]{:S(2)}) %collective-permute-start) | collective-permute-done | bytes 2097184 | tf_op jit(solution)/shard_map/ppermute | solution.py:111
  51.4 0.7 fusion.109
  52.2 0.7 fusion.100
  53.0 0.7 fusion.91
  53.7 0.8 fusion.82
  54.6 1.4 collective-permute-start.7
  56.0 4.2 %collective-permute-start.1 = (bf16[4,160,1024]{2,1,0:T(8,128)(2,1)S(1)}, bf16[4,160,1024]{2,1,0:T(8,128)(2,1)S(1)}, u32[]{:S(2)}, u32[]{:S(2)}) collective-permute-start(bf16[4,160,1024]{2,1,0:T(8,128)(2,1)S(1)} %slice.33), channel_id=1, source_target_pairs={{0,12},{4,0},{8,4},{12,8},{1,13},{5,1},{9,5},{13,9},{2,14},{6,2},{... | collective-permute-start | bytes 3932168 | tf_op jit(solution)/shard_map/ppermute | solution.py:113
  60.2 37.0 %collective-permute-done.3 = bf16[4,256,1024]{2,1,0:T(8,128)(2,1)S(1)} collective-permute-done((bf16[4,256,1024]{2,1,0:T(8,128)(2,1)S(1)}, bf16[4,256,1024]{2,1,0:T(8,128)(2,1)S(1)}, u32[]{:S(2)}, u32[]{:S(2)}) %collective-permute-start.3) | collective-permute-done | bytes 2097184 | tf_op jit(solution)/shard_map/ppermute | solution.py:112
  97.2 0.7 fusion.103
  97.9 0.7 fusion.94
  98.7 0.7 fusion.85
  99.4 0.9 fusion.52
  100.3 1.4 collective-permute-start.4
  101.9 0.7 collective-permute-start.8
  102.6 21.5 %collective-permute-done.1 = bf16[4,160,1024]{2,1,0:T(8,128)(2,1)S(1)} collective-permute-done((bf16[4,160,1024]{2,1,0:T(8,128)(2,1)S(1)}, bf16[4,160,1024]{2,1,0:T(8,128)(2,1)S(1)}, u32[]{:S(2)}, u32[]{:S(2)}) %collective-permute-start.1) | collective-permute-done | bytes 1310752 | tf_op jit(solution)/shard_map/ppermute | solution.py:113
  124.1 3.4 %collective-permute-start.2 = (bf16[4,96,1024]{2,1,0:T(8,128)(2,1)S(1)}, bf16[4,96,1024]{2,1,0:T(8,128)(2,1)S(1)}, u32[]{:S(2)}, u32[]{:S(2)}) collective-permute-start(bf16[4,96,1024]{2,1,0:T(8,128)(2,1)S(1)} %slice.32), channel_id=1, source_target_pairs={{0,12},{4,0},{8,4},{12,8},{1,13},{5,1},{9,5},{13,9},{2,14},{6,2},{... | collective-permute-start | bytes 2359304 | tf_op jit(solution)/shard_map/ppermute | solution.py:114
  127.5 0.8 fusion.133
  128.3 0.8 fusion.130
  129.2 0.8 fusion.127
  130.0 0.9 fusion.124
  130.9 1.3 collective-permute-start.11
  132.6 2.3 %collective-permute-done.11 = f32[160,1024]{1,0:T(8,128)S(1)} collective-permute-done((f32[160,1024]{1,0:T(8,128)S(1)}, f32[160,1024]{1,0:T(8,128)S(1)}, u32[]{:S(2)}, u32[]{:S(2)}) %collective-permute-start.11) | collective-permute-done | bytes 655392 | tf_op jit(solution)/shard_map/ppermute | solution.py:59
  134.9 0.9 add.97
  135.8 4.2 %collective-permute-start.12 = (f32[160,1024]{1,0:T(8,128)}, f32[160,1024]{1,0:T(8,128)}, u32[]{:S(2)}, u32[]{:S(2)}) collective-permute-start(f32[160,1024]{1,0:T(8,128)} %add.97), channel_id=1, source_target_pairs={{0,2},{5,7},{10,8},{15,13},{16,18},{21,23},{26,24},{31,29}} | collective-permute-start | bytes 1966088 | tf_op jit(solution)/shard_map/ppermute | solution.py:69
  140.2 0.7 collective-permute-start.9
  141.0 2.5 %collective-permute-done.2 = bf16[4,96,1024]{2,1,0:T(8,128)(2,1)S(1)} collective-permute-done((bf16[4,96,1024]{2,1,0:T(8,128)(2,1)S(1)}, bf16[4,96,1024]{2,1,0:T(8,128)(2,1)S(1)}, u32[]{:S(2)}, u32[]{:S(2)}) %collective-permute-start.2) | collective-permute-done | bytes 786464 | tf_op jit(solution)/shard_map/ppermute | solution.py:114
  143.5 0.8 fusion.145
  144.3 0.8 fusion.142
  145.1 0.8 fusion.139
  145.9 0.8 fusion.157
  146.9 1.3 collective-permute-start.10
  148.2 5.9 %collective-permute-done.12 = f32[160,1024]{1,0:T(8,128)} collective-permute-done((f32[160,1024]{1,0:T(8,128)}, f32[160,1024]{1,0:T(8,128)}, u32[]{:S(2)}, u32[]{:S(2)}) %collective-permute-start.12) | collective-permute-done | bytes 655392 | tf_op jit(solution)/shard_map/ppermute | solution.py:69
  154.1 1.6 fusion.181
  155.7 6.0 %collective-permute-done.10 = f32[96,1024]{1,0:T(8,128)} collective-permute-done((f32[96,1024]{1,0:T(8,128)S(1)}, f32[96,1024]{1,0:T(8,128)}, u32[]{:S(2)}, u32[]{:S(2)}) %collective-permute-start.10) | collective-permute-done | bytes 393248 | tf_op jit(solution)/shard_map/ppermute | solution.py:59
  161.7 1.0 add.93
  162.7 4.1 %collective-permute-start.13 = (f32[96,1024]{1,0:T(8,128)S(1)}, f32[96,1024]{1,0:T(8,128)S(1)}, u32[]{:S(2)}, u32[]{:S(2)}) collective-permute-start(f32[96,1024]{1,0:T(8,128)S(1)} %add.93), channel_id=1, source_target_pairs={{0,2},{5,7},{10,8},{15,13},{16,18},{21,23},{26,24},{31,29}} | collective-permute-start | bytes 1179656 | tf_op jit(solution)/shard_map/ppermute | solution.py:69
  166.9 5.3 %collective-permute-done.13 = f32[96,1024]{1,0:T(8,128)S(1)} collective-permute-done((f32[96,1024]{1,0:T(8,128)S(1)}, f32[96,1024]{1,0:T(8,128)S(1)}, u32[]{:S(2)}, u32[]{:S(2)}) %collective-permute-start.13) | collective-permute-done | bytes 393248 | tf_op jit(solution)/shard_map/ppermute | solution.py:69
  172.2 1.0 pad_maximum_fusion
  (18 shorter events, 1.1 us)
Async XLA Ops:
  0.0 51.4 %collective-permute-start = (bf16[4,256,1024]{2,1,0:T(8,128)(2,1)}, bf16[4,256,1024]{2,1,0:T(8,128)(2,1)S(1)}, u32[]{:S(2)}, u32[]{:S(2)}) collective-permute-start(bf16[4,256,1024]{2,1,0:T(8,128)(2,1)} %param.4), channel_id=1, source_target_pairs={{0,12},{4,0},{8,4},{12,8},{1,13},{5,1},{9,5},{13,9},{2,14},{6,2},{... | collective-permute-start | bytes 6291464 | tf_op jit(solution)/shard_map/ppermute | solution.py:111
  5.9 5.7 %copy-start = (bf16[4,1024,1024]{2,1,0:T(8,128)(2,1)S(1)}, bf16[4,1024,1024]{2,1,0:T(8,128)(2,1)}, u32[]{:S(2)}) copy-start(bf16[4,1024,1024]{2,1,0:T(8,128)(2,1)} %param.3) | copy-start | bytes 25165828
  11.6 2.0 %copy-start.1 = (bf16[4,256,1024]{2,1,0:T(8,128)(2,1)S(1)}, bf16[4,256,1024]{2,1,0:T(8,128)(2,1)}, u32[]{:S(2)}) copy-start(bf16[4,256,1024]{2,1,0:T(8,128)(2,1)} %param.4) | copy-start | bytes 6291460
  14.4 4.6 %collective-permute-start.5 = (f32[256,1024]{1,0:T(8,128)S(1)}, f32[256,1024]{1,0:T(8,128)S(1)}, u32[]{:S(2)}, u32[]{:S(2)}) collective-permute-start(f32[256,1024]{1,0:T(8,128)S(1)} %fusion.67), channel_id=1, source_target_pairs={{1,0},{3,2},{4,5},{6,7},{9,8},{11,10},{12,13},{14,15},{17,16},{19,... | collective-permute-start | bytes 3145736 | tf_op jit(solution)/shard_map/ppermute | solution.py:59
  15.7 81.4 %collective-permute-start.3 = (bf16[4,256,1024]{2,1,0:T(8,128)(2,1)S(1)}, bf16[4,256,1024]{2,1,0:T(8,128)(2,1)S(1)}, u32[]{:S(2)}, u32[]{:S(2)}) collective-permute-start(bf16[4,256,1024]{2,1,0:T(8,128)(2,1)S(1)} %copy-done.1), channel_id=1, source_target_pairs={{0,4},{4,8},{8,12},{12,0},{1,5},{5,9},{9,13},{13,1},{2,6},{6,10},{... | collective-permute-start | bytes 6291464 | tf_op jit(solution)/shard_map/ppermute | solution.py:112
  19.2 113.1 %collective-permute-start.6 = (f32[256,1024]{1,0:T(8,128)S(1)}, f32[256,1024]{1,0:T(8,128)S(1)}, u32[]{:S(2)}, u32[]{:S(2)}) collective-permute-start(f32[256,1024]{1,0:T(8,128)S(1)} %add.85), channel_id=1, source_target_pairs={{2,0},{7,5},{8,10},{13,15},{18,16},{23,21},{24,26},{29,31}} | collective-permute-start | bytes 3145736 | tf_op jit(solution)/shard_map/ppermute | solution.py:69
  54.6 47.2 %collective-permute-start.7 = (f32[256,1024]{1,0:T(8,128)S(1)}, f32[256,1024]{1,0:T(8,128)S(1)}, u32[]{:S(2)}, u32[]{:S(2)}) collective-permute-start(f32[256,1024]{1,0:T(8,128)S(1)} %fusion.82), channel_id=1, source_target_pairs={{0,1},{2,3},{5,4},{7,6},{8,9},{10,11},{13,12},{15,14},{16,17},{18,... | collective-permute-start | bytes 3145736 | tf_op jit(solution)/shard_map/ppermute | solution.py:59
  56.0 68.1 %collective-permute-start.1 = (bf16[4,160,1024]{2,1,0:T(8,128)(2,1)S(1)}, bf16[4,160,1024]{2,1,0:T(8,128)(2,1)S(1)}, u32[]{:S(2)}, u32[]{:S(2)}) collective-permute-start(bf16[4,160,1024]{2,1,0:T(8,128)(2,1)S(1)} %slice.33), channel_id=1, source_target_pairs={{0,12},{4,0},{8,4},{12,8},{1,13},{5,1},{9,5},{13,9},{2,14},{6,2},{... | collective-permute-start | bytes 3932168 | tf_op jit(solution)/shard_map/ppermute | solution.py:113
  100.3 32.1 %collective-permute-start.4 = (f32[256,1024]{1,0:T(8,128)S(1)}, f32[256,1024]{1,0:T(8,128)S(1)}, u32[]{:S(2)}, u32[]{:S(2)}) collective-permute-start(f32[256,1024]{1,0:T(8,128)S(1)} %fusion.52), channel_id=1, source_target_pairs={{0,1},{2,3},{5,4},{7,6},{8,9},{10,11},{13,12},{15,14},{16,17},{18,... | collective-permute-start | bytes 3145736 | tf_op jit(solution)/shard_map/ppermute | solution.py:59
  101.9 38.2 %collective-permute-start.8 = (f32[256,1024]{1,0:T(8,128)S(1)}, f32[256,1024]{1,0:T(8,128)S(1)}, u32[]{:S(2)}, u32[]{:S(2)}) collective-permute-start(f32[256,1024]{1,0:T(8,128)S(1)} %add.90), channel_id=1, source_target_pairs={{3,1},{4,6},{9,11},{14,12},{19,17},{20,22},{25,27},{30,28}} | collective-permute-start | bytes 3145736 | tf_op jit(solution)/shard_map/ppermute | solution.py:69
  124.1 19.4 %collective-permute-start.2 = (bf16[4,96,1024]{2,1,0:T(8,128)(2,1)S(1)}, bf16[4,96,1024]{2,1,0:T(8,128)(2,1)S(1)}, u32[]{:S(2)}, u32[]{:S(2)}) collective-permute-start(bf16[4,96,1024]{2,1,0:T(8,128)(2,1)S(1)} %slice.32), channel_id=1, source_target_pairs={{0,12},{4,0},{8,4},{12,8},{1,13},{5,1},{9,5},{13,9},{2,14},{6,2},{... | collective-permute-start | bytes 2359304 | tf_op jit(solution)/shard_map/ppermute | solution.py:114
  130.9 4.0 %collective-permute-start.11 = (f32[160,1024]{1,0:T(8,128)S(1)}, f32[160,1024]{1,0:T(8,128)S(1)}, u32[]{:S(2)}, u32[]{:S(2)}) collective-permute-start(f32[160,1024]{1,0:T(8,128)S(1)} %fusion.124), channel_id=1, source_target_pairs={{1,0},{3,2},{4,5},{6,7},{9,8},{11,10},{12,13},{14,15},{17,16},{19,... | collective-permute-start | bytes 1966088 | tf_op jit(solution)/shard_map/ppermute | solution.py:59
  135.8 18.2 %collective-permute-start.12 = (f32[160,1024]{1,0:T(8,128)}, f32[160,1024]{1,0:T(8,128)}, u32[]{:S(2)}, u32[]{:S(2)}) collective-permute-start(f32[160,1024]{1,0:T(8,128)} %add.97), channel_id=1, source_target_pairs={{0,2},{5,7},{10,8},{15,13},{16,18},{21,23},{26,24},{31,29}} | collective-permute-start | bytes 1966088 | tf_op jit(solution)/shard_map/ppermute | solution.py:69
  140.2 6.4 %collective-permute-start.9 = (f32[256,1024]{1,0:T(8,128)S(1)}, f32[256,1024]{1,0:T(8,128)S(1)}, u32[]{:S(2)}, u32[]{:S(2)}) collective-permute-start(f32[256,1024]{1,0:T(8,128)S(1)} %add.81), channel_id=1, source_target_pairs={{1,3},{6,4},{11,9},{12,14},{17,19},{22,20},{27,25},{28,30}} | collective-permute-start | bytes 3145736 | tf_op jit(solution)/shard_map/ppermute | solution.py:69
  146.9 14.8 %collective-permute-start.10 = (f32[96,1024]{1,0:T(8,128)S(1)}, f32[96,1024]{1,0:T(8,128)}, u32[]{:S(2)}, u32[]{:S(2)}) collective-permute-start(f32[96,1024]{1,0:T(8,128)S(1)} %fusion.157), channel_id=1, source_target_pairs={{1,0},{3,2},{4,5},{6,7},{9,8},{11,10},{12,13},{14,15},{17,16},{19,... | collective-permute-start | bytes 1179656 | tf_op jit(solution)/shard_map/ppermute | solution.py:59
  162.7 9.4 %collective-permute-start.13 = (f32[96,1024]{1,0:T(8,128)S(1)}, f32[96,1024]{1,0:T(8,128)S(1)}, u32[]{:S(2)}, u32[]{:S(2)}) collective-permute-start(f32[96,1024]{1,0:T(8,128)S(1)} %add.93), channel_id=1, source_target_pairs={{0,2},{5,7},{10,8},{15,13},{16,18},{21,23},{26,24},{31,29}} | collective-permute-start | bytes 1179656 | tf_op jit(solution)/shard_map/ppermute | solution.py:69

commit v13 on v12

--- a/solution.py
+++ b/solution.py
@@ -78,17 +78,21 @@
     left = [(s, (s - 1) % planes) for s in range(planes)]
     tops, lows = [], []
 
-    def finish(queries, step, into, near=(), far=()):
-        blocks = [(s + step) % planes for s in range(planes)]
+    def near(queries, step, *earlier):
         found = weighted(list(queries), train_features, residual_weights, scale)
-        total = keepers.near_sums(after(found, *near) if near else found, blocks)
-        whole = keepers.far_sums(after(total, *far) if far else total, blocks)
+        return keepers.near_sums(after(found, *earlier) if earlier else found, blocks_at(step))
+
+    def far(total, step, into, *earlier):
+        whole = keepers.far_sums(after(total, *earlier) if earlier else total, blocks_at(step))
         for parts in into:
             part = whole
             if len(into) == 2:
                 part = whole[:cut] if parts is tops else whole[cut:]
-            parts.append((blocks, part))
+            parts.append((blocks_at(step), part))
         return whole
+
+    def blocks_at(step):
+        return [(s + step) % planes for s in range(planes)]
 
     def chosen(parts):
         found = []
@@ -105,17 +109,19 @@
     for step in range(1, half - 1):
         from_right = lax.ppermute(from_right, "ex", left)
         from_left = lax.ppermute(from_left, "ex", right)
-        finish(from_right, step, both)
-        finish(from_left, -step, both)
-    own = finish(query_features, 0, both)
+        far(near(from_right, step), step, both)
+        far(near(from_left, -step), -step, both)
+    own = far(near(query_features, 0), 0, both)
+    step = half - 1
     from_right = lax.ppermute(from_right, "ex", left)
     from_left = lax.ppermute(from_left, "ex", right)
     low = lax.ppermute(from_right[:, cut:], "ex", left)
     top = lax.ppermute(after(from_right[:, :cut], low), "ex", left)
-    ahead = finish(from_right, half - 1, both)
-    behind = finish(from_left, 1 - half, both, far=(low, own, ahead))
-    below = finish(low, half, (lows,))
-    finish(top, half, (tops,), near=(behind,), far=(below,))
+    ahead = far(near(from_right, step), step, both)
+    total = near(from_left, -step)
+    behind = far(total, -step, both, low, own, ahead)
+    below = far(near(low, half, behind), half, (lows,))
+    far(near(top, half), half, (tops,), below)
     return jnp.concatenate([part for pair in zip(chosen(tops), chosen(lows)) for part in pair], axis=0)
 
 

time: 174 us -> 172 us (0.989)
  waiting for transfers between devices: 115 us -> 112 us
    ppermute x1, waiting for transfers between devices: 2.53 us -> 9.95 us  [ring(): top = lax.ppermute(after(from_right[:, :cut], low), 'ex', left)]
    ppermute x5, waiting for transfers between devices: 11.5 us -> 6.67 us  [near_sums(): total = total + lax.ppermute(partial, PLACE, pairs)]
    ppermute x5, waiting for transfers between devices: 11.1 us -> 7.2 us  [far_sums(): whole = whole + lax.ppermute(total, PLACE, pairs)]
  transfers between devices with their start and end apart: 14 -> 14, of which waited for: 9 -> 9; matrix products, arithmetic and copies ran while one was open for 15% -> 14% of each run, Pallas kernels for 0% -> 0%
where the time goes in v13:
time: 172 us; the launch traced here: 171 us
  waiting for transfers between devices  112 us (65%)
  starting transfers between devices  30.8 us (18%)
  matrix products  21.5 us (12%)
  other arithmetic  5.67 us (3%)
    ppermute x1, waiting for transfers between devices, ring(): from_left = lax.ppermute(from_left, 'ex', right)  37 us
    ppermute x1, waiting for transfers between devices, ring(): from_right = lax.ppermute(from_right, 'ex', left)  31 us
    dot_general x20, matrix products, weighted(): lax.dot_general(piece, examples, (((1,), (1,)), ((), ())), preferred_elem...  21.5 us
    ppermute x1, waiting for transfers between devices, ring(): low = lax.ppermute(from_right[:, cut:], 'ex', left)  19.8 us
    ppermute x5, starting transfers between devices, far_sums(): whole = whole + lax.ppermute(total, PLACE, pairs)  11.6 us
    ppermute x1, waiting for transfers between devices, ring(): top = lax.ppermute(after(from_right[:, :cut], low), 'ex', left)  9.95 us
    ppermute x5, waiting for transfers between devices, far_sums(): whole = whole + lax.ppermute(total, PLACE, pairs)  7.2 us
    ppermute x5, waiting for transfers between devices, near_sums(): total = total + lax.ppermute(partial, PLACE, pairs)  6.67 us
  transfers between devices with their start and end apart: 14, of which 9 were waited for; matrix products, arithmetic and copies ran while one was open for 14% of the time, Pallas kernels for 0%

profile of v13, /device:TPU:0, one launch (start us, length us, event | category | flops | bytes accessed | tf_op | source)
XLA Modules:
  0.0 171.1 jit_solution(10095131694198810901)
XLA Ops:
  0.0 5.0 %collective-permute-start = (bf16[4,256,1024]{2,1,0:T(8,128)(2,1)}, bf16[4,256,1024]{2,1,0:T(8,128)(2,1)S(1)}, u32[]{:S(2)}, u32[]{:S(2)}) collective-permute-start(bf16[4,256,1024]{2,1,0:T(8,128)(2,1)} %param.4), channel_id=1, source_target_pairs={{0,12},{4,0},{8,4},{12,8},{1,13},{5,1},{9,5},{13,9},{2,14},{6,2},{... | collective-permute-start | bytes 6291464 | tf_op jit(solution)/shard_map/ppermute | solution.py:116
  5.0 0.9 fusion.192
  5.9 2.6 %fusion.88 = f32[256,1024]{1,0:T(8,128)S(1)} fusion(bf16[4,1024,1024]{2,1,0:T(8,128)(2,1)} %param.3, bf16[4,256,1024]{2,1,0:T(8,128)(2,1)} %param.4, f32[1024]{0:T(1024)S(1)} %bitcast.193), kind=kOutput, calls=%fused_computation.56 | convolution fusion | flops 537133056 | bytes 3674112 | tf_op jit(solution)/shard_map/dot_general | solution.py:16
  8.6 3.0 %fusion.106 = f32[256,1024]{1,0:T(8,128)S(1)} fusion(bf16[4,1024,1024]{2,1,0:T(8,128)(2,1)} %param.3, bf16[4,256,1024]{2,1,0:T(8,128)(2,1)} %param.4, f32[1024]{0:T(1024)S(1)} %bitcast.203), kind=kOutput, calls=%fused_computation.62 | convolution fusion | flops 537133056 | bytes 3674112 | tf_op jit(solution)/shard_map/dot_general | solution.py:16
  11.6 1.9 %fusion.97 = f32[256,1024]{1,0:T(8,128)S(1)} fusion(bf16[4,1024,1024]{2,1,0:T(8,128)(2,1)S(1)} %copy-done, bf16[4,256,1024]{2,1,0:T(8,128)(2,1)} %param.4, f32[1024]{0:T(1024)S(1)} %bitcast.198), kind=kOutput, calls=%fused_computation.59 | convolution fusion | flops 537133056 | bytes 3674112 | tf_op jit(solution)/shard_map/dot_general | solution.py:16
  13.6 0.9 fusion.67
  14.4 1.3 collective-permute-start.6
  15.8 3.2 %collective-permute-done.6 = f32[256,1024]{1,0:T(8,128)S(1)} collective-permute-done((f32[256,1024]{1,0:T(8,128)S(1)}, f32[256,1024]{1,0:T(8,128)S(1)}, u32[]{:S(2)}, u32[]{:S(2)}) %collective-permute-start.6) | collective-permute-done | bytes 1048608 | tf_op jit(solution)/shard_map/ppermute | solution.py:59
  19.0 0.2 add.89
  19.2 1.3 collective-permute-start.7
  20.5 31.0 %collective-permute-done = bf16[4,256,1024]{2,1,0:T(8,128)(2,1)S(1)} collective-permute-done((bf16[4,256,1024]{2,1,0:T(8,128)(2,1)}, bf16[4,256,1024]{2,1,0:T(8,128)(2,1)S(1)}, u32[]{:S(2)}, u32[]{:S(2)}) %collective-permute-start) | collective-permute-done | bytes 2097184 | tf_op jit(solution)/shard_map/ppermute | solution.py:116
  51.4 0.7 fusion.109
  52.2 0.7 fusion.100
  53.0 0.7 fusion.91
  53.7 0.9 fusion.82
  54.6 1.4 collective-permute-start.8
  56.0 4.2 %collective-permute-start.1 = (bf16[4,160,1024]{2,1,0:T(8,128)(2,1)S(1)}, bf16[4,160,1024]{2,1,0:T(8,128)(2,1)S(1)}, u32[]{:S(2)}, u32[]{:S(2)}) collective-permute-start(bf16[4,160,1024]{2,1,0:T(8,128)(2,1)S(1)} %slice.33), channel_id=1, source_target_pairs={{0,12},{4,0},{8,4},{12,8},{1,13},{5,1},{9,5},{13,9},{2,14},{6,2},{... | collective-permute-start | bytes 3932168 | tf_op jit(solution)/shard_map/ppermute | solution.py:118
  60.2 37.0 %collective-permute-done.4 = bf16[4,256,1024]{2,1,0:T(8,128)(2,1)S(1)} collective-permute-done((bf16[4,256,1024]{2,1,0:T(8,128)(2,1)S(1)}, bf16[4,256,1024]{2,1,0:T(8,128)(2,1)S(1)}, u32[]{:S(2)}, u32[]{:S(2)}) %collective-permute-start.4) | collective-permute-done | bytes 2097184 | tf_op jit(solution)/shard_map/ppermute | solution.py:117
  97.2 0.8 fusion.103
  98.0 0.8 fusion.94
  98.8 0.8 fusion.85
  99.6 0.9 fusion.52
  100.5 1.4 collective-permute-start.5
  102.0 0.7 collective-permute-start.9
  103.0 1.1 collective-permute-done.5
  104.2 19.8 %collective-permute-done.1 = bf16[4,160,1024]{2,1,0:T(8,128)(2,1)S(1)} collective-permute-done((bf16[4,160,1024]{2,1,0:T(8,128)(2,1)S(1)}, bf16[4,160,1024]{2,1,0:T(8,128)(2,1)S(1)}, u32[]{:S(2)}, u32[]{:S(2)}) %collective-permute-start.1) | collective-permute-done | bytes 1310752 | tf_op jit(solution)/shard_map/ppermute | solution.py:118
  124.1 3.4 %collective-permute-start.2 = (bf16[4,96,1024]{2,1,0:T(8,128)(2,1)S(1)}, bf16[4,96,1024]{2,1,0:T(8,128)(2,1)S(1)}, u32[]{:S(2)}, u32[]{:S(2)}) collective-permute-start(bf16[4,96,1024]{2,1,0:T(8,128)(2,1)S(1)} %slice.32), channel_id=1, source_target_pairs={{0,12},{4,0},{8,4},{12,8},{1,13},{5,1},{9,5},{13,9},{2,14},{6,2},{... | collective-permute-start | bytes 2359304 | tf_op jit(solution)/shard_map/ppermute | solution.py:119
  127.7 0.9 collective-permute-start.10
  128.6 0.9 fusion.133
  129.4 0.9 fusion.130
  130.3 0.9 fusion.127
  131.2 0.9 fusion.124
  132.2 1.3 collective-permute-start.11
  133.5 9.9 %collective-permute-done.2 = bf16[4,96,1024]{2,1,0:T(8,128)(2,1)S(1)} collective-permute-done((bf16[4,96,1024]{2,1,0:T(8,128)(2,1)S(1)}, bf16[4,96,1024]{2,1,0:T(8,128)(2,1)S(1)}, u32[]{:S(2)}, u32[]{:S(2)}) %collective-permute-start.2) | collective-permute-done | bytes 786464 | tf_op jit(solution)/shard_map/ppermute | solution.py:119
  143.5 0.8 fusion.145
  144.3 0.8 fusion.142
  145.1 0.8 fusion.139
  145.9 0.9 add.97
  146.8 4.2 %collective-permute-start.12 = (f32[160,1024]{1,0:T(8,128)}, f32[160,1024]{1,0:T(8,128)}, u32[]{:S(2)}, u32[]{:S(2)}) collective-permute-start(f32[160,1024]{1,0:T(8,128)} %add.97), channel_id=1, source_target_pairs={{0,2},{5,7},{10,8},{15,13},{16,18},{21,23},{26,24},{31,29}} | collective-permute-start | bytes 1966088 | tf_op jit(solution)/shard_map/ppermute | solution.py:69
  151.1 0.8 fusion.157
  151.9 1.3 collective-permute-start.3
  153.2 2.4 %collective-permute-done.3 = f32[96,1024]{1,0:T(8,128)} collective-permute-done((f32[96,1024]{1,0:T(8,128)S(1)}, f32[96,1024]{1,0:T(8,128)}, u32[]{:S(2)}, u32[]{:S(2)}) %collective-permute-start.3) | collective-permute-done | bytes 393248 | tf_op jit(solution)/shard_map/ppermute | solution.py:59
  155.6 1.0 add.78
  156.7 1.9 %collective-permute-done.12 = f32[160,1024]{1,0:T(8,128)} collective-permute-done((f32[160,1024]{1,0:T(8,128)}, f32[160,1024]{1,0:T(8,128)}, u32[]{:S(2)}, u32[]{:S(2)}) %collective-permute-start.12) | collective-permute-done | bytes 655392 | tf_op jit(solution)/shard_map/ppermute | solution.py:69
  158.6 1.6 fusion.181
  160.2 4.4 %collective-permute-start.13 = (f32[96,1024]{1,0:T(8,128)S(1)}, f32[96,1024]{1,0:T(8,128)S(1)}, u32[]{:S(2)}, u32[]{:S(2)}) collective-permute-start(f32[96,1024]{1,0:T(8,128)S(1)} %add.78), channel_id=1, source_target_pairs={{0,2},{5,7},{10,8},{15,13},{16,18},{21,23},{26,24},{31,29}} | collective-permute-start | bytes 1179656 | tf_op jit(solution)/shard_map/ppermute | solution.py:69
  164.6 5.3 %collective-permute-done.13 = f32[96,1024]{1,0:T(8,128)S(1)} collective-permute-done((f32[96,1024]{1,0:T(8,128)S(1)}, f32[96,1024]{1,0:T(8,128)S(1)}, u32[]{:S(2)}, u32[]{:S(2)}) %collective-permute-start.13) | collective-permute-done | bytes 393248 | tf_op jit(solution)/shard_map/ppermute | solution.py:69
  170.0 1.0 pad_maximum_fusion
  (18 shorter events, 1.1 us)
Async XLA Ops:
  0.0 51.4 %collective-permute-start = (bf16[4,256,1024]{2,1,0:T(8,128)(2,1)}, bf16[4,256,1024]{2,1,0:T(8,128)(2,1)S(1)}, u32[]{:S(2)}, u32[]{:S(2)}) collective-permute-start(bf16[4,256,1024]{2,1,0:T(8,128)(2,1)} %param.4), channel_id=1, source_target_pairs={{0,12},{4,0},{8,4},{12,8},{1,13},{5,1},{9,5},{13,9},{2,14},{6,2},{... | collective-permute-start | bytes 6291464 | tf_op jit(solution)/shard_map/ppermute | solution.py:116
  5.9 5.7 %copy-start = (bf16[4,1024,1024]{2,1,0:T(8,128)(2,1)S(1)}, bf16[4,1024,1024]{2,1,0:T(8,128)(2,1)}, u32[]{:S(2)}) copy-start(bf16[4,1024,1024]{2,1,0:T(8,128)(2,1)} %param.3) | copy-start | bytes 25165828
  11.6 2.0 %copy-start.1 = (bf16[4,256,1024]{2,1,0:T(8,128)(2,1)S(1)}, bf16[4,256,1024]{2,1,0:T(8,128)(2,1)}, u32[]{:S(2)}) copy-start(bf16[4,256,1024]{2,1,0:T(8,128)(2,1)} %param.4) | copy-start | bytes 6291460
  14.4 4.6 %collective-permute-start.6 = (f32[256,1024]{1,0:T(8,128)S(1)}, f32[256,1024]{1,0:T(8,128)S(1)}, u32[]{:S(2)}, u32[]{:S(2)}) collective-permute-start(f32[256,1024]{1,0:T(8,128)S(1)} %fusion.67), channel_id=1, source_target_pairs={{1,0},{3,2},{4,5},{6,7},{9,8},{11,10},{12,13},{14,15},{17,16},{19,... | collective-permute-start | bytes 3145736 | tf_op jit(solution)/shard_map/ppermute | solution.py:59
  15.7 81.4 %collective-permute-start.4 = (bf16[4,256,1024]{2,1,0:T(8,128)(2,1)S(1)}, bf16[4,256,1024]{2,1,0:T(8,128)(2,1)S(1)}, u32[]{:S(2)}, u32[]{:S(2)}) collective-permute-start(bf16[4,256,1024]{2,1,0:T(8,128)(2,1)S(1)} %copy-done.1), channel_id=1, source_target_pairs={{0,4},{4,8},{8,12},{12,0},{1,5},{5,9},{9,13},{13,1},{2,6},{6,10},{... | collective-permute-start | bytes 6291464 | tf_op jit(solution)/shard_map/ppermute | solution.py:117
  19.2 83.7 %collective-permute-start.7 = (f32[256,1024]{1,0:T(8,128)S(1)}, f32[256,1024]{1,0:T(8,128)S(1)}, u32[]{:S(2)}, u32[]{:S(2)}) collective-permute-start(f32[256,1024]{1,0:T(8,128)S(1)} %add.89), channel_id=1, source_target_pairs={{2,0},{7,5},{8,10},{13,15},{18,16},{23,21},{24,26},{29,31}} | collective-permute-start | bytes 3145736 | tf_op jit(solution)/shard_map/ppermute | solution.py:69
  54.6 47.3 %collective-permute-start.8 = (f32[256,1024]{1,0:T(8,128)S(1)}, f32[256,1024]{1,0:T(8,128)S(1)}, u32[]{:S(2)}, u32[]{:S(2)}) collective-permute-start(f32[256,1024]{1,0:T(8,128)S(1)} %fusion.82), channel_id=1, source_target_pairs={{0,1},{2,3},{5,4},{7,6},{8,9},{10,11},{13,12},{15,14},{16,17},{18,... | collective-permute-start | bytes 3145736 | tf_op jit(solution)/shard_map/ppermute | solution.py:59
  56.0 68.0 %collective-permute-start.1 = (bf16[4,160,1024]{2,1,0:T(8,128)(2,1)S(1)}, bf16[4,160,1024]{2,1,0:T(8,128)(2,1)S(1)}, u32[]{:S(2)}, u32[]{:S(2)}) collective-permute-start(bf16[4,160,1024]{2,1,0:T(8,128)(2,1)S(1)} %slice.33), channel_id=1, source_target_pairs={{0,12},{4,0},{8,4},{12,8},{1,13},{5,1},{9,5},{13,9},{2,14},{6,2},{... | collective-permute-start | bytes 3932168 | tf_op jit(solution)/shard_map/ppermute | solution.py:118
  100.5 3.6 %collective-permute-start.5 = (f32[256,1024]{1,0:T(8,128)S(1)}, f32[256,1024]{1,0:T(8,128)S(1)}, u32[]{:S(2)}, u32[]{:S(2)}) collective-permute-start(f32[256,1024]{1,0:T(8,128)S(1)} %fusion.52), channel_id=1, source_target_pairs={{0,1},{2,3},{5,4},{7,6},{8,9},{10,11},{13,12},{15,14},{16,17},{18,... | collective-permute-start | bytes 3145736 | tf_op jit(solution)/shard_map/ppermute | solution.py:59
  102.0 25.5 %collective-permute-start.9 = (f32[256,1024]{1,0:T(8,128)S(1)}, f32[256,1024]{1,0:T(8,128)S(1)}, u32[]{:S(2)}, u32[]{:S(2)}) collective-permute-start(f32[256,1024]{1,0:T(8,128)S(1)} %add.94), channel_id=1, source_target_pairs={{3,1},{4,6},{9,11},{14,12},{19,17},{20,22},{25,27},{30,28}} | collective-permute-start | bytes 3145736 | tf_op jit(solution)/shard_map/ppermute | solution.py:69
  124.1 19.4 %collective-permute-start.2 = (bf16[4,96,1024]{2,1,0:T(8,128)(2,1)S(1)}, bf16[4,96,1024]{2,1,0:T(8,128)(2,1)S(1)}, u32[]{:S(2)}, u32[]{:S(2)}) collective-permute-start(bf16[4,96,1024]{2,1,0:T(8,128)(2,1)S(1)} %slice.32), channel_id=1, source_target_pairs={{0,12},{4,0},{8,4},{12,8},{1,13},{5,1},{9,5},{13,9},{2,14},{6,2},{... | collective-permute-start | bytes 2359304 | tf_op jit(solution)/shard_map/ppermute | solution.py:119
  127.7 4.4 %collective-permute-start.10 = (f32[256,1024]{1,0:T(8,128)S(1)}, f32[256,1024]{1,0:T(8,128)S(1)}, u32[]{:S(2)}, u32[]{:S(2)}) collective-permute-start(f32[256,1024]{1,0:T(8,128)S(1)} %add.85), channel_id=1, source_target_pairs={{1,3},{6,4},{11,9},{12,14},{17,19},{22,20},{27,25},{28,30}} | collective-permute-start | bytes 3145736 | tf_op jit(solution)/shard_map/ppermute | solution.py:69
  132.2 13.6 %collective-permute-start.11 = (f32[160,1024]{1,0:T(8,128)S(1)}, f32[160,1024]{1,0:T(8,128)S(1)}, u32[]{:S(2)}, u32[]{:S(2)}) collective-permute-start(f32[160,1024]{1,0:T(8,128)S(1)} %fusion.124), channel_id=1, source_target_pairs={{1,0},{3,2},{4,5},{6,7},{9,8},{11,10},{12,13},{14,15},{17,16},{19,... | collective-permute-start | bytes 1966088 | tf_op jit(solution)/shard_map/ppermute | solution.py:59
  146.8 11.8 %collective-permute-start.12 = (f32[160,1024]{1,0:T(8,128)}, f32[160,1024]{1,0:T(8,128)}, u32[]{:S(2)}, u32[]{:S(2)}) collective-permute-start(f32[160,1024]{1,0:T(8,128)} %add.97), channel_id=1, source_target_pairs={{0,2},{5,7},{10,8},{15,13},{16,18},{21,23},{26,24},{31,29}} | collective-permute-start | bytes 1966088 | tf_op jit(solution)/shard_map/ppermute | solution.py:69
  151.9 3.7 %collective-permute-start.3 = (f32[96,1024]{1,0:T(8,128)S(1)}, f32[96,1024]{1,0:T(8,128)}, u32[]{:S(2)}, u32[]{:S(2)}) collective-permute-start(f32[96,1024]{1,0:T(8,128)S(1)} %fusion.157), channel_id=1, source_target_pairs={{1,0},{3,2},{4,5},{6,7},{9,8},{11,10},{12,13},{14,15},{17,16},{19,... | collective-permute-start | bytes 1179656 | tf_op jit(solution)/shard_map/ppermute | solution.py:59
  160.2 9.7 %collective-permute-start.13 = (f32[96,1024]{1,0:T(8,128)S(1)}, f32[96,1024]{1,0:T(8,128)S(1)}, u32[]{:S(2)}, u32[]{:S(2)}) collective-permute-start(f32[96,1024]{1,0:T(8,128)S(1)} %add.78), channel_id=1, source_target_pairs={{0,2},{5,7},{10,8},{15,13},{16,18},{21,23},{26,24},{31,29}} | collective-permute-start | bytes 1179656 | tf_op jit(solution)/shard_map/ppermute | solution.py:69

commit v14 on v13

--- a/solution.py
+++ b/solution.py
@@ -73,7 +73,7 @@
 def ring(train_features, query_features, residual_weights, keepers, scale):
     planes, ratio = keepers.planes, keepers.ratio
     rows = query_features.shape[1]
-    cut = 3 * rows // 8
+    cut = 5 * rows // 8
     right = [(s, (s + 1) % planes) for s in range(planes)]
     left = [(s, (s - 1) % planes) for s in range(planes)]
     tops, lows = [], []
@@ -120,8 +120,8 @@
     ahead = far(near(from_right, step), step, both)
     total = near(from_left, -step)
     behind = far(total, -step, both, low, own, ahead)
-    below = far(near(low, half, behind), half, (lows,))
-    far(near(top, half), half, (tops,), below)
+    below = far(near(low, half), half, (lows,))
+    far(near(top, half, behind), half, (tops,), below)
     return jnp.concatenate([part for pair in zip(chosen(tops), chosen(lows)) for part in pair], axis=0)
 
 

time: 172 us -> 167 us (0.971)
  waiting for transfers between devices: 112 us -> 108 us
    ppermute x1, waiting for transfers between devices: 19.8 us -> 10.7 us  [ring(): low = lax.ppermute(from_right[:, cut:], 'ex', left)]
    ppermute x1, waiting for transfers between devices: 9.95 us -> 14.1 us  [ring(): top = lax.ppermute(after(from_right[:, :cut], low), 'ex', left)]
  transfers between devices with their start and end apart: 14 -> 14, of which waited for: 9 -> 8; matrix products, arithmetic and copies ran while one was open for 14% -> 15% of each run, Pallas kernels for 0% -> 0%
where the time goes in v14:
time: 167 us; the launch traced here: 166 us
  waiting for transfers between devices  108 us (65%)
  starting transfers between devices  30 us (18%)
  matrix products  22.3 us (13%)
  other arithmetic  4.92 us (3%)
    ppermute x1, waiting for transfers between devices, ring(): from_left = lax.ppermute(from_left, 'ex', right)  37 us
    ppermute x1, waiting for transfers between devices, ring(): from_right = lax.ppermute(from_right, 'ex', left)  30.9 us
    dot_general x20, matrix products, weighted(): lax.dot_general(piece, examples, (((1,), (1,)), ((), ())), preferred_elem...  22.3 us
    ppermute x1, waiting for transfers between devices, ring(): top = lax.ppermute(after(from_right[:, :cut], low), 'ex', left)  14.1 us
    ppermute x1, waiting for transfers between devices, ring(): low = lax.ppermute(from_right[:, cut:], 'ex', left)  10.7 us
    ppermute x5, starting transfers between devices, far_sums(): whole = whole + lax.ppermute(total, PLACE, pairs)  10.5 us
    ppermute x5, waiting for transfers between devices, far_sums(): whole = whole + lax.ppermute(total, PLACE, pairs)  8.06 us
    ppermute x5, waiting for transfers between devices, near_sums(): total = total + lax.ppermute(partial, PLACE, pairs)  7.01 us
  transfers between devices with their start and end apart: 14, of which 8 were waited for; matrix products, arithmetic and copies ran while one was open for 15% of the time, Pallas kernels for 0%

profile of v14, /device:TPU:0, one launch (start us, length us, event | category | flops | bytes accessed | tf_op | source)
XLA Modules:
  0.0 166.5 jit_solution(5103848157752188482)
XLA Ops:
  0.0 5.0 %collective-permute-start = (bf16[4,256,1024]{2,1,0:T(8,128)(2,1)}, bf16[4,256,1024]{2,1,0:T(8,128)(2,1)S(1)}, u32[]{:S(2)}, u32[]{:S(2)}) collective-permute-start(bf16[4,256,1024]{2,1,0:T(8,128)(2,1)} %param.4), channel_id=1, source_target_pairs={{0,12},{4,0},{8,4},{12,8},{1,13},{5,1},{9,5},{13,9},{2,14},{6,2},{... | collective-permute-start | bytes 6291464 | tf_op jit(solution)/shard_map/ppermute | solution.py:116
  5.0 0.9 fusion.192
  5.9 2.6 %fusion.88 = f32[256,1024]{1,0:T(8,128)S(1)} fusion(bf16[4,1024,1024]{2,1,0:T(8,128)(2,1)} %param.3, bf16[4,256,1024]{2,1,0:T(8,128)(2,1)} %param.4, f32[1024]{0:T(1024)S(1)} %bitcast.193), kind=kOutput, calls=%fused_computation.56 | convolution fusion | flops 537133056 | bytes 3674112 | tf_op jit(solution)/shard_map/dot_general | solution.py:16
  8.6 3.0 %fusion.106 = f32[256,1024]{1,0:T(8,128)S(1)} fusion(bf16[4,1024,1024]{2,1,0:T(8,128)(2,1)} %param.3, bf16[4,256,1024]{2,1,0:T(8,128)(2,1)} %param.4, f32[1024]{0:T(1024)S(1)} %bitcast.203), kind=kOutput, calls=%fused_computation.62 | convolution fusion | flops 537133056 | bytes 3674112 | tf_op jit(solution)/shard_map/dot_general | solution.py:16
  11.6 1.9 %fusion.97 = f32[256,1024]{1,0:T(8,128)S(1)} fusion(bf16[4,1024,1024]{2,1,0:T(8,128)(2,1)S(1)} %copy-done, bf16[4,256,1024]{2,1,0:T(8,128)(2,1)} %param.4, f32[1024]{0:T(1024)S(1)} %bitcast.198), kind=kOutput, calls=%fused_computation.59 | convolution fusion | flops 537133056 | bytes 3674112 | tf_op jit(solution)/shard_map/dot_general | solution.py:16
  13.6 0.9 fusion.67
  14.5 1.3 collective-permute-start.5
  15.9 3.2 %collective-permute-done.5 = f32[256,1024]{1,0:T(8,128)S(1)} collective-permute-done((f32[256,1024]{1,0:T(8,128)S(1)}, f32[256,1024]{1,0:T(8,128)S(1)}, u32[]{:S(2)}, u32[]{:S(2)}) %collective-permute-start.5) | collective-permute-done | bytes 1048608 | tf_op jit(solution)/shard_map/ppermute | solution.py:59
  19.1 0.2 add.85
  19.2 1.3 collective-permute-start.6
  20.5 30.9 %collective-permute-done = bf16[4,256,1024]{2,1,0:T(8,128)(2,1)S(1)} collective-permute-done((bf16[4,256,1024]{2,1,0:T(8,128)(2,1)}, bf16[4,256,1024]{2,1,0:T(8,128)(2,1)S(1)}, u32[]{:S(2)}, u32[]{:S(2)}) %collective-permute-start) | collective-permute-done | bytes 2097184 | tf_op jit(solution)/shard_map/ppermute | solution.py:116
  51.5 4.2 %collective-permute-start.1 = (bf16[4,96,1024]{2,1,0:T(8,128)(2,1)S(1)}, bf16[4,96,1024]{2,1,0:T(8,128)(2,1)S(1)}, u32[]{:S(2)}, u32[]{:S(2)}) collective-permute-start(bf16[4,96,1024]{2,1,0:T(8,128)(2,1)S(1)} %slice.33), channel_id=1, source_target_pairs={{0,12},{4,0},{8,4},{12,8},{1,13},{5,1},{9,5},{13,9},{2,14},{6,2},{... | collective-permute-start | bytes 2359304 | tf_op jit(solution)/shard_map/ppermute | solution.py:118
  55.7 0.7 fusion.109
  56.5 0.7 fusion.100
  57.2 0.7 fusion.91
  58.0 0.9 fusion.82
  58.8 1.4 collective-permute-start.7
  60.2 37.0 %collective-permute-done.3 = bf16[4,256,1024]{2,1,0:T(8,128)(2,1)S(1)} collective-permute-done((bf16[4,256,1024]{2,1,0:T(8,128)(2,1)S(1)}, bf16[4,256,1024]{2,1,0:T(8,128)(2,1)S(1)}, u32[]{:S(2)}, u32[]{:S(2)}) %collective-permute-start.3) | collective-permute-done | bytes 2097184 | tf_op jit(solution)/shard_map/ppermute | solution.py:117
  97.2 0.8 fusion.103
  98.0 0.8 fusion.94
  98.8 0.8 fusion.85
  99.6 0.9 fusion.52
  100.5 1.4 collective-permute-start.4
  102.0 10.7 %collective-permute-done.1 = bf16[4,96,1024]{2,1,0:T(8,128)(2,1)S(1)} collective-permute-done((bf16[4,96,1024]{2,1,0:T(8,128)(2,1)S(1)}, bf16[4,96,1024]{2,1,0:T(8,128)(2,1)S(1)}, u32[]{:S(2)}, u32[]{:S(2)}) %collective-permute-start.1) | collective-permute-done | bytes 786464 | tf_op jit(solution)/shard_map/ppermute | solution.py:118
  112.7 3.5 %collective-permute-start.2 = (bf16[4,160,1024]{2,1,0:T(8,128)(2,1)S(1)}, bf16[4,160,1024]{2,1,0:T(8,128)(2,1)S(1)}, u32[]{:S(2)}, u32[]{:S(2)}) collective-permute-start(bf16[4,160,1024]{2,1,0:T(8,128)(2,1)S(1)} %slice.32), channel_id=1, source_target_pairs={{0,12},{4,0},{8,4},{12,8},{1,13},{5,1},{9,5},{13,9},{2,14},{6,2},{... | collective-permute-start | bytes 3932168 | tf_op jit(solution)/shard_map/ppermute | solution.py:119
  116.3 0.8 fusion.145
  117.2 0.9 collective-permute-start.8
  118.2 0.8 fusion.142
  119.0 0.8 fusion.139
  119.7 0.8 fusion.157
  120.6 1.3 collective-permute-start.11
  122.2 2.0 %collective-permute-done.11 = f32[96,1024]{1,0:T(8,128)S(1)} collective-permute-done((f32[96,1024]{1,0:T(8,128)S(1)}, f32[96,1024]{1,0:T(8,128)S(1)}, u32[]{:S(2)}, u32[]{:S(2)}) %collective-permute-start.11) | collective-permute-done | bytes 393248 | tf_op jit(solution)/shard_map/ppermute | solution.py:59
  124.2 4.2 %collective-permute-start.12 = (f32[96,1024]{1,0:T(8,128)S(1)}, f32[96,1024]{1,0:T(8,128)}, u32[]{:S(2)}, u32[]{:S(2)}) collective-permute-start(f32[96,1024]{1,0:T(8,128)S(1)} %add.97), channel_id=1, source_target_pairs={{0,2},{5,7},{10,8},{15,13},{16,18},{21,23},{26,24},{31,29}} | collective-permute-start | bytes 1179656 | tf_op jit(solution)/shard_map/ppermute | solution.py:69
  128.4 0.2 add.91
  128.6 0.7 collective-permute-start.9
  129.3 14.1 %collective-permute-done.2 = bf16[4,160,1024]{2,1,0:T(8,128)(2,1)S(1)} collective-permute-done((bf16[4,160,1024]{2,1,0:T(8,128)(2,1)S(1)}, bf16[4,160,1024]{2,1,0:T(8,128)(2,1)S(1)}, u32[]{:S(2)}, u32[]{:S(2)}) %collective-permute-start.2) | collective-permute-done | bytes 1310752 | tf_op jit(solution)/shard_map/ppermute | solution.py:119
  143.4 0.8 fusion.133
  144.3 0.8 fusion.130
  145.1 0.8 fusion.127
  146.0 1.7 %fusion.124 = f32[160,1024]{1,0:T(8,128)} fusion(f32[160,1024]{1,0:T(8,128)S(1)} %fusion.133, f32[160,1024]{1,0:T(8,128)S(1)} %fusion.130, f32[160,1024]{1,0:T(8,128)S(1)} %fusion.127, bf16[4,1024,1024]{2,1,0:T(8,128)(2,1)S(1)} %copy-done, bf16[4,160,1024]{2,1,0:T(8,128)(2,1)S(1)} %collective-permute-done.2, f32[1024]{0:T(1024)S(1)} %bitcast.192), kind=kOutput, calls=%fused_computation.68 | convolution fusion | flops 336363520 | bytes 5050368 | tf_op jit(solution)/shard_map/dot_general | solution.py:16
  147.9 1.3 collective-permute-start.10
  149.2 1.1 fusion.191
  150.4 1.8 %collective-permute-done.10 = f32[160,1024]{1,0:T(8,128)} collective-permute-done((f32[160,1024]{1,0:T(8,128)}, f32[160,1024]{1,0:T(8,128)}, u32[]{:S(2)}, u32[]{:S(2)}) %collective-permute-start.10) | collective-permute-done | bytes 655392 | tf_op jit(solution)/shard_map/ppermute | solution.py:59
  152.2 1.4 add.93
  153.6 3.4 %collective-permute-start.13 = (f32[160,1024]{1,0:T(8,128)S(1)}, f32[160,1024]{1,0:T(8,128)S(1)}, u32[]{:S(2)}, u32[]{:S(2)}) collective-permute-start(f32[160,1024]{1,0:T(8,128)S(1)} %add.93), channel_id=1, source_target_pairs={{0,2},{5,7},{10,8},{15,13},{16,18},{21,23},{26,24},{31,29}} | collective-permute-start | bytes 1966088 | tf_op jit(solution)/shard_map/ppermute | solution.py:69
  157.0 8.0 %collective-permute-done.13 = f32[160,1024]{1,0:T(8,128)S(1)} collective-permute-done((f32[160,1024]{1,0:T(8,128)S(1)}, f32[160,1024]{1,0:T(8,128)S(1)}, u32[]{:S(2)}, u32[]{:S(2)}) %collective-permute-start.13) | collective-permute-done | bytes 655392 | tf_op jit(solution)/shard_map/ppermute | solution.py:69
  165.0 0.3 fusion.181
  165.4 1.1 pad_maximum_fusion
  (18 shorter events, 0.9 us)
Async XLA Ops:
  0.0 51.4 %collective-permute-start = (bf16[4,256,1024]{2,1,0:T(8,128)(2,1)}, bf16[4,256,1024]{2,1,0:T(8,128)(2,1)S(1)}, u32[]{:S(2)}, u32[]{:S(2)}) collective-permute-start(bf16[4,256,1024]{2,1,0:T(8,128)(2,1)} %param.4), channel_id=1, source_target_pairs={{0,12},{4,0},{8,4},{12,8},{1,13},{5,1},{9,5},{13,9},{2,14},{6,2},{... | collective-permute-start | bytes 6291464 | tf_op jit(solution)/shard_map/ppermute | solution.py:116
  5.9 5.7 %copy-start = (bf16[4,1024,1024]{2,1,0:T(8,128)(2,1)S(1)}, bf16[4,1024,1024]{2,1,0:T(8,128)(2,1)}, u32[]{:S(2)}) copy-start(bf16[4,1024,1024]{2,1,0:T(8,128)(2,1)} %param.3) | copy-start | bytes 25165828
  11.6 2.0 %copy-start.1 = (bf16[4,256,1024]{2,1,0:T(8,128)(2,1)S(1)}, bf16[4,256,1024]{2,1,0:T(8,128)(2,1)}, u32[]{:S(2)}) copy-start(bf16[4,256,1024]{2,1,0:T(8,128)(2,1)} %param.4) | copy-start | bytes 6291460
  14.5 4.6 %collective-permute-start.5 = (f32[256,1024]{1,0:T(8,128)S(1)}, f32[256,1024]{1,0:T(8,128)S(1)}, u32[]{:S(2)}, u32[]{:S(2)}) collective-permute-start(f32[256,1024]{1,0:T(8,128)S(1)} %fusion.67), channel_id=1, source_target_pairs={{1,0},{3,2},{4,5},{6,7},{9,8},{11,10},{12,13},{14,15},{17,16},{19,... | collective-permute-start | bytes 3145736 | tf_op jit(solution)/shard_map/ppermute | solution.py:59
  15.8 81.4 %collective-permute-start.3 = (bf16[4,256,1024]{2,1,0:T(8,128)(2,1)S(1)}, bf16[4,256,1024]{2,1,0:T(8,128)(2,1)S(1)}, u32[]{:S(2)}, u32[]{:S(2)}) collective-permute-start(bf16[4,256,1024]{2,1,0:T(8,128)(2,1)S(1)} %copy-done.1), channel_id=1, source_target_pairs={{0,4},{4,8},{8,12},{12,0},{1,5},{5,9},{9,13},{13,1},{2,6},{6,10},{... | collective-permute-start | bytes 6291464 | tf_op jit(solution)/shard_map/ppermute | solution.py:117
  19.2 102.6 %collective-permute-start.6 = (f32[256,1024]{1,0:T(8,128)S(1)}, f32[256,1024]{1,0:T(8,128)S(1)}, u32[]{:S(2)}, u32[]{:S(2)}) collective-permute-start(f32[256,1024]{1,0:T(8,128)S(1)} %add.85), channel_id=1, source_target_pairs={{2,0},{7,5},{8,10},{13,15},{18,16},{23,21},{24,26},{29,31}} | collective-permute-start | bytes 3145736 | tf_op jit(solution)/shard_map/ppermute | solution.py:69
  51.5 61.2 %collective-permute-start.1 = (bf16[4,96,1024]{2,1,0:T(8,128)(2,1)S(1)}, bf16[4,96,1024]{2,1,0:T(8,128)(2,1)S(1)}, u32[]{:S(2)}, u32[]{:S(2)}) collective-permute-start(bf16[4,96,1024]{2,1,0:T(8,128)(2,1)S(1)} %slice.33), channel_id=1, source_target_pairs={{0,12},{4,0},{8,4},{12,8},{1,13},{5,1},{9,5},{13,9},{2,14},{6,2},{... | collective-permute-start | bytes 2359304 | tf_op jit(solution)/shard_map/ppermute | solution.py:118
  58.8 58.2 %collective-permute-start.7 = (f32[256,1024]{1,0:T(8,128)S(1)}, f32[256,1024]{1,0:T(8,128)S(1)}, u32[]{:S(2)}, u32[]{:S(2)}) collective-permute-start(f32[256,1024]{1,0:T(8,128)S(1)} %fusion.82), channel_id=1, source_target_pairs={{0,1},{2,3},{5,4},{7,6},{8,9},{10,11},{13,12},{15,14},{16,17},{18,... | collective-permute-start | bytes 3145736 | tf_op jit(solution)/shard_map/ppermute | solution.py:59
  100.5 21.5 %collective-permute-start.4 = (f32[256,1024]{1,0:T(8,128)S(1)}, f32[256,1024]{1,0:T(8,128)S(1)}, u32[]{:S(2)}, u32[]{:S(2)}) collective-permute-start(f32[256,1024]{1,0:T(8,128)S(1)} %fusion.52), channel_id=1, source_target_pairs={{0,1},{2,3},{5,4},{7,6},{8,9},{10,11},{13,12},{15,14},{16,17},{18,... | collective-permute-start | bytes 3145736 | tf_op jit(solution)/shard_map/ppermute | solution.py:59
  112.7 30.7 %collective-permute-start.2 = (bf16[4,160,1024]{2,1,0:T(8,128)(2,1)S(1)}, bf16[4,160,1024]{2,1,0:T(8,128)(2,1)S(1)}, u32[]{:S(2)}, u32[]{:S(2)}) collective-permute-start(bf16[4,160,1024]{2,1,0:T(8,128)(2,1)S(1)} %slice.32), channel_id=1, source_target_pairs={{0,12},{4,0},{8,4},{12,8},{1,13},{5,1},{9,5},{13,9},{2,14},{6,2},{... | collective-permute-start | bytes 3932168 | tf_op jit(solution)/shard_map/ppermute | solution.py:119
  117.2 11.2 %collective-permute-start.8 = (f32[256,1024]{1,0:T(8,128)S(1)}, f32[256,1024]{1,0:T(8,128)S(1)}, u32[]{:S(2)}, u32[]{:S(2)}) collective-permute-start(f32[256,1024]{1,0:T(8,128)S(1)} %add.90), channel_id=1, source_target_pairs={{3,1},{4,6},{9,11},{14,12},{19,17},{20,22},{25,27},{30,28}} | collective-permute-start | bytes 3145736 | tf_op jit(solution)/shard_map/ppermute | solution.py:69
  120.6 3.6 %collective-permute-start.11 = (f32[96,1024]{1,0:T(8,128)S(1)}, f32[96,1024]{1,0:T(8,128)S(1)}, u32[]{:S(2)}, u32[]{:S(2)}) collective-permute-start(f32[96,1024]{1,0:T(8,128)S(1)} %fusion.157), channel_id=1, source_target_pairs={{1,0},{3,2},{4,5},{6,7},{9,8},{11,10},{12,13},{14,15},{17,16},{19,... | collective-permute-start | bytes 1179656 | tf_op jit(solution)/shard_map/ppermute | solution.py:59
  124.2 25.0 %collective-permute-start.12 = (f32[96,1024]{1,0:T(8,128)S(1)}, f32[96,1024]{1,0:T(8,128)}, u32[]{:S(2)}, u32[]{:S(2)}) collective-permute-start(f32[96,1024]{1,0:T(8,128)S(1)} %add.97), channel_id=1, source_target_pairs={{0,2},{5,7},{10,8},{15,13},{16,18},{21,23},{26,24},{31,29}} | collective-permute-start | bytes 1179656 | tf_op jit(solution)/shard_map/ppermute | solution.py:69
  128.6 19.1 %collective-permute-start.9 = (f32[256,1024]{1,0:T(8,128)S(1)}, f32[256,1024]{1,0:T(8,128)S(1)}, u32[]{:S(2)}, u32[]{:S(2)}) collective-permute-start(f32[256,1024]{1,0:T(8,128)S(1)} %add.81), channel_id=1, source_target_pairs={{1,3},{6,4},{11,9},{12,14},{17,19},{22,20},{27,25},{28,30}} | collective-permute-start | bytes 3145736 | tf_op jit(solution)/shard_map/ppermute | solution.py:69
  147.9 4.3 %collective-permute-start.10 = (f32[160,1024]{1,0:T(8,128)}, f32[160,1024]{1,0:T(8,128)}, u32[]{:S(2)}, u32[]{:S(2)}) collective-permute-start(f32[160,1024]{1,0:T(8,128)} %fusion.124), channel_id=1, source_target_pairs={{1,0},{3,2},{4,5},{6,7},{9,8},{11,10},{12,13},{14,15},{17,16},{19,... | collective-permute-start | bytes 1966088 | tf_op jit(solution)/shard_map/ppermute | solution.py:59
  153.6 11.5 %collective-permute-start.13 = (f32[160,1024]{1,0:T(8,128)S(1)}, f32[160,1024]{1,0:T(8,128)S(1)}, u32[]{:S(2)}, u32[]{:S(2)}) collective-permute-start(f32[160,1024]{1,0:T(8,128)S(1)} %add.93), channel_id=1, source_target_pairs={{0,2},{5,7},{10,8},{15,13},{16,18},{21,23},{26,24},{31,29}} | collective-permute-start | bytes 1966088 | tf_op jit(solution)/shard_map/ppermute | solution.py:69

commit v15 on v14

--- a/solution.py
+++ b/solution.py
@@ -73,7 +73,7 @@
 def ring(train_features, query_features, residual_weights, keepers, scale):
     planes, ratio = keepers.planes, keepers.ratio
     rows = query_features.shape[1]
-    cut = 5 * rows // 8
+    cut = rows // 2
     right = [(s, (s + 1) % planes) for s in range(planes)]
     left = [(s, (s - 1) % planes) for s in range(planes)]
     tops, lows = [], []
@@ -116,7 +116,7 @@
     from_right = lax.ppermute(from_right, "ex", left)
     from_left = lax.ppermute(from_left, "ex", right)
     low = lax.ppermute(from_right[:, cut:], "ex", left)
-    top = lax.ppermute(after(from_right[:, :cut], low), "ex", left)
+    top = lax.ppermute(from_right[:, :cut], "ex", left)
     ahead = far(near(from_right, step), step, both)
     total = near(from_left, -step)
     behind = far(total, -step, both, low, own, ahead)

time: 167 us -> 170 us (1.018)
    ppermute x5, waiting for transfers between devices: 7.01 us -> 3.2 us  [near_sums(): total = total + lax.ppermute(partial, PLACE, pairs)]
    ppermute x1, waiting for transfers between devices: 14.1 us -> 16.3 us  [ring(): top = lax.ppermute(from_right[:, :cut], 'ex', left)]
  transfers between devices with their start and end apart: 14 -> 14, of which waited for: 8 -> 7; matrix products, arithmetic and copies ran while one was open for 15% -> 16% of each run, Pallas kernels for 0% -> 0%
where the time goes in v15:
time: 170 us
  waiting for transfers between devices  109 us (64%)
  starting transfers between devices  30.7 us (18%)
  matrix products  22.5 us (13%)
  other arithmetic  5.82 us (3%)
    ppermute x1, waiting for transfers between devices, ring(): from_left = lax.ppermute(from_left, 'ex', right)  36.9 us
    ppermute x1, waiting for transfers between devices, ring(): from_right = lax.ppermute(from_right, 'ex', left)  30.9 us
    dot_general x20, matrix products, weighted(): lax.dot_general(piece, examples, (((1,), (1,)), ((), ())), preferred_elem...  22.5 us
    ppermute x1, waiting for transfers between devices, ring(): top = lax.ppermute(from_right[:, :cut], 'ex', left)  16.3 us
    ppermute x1, waiting for transfers between devices, ring(): low = lax.ppermute(from_right[:, cut:], 'ex', left)  12.3 us
    ppermute x5, starting transfers between devices, far_sums(): whole = whole + lax.ppermute(total, PLACE, pairs)  11.5 us
    ppermute x5, waiting for transfers between devices, far_sums(): whole = whole + lax.ppermute(total, PLACE, pairs)  9.64 us
    ppermute x5, starting transfers between devices, near_sums(): total = total + lax.ppermute(partial, PLACE, pairs)  6.59 us
  transfers between devices with their start and end apart: 14, of which 7 were waited for; matrix products, arithmetic and copies ran while one was open for 16% of the time, Pallas kernels for 0%

profile of v15, /device:TPU:0, one launch (start us, length us, event | category | flops | bytes accessed | tf_op | source)
XLA Modules:
  0.0 169.7 jit_solution(5496630702503650)
XLA Ops:
  0.0 5.0 %collective-permute-start = (bf16[4,256,1024]{2,1,0:T(8,128)(2,1)}, bf16[4,256,1024]{2,1,0:T(8,128)(2,1)S(1)}, u32[]{:S(2)}, u32[]{:S(2)}) collective-permute-start(bf16[4,256,1024]{2,1,0:T(8,128)(2,1)} %param.4), channel_id=1, source_target_pairs={{0,12},{4,0},{8,4},{12,8},{1,13},{5,1},{9,5},{13,9},{2,14},{6,2},{... | collective-permute-start | bytes 6291464 | tf_op jit(solution)/shard_map/ppermute | solution.py:116
  5.0 0.9 fusion.193
  5.9 2.6 %fusion.88 = f32[256,1024]{1,0:T(8,128)S(1)} fusion(bf16[4,1024,1024]{2,1,0:T(8,128)(2,1)} %param.3, bf16[4,256,1024]{2,1,0:T(8,128)(2,1)} %param.4, f32[1024]{0:T(1024)S(1)} %bitcast.193), kind=kOutput, calls=%fused_computation.56 | convolution fusion | flops 537133056 | bytes 3674112 | tf_op jit(solution)/shard_map/dot_general | solution.py:16
  8.6 3.0 %fusion.106 = f32[256,1024]{1,0:T(8,128)S(1)} fusion(bf16[4,1024,1024]{2,1,0:T(8,128)(2,1)} %param.3, bf16[4,256,1024]{2,1,0:T(8,128)(2,1)} %param.4, f32[1024]{0:T(1024)S(1)} %bitcast.203), kind=kOutput, calls=%fused_computation.62 | convolution fusion | flops 537133056 | bytes 3674112 | tf_op jit(solution)/shard_map/dot_general | solution.py:16
  11.6 1.9 %fusion.97 = f32[256,1024]{1,0:T(8,128)S(1)} fusion(bf16[4,1024,1024]{2,1,0:T(8,128)(2,1)S(1)} %copy-done, bf16[4,256,1024]{2,1,0:T(8,128)(2,1)} %param.4, f32[1024]{0:T(1024)S(1)} %bitcast.198), kind=kOutput, calls=%fused_computation.59 | convolution fusion | flops 537133056 | bytes 3674112 | tf_op jit(solution)/shard_map/dot_general | solution.py:16
  13.6 0.9 fusion.67
  14.5 1.3 collective-permute-start.5
  15.9 3.2 %collective-permute-done.5 = f32[256,1024]{1,0:T(8,128)S(1)} collective-permute-done((f32[256,1024]{1,0:T(8,128)S(1)}, f32[256,1024]{1,0:T(8,128)S(1)}, u32[]{:S(2)}, u32[]{:S(2)}) %collective-permute-start.5) | collective-permute-done | bytes 1048608 | tf_op jit(solution)/shard_map/ppermute | solution.py:59
  19.1 0.2 add.85
  19.2 1.3 collective-permute-start.6
  20.5 30.9 %collective-permute-done = bf16[4,256,1024]{2,1,0:T(8,128)(2,1)S(1)} collective-permute-done((bf16[4,256,1024]{2,1,0:T(8,128)(2,1)}, bf16[4,256,1024]{2,1,0:T(8,128)(2,1)S(1)}, u32[]{:S(2)}, u32[]{:S(2)}) %collective-permute-start) | collective-permute-done | bytes 2097184 | tf_op jit(solution)/shard_map/ppermute | solution.py:116
  51.6 4.2 %collective-permute-start.4 = (bf16[4,128,1024]{2,1,0:T(8,128)(2,1)S(1)}, bf16[4,128,1024]{2,1,0:T(8,128)(2,1)S(1)}, u32[]{:S(2)}, u32[]{:S(2)}) collective-permute-start(bf16[4,128,1024]{2,1,0:T(8,128)(2,1)S(1)} %get-tuple-element.14), channel_id=1, source_target_pairs={{0,12},{4,0},{8,4},{12,8},{1,13},{5,1},{9,5},{13,9},{2,14},{6,2},{... | collective-permute-start | bytes 3145736 | tf_op jit(solution)/shard_map/ppermute | solution.py:118
  55.8 0.7 fusion.100
  56.6 0.7 fusion.91
  57.4 0.7 fusion.109
  58.1 0.9 fusion.82
  59.0 1.4 collective-permute-start.7
  60.3 36.9 %collective-permute-done.2 = bf16[4,256,1024]{2,1,0:T(8,128)(2,1)S(1)} collective-permute-done((bf16[4,256,1024]{2,1,0:T(8,128)(2,1)S(1)}, bf16[4,256,1024]{2,1,0:T(8,128)(2,1)S(1)}, u32[]{:S(2)}, u32[]{:S(2)}) %collective-permute-start.2) | collective-permute-done | bytes 2097184 | tf_op jit(solution)/shard_map/ppermute | solution.py:117
  97.2 0.8 fusion.103
  98.0 0.8 fusion.94
  98.8 0.8 fusion.85
  99.6 0.9 fusion.52
  100.5 1.4 collective-permute-start.3
  101.9 3.3 %collective-permute-start.1 = (bf16[4,128,1024]{2,1,0:T(8,128)(2,1)S(1)}, bf16[4,128,1024]{2,1,0:T(8,128)(2,1)S(1)}, u32[]{:S(2)}, u32[]{:S(2)}) collective-permute-start(bf16[4,128,1024]{2,1,0:T(8,128)(2,1)S(1)} %get-tuple-element.13), channel_id=1, source_target_pairs={{0,12},{4,0},{8,4},{12,8},{1,13},{5,1},{9,5},{13,9},{2,14},{6,2},{... | collective-permute-start | bytes 3145736 | tf_op jit(solution)/shard_map/ppermute | solution.py:119
  105.5 0.9 collective-permute-start.8
  106.4 12.3 %collective-permute-done.4 = bf16[4,128,1024]{2,1,0:T(8,128)(2,1)S(1)} collective-permute-done((bf16[4,128,1024]{2,1,0:T(8,128)(2,1)S(1)}, bf16[4,128,1024]{2,1,0:T(8,128)(2,1)S(1)}, u32[]{:S(2)}, u32[]{:S(2)}) %collective-permute-start.4) | collective-permute-done | bytes 1048608 | tf_op jit(solution)/shard_map/ppermute | solution.py:118
  118.8 0.8 fusion.157
  119.6 0.8 fusion.151
  120.5 0.8 fusion.145
  121.3 0.9 fusion.139
  122.2 1.3 collective-permute-start.11
  123.5 0.2 add.81
  123.9 0.7 collective-permute-start.9
  124.6 16.3 %collective-permute-done.1 = bf16[4,128,1024]{2,1,0:T(8,128)(2,1)S(1)} collective-permute-done((bf16[4,128,1024]{2,1,0:T(8,128)(2,1)S(1)}, bf16[4,128,1024]{2,1,0:T(8,128)(2,1)S(1)}, u32[]{:S(2)}, u32[]{:S(2)}) %collective-permute-start.1) | collective-permute-done | bytes 1048608 | tf_op jit(solution)/shard_map/ppermute | solution.py:119
  140.9 0.8 fusion.154
  141.7 0.8 fusion.148
  142.6 0.8 fusion.142
  143.4 0.9 add.97
  144.3 4.2 %collective-permute-start.12 = (f32[128,1024]{1,0:T(8,128)}, f32[128,1024]{1,0:T(8,128)}, u32[]{:S(2)}, u32[]{:S(2)}) collective-permute-start(f32[128,1024]{1,0:T(8,128)} %add.97), channel_id=1, source_target_pairs={{0,2},{5,7},{10,8},{15,13},{16,18},{21,23},{26,24},{31,29}} | collective-permute-start | bytes 1572872 | tf_op jit(solution)/shard_map/ppermute | solution.py:69
  148.5 1.7 fusion.124
  150.3 1.3 collective-permute-start.10
  151.7 3.0 %collective-permute-done.12 = f32[128,1024]{1,0:T(8,128)} collective-permute-done((f32[128,1024]{1,0:T(8,128)}, f32[128,1024]{1,0:T(8,128)}, u32[]{:S(2)}, u32[]{:S(2)}) %collective-permute-start.12) | collective-permute-done | bytes 524320 | tf_op jit(solution)/shard_map/ppermute | solution.py:69
  154.7 1.4 fusion.181
  156.1 1.3 add.93
  157.4 4.4 %collective-permute-start.13 = (f32[128,1024]{1,0:T(8,128)S(1)}, f32[128,1024]{1,0:T(8,128)S(1)}, u32[]{:S(2)}, u32[]{:S(2)}) collective-permute-start(f32[128,1024]{1,0:T(8,128)S(1)} %add.93), channel_id=1, source_target_pairs={{0,2},{5,7},{10,8},{15,13},{16,18},{21,23},{26,24},{31,29}} | collective-permute-start | bytes 1572872 | tf_op jit(solution)/shard_map/ppermute | solution.py:69
  161.8 6.6 %collective-permute-done.13 = f32[128,1024]{1,0:T(8,128)S(1)} collective-permute-done((f32[128,1024]{1,0:T(8,128)S(1)}, f32[128,1024]{1,0:T(8,128)S(1)}, u32[]{:S(2)}, u32[]{:S(2)}) %collective-permute-start.13) | collective-permute-done | bytes 524320 | tf_op jit(solution)/shard_map/ppermute | solution.py:69
  168.4 0.2 fusion.183
  168.7 1.1 pad_maximum_fusion
  (17 shorter events, 0.9 us)
Async XLA Ops:
  0.0 51.4 %collective-permute-start = (bf16[4,256,1024]{2,1,0:T(8,128)(2,1)}, bf16[4,256,1024]{2,1,0:T(8,128)(2,1)S(1)}, u32[]{:S(2)}, u32[]{:S(2)}) collective-permute-start(bf16[4,256,1024]{2,1,0:T(8,128)(2,1)} %param.4), channel_id=1, source_target_pairs={{0,12},{4,0},{8,4},{12,8},{1,13},{5,1},{9,5},{13,9},{2,14},{6,2},{... | collective-permute-start | bytes 6291464 | tf_op jit(solution)/shard_map/ppermute | solution.py:116
  5.9 5.7 %copy-start = (bf16[4,1024,1024]{2,1,0:T(8,128)(2,1)S(1)}, bf16[4,1024,1024]{2,1,0:T(8,128)(2,1)}, u32[]{:S(2)}) copy-start(bf16[4,1024,1024]{2,1,0:T(8,128)(2,1)} %param.3) | copy-start | bytes 25165828
  11.6 2.0 %copy-start.1 = (bf16[4,256,1024]{2,1,0:T(8,128)(2,1)S(1)}, bf16[4,256,1024]{2,1,0:T(8,128)(2,1)}, u32[]{:S(2)}) copy-start(bf16[4,256,1024]{2,1,0:T(8,128)(2,1)} %param.4) | copy-start | bytes 6291460
  14.5 4.6 %collective-permute-start.5 = (f32[256,1024]{1,0:T(8,128)S(1)}, f32[256,1024]{1,0:T(8,128)S(1)}, u32[]{:S(2)}, u32[]{:S(2)}) collective-permute-start(f32[256,1024]{1,0:T(8,128)S(1)} %fusion.67), channel_id=1, source_target_pairs={{1,0},{3,2},{4,5},{6,7},{9,8},{11,10},{12,13},{14,15},{17,16},{19,... | collective-permute-start | bytes 3145736 | tf_op jit(solution)/shard_map/ppermute | solution.py:59
  15.8 81.4 %collective-permute-start.2 = (bf16[4,256,1024]{2,1,0:T(8,128)(2,1)S(1)}, bf16[4,256,1024]{2,1,0:T(8,128)(2,1)S(1)}, u32[]{:S(2)}, u32[]{:S(2)}) collective-permute-start(bf16[4,256,1024]{2,1,0:T(8,128)(2,1)S(1)} %copy-done.1), channel_id=1, source_target_pairs={{0,4},{4,8},{8,12},{12,0},{1,5},{5,9},{9,13},{13,1},{2,6},{6,10},{... | collective-permute-start | bytes 6291464 | tf_op jit(solution)/shard_map/ppermute | solution.py:117
  19.2 85.9 %collective-permute-start.6 = (f32[256,1024]{1,0:T(8,128)S(1)}, f32[256,1024]{1,0:T(8,128)S(1)}, u32[]{:S(2)}, u32[]{:S(2)}) collective-permute-start(f32[256,1024]{1,0:T(8,128)S(1)} %add.85), channel_id=1, source_target_pairs={{2,0},{7,5},{8,10},{13,15},{18,16},{23,21},{24,26},{29,31}} | collective-permute-start | bytes 3145736 | tf_op jit(solution)/shard_map/ppermute | solution.py:69
  51.6 67.1 %collective-permute-start.4 = (bf16[4,128,1024]{2,1,0:T(8,128)(2,1)S(1)}, bf16[4,128,1024]{2,1,0:T(8,128)(2,1)S(1)}, u32[]{:S(2)}, u32[]{:S(2)}) collective-permute-start(bf16[4,128,1024]{2,1,0:T(8,128)(2,1)S(1)} %get-tuple-element.14), channel_id=1, source_target_pairs={{0,12},{4,0},{8,4},{12,8},{1,13},{5,1},{9,5},{13,9},{2,14},{6,2},{... | collective-permute-start | bytes 3145736 | tf_op jit(solution)/shard_map/ppermute | solution.py:118
  59.0 46.3 %collective-permute-start.7 = (f32[256,1024]{1,0:T(8,128)S(1)}, f32[256,1024]{1,0:T(8,128)S(1)}, u32[]{:S(2)}, u32[]{:S(2)}) collective-permute-start(f32[256,1024]{1,0:T(8,128)S(1)} %fusion.82), channel_id=1, source_target_pairs={{0,1},{2,3},{5,4},{7,6},{8,9},{10,11},{13,12},{15,14},{16,17},{18,... | collective-permute-start | bytes 3145736 | tf_op jit(solution)/shard_map/ppermute | solution.py:59
  100.5 23.0 %collective-permute-start.3 = (f32[256,1024]{1,0:T(8,128)S(1)}, f32[256,1024]{1,0:T(8,128)S(1)}, u32[]{:S(2)}, u32[]{:S(2)}) collective-permute-start(f32[256,1024]{1,0:T(8,128)S(1)} %fusion.52), channel_id=1, source_target_pairs={{0,1},{2,3},{5,4},{7,6},{8,9},{10,11},{13,12},{15,14},{16,17},{18,... | collective-permute-start | bytes 3145736 | tf_op jit(solution)/shard_map/ppermute | solution.py:59
  101.9 39.0 %collective-permute-start.1 = (bf16[4,128,1024]{2,1,0:T(8,128)(2,1)S(1)}, bf16[4,128,1024]{2,1,0:T(8,128)(2,1)S(1)}, u32[]{:S(2)}, u32[]{:S(2)}) collective-permute-start(bf16[4,128,1024]{2,1,0:T(8,128)(2,1)S(1)} %get-tuple-element.13), channel_id=1, source_target_pairs={{0,12},{4,0},{8,4},{12,8},{1,13},{5,1},{9,5},{13,9},{2,14},{6,2},{... | collective-permute-start | bytes 3145736 | tf_op jit(solution)/shard_map/ppermute | solution.py:119
  105.5 18.2 %collective-permute-start.8 = (f32[256,1024]{1,0:T(8,128)S(1)}, f32[256,1024]{1,0:T(8,128)S(1)}, u32[]{:S(2)}, u32[]{:S(2)}) collective-permute-start(f32[256,1024]{1,0:T(8,128)S(1)} %add.90), channel_id=1, source_target_pairs={{3,1},{4,6},{9,11},{14,12},{19,17},{20,22},{25,27},{30,28}} | collective-permute-start | bytes 3145736 | tf_op jit(solution)/shard_map/ppermute | solution.py:69
  122.2 21.2 %collective-permute-start.11 = (f32[128,1024]{1,0:T(8,128)S(1)}, f32[128,1024]{1,0:T(8,128)S(1)}, u32[]{:S(2)}, u32[]{:S(2)}) collective-permute-start(f32[128,1024]{1,0:T(8,128)S(1)} %fusion.139), channel_id=1, source_target_pairs={{1,0},{3,2},{4,5},{6,7},{9,8},{11,10},{12,13},{14,15},{17,16},{19,... | collective-permute-start | bytes 1572872 | tf_op jit(solution)/shard_map/ppermute | solution.py:59
  123.9 26.2 %collective-permute-start.9 = (f32[256,1024]{1,0:T(8,128)S(1)}, f32[256,1024]{1,0:T(8,128)S(1)}, u32[]{:S(2)}, u32[]{:S(2)}) collective-permute-start(f32[256,1024]{1,0:T(8,128)S(1)} %add.81), channel_id=1, source_target_pairs={{1,3},{6,4},{11,9},{12,14},{17,19},{22,20},{27,25},{28,30}} | collective-permute-start | bytes 3145736 | tf_op jit(solution)/shard_map/ppermute | solution.py:69
  144.3 10.4 %collective-permute-start.12 = (f32[128,1024]{1,0:T(8,128)}, f32[128,1024]{1,0:T(8,128)}, u32[]{:S(2)}, u32[]{:S(2)}) collective-permute-start(f32[128,1024]{1,0:T(8,128)} %add.97), channel_id=1, source_target_pairs={{0,2},{5,7},{10,8},{15,13},{16,18},{21,23},{26,24},{31,29}} | collective-permute-start | bytes 1572872 | tf_op jit(solution)/shard_map/ppermute | solution.py:69
  150.3 5.8 %collective-permute-start.10 = (f32[128,1024]{1,0:T(8,128)}, f32[128,1024]{1,0:T(8,128)}, u32[]{:S(2)}, u32[]{:S(2)}) collective-permute-start(f32[128,1024]{1,0:T(8,128)} %fusion.124), channel_id=1, source_target_pairs={{1,0},{3,2},{4,5},{6,7},{9,8},{11,10},{12,13},{14,15},{17,16},{19,... | collective-permute-start | bytes 1572872 | tf_op jit(solution)/shard_map/ppermute | solution.py:59
  157.4 11.1 %collective-permute-start.13 = (f32[128,1024]{1,0:T(8,128)S(1)}, f32[128,1024]{1,0:T(8,128)S(1)}, u32[]{:S(2)}, u32[]{:S(2)}) collective-permute-start(f32[128,1024]{1,0:T(8,128)S(1)} %add.93), channel_id=1, source_target_pairs={{0,2},{5,7},{10,8},{15,13},{16,18},{21,23},{26,24},{31,29}} | collective-permute-start | bytes 1572872 | tf_op jit(solution)/shard_map/ppermute | solution.py:69

commit v16 on v14

--- a/solution.py
+++ b/solution.py
@@ -116,8 +116,8 @@
     from_right = lax.ppermute(from_right, "ex", left)
     from_left = lax.ppermute(from_left, "ex", right)
     low = lax.ppermute(from_right[:, cut:], "ex", left)
-    top = lax.ppermute(after(from_right[:, :cut], low), "ex", left)
     ahead = far(near(from_right, step), step, both)
+    top = lax.ppermute(after(from_right[:, :cut], ahead), "ex", left)
     total = near(from_left, -step)
     behind = far(total, -step, both, low, own, ahead)
     below = far(near(low, half), half, (lows,))

time: 167 us -> 166 us (level)
  waiting for transfers between devices: 108 us -> 99.5 us
  starting transfers between devices: 30 us -> 36.2 us
    ppermute x1, waiting for transfers between devices: 10.7 us -> 0.01 us  [ring(): low = lax.ppermute(from_right[:, cut:], 'ex', left)]
    ppermute x1, starting transfers between devices: 3.53 us -> 14 us  [ring(): top = lax.ppermute(after(from_right[:, :cut], ahead), 'ex', left)]
    ppermute x1, waiting for transfers between devices: 30.9 us -> 34.8 us  [ring(): from_right = lax.ppermute(from_right, 'ex', left)]
    ppermute x5, starting transfers between devices: 10.5 us -> 6.93 us  [far_sums(): whole = whole + lax.ppermute(total, PLACE, pairs)]
    ppermute x5, waiting for transfers between devices: 7.01 us -> 4.14 us  [near_sums(): total = total + lax.ppermute(partial, PLACE, pairs)]
    ppermute x1, waiting for transfers between devices: 14.1 us -> 16.4 us  [ring(): top = lax.ppermute(after(from_right[:, :cut], ahead), 'ex', left)]
  transfers between devices with their start and end apart: 14 -> 14, of which waited for: 8 -> 6; matrix products, arithmetic and copies ran while one was open for 15% -> 16% of each run, Pallas kernels for 0% -> 0%
where the time goes in v16:
time: 166 us; the launch traced here: 165 us
  waiting for transfers between devices  99.5 us (60%)
  starting transfers between devices  36.2 us (22%)
  matrix products  23.2 us (14%)
  other arithmetic  4.95 us (3%)
    ppermute x1, waiting for transfers between devices, ring(): from_left = lax.ppermute(from_left, 'ex', right)  36.1 us
    ppermute x1, waiting for transfers between devices, ring(): from_right = lax.ppermute(from_right, 'ex', left)  34.8 us
    dot_general x20, matrix products, weighted(): lax.dot_general(piece, examples, (((1,), (1,)), ((), ())), preferred_elem...  23.2 us
    ppermute x1, waiting for transfers between devices, ring(): top = lax.ppermute(after(from_right[:, :cut], ahead), 'ex', left)  16.4 us
    ppermute x1, starting transfers between devices, ring(): top = lax.ppermute(after(from_right[:, :cut], ahead), 'ex', left)  14 us
    ppermute x5, waiting for transfers between devices, far_sums(): whole = whole + lax.ppermute(total, PLACE, pairs)  8.06 us
    ppermute x5, starting transfers between devices, far_sums(): whole = whole + lax.ppermute(total, PLACE, pairs)  6.93 us
    ppermute x5, starting transfers between devices, near_sums(): total = total + lax.ppermute(partial, PLACE, pairs)  6.58 us
  transfers between devices with their start and end apart: 14, of which 6 were waited for; matrix products, arithmetic and copies ran while one was open for 16% of the time, Pallas kernels for 0%

profile of v16, /device:TPU:0, one launch (start us, length us, event | category | flops | bytes accessed | tf_op | source)
XLA Modules:
  0.0 165.3 jit_solution(5958669662355345598)
XLA Ops:
  0.0 5.0 %collective-permute-start = (bf16[4,256,1024]{2,1,0:T(8,128)(2,1)}, bf16[4,256,1024]{2,1,0:T(8,128)(2,1)S(1)}, u32[]{:S(2)}, u32[]{:S(2)}) collective-permute-start(bf16[4,256,1024]{2,1,0:T(8,128)(2,1)} %param.4), channel_id=1, source_target_pairs={{0,12},{4,0},{8,4},{12,8},{1,13},{5,1},{9,5},{13,9},{2,14},{6,2},{... | collective-permute-start | bytes 6291464 | tf_op jit(solution)/shard_map/ppermute | solution.py:116
  5.1 0.9 fusion.192
  6.0 2.6 %fusion.91 = f32[256,1024]{1,0:T(8,128)S(1)} fusion(bf16[4,1024,1024]{2,1,0:T(8,128)(2,1)} %param.3, bf16[4,256,1024]{2,1,0:T(8,128)(2,1)} %param.4, f32[1024]{0:T(1024)S(1)} %bitcast.193), kind=kOutput, calls=%fused_computation.57 | convolution fusion | flops 537133056 | bytes 3674112 | tf_op jit(solution)/shard_map/dot_general | solution.py:16
  8.6 3.0 %fusion.109 = f32[256,1024]{1,0:T(8,128)S(1)} fusion(bf16[4,1024,1024]{2,1,0:T(8,128)(2,1)} %param.3, bf16[4,256,1024]{2,1,0:T(8,128)(2,1)} %param.4, f32[1024]{0:T(1024)S(1)} %bitcast.203), kind=kOutput, calls=%fused_computation.63 | convolution fusion | flops 537133056 | bytes 3674112 | tf_op jit(solution)/shard_map/dot_general | solution.py:16
  11.6 1.8 %fusion.100 = f32[256,1024]{1,0:T(8,128)S(1)} fusion(bf16[4,1024,1024]{2,1,0:T(8,128)(2,1)S(1)} %copy-done, bf16[4,256,1024]{2,1,0:T(8,128)(2,1)} %param.4, f32[1024]{0:T(1024)S(1)} %bitcast.198), kind=kOutput, calls=%fused_computation.60 | convolution fusion | flops 537133056 | bytes 3674112 | tf_op jit(solution)/shard_map/dot_general | solution.py:16
  13.4 1.9 %fusion.82 = f32[256,1024]{1,0:T(8,128)S(1)} fusion(f32[256,1024]{1,0:T(8,128)S(1)} %fusion.109, f32[256,1024]{1,0:T(8,128)S(1)} %fusion.100, f32[256,1024]{1,0:T(8,128)S(1)} %fusion.91, bf16[4,1024,1024]{2,1,0:T(8,128)(2,1)S(1)} %copy-done, bf16[4,256,1024]{2,1,0:T(8,128)(2,1)} %param.4, f32[1024]{0:T(1024)S(1)} %bitcast.188), kind=kOutput, calls=%fused_computation.54 | convolution fusion | flops 538181632 | bytes 6819840 | tf_op jit(solution)/shard_map/dot_general | solution.py:16
  15.3 1.3 collective-permute-start.7
  16.6 34.8 %collective-permute-done = bf16[4,256,1024]{2,1,0:T(8,128)(2,1)S(1)} collective-permute-done((bf16[4,256,1024]{2,1,0:T(8,128)(2,1)}, bf16[4,256,1024]{2,1,0:T(8,128)(2,1)S(1)}, u32[]{:S(2)}, u32[]{:S(2)}) %collective-permute-start) | collective-permute-done | bytes 2097184 | tf_op jit(solution)/shard_map/ppermute | solution.py:116
  51.4 0.7 fusion.103
  52.2 0.7 fusion.94
  52.9 0.7 fusion.85
  53.7 0.9 fusion.52
  54.5 1.4 collective-permute-start.1
  55.9 0.2 add.90
  56.1 1.3 collective-permute-start.8
  57.4 3.6 %collective-permute-start.6 = (bf16[4,96,1024]{2,1,0:T(8,128)(2,1)S(1)}, bf16[4,96,1024]{2,1,0:T(8,128)(2,1)S(1)}, u32[]{:S(2)}, u32[]{:S(2)}) collective-permute-start(bf16[4,96,1024]{2,1,0:T(8,128)(2,1)S(1)} %slice.33), channel_id=1, source_target_pairs={{0,12},{4,0},{8,4},{12,8},{1,13},{5,1},{9,5},{13,9},{2,14},{6,2},{... | collective-permute-start | bytes 2359304 | tf_op jit(solution)/shard_map/ppermute | solution.py:118
  61.1 36.1 %collective-permute-done.4 = bf16[4,256,1024]{2,1,0:T(8,128)(2,1)S(1)} collective-permute-done((bf16[4,256,1024]{2,1,0:T(8,128)(2,1)}, bf16[4,256,1024]{2,1,0:T(8,128)(2,1)S(1)}, u32[]{:S(2)}, u32[]{:S(2)}) %collective-permute-start.4) | collective-permute-done | bytes 2097184 | tf_op jit(solution)/shard_map/ppermute | solution.py:117
  97.2 0.8 fusion.106
  98.0 0.8 fusion.97
  98.8 0.8 fusion.88
  99.6 0.2 add.78
  99.8 0.7 collective-permute-start.2
  100.5 0.9 fusion.67
  101.4 1.4 collective-permute-start.5
  103.2 14.0 %collective-permute-start.3 = (bf16[4,160,1024]{2,1,0:T(8,128)(2,1)S(1)}, bf16[4,160,1024]{2,1,0:T(8,128)(2,1)S(1)}, u32[]{:S(2)}, u32[]{:S(2)}) collective-permute-start(bf16[4,160,1024]{2,1,0:T(8,128)(2,1)S(1)} %slice.32), channel_id=1, source_target_pairs={{0,12},{4,0},{8,4},{12,8},{1,13},{5,1},{9,5},{13,9},{2,14},{6,2},{... | collective-permute-start | bytes 3932168 | tf_op jit(solution)/shard_map/ppermute | solution.py:120
  117.2 0.8 fusion.145
  118.1 0.2 add.86
  118.2 0.9 collective-permute-start.9
  119.1 0.8 fusion.142
  119.9 0.8 fusion.139
  120.7 0.8 fusion.157
  121.6 1.3 collective-permute-start.11
  122.9 2.3 %collective-permute-done.11 = f32[96,1024]{1,0:T(8,128)S(1)} collective-permute-done((f32[96,1024]{1,0:T(8,128)S(1)}, f32[96,1024]{1,0:T(8,128)S(1)}, u32[]{:S(2)}, u32[]{:S(2)}) %collective-permute-start.11) | collective-permute-done | bytes 393248 | tf_op jit(solution)/shard_map/ppermute | solution.py:59
  125.2 2.2 %collective-permute-start.12 = (f32[96,1024]{1,0:T(8,128)S(1)}, f32[96,1024]{1,0:T(8,128)}, u32[]{:S(2)}, u32[]{:S(2)}) collective-permute-start(f32[96,1024]{1,0:T(8,128)S(1)} %add.97), channel_id=1, source_target_pairs={{0,2},{5,7},{10,8},{15,13},{16,18},{21,23},{26,24},{31,29}} | collective-permute-start | bytes 1179656 | tf_op jit(solution)/shard_map/ppermute | solution.py:69
  127.4 0.2 add.92
  127.6 16.4 %collective-permute-done.3 = bf16[4,160,1024]{2,1,0:T(8,128)(2,1)S(1)} collective-permute-done((bf16[4,160,1024]{2,1,0:T(8,128)(2,1)S(1)}, bf16[4,160,1024]{2,1,0:T(8,128)(2,1)S(1)}, u32[]{:S(2)}, u32[]{:S(2)}) %collective-permute-start.3) | collective-permute-done | bytes 1310752 | tf_op jit(solution)/shard_map/ppermute | solution.py:120
  144.0 0.8 fusion.133
  144.9 0.8 fusion.130
  145.7 0.8 fusion.127
  146.6 1.7 %fusion.124 = f32[160,1024]{1,0:T(8,128)} fusion(f32[160,1024]{1,0:T(8,128)S(1)} %fusion.133, f32[160,1024]{1,0:T(8,128)S(1)} %fusion.130, f32[160,1024]{1,0:T(8,128)S(1)} %fusion.127, bf16[4,1024,1024]{2,1,0:T(8,128)(2,1)S(1)} %copy-done, bf16[4,160,1024]{2,1,0:T(8,128)(2,1)S(1)} %collective-permute-done.3, f32[1024]{0:T(1024)S(1)} %bitcast.192), kind=kOutput, calls=%fused_computation.68 | convolution fusion | flops 336363520 | bytes 5050368 | tf_op jit(solution)/shard_map/dot_general | solution.py:16
  148.3 1.3 collective-permute-start.10
  149.7 1.1 fusion.191
  150.8 1.8 %collective-permute-done.10 = f32[160,1024]{1,0:T(8,128)} collective-permute-done((f32[160,1024]{1,0:T(8,128)}, f32[160,1024]{1,0:T(8,128)}, u32[]{:S(2)}, u32[]{:S(2)}) %collective-permute-start.10) | collective-permute-done | bytes 655392 | tf_op jit(solution)/shard_map/ppermute | solution.py:59
  152.6 1.4 add.93
  154.0 1.8 %collective-permute-start.13 = (f32[160,1024]{1,0:T(8,128)S(1)}, f32[160,1024]{1,0:T(8,128)S(1)}, u32[]{:S(2)}, u32[]{:S(2)}) collective-permute-start(f32[160,1024]{1,0:T(8,128)S(1)} %add.93), channel_id=1, source_target_pairs={{0,2},{5,7},{10,8},{15,13},{16,18},{21,23},{26,24},{31,29}} | collective-permute-start | bytes 1966088 | tf_op jit(solution)/shard_map/ppermute | solution.py:69
  155.8 8.0 %collective-permute-done.13 = f32[160,1024]{1,0:T(8,128)S(1)} collective-permute-done((f32[160,1024]{1,0:T(8,128)S(1)}, f32[160,1024]{1,0:T(8,128)S(1)}, u32[]{:S(2)}, u32[]{:S(2)}) %collective-permute-start.13) | collective-permute-done | bytes 655392 | tf_op jit(solution)/shard_map/ppermute | solution.py:69
  163.8 0.3 fusion.181
  164.2 1.1 pad_maximum_fusion
  (16 shorter events, 0.5 us)
Async XLA Ops:
  0.0 51.4 %collective-permute-start = (bf16[4,256,1024]{2,1,0:T(8,128)(2,1)}, bf16[4,256,1024]{2,1,0:T(8,128)(2,1)S(1)}, u32[]{:S(2)}, u32[]{:S(2)}) collective-permute-start(bf16[4,256,1024]{2,1,0:T(8,128)(2,1)} %param.4), channel_id=1, source_target_pairs={{0,12},{4,0},{8,4},{12,8},{1,13},{5,1},{9,5},{13,9},{2,14},{6,2},{... | collective-permute-start | bytes 6291464 | tf_op jit(solution)/shard_map/ppermute | solution.py:116
  5.0 92.1 %collective-permute-start.4 = (bf16[4,256,1024]{2,1,0:T(8,128)(2,1)}, bf16[4,256,1024]{2,1,0:T(8,128)(2,1)S(1)}, u32[]{:S(2)}, u32[]{:S(2)}) collective-permute-start(bf16[4,256,1024]{2,1,0:T(8,128)(2,1)} %param.4), channel_id=1, source_target_pairs={{0,4},{4,8},{8,12},{12,0},{1,5},{5,9},{9,13},{13,1},{2,6},{6,10},{... | collective-permute-start | bytes 6291464 | tf_op jit(solution)/shard_map/ppermute | solution.py:117
  5.9 5.7 %copy-start = (bf16[4,1024,1024]{2,1,0:T(8,128)(2,1)S(1)}, bf16[4,1024,1024]{2,1,0:T(8,128)(2,1)}, u32[]{:S(2)}) copy-start(bf16[4,1024,1024]{2,1,0:T(8,128)(2,1)} %param.3) | copy-start | bytes 25165828
  15.3 40.6 %collective-permute-start.7 = (f32[256,1024]{1,0:T(8,128)S(1)}, f32[256,1024]{1,0:T(8,128)S(1)}, u32[]{:S(2)}, u32[]{:S(2)}) collective-permute-start(f32[256,1024]{1,0:T(8,128)S(1)} %fusion.82), channel_id=1, source_target_pairs={{1,0},{3,2},{4,5},{6,7},{9,8},{11,10},{12,13},{14,15},{17,16},{19,... | collective-permute-start | bytes 3145736 | tf_op jit(solution)/shard_map/ppermute | solution.py:59
  54.5 45.1 %collective-permute-start.1 = (f32[256,1024]{1,0:T(8,128)S(1)}, f32[256,1024]{1,0:T(8,128)S(1)}, u32[]{:S(2)}, u32[]{:S(2)}) collective-permute-start(f32[256,1024]{1,0:T(8,128)S(1)} %fusion.52), channel_id=1, source_target_pairs={{0,1},{2,3},{5,4},{7,6},{8,9},{10,11},{13,12},{15,14},{16,17},{18,... | collective-permute-start | bytes 3145736 | tf_op jit(solution)/shard_map/ppermute | solution.py:59
  56.1 46.8 %collective-permute-start.8 = (f32[256,1024]{1,0:T(8,128)S(1)}, f32[256,1024]{1,0:T(8,128)S(1)}, u32[]{:S(2)}, u32[]{:S(2)}) collective-permute-start(f32[256,1024]{1,0:T(8,128)S(1)} %add.90), channel_id=1, source_target_pairs={{2,0},{7,5},{8,10},{13,15},{18,16},{23,21},{24,26},{29,31}} | collective-permute-start | bytes 3145736 | tf_op jit(solution)/shard_map/ppermute | solution.py:69
  57.4 59.8 %collective-permute-start.6 = (bf16[4,96,1024]{2,1,0:T(8,128)(2,1)S(1)}, bf16[4,96,1024]{2,1,0:T(8,128)(2,1)S(1)}, u32[]{:S(2)}, u32[]{:S(2)}) collective-permute-start(bf16[4,96,1024]{2,1,0:T(8,128)(2,1)S(1)} %slice.33), channel_id=1, source_target_pairs={{0,12},{4,0},{8,4},{12,8},{1,13},{5,1},{9,5},{13,9},{2,14},{6,2},{... | collective-permute-start | bytes 2359304 | tf_op jit(solution)/shard_map/ppermute | solution.py:118
  99.8 3.3 %collective-permute-start.2 = (f32[256,1024]{1,0:T(8,128)S(1)}, f32[256,1024]{1,0:T(8,128)S(1)}, u32[]{:S(2)}, u32[]{:S(2)}) collective-permute-start(f32[256,1024]{1,0:T(8,128)S(1)} %add.78), channel_id=1, source_target_pairs={{3,1},{4,6},{9,11},{14,12},{19,17},{20,22},{25,27},{30,28}} | collective-permute-start | bytes 3145736 | tf_op jit(solution)/shard_map/ppermute | solution.py:69
  101.4 16.6 %collective-permute-start.5 = (f32[256,1024]{1,0:T(8,128)S(1)}, f32[256,1024]{1,0:T(8,128)S(1)}, u32[]{:S(2)}, u32[]{:S(2)}) collective-permute-start(f32[256,1024]{1,0:T(8,128)S(1)} %fusion.67), channel_id=1, source_target_pairs={{0,1},{2,3},{5,4},{7,6},{8,9},{10,11},{13,12},{15,14},{16,17},{18,... | collective-permute-start | bytes 3145736 | tf_op jit(solution)/shard_map/ppermute | solution.py:59
  103.2 40.8 %collective-permute-start.3 = (bf16[4,160,1024]{2,1,0:T(8,128)(2,1)S(1)}, bf16[4,160,1024]{2,1,0:T(8,128)(2,1)S(1)}, u32[]{:S(2)}, u32[]{:S(2)}) collective-permute-start(bf16[4,160,1024]{2,1,0:T(8,128)(2,1)S(1)} %slice.32), channel_id=1, source_target_pairs={{0,12},{4,0},{8,4},{12,8},{1,13},{5,1},{9,5},{13,9},{2,14},{6,2},{... | collective-permute-start | bytes 3932168 | tf_op jit(solution)/shard_map/ppermute | solution.py:120
  118.2 9.2 %collective-permute-start.9 = (f32[256,1024]{1,0:T(8,128)S(1)}, f32[256,1024]{1,0:T(8,128)S(1)}, u32[]{:S(2)}, u32[]{:S(2)}) collective-permute-start(f32[256,1024]{1,0:T(8,128)S(1)} %add.86), channel_id=1, source_target_pairs={{1,3},{6,4},{11,9},{12,14},{17,19},{22,20},{27,25},{28,30}} | collective-permute-start | bytes 3145736 | tf_op jit(solution)/shard_map/ppermute | solution.py:69
  121.6 3.6 %collective-permute-start.11 = (f32[96,1024]{1,0:T(8,128)S(1)}, f32[96,1024]{1,0:T(8,128)S(1)}, u32[]{:S(2)}, u32[]{:S(2)}) collective-permute-start(f32[96,1024]{1,0:T(8,128)S(1)} %fusion.157), channel_id=1, source_target_pairs={{1,0},{3,2},{4,5},{6,7},{9,8},{11,10},{12,13},{14,15},{17,16},{19,... | collective-permute-start | bytes 1179656 | tf_op jit(solution)/shard_map/ppermute | solution.py:59
  125.2 24.4 %collective-permute-start.12 = (f32[96,1024]{1,0:T(8,128)S(1)}, f32[96,1024]{1,0:T(8,128)}, u32[]{:S(2)}, u32[]{:S(2)}) collective-permute-start(f32[96,1024]{1,0:T(8,128)S(1)} %add.97), channel_id=1, source_target_pairs={{0,2},{5,7},{10,8},{15,13},{16,18},{21,23},{26,24},{31,29}} | collective-permute-start | bytes 1179656 | tf_op jit(solution)/shard_map/ppermute | solution.py:69
  148.3 4.3 %collective-permute-start.10 = (f32[160,1024]{1,0:T(8,128)}, f32[160,1024]{1,0:T(8,128)}, u32[]{:S(2)}, u32[]{:S(2)}) collective-permute-start(f32[160,1024]{1,0:T(8,128)} %fusion.124), channel_id=1, source_target_pairs={{1,0},{3,2},{4,5},{6,7},{9,8},{11,10},{12,13},{14,15},{17,16},{19,... | collective-permute-start | bytes 1966088 | tf_op jit(solution)/shard_map/ppermute | solution.py:59
  154.0 9.8 %collective-permute-start.13 = (f32[160,1024]{1,0:T(8,128)S(1)}, f32[160,1024]{1,0:T(8,128)S(1)}, u32[]{:S(2)}, u32[]{:S(2)}) collective-permute-start(f32[160,1024]{1,0:T(8,128)S(1)} %add.93), channel_id=1, source_target_pairs={{0,2},{5,7},{10,8},{15,13},{16,18},{21,23},{26,24},{31,29}} | collective-permute-start | bytes 1966088 | tf_op jit(solution)/shard_map/ppermute | solution.py:69

commit v17 on v16

--- a/solution.py
+++ b/solution.py
@@ -116,8 +116,8 @@
     from_right = lax.ppermute(from_right, "ex", left)
     from_left = lax.ppermute(from_left, "ex", right)
     low = lax.ppermute(from_right[:, cut:], "ex", left)
+    top = lax.ppermute(from_right[:, :cut], "ex", left)
     ahead = far(near(from_right, step), step, both)
-    top = lax.ppermute(after(from_right[:, :cut], ahead), "ex", left)
     total = near(from_left, -step)
     behind = far(total, -step, both, low, own, ahead)
     below = far(near(low, half), half, (lows,))

time: 166 us -> 167 us (level); the launches traced: 165 us -> 164 us
  starting transfers between devices: 36.2 us -> 29.7 us
  waiting for transfers between devices: 99.5 us -> 105 us
    ppermute x1, starting transfers between devices: 14 us -> 3.27 us  [ring(): top = lax.ppermute(from_right[:, :cut], 'ex', left)]
    ppermute x1, waiting for transfers between devices: 0.01 us -> 7.87 us  [ring(): low = lax.ppermute(from_right[:, cut:], 'ex', left)]
    ppermute x1, waiting for transfers between devices: 34.8 us -> 30.9 us  [ring(): from_right = lax.ppermute(from_right, 'ex', left)]
    ppermute x5, starting transfers between devices: 6.93 us -> 10.5 us  [far_sums(): whole = whole + lax.ppermute(total, PLACE, pairs)]
    ppermute x5, waiting for transfers between devices: 4.14 us -> 7.01 us  [near_sums(): total = total + lax.ppermute(partial, PLACE, pairs)]
    ppermute x1, waiting for transfers between devices: 16.4 us -> 14.6 us  [ring(): top = lax.ppermute(from_right[:, :cut], 'ex', left)]
  transfers between devices with their start and end apart: 14 -> 14, of which waited for: 6 -> 8; matrix products, arithmetic and copies ran while one was open for 16% -> 16% of each run, Pallas kernels for 0% -> 0%
where the time goes in v17:
time: 167 us; the launch traced here: 164 us
  waiting for transfers between devices  105 us (63%)
  starting transfers between devices  29.7 us (18%)
  matrix products  22.3 us (13%)
  other arithmetic  4.92 us (3%)
    ppermute x1, waiting for transfers between devices, ring(): from_left = lax.ppermute(from_left, 'ex', right)  37 us
    ppermute x1, waiting for transfers between devices, ring(): from_right = lax.ppermute(from_right, 'ex', left)  30.9 us
    dot_general x20, matrix products, weighted(): lax.dot_general(piece, examples, (((1,), (1,)), ((), ())), preferred_elem...  22.3 us
    ppermute x1, waiting for transfers between devices, ring(): top = lax.ppermute(from_right[:, :cut], 'ex', left)  14.6 us
    ppermute x5, starting transfers between devices, far_sums(): whole = whole + lax.ppermute(total, PLACE, pairs)  10.5 us
    ppermute x5, waiting for transfers between devices, far_sums(): whole = whole + lax.ppermute(total, PLACE, pairs)  8.06 us
    ppermute x1, waiting for transfers between devices, ring(): low = lax.ppermute(from_right[:, cut:], 'ex', left)  7.87 us
    ppermute x5, waiting for transfers between devices, near_sums(): total = total + lax.ppermute(partial, PLACE, pairs)  7.01 us
  transfers between devices with their start and end apart: 14, of which 8 were waited for; matrix products, arithmetic and copies ran while one was open for 16% of the time, Pallas kernels for 0%

profile of v17, /device:TPU:0, one launch (start us, length us, event | category | flops | bytes accessed | tf_op | source)
XLA Modules:
  0.0 163.9 jit_solution(16128980339754033991)
XLA Ops:
  0.0 5.0 %collective-permute-start = (bf16[4,256,1024]{2,1,0:T(8,128)(2,1)}, bf16[4,256,1024]{2,1,0:T(8,128)(2,1)S(1)}, u32[]{:S(2)}, u32[]{:S(2)}) collective-permute-start(bf16[4,256,1024]{2,1,0:T(8,128)(2,1)} %param.4), channel_id=1, source_target_pairs={{0,12},{4,0},{8,4},{12,8},{1,13},{5,1},{9,5},{13,9},{2,14},{6,2},{... | collective-permute-start | bytes 6291464 | tf_op jit(solution)/shard_map/ppermute | solution.py:116
  5.0 0.9 fusion.192
  5.9 2.6 %fusion.88 = f32[256,1024]{1,0:T(8,128)S(1)} fusion(bf16[4,1024,1024]{2,1,0:T(8,128)(2,1)} %param.3, bf16[4,256,1024]{2,1,0:T(8,128)(2,1)} %param.4, f32[1024]{0:T(1024)S(1)} %bitcast.193), kind=kOutput, calls=%fused_computation.56 | convolution fusion | flops 537133056 | bytes 3674112 | tf_op jit(solution)/shard_map/dot_general | solution.py:16
  8.6 3.0 %fusion.106 = f32[256,1024]{1,0:T(8,128)S(1)} fusion(bf16[4,1024,1024]{2,1,0:T(8,128)(2,1)} %param.3, bf16[4,256,1024]{2,1,0:T(8,128)(2,1)} %param.4, f32[1024]{0:T(1024)S(1)} %bitcast.203), kind=kOutput, calls=%fused_computation.62 | convolution fusion | flops 537133056 | bytes 3674112 | tf_op jit(solution)/shard_map/dot_general | solution.py:16
  11.6 1.9 %fusion.97 = f32[256,1024]{1,0:T(8,128)S(1)} fusion(bf16[4,1024,1024]{2,1,0:T(8,128)(2,1)S(1)} %copy-done, bf16[4,256,1024]{2,1,0:T(8,128)(2,1)} %param.4, f32[1024]{0:T(1024)S(1)} %bitcast.198), kind=kOutput, calls=%fused_computation.59 | convolution fusion | flops 537133056 | bytes 3674112 | tf_op jit(solution)/shard_map/dot_general | solution.py:16
  13.6 0.9 fusion.67
  14.5 1.3 collective-permute-start.5
  15.9 3.2 %collective-permute-done.5 = f32[256,1024]{1,0:T(8,128)S(1)} collective-permute-done((f32[256,1024]{1,0:T(8,128)S(1)}, f32[256,1024]{1,0:T(8,128)S(1)}, u32[]{:S(2)}, u32[]{:S(2)}) %collective-permute-start.5) | collective-permute-done | bytes 1048608 | tf_op jit(solution)/shard_map/ppermute | solution.py:59
  19.1 0.2 add.85
  19.2 1.3 collective-permute-start.6
  20.5 30.9 %collective-permute-done = bf16[4,256,1024]{2,1,0:T(8,128)(2,1)S(1)} collective-permute-done((bf16[4,256,1024]{2,1,0:T(8,128)(2,1)}, bf16[4,256,1024]{2,1,0:T(8,128)(2,1)S(1)}, u32[]{:S(2)}, u32[]{:S(2)}) %collective-permute-start) | collective-permute-done | bytes 2097184 | tf_op jit(solution)/shard_map/ppermute | solution.py:116
  51.5 4.2 %collective-permute-start.4 = (bf16[4,96,1024]{2,1,0:T(8,128)(2,1)S(1)}, bf16[4,96,1024]{2,1,0:T(8,128)(2,1)S(1)}, u32[]{:S(2)}, u32[]{:S(2)}) collective-permute-start(bf16[4,96,1024]{2,1,0:T(8,128)(2,1)S(1)} %slice.33), channel_id=1, source_target_pairs={{0,12},{4,0},{8,4},{12,8},{1,13},{5,1},{9,5},{13,9},{2,14},{6,2},{... | collective-permute-start | bytes 2359304 | tf_op jit(solution)/shard_map/ppermute | solution.py:118
  55.7 0.7 fusion.109
  56.5 0.7 fusion.100
  57.2 0.7 fusion.91
  58.0 0.9 fusion.82
  58.8 1.4 collective-permute-start.7
  60.2 37.0 %collective-permute-done.2 = bf16[4,256,1024]{2,1,0:T(8,128)(2,1)S(1)} collective-permute-done((bf16[4,256,1024]{2,1,0:T(8,128)(2,1)S(1)}, bf16[4,256,1024]{2,1,0:T(8,128)(2,1)S(1)}, u32[]{:S(2)}, u32[]{:S(2)}) %collective-permute-start.2) | collective-permute-done | bytes 2097184 | tf_op jit(solution)/shard_map/ppermute | solution.py:117
  97.2 0.8 fusion.103
  98.0 0.8 fusion.94
  98.8 0.8 fusion.85
  99.6 0.9 fusion.52
  100.5 1.4 collective-permute-start.3
  102.0 3.3 %collective-permute-start.1 = (bf16[4,160,1024]{2,1,0:T(8,128)(2,1)S(1)}, bf16[4,160,1024]{2,1,0:T(8,128)(2,1)S(1)}, u32[]{:S(2)}, u32[]{:S(2)}) collective-permute-start(bf16[4,160,1024]{2,1,0:T(8,128)(2,1)S(1)} %slice.32), channel_id=1, source_target_pairs={{0,12},{4,0},{8,4},{12,8},{1,13},{5,1},{9,5},{13,9},{2,14},{6,2},{... | collective-permute-start | bytes 3932168 | tf_op jit(solution)/shard_map/ppermute | solution.py:119
  105.3 7.9 %collective-permute-done.4 = bf16[4,96,1024]{2,1,0:T(8,128)(2,1)S(1)} collective-permute-done((bf16[4,96,1024]{2,1,0:T(8,128)(2,1)S(1)}, bf16[4,96,1024]{2,1,0:T(8,128)(2,1)S(1)}, u32[]{:S(2)}, u32[]{:S(2)}) %collective-permute-start.4) | collective-permute-done | bytes 786464 | tf_op jit(solution)/shard_map/ppermute | solution.py:118
  113.1 0.8 fusion.145
  114.1 0.9 collective-permute-start.8
  115.0 0.8 fusion.142
  115.8 0.8 fusion.139
  116.6 0.8 fusion.157
  117.4 1.3 collective-permute-start.11
  119.1 2.0 %collective-permute-done.11 = f32[96,1024]{1,0:T(8,128)S(1)} collective-permute-done((f32[96,1024]{1,0:T(8,128)S(1)}, f32[96,1024]{1,0:T(8,128)S(1)}, u32[]{:S(2)}, u32[]{:S(2)}) %collective-permute-start.11) | collective-permute-done | bytes 393248 | tf_op jit(solution)/shard_map/ppermute | solution.py:59
  121.1 4.2 %collective-permute-start.12 = (f32[96,1024]{1,0:T(8,128)S(1)}, f32[96,1024]{1,0:T(8,128)}, u32[]{:S(2)}, u32[]{:S(2)}) collective-permute-start(f32[96,1024]{1,0:T(8,128)S(1)} %add.97), channel_id=1, source_target_pairs={{0,2},{5,7},{10,8},{15,13},{16,18},{21,23},{26,24},{31,29}} | collective-permute-start | bytes 1179656 | tf_op jit(solution)/shard_map/ppermute | solution.py:69
  125.3 0.2 add.91
  125.5 0.7 collective-permute-start.9
  126.2 14.6 %collective-permute-done.1 = bf16[4,160,1024]{2,1,0:T(8,128)(2,1)S(1)} collective-permute-done((bf16[4,160,1024]{2,1,0:T(8,128)(2,1)S(1)}, bf16[4,160,1024]{2,1,0:T(8,128)(2,1)S(1)}, u32[]{:S(2)}, u32[]{:S(2)}) %collective-permute-start.1) | collective-permute-done | bytes 1310752 | tf_op jit(solution)/shard_map/ppermute | solution.py:119
  140.8 0.8 fusion.133
  141.7 0.8 fusion.130
  142.5 0.8 fusion.127
  143.4 1.7 %fusion.124 = f32[160,1024]{1,0:T(8,128)} fusion(f32[160,1024]{1,0:T(8,128)S(1)} %fusion.133, f32[160,1024]{1,0:T(8,128)S(1)} %fusion.130, f32[160,1024]{1,0:T(8,128)S(1)} %fusion.127, bf16[4,1024,1024]{2,1,0:T(8,128)(2,1)S(1)} %copy-done, bf16[4,160,1024]{2,1,0:T(8,128)(2,1)S(1)} %collective-permute-done.1, f32[1024]{0:T(1024)S(1)} %bitcast.192), kind=kOutput, calls=%fused_computation.68 | convolution fusion | flops 336363520 | bytes 5050368 | tf_op jit(solution)/shard_map/dot_general | solution.py:16
  145.2 1.3 collective-permute-start.10
  146.6 1.1 fusion.191
  147.8 1.8 %collective-permute-done.10 = f32[160,1024]{1,0:T(8,128)} collective-permute-done((f32[160,1024]{1,0:T(8,128)}, f32[160,1024]{1,0:T(8,128)}, u32[]{:S(2)}, u32[]{:S(2)}) %collective-permute-start.10) | collective-permute-done | bytes 655392 | tf_op jit(solution)/shard_map/ppermute | solution.py:59
  149.6 1.4 add.93
  151.0 3.4 %collective-permute-start.13 = (f32[160,1024]{1,0:T(8,128)S(1)}, f32[160,1024]{1,0:T(8,128)S(1)}, u32[]{:S(2)}, u32[]{:S(2)}) collective-permute-start(f32[160,1024]{1,0:T(8,128)S(1)} %add.93), channel_id=1, source_target_pairs={{0,2},{5,7},{10,8},{15,13},{16,18},{21,23},{26,24},{31,29}} | collective-permute-start | bytes 1966088 | tf_op jit(solution)/shard_map/ppermute | solution.py:69
  154.4 8.0 %collective-permute-done.13 = f32[160,1024]{1,0:T(8,128)S(1)} collective-permute-done((f32[160,1024]{1,0:T(8,128)S(1)}, f32[160,1024]{1,0:T(8,128)S(1)}, u32[]{:S(2)}, u32[]{:S(2)}) %collective-permute-start.13) | collective-permute-done | bytes 655392 | tf_op jit(solution)/shard_map/ppermute | solution.py:69
  162.4 0.3 fusion.181
  162.8 1.1 pad_maximum_fusion
  (18 shorter events, 0.9 us)
Async XLA Ops:
  0.0 51.4 %collective-permute-start = (bf16[4,256,1024]{2,1,0:T(8,128)(2,1)}, bf16[4,256,1024]{2,1,0:T(8,128)(2,1)S(1)}, u32[]{:S(2)}, u32[]{:S(2)}) collective-permute-start(bf16[4,256,1024]{2,1,0:T(8,128)(2,1)} %param.4), channel_id=1, source_target_pairs={{0,12},{4,0},{8,4},{12,8},{1,13},{5,1},{9,5},{13,9},{2,14},{6,2},{... | collective-permute-start | bytes 6291464 | tf_op jit(solution)/shard_map/ppermute | solution.py:116
  5.9 5.7 %copy-start = (bf16[4,1024,1024]{2,1,0:T(8,128)(2,1)S(1)}, bf16[4,1024,1024]{2,1,0:T(8,128)(2,1)}, u32[]{:S(2)}) copy-start(bf16[4,1024,1024]{2,1,0:T(8,128)(2,1)} %param.3) | copy-start | bytes 25165828
  11.6 2.0 %copy-start.1 = (bf16[4,256,1024]{2,1,0:T(8,128)(2,1)S(1)}, bf16[4,256,1024]{2,1,0:T(8,128)(2,1)}, u32[]{:S(2)}) copy-start(bf16[4,256,1024]{2,1,0:T(8,128)(2,1)} %param.4) | copy-start | bytes 6291460
  14.5 4.6 %collective-permute-start.5 = (f32[256,1024]{1,0:T(8,128)S(1)}, f32[256,1024]{1,0:T(8,128)S(1)}, u32[]{:S(2)}, u32[]{:S(2)}) collective-permute-start(f32[256,1024]{1,0:T(8,128)S(1)} %fusion.67), channel_id=1, source_target_pairs={{1,0},{3,2},{4,5},{6,7},{9,8},{11,10},{12,13},{14,15},{17,16},{19,... | collective-permute-start | bytes 3145736 | tf_op jit(solution)/shard_map/ppermute | solution.py:59
  15.8 81.4 %collective-permute-start.2 = (bf16[4,256,1024]{2,1,0:T(8,128)(2,1)S(1)}, bf16[4,256,1024]{2,1,0:T(8,128)(2,1)S(1)}, u32[]{:S(2)}, u32[]{:S(2)}) collective-permute-start(bf16[4,256,1024]{2,1,0:T(8,128)(2,1)S(1)} %copy-done.1), channel_id=1, source_target_pairs={{0,4},{4,8},{8,12},{12,0},{1,5},{5,9},{9,13},{13,1},{2,6},{6,10},{... | collective-permute-start | bytes 6291464 | tf_op jit(solution)/shard_map/ppermute | solution.py:117
  19.2 99.5 %collective-permute-start.6 = (f32[256,1024]{1,0:T(8,128)S(1)}, f32[256,1024]{1,0:T(8,128)S(1)}, u32[]{:S(2)}, u32[]{:S(2)}) collective-permute-start(f32[256,1024]{1,0:T(8,128)S(1)} %add.85), channel_id=1, source_target_pairs={{2,0},{7,5},{8,10},{13,15},{18,16},{23,21},{24,26},{29,31}} | collective-permute-start | bytes 3145736 | tf_op jit(solution)/shard_map/ppermute | solution.py:69
  51.5 61.6 %collective-permute-start.4 = (bf16[4,96,1024]{2,1,0:T(8,128)(2,1)S(1)}, bf16[4,96,1024]{2,1,0:T(8,128)(2,1)S(1)}, u32[]{:S(2)}, u32[]{:S(2)}) collective-permute-start(bf16[4,96,1024]{2,1,0:T(8,128)(2,1)S(1)} %slice.33), channel_id=1, source_target_pairs={{0,12},{4,0},{8,4},{12,8},{1,13},{5,1},{9,5},{13,9},{2,14},{6,2},{... | collective-permute-start | bytes 2359304 | tf_op jit(solution)/shard_map/ppermute | solution.py:118
  58.8 55.1 %collective-permute-start.7 = (f32[256,1024]{1,0:T(8,128)S(1)}, f32[256,1024]{1,0:T(8,128)S(1)}, u32[]{:S(2)}, u32[]{:S(2)}) collective-permute-start(f32[256,1024]{1,0:T(8,128)S(1)} %fusion.82), channel_id=1, source_target_pairs={{0,1},{2,3},{5,4},{7,6},{8,9},{10,11},{13,12},{15,14},{16,17},{18,... | collective-permute-start | bytes 3145736 | tf_op jit(solution)/shard_map/ppermute | solution.py:59
  100.5 18.4 %collective-permute-start.3 = (f32[256,1024]{1,0:T(8,128)S(1)}, f32[256,1024]{1,0:T(8,128)S(1)}, u32[]{:S(2)}, u32[]{:S(2)}) collective-permute-start(f32[256,1024]{1,0:T(8,128)S(1)} %fusion.52), channel_id=1, source_target_pairs={{0,1},{2,3},{5,4},{7,6},{8,9},{10,11},{13,12},{15,14},{16,17},{18,... | collective-permute-start | bytes 3145736 | tf_op jit(solution)/shard_map/ppermute | solution.py:59
  102.0 38.8 %collective-permute-start.1 = (bf16[4,160,1024]{2,1,0:T(8,128)(2,1)S(1)}, bf16[4,160,1024]{2,1,0:T(8,128)(2,1)S(1)}, u32[]{:S(2)}, u32[]{:S(2)}) collective-permute-start(bf16[4,160,1024]{2,1,0:T(8,128)(2,1)S(1)} %slice.32), channel_id=1, source_target_pairs={{0,12},{4,0},{8,4},{12,8},{1,13},{5,1},{9,5},{13,9},{2,14},{6,2},{... | collective-permute-start | bytes 3932168 | tf_op jit(solution)/shard_map/ppermute | solution.py:119
  114.1 11.2 %collective-permute-start.8 = (f32[256,1024]{1,0:T(8,128)S(1)}, f32[256,1024]{1,0:T(8,128)S(1)}, u32[]{:S(2)}, u32[]{:S(2)}) collective-permute-start(f32[256,1024]{1,0:T(8,128)S(1)} %add.90), channel_id=1, source_target_pairs={{3,1},{4,6},{9,11},{14,12},{19,17},{20,22},{25,27},{30,28}} | collective-permute-start | bytes 3145736 | tf_op jit(solution)/shard_map/ppermute | solution.py:69
  117.4 3.6 %collective-permute-start.11 = (f32[96,1024]{1,0:T(8,128)S(1)}, f32[96,1024]{1,0:T(8,128)S(1)}, u32[]{:S(2)}, u32[]{:S(2)}) collective-permute-start(f32[96,1024]{1,0:T(8,128)S(1)} %fusion.157), channel_id=1, source_target_pairs={{1,0},{3,2},{4,5},{6,7},{9,8},{11,10},{12,13},{14,15},{17,16},{19,... | collective-permute-start | bytes 1179656 | tf_op jit(solution)/shard_map/ppermute | solution.py:59
  121.1 25.5 %collective-permute-start.12 = (f32[96,1024]{1,0:T(8,128)S(1)}, f32[96,1024]{1,0:T(8,128)}, u32[]{:S(2)}, u32[]{:S(2)}) collective-permute-start(f32[96,1024]{1,0:T(8,128)S(1)} %add.97), channel_id=1, source_target_pairs={{0,2},{5,7},{10,8},{15,13},{16,18},{21,23},{26,24},{31,29}} | collective-permute-start | bytes 1179656 | tf_op jit(solution)/shard_map/ppermute | solution.py:69
  125.5 19.6 %collective-permute-start.9 = (f32[256,1024]{1,0:T(8,128)S(1)}, f32[256,1024]{1,0:T(8,128)S(1)}, u32[]{:S(2)}, u32[]{:S(2)}) collective-permute-start(f32[256,1024]{1,0:T(8,128)S(1)} %add.81), channel_id=1, source_target_pairs={{1,3},{6,4},{11,9},{12,14},{17,19},{22,20},{27,25},{28,30}} | collective-permute-start | bytes 3145736 | tf_op jit(solution)/shard_map/ppermute | solution.py:69
  145.2 4.3 %collective-permute-start.10 = (f32[160,1024]{1,0:T(8,128)}, f32[160,1024]{1,0:T(8,128)}, u32[]{:S(2)}, u32[]{:S(2)}) collective-permute-start(f32[160,1024]{1,0:T(8,128)} %fusion.124), channel_id=1, source_target_pairs={{1,0},{3,2},{4,5},{6,7},{9,8},{11,10},{12,13},{14,15},{17,16},{19,... | collective-permute-start | bytes 1966088 | tf_op jit(solution)/shard_map/ppermute | solution.py:59
  151.0 11.5 %collective-permute-start.13 = (f32[160,1024]{1,0:T(8,128)S(1)}, f32[160,1024]{1,0:T(8,128)S(1)}, u32[]{:S(2)}, u32[]{:S(2)}) collective-permute-start(f32[160,1024]{1,0:T(8,128)S(1)} %add.93), channel_id=1, source_target_pairs={{0,2},{5,7},{10,8},{15,13},{16,18},{21,23},{26,24},{31,29}} | collective-permute-start | bytes 1966088 | tf_op jit(solution)/shard_map/ppermute | solution.py:69

commit v18 on v17

--- a/solution.py
+++ b/solution.py
@@ -73,7 +73,7 @@
 def ring(train_features, query_features, residual_weights, keepers, scale):
     planes, ratio = keepers.planes, keepers.ratio
     rows = query_features.shape[1]
-    cut = 5 * rows // 8
+    cut = 9 * rows // 16
     right = [(s, (s + 1) % planes) for s in range(planes)]
     left = [(s, (s - 1) % planes) for s in range(planes)]
     tops, lows = [], []

time: 167 us -> 170 us (1.018); the launches traced: 164 us -> 170 us
  waiting for transfers between devices: 105 us -> 109 us
    ppermute x1, waiting for transfers between devices: 14.6 us -> 19.1 us  [ring(): top = lax.ppermute(from_right[:, :cut], 'ex', left)]
    ppermute x5, waiting for transfers between devices: 7.01 us -> 3.2 us  [near_sums(): total = total + lax.ppermute(partial, PLACE, pairs)]
  transfers between devices with their start and end apart: 14 -> 14, of which waited for: 8 -> 7; matrix products, arithmetic and copies ran while one was open for 16% -> 16% of each run, Pallas kernels for 0% -> 0%
where the time goes in v18:
time: 170 us
  waiting for transfers between devices  109 us (64%)
  starting transfers between devices  30.7 us (18%)
  matrix products  22.4 us (13%)
  other arithmetic  5.88 us (3%)
    ppermute x1, waiting for transfers between devices, ring(): from_left = lax.ppermute(from_left, 'ex', right)  37 us
    ppermute x1, waiting for transfers between devices, ring(): from_right = lax.ppermute(from_right, 'ex', left)  31 us
    dot_general x20, matrix products, weighted(): lax.dot_general(piece, examples, (((1,), (1,)), ((), ())), preferred_elem...  22.4 us
    ppermute x1, waiting for transfers between devices, ring(): top = lax.ppermute(from_right[:, :cut], 'ex', left)  19.1 us
    ppermute x5, starting transfers between devices, far_sums(): whole = whole + lax.ppermute(total, PLACE, pairs)  11.5 us
    ppermute x5, waiting for transfers between devices, far_sums(): whole = whole + lax.ppermute(total, PLACE, pairs)  9.6 us
    ppermute x1, waiting for transfers between devices, ring(): low = lax.ppermute(from_right[:, cut:], 'ex', left)  9.44 us
    ppermute x5, starting transfers between devices, near_sums(): total = total + lax.ppermute(partial, PLACE, pairs)  6.59 us
  transfers between devices with their start and end apart: 14, of which 7 were waited for; matrix products, arithmetic and copies ran while one was open for 16% of the time, Pallas kernels for 0%

profile of v18, /device:TPU:0, one launch (start us, length us, event | category | flops | bytes accessed | tf_op | source)
XLA Modules:
  0.0 169.8 jit_solution(4158218795796998910)
XLA Ops:
  0.0 5.0 %collective-permute-start = (bf16[4,256,1024]{2,1,0:T(8,128)(2,1)}, bf16[4,256,1024]{2,1,0:T(8,128)(2,1)S(1)}, u32[]{:S(2)}, u32[]{:S(2)}) collective-permute-start(bf16[4,256,1024]{2,1,0:T(8,128)(2,1)} %param.4), channel_id=1, source_target_pairs={{0,12},{4,0},{8,4},{12,8},{1,13},{5,1},{9,5},{13,9},{2,14},{6,2},{... | collective-permute-start | bytes 6291464 | tf_op jit(solution)/shard_map/ppermute | solution.py:116
  5.0 0.9 fusion.192
  5.9 2.6 %fusion.88 = f32[256,1024]{1,0:T(8,128)S(1)} fusion(bf16[4,1024,1024]{2,1,0:T(8,128)(2,1)} %param.3, bf16[4,256,1024]{2,1,0:T(8,128)(2,1)} %param.4, f32[1024]{0:T(1024)S(1)} %bitcast.193), kind=kOutput, calls=%fused_computation.56 | convolution fusion | flops 537133056 | bytes 3674112 | tf_op jit(solution)/shard_map/dot_general | solution.py:16
  8.6 3.0 %fusion.106 = f32[256,1024]{1,0:T(8,128)S(1)} fusion(bf16[4,1024,1024]{2,1,0:T(8,128)(2,1)} %param.3, bf16[4,256,1024]{2,1,0:T(8,128)(2,1)} %param.4, f32[1024]{0:T(1024)S(1)} %bitcast.203), kind=kOutput, calls=%fused_computation.62 | convolution fusion | flops 537133056 | bytes 3674112 | tf_op jit(solution)/shard_map/dot_general | solution.py:16
  11.6 1.9 %fusion.97 = f32[256,1024]{1,0:T(8,128)S(1)} fusion(bf16[4,1024,1024]{2,1,0:T(8,128)(2,1)S(1)} %copy-done, bf16[4,256,1024]{2,1,0:T(8,128)(2,1)} %param.4, f32[1024]{0:T(1024)S(1)} %bitcast.198), kind=kOutput, calls=%fused_computation.59 | convolution fusion | flops 537133056 | bytes 3674112 | tf_op jit(solution)/shard_map/dot_general | solution.py:16
  13.6 0.9 fusion.67
  14.4 1.3 collective-permute-start.5
  15.8 3.2 %collective-permute-done.5 = f32[256,1024]{1,0:T(8,128)S(1)} collective-permute-done((f32[256,1024]{1,0:T(8,128)S(1)}, f32[256,1024]{1,0:T(8,128)S(1)}, u32[]{:S(2)}, u32[]{:S(2)}) %collective-permute-start.5) | collective-permute-done | bytes 1048608 | tf_op jit(solution)/shard_map/ppermute | solution.py:59
  19.0 0.2 add.85
  19.2 1.3 collective-permute-start.6
  20.5 31.0 %collective-permute-done = bf16[4,256,1024]{2,1,0:T(8,128)(2,1)S(1)} collective-permute-done((bf16[4,256,1024]{2,1,0:T(8,128)(2,1)}, bf16[4,256,1024]{2,1,0:T(8,128)(2,1)S(1)}, u32[]{:S(2)}, u32[]{:S(2)}) %collective-permute-start) | collective-permute-done | bytes 2097184 | tf_op jit(solution)/shard_map/ppermute | solution.py:116
  51.5 4.2 %collective-permute-start.4 = (bf16[4,112,1024]{2,1,0:T(8,128)(2,1)S(1)}, bf16[4,112,1024]{2,1,0:T(8,128)(2,1)S(1)}, u32[]{:S(2)}, u32[]{:S(2)}) collective-permute-start(bf16[4,112,1024]{2,1,0:T(8,128)(2,1)S(1)} %slice.33), channel_id=1, source_target_pairs={{0,12},{4,0},{8,4},{12,8},{1,13},{5,1},{9,5},{13,9},{2,14},{6,2},{... | collective-permute-start | bytes 2752520 | tf_op jit(solution)/shard_map/ppermute | solution.py:118
  55.7 0.7 fusion.109
  56.5 0.7 fusion.100
  57.2 0.7 fusion.91
  58.0 0.9 fusion.82
  58.9 1.4 collective-permute-start.7
  60.2 37.0 %collective-permute-done.2 = bf16[4,256,1024]{2,1,0:T(8,128)(2,1)S(1)} collective-permute-done((bf16[4,256,1024]{2,1,0:T(8,128)(2,1)S(1)}, bf16[4,256,1024]{2,1,0:T(8,128)(2,1)S(1)}, u32[]{:S(2)}, u32[]{:S(2)}) %collective-permute-start.2) | collective-permute-done | bytes 2097184 | tf_op jit(solution)/shard_map/ppermute | solution.py:117
  97.2 0.8 fusion.103
  98.0 0.8 fusion.94
  98.8 0.8 fusion.85
  99.6 0.9 fusion.52
  100.5 1.4 collective-permute-start.3
  102.0 3.3 %collective-permute-start.1 = (bf16[4,144,1024]{2,1,0:T(8,128)(2,1)S(1)}, bf16[4,144,1024]{2,1,0:T(8,128)(2,1)S(1)}, u32[]{:S(2)}, u32[]{:S(2)}) collective-permute-start(bf16[4,144,1024]{2,1,0:T(8,128)(2,1)S(1)} %slice.32), channel_id=1, source_target_pairs={{0,12},{4,0},{8,4},{12,8},{1,13},{5,1},{9,5},{13,9},{2,14},{6,2},{... | collective-permute-start | bytes 3538952 | tf_op jit(solution)/shard_map/ppermute | solution.py:119
  105.6 0.9 collective-permute-start.8
  106.5 9.4 %collective-permute-done.4 = bf16[4,112,1024]{2,1,0:T(8,128)(2,1)S(1)} collective-permute-done((bf16[4,112,1024]{2,1,0:T(8,128)(2,1)S(1)}, bf16[4,112,1024]{2,1,0:T(8,128)(2,1)S(1)}, u32[]{:S(2)}, u32[]{:S(2)}) %collective-permute-start.4) | collective-permute-done | bytes 917536 | tf_op jit(solution)/shard_map/ppermute | solution.py:118
  115.9 0.8 fusion.157
  116.8 0.8 fusion.154
  117.6 0.8 fusion.151
  118.4 0.9 fusion.148
  119.3 1.3 collective-permute-start.11
  120.6 0.2 add.81
  121.0 0.7 collective-permute-start.9
  121.7 19.1 %collective-permute-done.1 = bf16[4,144,1024]{2,1,0:T(8,128)(2,1)S(1)} collective-permute-done((bf16[4,144,1024]{2,1,0:T(8,128)(2,1)S(1)}, bf16[4,144,1024]{2,1,0:T(8,128)(2,1)S(1)}, u32[]{:S(2)}, u32[]{:S(2)}) %collective-permute-start.1) | collective-permute-done | bytes 1179680 | tf_op jit(solution)/shard_map/ppermute | solution.py:119
  140.8 0.8 fusion.127
  141.7 0.8 fusion.124
  142.5 0.8 fusion.121
  143.4 0.8 add.97
  144.2 4.2 %collective-permute-start.12 = (f32[112,1024]{1,0:T(8,128)}, f32[112,1024]{1,0:T(8,128)}, u32[]{:S(2)}, u32[]{:S(2)}) collective-permute-start(f32[112,1024]{1,0:T(8,128)} %add.97), channel_id=1, source_target_pairs={{0,2},{5,7},{10,8},{15,13},{16,18},{21,23},{26,24},{31,29}} | collective-permute-start | bytes 1376264 | tf_op jit(solution)/shard_map/ppermute | solution.py:69
  148.4 1.7 %fusion.133 = f32[144,1024]{1,0:T(8,128)} fusion(f32[144,1024]{1,0:T(8,128)S(1)} %fusion.127, f32[144,1024]{1,0:T(8,128)S(1)} %fusion.124, f32[144,1024]{1,0:T(8,128)S(1)} %fusion.121, bf16[4,1024,1024]{2,1,0:T(8,128)(2,1)S(1)} %copy-done, bf16[4,144,1024]{2,1,0:T(8,128)(2,1)S(1)} %collective-permute-done.1, f32[1024]{0:T(1024)S(1)} %bitcast.192), kind=kOutput, calls=%fused_computation.71 | convolution fusion | flops 302727168 | bytes 4755456 | tf_op jit(solution)/shard_map/dot_general | solution.py:16
  150.3 1.3 collective-permute-start.10
  151.7 2.2 %collective-permute-done.12 = f32[112,1024]{1,0:T(8,128)} collective-permute-done((f32[112,1024]{1,0:T(8,128)}, f32[112,1024]{1,0:T(8,128)}, u32[]{:S(2)}, u32[]{:S(2)}) %collective-permute-start.12) | collective-permute-done | bytes 458784 | tf_op jit(solution)/shard_map/ppermute | solution.py:69
  153.9 1.3 fusion.191
  155.3 1.3 add.93
  156.6 4.4 %collective-permute-start.13 = (f32[144,1024]{1,0:T(8,128)S(1)}, f32[144,1024]{1,0:T(8,128)S(1)}, u32[]{:S(2)}, u32[]{:S(2)}) collective-permute-start(f32[144,1024]{1,0:T(8,128)S(1)} %add.93), channel_id=1, source_target_pairs={{0,2},{5,7},{10,8},{15,13},{16,18},{21,23},{26,24},{31,29}} | collective-permute-start | bytes 1769480 | tf_op jit(solution)/shard_map/ppermute | solution.py:69
  161.0 7.3 %collective-permute-done.13 = f32[144,1024]{1,0:T(8,128)S(1)} collective-permute-done((f32[144,1024]{1,0:T(8,128)S(1)}, f32[144,1024]{1,0:T(8,128)S(1)}, u32[]{:S(2)}, u32[]{:S(2)}) %collective-permute-start.13) | collective-permute-done | bytes 589856 | tf_op jit(solution)/shard_map/ppermute | solution.py:69
  168.4 0.3 fusion.181
  168.7 1.1 pad_maximum_fusion
  (18 shorter events, 0.9 us)
Async XLA Ops:
  0.0 51.4 %collective-permute-start = (bf16[4,256,1024]{2,1,0:T(8,128)(2,1)}, bf16[4,256,1024]{2,1,0:T(8,128)(2,1)S(1)}, u32[]{:S(2)}, u32[]{:S(2)}) collective-permute-start(bf16[4,256,1024]{2,1,0:T(8,128)(2,1)} %param.4), channel_id=1, source_target_pairs={{0,12},{4,0},{8,4},{12,8},{1,13},{5,1},{9,5},{13,9},{2,14},{6,2},{... | collective-permute-start | bytes 6291464 | tf_op jit(solution)/shard_map/ppermute | solution.py:116
  5.9 5.7 %copy-start = (bf16[4,1024,1024]{2,1,0:T(8,128)(2,1)S(1)}, bf16[4,1024,1024]{2,1,0:T(8,128)(2,1)}, u32[]{:S(2)}) copy-start(bf16[4,1024,1024]{2,1,0:T(8,128)(2,1)} %param.3) | copy-start | bytes 25165828
  11.6 2.0 %copy-start.1 = (bf16[4,256,1024]{2,1,0:T(8,128)(2,1)S(1)}, bf16[4,256,1024]{2,1,0:T(8,128)(2,1)}, u32[]{:S(2)}) copy-start(bf16[4,256,1024]{2,1,0:T(8,128)(2,1)} %param.4) | copy-start | bytes 6291460
  14.4 4.6 %collective-permute-start.5 = (f32[256,1024]{1,0:T(8,128)S(1)}, f32[256,1024]{1,0:T(8,128)S(1)}, u32[]{:S(2)}, u32[]{:S(2)}) collective-permute-start(f32[256,1024]{1,0:T(8,128)S(1)} %fusion.67), channel_id=1, source_target_pairs={{1,0},{3,2},{4,5},{6,7},{9,8},{11,10},{12,13},{14,15},{17,16},{19,... | collective-permute-start | bytes 3145736 | tf_op jit(solution)/shard_map/ppermute | solution.py:59
  15.7 81.4 %collective-permute-start.2 = (bf16[4,256,1024]{2,1,0:T(8,128)(2,1)S(1)}, bf16[4,256,1024]{2,1,0:T(8,128)(2,1)S(1)}, u32[]{:S(2)}, u32[]{:S(2)}) collective-permute-start(bf16[4,256,1024]{2,1,0:T(8,128)(2,1)S(1)} %copy-done.1), channel_id=1, source_target_pairs={{0,4},{4,8},{8,12},{12,0},{1,5},{5,9},{9,13},{13,1},{2,6},{6,10},{... | collective-permute-start | bytes 6291464 | tf_op jit(solution)/shard_map/ppermute | solution.py:117
  19.2 86.1 %collective-permute-start.6 = (f32[256,1024]{1,0:T(8,128)S(1)}, f32[256,1024]{1,0:T(8,128)S(1)}, u32[]{:S(2)}, u32[]{:S(2)}) collective-permute-start(f32[256,1024]{1,0:T(8,128)S(1)} %add.85), channel_id=1, source_target_pairs={{2,0},{7,5},{8,10},{13,15},{18,16},{23,21},{24,26},{29,31}} | collective-permute-start | bytes 3145736 | tf_op jit(solution)/shard_map/ppermute | solution.py:69
  51.5 64.4 %collective-permute-start.4 = (bf16[4,112,1024]{2,1,0:T(8,128)(2,1)S(1)}, bf16[4,112,1024]{2,1,0:T(8,128)(2,1)S(1)}, u32[]{:S(2)}, u32[]{:S(2)}) collective-permute-start(bf16[4,112,1024]{2,1,0:T(8,128)(2,1)S(1)} %slice.33), channel_id=1, source_target_pairs={{0,12},{4,0},{8,4},{12,8},{1,13},{5,1},{9,5},{13,9},{2,14},{6,2},{... | collective-permute-start | bytes 2752520 | tf_op jit(solution)/shard_map/ppermute | solution.py:118
  58.9 46.5 %collective-permute-start.7 = (f32[256,1024]{1,0:T(8,128)S(1)}, f32[256,1024]{1,0:T(8,128)S(1)}, u32[]{:S(2)}, u32[]{:S(2)}) collective-permute-start(f32[256,1024]{1,0:T(8,128)S(1)} %fusion.82), channel_id=1, source_target_pairs={{0,1},{2,3},{5,4},{7,6},{8,9},{10,11},{13,12},{15,14},{16,17},{18,... | collective-permute-start | bytes 3145736 | tf_op jit(solution)/shard_map/ppermute | solution.py:59
  100.5 20.1 %collective-permute-start.3 = (f32[256,1024]{1,0:T(8,128)S(1)}, f32[256,1024]{1,0:T(8,128)S(1)}, u32[]{:S(2)}, u32[]{:S(2)}) collective-permute-start(f32[256,1024]{1,0:T(8,128)S(1)} %fusion.52), channel_id=1, source_target_pairs={{0,1},{2,3},{5,4},{7,6},{8,9},{10,11},{13,12},{15,14},{16,17},{18,... | collective-permute-start | bytes 3145736 | tf_op jit(solution)/shard_map/ppermute | solution.py:59
  102.0 38.8 %collective-permute-start.1 = (bf16[4,144,1024]{2,1,0:T(8,128)(2,1)S(1)}, bf16[4,144,1024]{2,1,0:T(8,128)(2,1)S(1)}, u32[]{:S(2)}, u32[]{:S(2)}) collective-permute-start(bf16[4,144,1024]{2,1,0:T(8,128)(2,1)S(1)} %slice.32), channel_id=1, source_target_pairs={{0,12},{4,0},{8,4},{12,8},{1,13},{5,1},{9,5},{13,9},{2,14},{6,2},{... | collective-permute-start | bytes 3538952 | tf_op jit(solution)/shard_map/ppermute | solution.py:119
  105.6 15.2 %collective-permute-start.8 = (f32[256,1024]{1,0:T(8,128)S(1)}, f32[256,1024]{1,0:T(8,128)S(1)}, u32[]{:S(2)}, u32[]{:S(2)}) collective-permute-start(f32[256,1024]{1,0:T(8,128)S(1)} %add.90), channel_id=1, source_target_pairs={{3,1},{4,6},{9,11},{14,12},{19,17},{20,22},{25,27},{30,28}} | collective-permute-start | bytes 3145736 | tf_op jit(solution)/shard_map/ppermute | solution.py:69
  119.3 24.1 %collective-permute-start.11 = (f32[112,1024]{1,0:T(8,128)S(1)}, f32[112,1024]{1,0:T(8,128)S(1)}, u32[]{:S(2)}, u32[]{:S(2)}) collective-permute-start(f32[112,1024]{1,0:T(8,128)S(1)} %fusion.148), channel_id=1, source_target_pairs={{1,0},{3,2},{4,5},{6,7},{9,8},{11,10},{12,13},{14,15},{17,16},{19,... | collective-permute-start | bytes 1376264 | tf_op jit(solution)/shard_map/ppermute | solution.py:59
  121.0 29.2 %collective-permute-start.9 = (f32[256,1024]{1,0:T(8,128)S(1)}, f32[256,1024]{1,0:T(8,128)S(1)}, u32[]{:S(2)}, u32[]{:S(2)}) collective-permute-start(f32[256,1024]{1,0:T(8,128)S(1)} %add.81), channel_id=1, source_target_pairs={{1,3},{6,4},{11,9},{12,14},{17,19},{22,20},{27,25},{28,30}} | collective-permute-start | bytes 3145736 | tf_op jit(solution)/shard_map/ppermute | solution.py:69
  144.2 9.7 %collective-permute-start.12 = (f32[112,1024]{1,0:T(8,128)}, f32[112,1024]{1,0:T(8,128)}, u32[]{:S(2)}, u32[]{:S(2)}) collective-permute-start(f32[112,1024]{1,0:T(8,128)} %add.97), channel_id=1, source_target_pairs={{0,2},{5,7},{10,8},{15,13},{16,18},{21,23},{26,24},{31,29}} | collective-permute-start | bytes 1376264 | tf_op jit(solution)/shard_map/ppermute | solution.py:69
  150.3 5.0 %collective-permute-start.10 = (f32[144,1024]{1,0:T(8,128)}, f32[144,1024]{1,0:T(8,128)}, u32[]{:S(2)}, u32[]{:S(2)}) collective-permute-start(f32[144,1024]{1,0:T(8,128)} %fusion.133), channel_id=1, source_target_pairs={{1,0},{3,2},{4,5},{6,7},{9,8},{11,10},{12,13},{14,15},{17,16},{19,... | collective-permute-start | bytes 1769480 | tf_op jit(solution)/shard_map/ppermute | solution.py:59
  156.6 11.8 %collective-permute-start.13 = (f32[144,1024]{1,0:T(8,128)S(1)}, f32[144,1024]{1,0:T(8,128)S(1)}, u32[]{:S(2)}, u32[]{:S(2)}) collective-permute-start(f32[144,1024]{1,0:T(8,128)S(1)} %add.93), channel_id=1, source_target_pairs={{0,2},{5,7},{10,8},{15,13},{16,18},{21,23},{26,24},{31,29}} | collective-permute-start | bytes 1769480 | tf_op jit(solution)/shard_map/ppermute | solution.py:69

commit v19 on v17

--- a/solution.py
+++ b/solution.py
@@ -116,8 +116,9 @@
     from_right = lax.ppermute(from_right, "ex", left)
     from_left = lax.ppermute(from_left, "ex", right)
     low = lax.ppermute(from_right[:, cut:], "ex", left)
-    top = lax.ppermute(from_right[:, :cut], "ex", left)
-    ahead = far(near(from_right, step), step, both)
+    total_ahead = near(from_right, step)
+    ahead = far(total_ahead, step, both)
+    top = lax.ppermute(after(from_right[:, :cut], total_ahead), "ex", left)
     total = near(from_left, -step)
     behind = far(total, -step, both, low, own, ahead)
     below = far(near(low, half), half, (lows,))

time: 167 us -> 167 us (level)
  no operation moved by 1% of the time
where the time goes in v19:
time: 167 us; the launch traced here: 164 us
  waiting for transfers between devices  105 us (63%)
  starting transfers between devices  29.7 us (18%)
  matrix products  22.3 us (13%)
  other arithmetic  4.92 us (3%)
    ppermute x1, waiting for transfers between devices, ring(): from_left = lax.ppermute(from_left, 'ex', right)  37 us
    ppermute x1, waiting for transfers between devices, ring(): from_right = lax.ppermute(from_right, 'ex', left)  30.9 us
    dot_general x20, matrix products, weighted(): lax.dot_general(piece, examples, (((1,), (1,)), ((), ())), preferred_elem...  22.3 us
    ppermute x1, waiting for transfers between devices, ring(): top = lax.ppermute(after(from_right[:, :cut], total_ahead), 'ex', left)  14.8 us
    ppermute x5, starting transfers between devices, far_sums(): whole = whole + lax.ppermute(total, PLACE, pairs)  10.5 us
    ppermute x5, waiting for transfers between devices, far_sums(): whole = whole + lax.ppermute(total, PLACE, pairs)  8.06 us
    ppermute x1, waiting for transfers between devices, ring(): low = lax.ppermute(from_right[:, cut:], 'ex', left)  7.68 us
    ppermute x5, waiting for transfers between devices, near_sums(): total = total + lax.ppermute(partial, PLACE, pairs)  7.01 us
  transfers between devices with their start and end apart: 14, of which 8 were waited for; matrix products, arithmetic and copies ran while one was open for 16% of the time, Pallas kernels for 0%

profile of v19, /device:TPU:0, one launch (start us, length us, event | category | flops | bytes accessed | tf_op | source)
XLA Modules:
  0.0 163.9 jit_solution(6185200750325552663)
XLA Ops:
  0.0 5.0 %collective-permute-start = (bf16[4,256,1024]{2,1,0:T(8,128)(2,1)}, bf16[4,256,1024]{2,1,0:T(8,128)(2,1)S(1)}, u32[]{:S(2)}, u32[]{:S(2)}) collective-permute-start(bf16[4,256,1024]{2,1,0:T(8,128)(2,1)} %param.4), channel_id=1, source_target_pairs={{0,12},{4,0},{8,4},{12,8},{1,13},{5,1},{9,5},{13,9},{2,14},{6,2},{... | collective-permute-start | bytes 6291464 | tf_op jit(solution)/shard_map/ppermute | solution.py:116
  5.0 0.9 fusion.192
  5.9 2.6 %fusion.91 = f32[256,1024]{1,0:T(8,128)S(1)} fusion(bf16[4,1024,1024]{2,1,0:T(8,128)(2,1)} %param.3, bf16[4,256,1024]{2,1,0:T(8,128)(2,1)} %param.4, f32[1024]{0:T(1024)S(1)} %bitcast.193), kind=kOutput, calls=%fused_computation.57 | convolution fusion | flops 537133056 | bytes 3674112 | tf_op jit(solution)/shard_map/dot_general | solution.py:16
  8.6 3.0 %fusion.109 = f32[256,1024]{1,0:T(8,128)S(1)} fusion(bf16[4,1024,1024]{2,1,0:T(8,128)(2,1)} %param.3, bf16[4,256,1024]{2,1,0:T(8,128)(2,1)} %param.4, f32[1024]{0:T(1024)S(1)} %bitcast.203), kind=kOutput, calls=%fused_computation.63 | convolution fusion | flops 537133056 | bytes 3674112 | tf_op jit(solution)/shard_map/dot_general | solution.py:16
  11.6 1.9 %fusion.100 = f32[256,1024]{1,0:T(8,128)S(1)} fusion(bf16[4,1024,1024]{2,1,0:T(8,128)(2,1)S(1)} %copy-done, bf16[4,256,1024]{2,1,0:T(8,128)(2,1)} %param.4, f32[1024]{0:T(1024)S(1)} %bitcast.198), kind=kOutput, calls=%fused_computation.60 | convolution fusion | flops 537133056 | bytes 3674112 | tf_op jit(solution)/shard_map/dot_general | solution.py:16
  13.6 0.9 fusion.82
  14.5 1.3 collective-permute-start.6
  15.9 3.2 %collective-permute-done.6 = f32[256,1024]{1,0:T(8,128)S(1)} collective-permute-done((f32[256,1024]{1,0:T(8,128)S(1)}, f32[256,1024]{1,0:T(8,128)S(1)}, u32[]{:S(2)}, u32[]{:S(2)}) %collective-permute-start.6) | collective-permute-done | bytes 1048608 | tf_op jit(solution)/shard_map/ppermute | solution.py:59
  19.1 0.2 add.89
  19.2 1.3 collective-permute-start.7
  20.5 30.9 %collective-permute-done = bf16[4,256,1024]{2,1,0:T(8,128)(2,1)S(1)} collective-permute-done((bf16[4,256,1024]{2,1,0:T(8,128)(2,1)}, bf16[4,256,1024]{2,1,0:T(8,128)(2,1)S(1)}, u32[]{:S(2)}, u32[]{:S(2)}) %collective-permute-start) | collective-permute-done | bytes 2097184 | tf_op jit(solution)/shard_map/ppermute | solution.py:116
  51.5 4.2 %collective-permute-start.5 = (bf16[4,96,1024]{2,1,0:T(8,128)(2,1)S(1)}, bf16[4,96,1024]{2,1,0:T(8,128)(2,1)S(1)}, u32[]{:S(2)}, u32[]{:S(2)}) collective-permute-start(bf16[4,96,1024]{2,1,0:T(8,128)(2,1)S(1)} %slice.33), channel_id=1, source_target_pairs={{0,12},{4,0},{8,4},{12,8},{1,13},{5,1},{9,5},{13,9},{2,14},{6,2},{... | collective-permute-start | bytes 2359304 | tf_op jit(solution)/shard_map/ppermute | solution.py:118
  55.7 0.7 fusion.103
  56.5 0.7 fusion.94
  57.2 0.7 fusion.85
  58.0 0.9 fusion.52
  58.8 1.4 collective-permute-start.1
  60.2 37.0 %collective-permute-done.3 = bf16[4,256,1024]{2,1,0:T(8,128)(2,1)S(1)} collective-permute-done((bf16[4,256,1024]{2,1,0:T(8,128)(2,1)S(1)}, bf16[4,256,1024]{2,1,0:T(8,128)(2,1)S(1)}, u32[]{:S(2)}, u32[]{:S(2)}) %collective-permute-start.3) | collective-permute-done | bytes 2097184 | tf_op jit(solution)/shard_map/ppermute | solution.py:117
  97.2 0.8 fusion.106
  98.0 0.8 fusion.97
  98.8 0.8 fusion.88
  99.6 0.9 fusion.67
  100.5 1.4 collective-permute-start.4
  102.2 3.3 %collective-permute-start.2 = (bf16[4,160,1024]{2,1,0:T(8,128)(2,1)S(1)}, bf16[4,160,1024]{2,1,0:T(8,128)(2,1)S(1)}, u32[]{:S(2)}, u32[]{:S(2)}) collective-permute-start(bf16[4,160,1024]{2,1,0:T(8,128)(2,1)S(1)} %slice.32), channel_id=1, source_target_pairs={{0,12},{4,0},{8,4},{12,8},{1,13},{5,1},{9,5},{13,9},{2,14},{6,2},{... | collective-permute-start | bytes 3932168 | tf_op jit(solution)/shard_map/ppermute | solution.py:121
  105.5 7.7 %collective-permute-done.5 = bf16[4,96,1024]{2,1,0:T(8,128)(2,1)S(1)} collective-permute-done((bf16[4,96,1024]{2,1,0:T(8,128)(2,1)S(1)}, bf16[4,96,1024]{2,1,0:T(8,128)(2,1)S(1)}, u32[]{:S(2)}, u32[]{:S(2)}) %collective-permute-start.5) | collective-permute-done | bytes 786464 | tf_op jit(solution)/shard_map/ppermute | solution.py:118
  113.1 0.8 fusion.145
  113.9 0.9 collective-permute-start.8
  114.8 0.8 fusion.142
  115.6 0.8 fusion.139
  116.4 0.8 fusion.157
  117.3 1.3 collective-permute-start.11
  118.9 2.0 %collective-permute-done.11 = f32[96,1024]{1,0:T(8,128)S(1)} collective-permute-done((f32[96,1024]{1,0:T(8,128)S(1)}, f32[96,1024]{1,0:T(8,128)S(1)}, u32[]{:S(2)}, u32[]{:S(2)}) %collective-permute-start.11) | collective-permute-done | bytes 393248 | tf_op jit(solution)/shard_map/ppermute | solution.py:59
  120.9 4.2 %collective-permute-start.12 = (f32[96,1024]{1,0:T(8,128)S(1)}, f32[96,1024]{1,0:T(8,128)}, u32[]{:S(2)}, u32[]{:S(2)}) collective-permute-start(f32[96,1024]{1,0:T(8,128)S(1)} %add.97), channel_id=1, source_target_pairs={{0,2},{5,7},{10,8},{15,13},{16,18},{21,23},{26,24},{31,29}} | collective-permute-start | bytes 1179656 | tf_op jit(solution)/shard_map/ppermute | solution.py:69
  125.1 0.2 add.91
  125.3 0.7 collective-permute-start.9
  126.0 14.8 %collective-permute-done.2 = bf16[4,160,1024]{2,1,0:T(8,128)(2,1)S(1)} collective-permute-done((bf16[4,160,1024]{2,1,0:T(8,128)(2,1)S(1)}, bf16[4,160,1024]{2,1,0:T(8,128)(2,1)S(1)}, u32[]{:S(2)}, u32[]{:S(2)}) %collective-permute-start.2) | collective-permute-done | bytes 1310752 | tf_op jit(solution)/shard_map/ppermute | solution.py:121
  140.8 0.8 fusion.133
  141.7 0.8 fusion.130
  142.5 0.8 fusion.127
  143.4 1.7 %fusion.124 = f32[160,1024]{1,0:T(8,128)} fusion(f32[160,1024]{1,0:T(8,128)S(1)} %fusion.133, f32[160,1024]{1,0:T(8,128)S(1)} %fusion.130, f32[160,1024]{1,0:T(8,128)S(1)} %fusion.127, bf16[4,1024,1024]{2,1,0:T(8,128)(2,1)S(1)} %copy-done, bf16[4,160,1024]{2,1,0:T(8,128)(2,1)S(1)} %collective-permute-done.2, f32[1024]{0:T(1024)S(1)} %bitcast.192), kind=kOutput, calls=%fused_computation.68 | convolution fusion | flops 336363520 | bytes 5050368 | tf_op jit(solution)/shard_map/dot_general | solution.py:16
  145.2 1.3 collective-permute-start.10
  146.6 1.1 fusion.191
  147.8 1.8 %collective-permute-done.10 = f32[160,1024]{1,0:T(8,128)} collective-permute-done((f32[160,1024]{1,0:T(8,128)}, f32[160,1024]{1,0:T(8,128)}, u32[]{:S(2)}, u32[]{:S(2)}) %collective-permute-start.10) | collective-permute-done | bytes 655392 | tf_op jit(solution)/shard_map/ppermute | solution.py:59
  149.6 1.4 add.93
  151.0 3.4 %collective-permute-start.13 = (f32[160,1024]{1,0:T(8,128)S(1)}, f32[160,1024]{1,0:T(8,128)S(1)}, u32[]{:S(2)}, u32[]{:S(2)}) collective-permute-start(f32[160,1024]{1,0:T(8,128)S(1)} %add.93), channel_id=1, source_target_pairs={{0,2},{5,7},{10,8},{15,13},{16,18},{21,23},{26,24},{31,29}} | collective-permute-start | bytes 1966088 | tf_op jit(solution)/shard_map/ppermute | solution.py:69
  154.4 8.0 %collective-permute-done.13 = f32[160,1024]{1,0:T(8,128)S(1)} collective-permute-done((f32[160,1024]{1,0:T(8,128)S(1)}, f32[160,1024]{1,0:T(8,128)S(1)}, u32[]{:S(2)}, u32[]{:S(2)}) %collective-permute-start.13) | collective-permute-done | bytes 655392 | tf_op jit(solution)/shard_map/ppermute | solution.py:69
  162.4 0.3 fusion.181
  162.8 1.1 pad_maximum_fusion
  (18 shorter events, 0.9 us)
Async XLA Ops:
  0.0 51.4 %collective-permute-start = (bf16[4,256,1024]{2,1,0:T(8,128)(2,1)}, bf16[4,256,1024]{2,1,0:T(8,128)(2,1)S(1)}, u32[]{:S(2)}, u32[]{:S(2)}) collective-permute-start(bf16[4,256,1024]{2,1,0:T(8,128)(2,1)} %param.4), channel_id=1, source_target_pairs={{0,12},{4,0},{8,4},{12,8},{1,13},{5,1},{9,5},{13,9},{2,14},{6,2},{... | collective-permute-start | bytes 6291464 | tf_op jit(solution)/shard_map/ppermute | solution.py:116
  5.9 5.7 %copy-start = (bf16[4,1024,1024]{2,1,0:T(8,128)(2,1)S(1)}, bf16[4,1024,1024]{2,1,0:T(8,128)(2,1)}, u32[]{:S(2)}) copy-start(bf16[4,1024,1024]{2,1,0:T(8,128)(2,1)} %param.3) | copy-start | bytes 25165828
  11.6 2.0 %copy-start.1 = (bf16[4,256,1024]{2,1,0:T(8,128)(2,1)S(1)}, bf16[4,256,1024]{2,1,0:T(8,128)(2,1)}, u32[]{:S(2)}) copy-start(bf16[4,256,1024]{2,1,0:T(8,128)(2,1)} %param.4) | copy-start | bytes 6291460
  14.5 4.6 %collective-permute-start.6 = (f32[256,1024]{1,0:T(8,128)S(1)}, f32[256,1024]{1,0:T(8,128)S(1)}, u32[]{:S(2)}, u32[]{:S(2)}) collective-permute-start(f32[256,1024]{1,0:T(8,128)S(1)} %fusion.82), channel_id=1, source_target_pairs={{1,0},{3,2},{4,5},{6,7},{9,8},{11,10},{12,13},{14,15},{17,16},{19,... | collective-permute-start | bytes 3145736 | tf_op jit(solution)/shard_map/ppermute | solution.py:59
  15.8 81.4 %collective-permute-start.3 = (bf16[4,256,1024]{2,1,0:T(8,128)(2,1)S(1)}, bf16[4,256,1024]{2,1,0:T(8,128)(2,1)S(1)}, u32[]{:S(2)}, u32[]{:S(2)}) collective-permute-start(bf16[4,256,1024]{2,1,0:T(8,128)(2,1)S(1)} %copy-done.1), channel_id=1, source_target_pairs={{0,4},{4,8},{8,12},{12,0},{1,5},{5,9},{9,13},{13,1},{2,6},{6,10},{... | collective-permute-start | bytes 6291464 | tf_op jit(solution)/shard_map/ppermute | solution.py:117
  19.2 99.3 %collective-permute-start.7 = (f32[256,1024]{1,0:T(8,128)S(1)}, f32[256,1024]{1,0:T(8,128)S(1)}, u32[]{:S(2)}, u32[]{:S(2)}) collective-permute-start(f32[256,1024]{1,0:T(8,128)S(1)} %add.89), channel_id=1, source_target_pairs={{2,0},{7,5},{8,10},{13,15},{18,16},{23,21},{24,26},{29,31}} | collective-permute-start | bytes 3145736 | tf_op jit(solution)/shard_map/ppermute | solution.py:69
  51.5 61.6 %collective-permute-start.5 = (bf16[4,96,1024]{2,1,0:T(8,128)(2,1)S(1)}, bf16[4,96,1024]{2,1,0:T(8,128)(2,1)S(1)}, u32[]{:S(2)}, u32[]{:S(2)}) collective-permute-start(bf16[4,96,1024]{2,1,0:T(8,128)(2,1)S(1)} %slice.33), channel_id=1, source_target_pairs={{0,12},{4,0},{8,4},{12,8},{1,13},{5,1},{9,5},{13,9},{2,14},{6,2},{... | collective-permute-start | bytes 2359304 | tf_op jit(solution)/shard_map/ppermute | solution.py:118
  58.8 43.1 %collective-permute-start.1 = (f32[256,1024]{1,0:T(8,128)S(1)}, f32[256,1024]{1,0:T(8,128)S(1)}, u32[]{:S(2)}, u32[]{:S(2)}) collective-permute-start(f32[256,1024]{1,0:T(8,128)S(1)} %fusion.52), channel_id=1, source_target_pairs={{0,1},{2,3},{5,4},{7,6},{8,9},{10,11},{13,12},{15,14},{16,17},{18,... | collective-permute-start | bytes 3145736 | tf_op jit(solution)/shard_map/ppermute | solution.py:59
  100.5 18.2 %collective-permute-start.4 = (f32[256,1024]{1,0:T(8,128)S(1)}, f32[256,1024]{1,0:T(8,128)S(1)}, u32[]{:S(2)}, u32[]{:S(2)}) collective-permute-start(f32[256,1024]{1,0:T(8,128)S(1)} %fusion.67), channel_id=1, source_target_pairs={{0,1},{2,3},{5,4},{7,6},{8,9},{10,11},{13,12},{15,14},{16,17},{18,... | collective-permute-start | bytes 3145736 | tf_op jit(solution)/shard_map/ppermute | solution.py:59
  102.2 38.6 %collective-permute-start.2 = (bf16[4,160,1024]{2,1,0:T(8,128)(2,1)S(1)}, bf16[4,160,1024]{2,1,0:T(8,128)(2,1)S(1)}, u32[]{:S(2)}, u32[]{:S(2)}) collective-permute-start(bf16[4,160,1024]{2,1,0:T(8,128)(2,1)S(1)} %slice.32), channel_id=1, source_target_pairs={{0,12},{4,0},{8,4},{12,8},{1,13},{5,1},{9,5},{13,9},{2,14},{6,2},{... | collective-permute-start | bytes 3932168 | tf_op jit(solution)/shard_map/ppermute | solution.py:121
  113.9 11.2 %collective-permute-start.8 = (f32[256,1024]{1,0:T(8,128)S(1)}, f32[256,1024]{1,0:T(8,128)S(1)}, u32[]{:S(2)}, u32[]{:S(2)}) collective-permute-start(f32[256,1024]{1,0:T(8,128)S(1)} %add.78), channel_id=1, source_target_pairs={{3,1},{4,6},{9,11},{14,12},{19,17},{20,22},{25,27},{30,28}} | collective-permute-start | bytes 3145736 | tf_op jit(solution)/shard_map/ppermute | solution.py:69
  117.3 3.6 %collective-permute-start.11 = (f32[96,1024]{1,0:T(8,128)S(1)}, f32[96,1024]{1,0:T(8,128)S(1)}, u32[]{:S(2)}, u32[]{:S(2)}) collective-permute-start(f32[96,1024]{1,0:T(8,128)S(1)} %fusion.157), channel_id=1, source_target_pairs={{1,0},{3,2},{4,5},{6,7},{9,8},{11,10},{12,13},{14,15},{17,16},{19,... | collective-permute-start | bytes 1179656 | tf_op jit(solution)/shard_map/ppermute | solution.py:59
  120.9 25.7 %collective-permute-start.12 = (f32[96,1024]{1,0:T(8,128)S(1)}, f32[96,1024]{1,0:T(8,128)}, u32[]{:S(2)}, u32[]{:S(2)}) collective-permute-start(f32[96,1024]{1,0:T(8,128)S(1)} %add.97), channel_id=1, source_target_pairs={{0,2},{5,7},{10,8},{15,13},{16,18},{21,23},{26,24},{31,29}} | collective-permute-start | bytes 1179656 | tf_op jit(solution)/shard_map/ppermute | solution.py:69
  125.3 19.8 %collective-permute-start.9 = (f32[256,1024]{1,0:T(8,128)S(1)}, f32[256,1024]{1,0:T(8,128)S(1)}, u32[]{:S(2)}, u32[]{:S(2)}) collective-permute-start(f32[256,1024]{1,0:T(8,128)S(1)} %add.85), channel_id=1, source_target_pairs={{1,3},{6,4},{11,9},{12,14},{17,19},{22,20},{27,25},{28,30}} | collective-permute-start | bytes 3145736 | tf_op jit(solution)/shard_map/ppermute | solution.py:69
  145.2 4.3 %collective-permute-start.10 = (f32[160,1024]{1,0:T(8,128)}, f32[160,1024]{1,0:T(8,128)}, u32[]{:S(2)}, u32[]{:S(2)}) collective-permute-start(f32[160,1024]{1,0:T(8,128)} %fusion.124), channel_id=1, source_target_pairs={{1,0},{3,2},{4,5},{6,7},{9,8},{11,10},{12,13},{14,15},{17,16},{19,... | collective-permute-start | bytes 1966088 | tf_op jit(solution)/shard_map/ppermute | solution.py:59
  151.0 11.5 %collective-permute-start.13 = (f32[160,1024]{1,0:T(8,128)S(1)}, f32[160,1024]{1,0:T(8,128)S(1)}, u32[]{:S(2)}, u32[]{:S(2)}) collective-permute-start(f32[160,1024]{1,0:T(8,128)S(1)} %add.93), channel_id=1, source_target_pairs={{0,2},{5,7},{10,8},{15,13},{16,18},{21,23},{26,24},{31,29}} | collective-permute-start | bytes 1966088 | tf_op jit(solution)/shard_map/ppermute | solution.py:69
